TPU v7x, 32 devices: a whole 2x2x4 slice. The times are simulated.
32 devices in a mesh: row: 8 (over y, x, core), col: 4 (over z).
Axes of the slice: x: 2, y: 2, z: 4, core: 2. Of those that a mesh axis runs over, the one named last changes fastest.
Arguments:
- features: bfloat16 [16384, 256], P('col', 'row'), may hold values from -6 to 6
- weight: bfloat16 [256, 256], replicated, may hold values from -0.375 to 0.375
- adj_values: bfloat16 [8, 4, 96, 128, 128], P('row', 'col'), may hold values from -0.125 to 0.125
- block_rows: int32 [8, 4, 96], P('row', 'col'), may hold values from 0 to 15, as said below
- block_cols: int32 [8, 4, 96], P('row', 'col'), may hold values from 0 to 31
- block_counts: int32 [8, 4], P('row', 'col'), may hold values from 1 to 96, as said below
- cotangent: bfloat16 [16384, 256], P(('row', 'col')), may hold values from -6 to 6
Outputs:
- output: bfloat16 [16384, 256], P(('row', 'col'))
- grad_weight: float32 [256, 256], replicated
- grad_features: bfloat16 [16384, 256], P('col', 'row')
Inputs may be any that keep to these rules, and one draw needn't show every extreme that they name: Within one tile the pairs (block_rows, block_cols) over all 96 slots are distinct. `block_counts`: some tile holds exactly 96 live blocks and some other tile exactly one in every draw.
All inputs are finite; a program needn't handle non-finite values.
Results may differ from a plain program's by a relative error of at most 0.029.
Values may be sent and summed in bfloat16 or wider, within the bound.
No kernel may reach another device: no remote copies, remote signals or barrier semaphores. Data moves between devices by JAX's collectives and lax.ppermute only.
A program may use at most 64 MiB of HBM per device.

v0:
```python
import functools
import math

import jax
import jax.numpy as jnp
from jax import lax
from jax.experimental import pallas as pl
from jax.experimental.pallas import tpu as pltpu
from jax.sharding import PartitionSpec as P

VMEM = pl.BlockSpec(memory_space=pltpu.VMEM)
SMEM = pl.BlockSpec(memory_space=pltpu.SMEM)
HBM = pl.BlockSpec(memory_space=pltpu.HBM)
MIB = 1024 * 1024
NT = (((1,), (1,)), ((), ()))
NN = (((1,), (0,)), ((), ()))


COST = pl.CostEstimate(flops=1, bytes_accessed=1, transcendentals=0)


def params(mib):
    return pltpu.CompilerParams(vmem_limit_bytes=mib * MIB)


def fuse(name, function, *values):
    shapes = jax.eval_shape(function, *values)

    def kernel(*refs):
        results = function(*[ref[...] for ref in refs[: len(values)]])
        for ref, result in zip(refs[len(values) :], results):
            ref[...] = result

    return pl.pallas_call(
        kernel,
        out_shape=shapes,
        in_specs=[VMEM] * len(values),
        out_specs=[VMEM] * len(shapes),
        compiler_params=params(4),
        cost_estimate=COST,
        name=name,
    )(*values)


def turn_of(slots):
    return math.gcd(slots, 8)


def product_loop(count, source_ids, target_ids, adj, source, total, dims):
    turn = turn_of(adj.shape[0])
    spare = total.shape[0] - 1
    total[...] = jnp.zeros_like(total)

    def step(index, carry):
        first = index * turn
        for k in range(turn):
            slot = first + k
            product = lax.dot_general(
                source[source_ids[slot]], adj[slot], dims, preferred_element_type=jnp.float32
            )
            target = jnp.where(slot < count, target_ids[slot], spare)
            total[target] += product
        return carry

    lax.fori_loop(0, (count + turn - 1) // turn, step, 0)


def fetch_kernel(count, rows, cols, features, tile, *refs):
    outs, (sem, small_sem) = refs[:5], refs[5:]
    half = features.shape[0] // 2
    sources = (rows, cols, features.at[pl.ds(0, half)], features.at[pl.ds(half, half)])
    small = [
        pltpu.make_async_copy(source, target, small_sem.at[n])
        for n, (source, target) in enumerate(zip(sources, outs))
    ]
    for copy in small:
        copy.start()
    turn = turn_of(tile.shape[0])

    def copy_turn(index):
        blocks = pl.ds(index * turn, turn)
        return pltpu.make_async_copy(tile.at[blocks], outs[4].at[blocks], sem.at[index])

    def begin(index, carry):
        copy_turn(index).start()
        return carry

    def wait(index, carry):
        copy_turn(index).wait()
        return carry

    turns = (count[0, 0] + turn - 1) // turn
    lax.fori_loop(0, turns, begin, 0)
    lax.fori_loop(0, turns, wait, 0)
    for copy in small:
        copy.wait()


def fetch(count, rows, cols, features, tile):
    arrays = (rows, cols, features, tile)
    half = jax.ShapeDtypeStruct((features.shape[0] // 2, features.shape[1]), features.dtype)
    outs = [jax.ShapeDtypeStruct(array.shape, array.dtype) for array in (rows, cols)] + [half] * 2
    return pl.pallas_call(
        fetch_kernel,
        out_shape=outs + [jax.ShapeDtypeStruct(tile.shape, tile.dtype)],
        in_specs=[SMEM] + [HBM] * 4,
        out_specs=[VMEM] * 5,
        scratch_shapes=[
            pltpu.SemaphoreType.DMA((tile.shape[0] // turn_of(tile.shape[0]),)),
            pltpu.SemaphoreType.DMA((4,)),
        ],
        compiler_params=params(4),
        cost_estimate=COST,
        name="fetch",
    )(count, *[pltpu.with_memory_space_constraint(array, pltpu.HBM) for array in arrays])


def forward_kernel(n_parts, depths, layout, place, count, rows, cols, adj, *refs):
    parts = refs[:n_parts]
    outs = refs[n_parts:-2]
    source, total = refs[-2:]
    size = adj.shape[1]
    row = 0
    for part in parts:
        depth = part.shape[0]
        for c in range(source.shape[0]):
            source[c, row : row + depth, :] = part[:, c * size : (c + 1) * size]
        row += depth
    product_loop(count[0, 0], cols, rows, adj, source, total, NT)
    blocks = outs[0].shape[1] // size
    outs = iter(outs)
    row = 0
    for depth in depths:
        for chunks in layout:
            out = next(outs)
            for n, k in enumerate(chunks):
                first = (place[0] ^ k) * blocks
                for i in range(blocks):
                    out[n * depth : (n + 1) * depth, i * size : (i + 1) * size] = total[
                        first + i, row : row + depth, :
                    ].astype(out.dtype)
        row += depth


def forward(place, count, rows, cols, adj, parts, row_blocks, depths, layout):
    size = adj.shape[1]
    col_blocks = parts[0].shape[1] // size
    wide = row_blocks * size // sum(len(chunks) for chunks in layout)
    outs = [
        jax.ShapeDtypeStruct((len(chunks) * depth, wide), jnp.bfloat16)
        for depth in depths
        for chunks in layout
    ]
    return pl.pallas_call(
        functools.partial(forward_kernel, len(parts), depths, layout),
        out_shape=outs,
        in_specs=[SMEM] * 4 + [VMEM] * (1 + len(parts)),
        out_specs=[VMEM] * len(outs),
        scratch_shapes=[
            pltpu.VMEM((col_blocks, sum(depths), size), jnp.bfloat16),
            pltpu.VMEM((row_blocks + 1, sum(depths), size), jnp.float32),
        ],
        compiler_params=params(14),
        cost_estimate=COST,
        name="forward_products",
    )(place, count, rows, cols, adj, *parts)


def backward_kernel(spots, depths, place, count, rows, cols, adj, *refs):
    n_parts = 1 + max(part for places in spots for part, _ in places)
    parts = refs[:n_parts]
    outs = refs[n_parts:-2]
    source, total = refs[-2:]
    size = adj.shape[1]
    blocks = parts[0].shape[1] // size
    for k, places in enumerate(spots):
        first = (place[0] ^ k) * blocks
        row = 0
        for (part, offset), depth in zip(places, depths):
            for i in range(blocks):
                source[first + i, row : row + depth, :] = parts[part][
                    offset : offset + depth, i * size : (i + 1) * size
                ]
            row += depth
    product_loop(count[0, 0], rows, cols, adj, source, total, NN)
    row = 0
    for out in outs:
        depth = out.shape[0]
        for c in range(total.shape[0] - 1):
            out[:, c * size : (c + 1) * size] = total[c, row : row + depth, :].astype(out.dtype)
        row += depth


def backward(place, count, rows, cols, adj, parts, spots, depths, out_depths, col_blocks):
    size = adj.shape[1]
    row_blocks = len(spots) * parts[0].shape[1] // size
    return pl.pallas_call(
        functools.partial(backward_kernel, spots, depths),
        out_shape=[jax.ShapeDtypeStruct((depth, col_blocks * size), jnp.bfloat16) for depth in out_depths],
        in_specs=[SMEM] * 4 + [VMEM] * (1 + len(parts)),
        out_specs=[VMEM] * len(out_depths),
        scratch_shapes=[
            pltpu.VMEM((row_blocks, sum(out_depths), size), jnp.bfloat16),
            pltpu.VMEM((col_blocks + 1, sum(out_depths), size), jnp.float32),
        ],
        compiler_params=params(14),
        cost_estimate=COST,
        name="backward_products",
    )(place, count, rows, cols, adj, *parts)


def middle_kernel(sizes, order, n_sum, n_row, row, weight, cotangent, *refs):
    terms = refs[: n_sum * len(sizes)]
    outs = refs[n_sum * len(sizes) : -1]
    output, deltas, aggregated, *backs = outs
    ordered = refs[-1]
    depth = weight.shape[0] // n_row
    for j in range(n_row):
        first = pl.multiple_of((row[0] ^ j) * depth, depth)
        ordered[j * depth : (j + 1) * depth, :] = weight[pl.ds(first, depth), :]
    first = 0
    for p, size in enumerate(sizes):
        summed = terms[p * n_sum][:size, :].astype(jnp.float32)
        for k in range(1, n_sum):
            summed += terms[p * n_sum + k][:size, :].astype(jnp.float32)
        aggregated[first : first + size, :] = summed.astype(jnp.bfloat16)
        first += size
    nodes_first = aggregated[...].T
    preact = jnp.dot(nodes_first, ordered[...], preferred_element_type=jnp.float32)
    gate = jax.nn.sigmoid(preact)
    output[...] = (preact * gate).astype(jnp.bfloat16)
    slopes = gate * (1.0 + preact * (1.0 - gate))
    delta = (cotangent[...].astype(jnp.float32) * slopes).astype(jnp.bfloat16)
    deltas[...] = delta
    product = lax.dot_general(ordered[...], delta, NT, preferred_element_type=jnp.float32)
    product = product.astype(jnp.bfloat16)
    rows = [product[k * depth : (k + 1) * depth, :] for k in order]
    product = jnp.concatenate(rows)
    first = 0
    for back in backs:
        back[...] = product[first : first + back.shape[0], :]
        first += back.shape[0]


def middle(n_row, row, weight, cotangent, pieces, order, depths):
    sizes = [piece[0].shape[0] for piece in pieces]
    nodes = cotangent.shape[0]
    features = weight.shape[0]
    shape = jax.ShapeDtypeStruct
    outs = [
        shape((nodes, features), jnp.bfloat16),
        shape((nodes, features), jnp.bfloat16),
        shape((features, nodes), jnp.bfloat16),
    ] + [shape((depth, nodes), jnp.bfloat16) for depth in depths]
    flat = [term for piece in pieces for term in piece]
    return pl.pallas_call(
        functools.partial(middle_kernel, sizes, order, len(pieces[0]), n_row),
        out_shape=outs,
        in_specs=[SMEM] + [VMEM] * (2 + len(flat)),
        out_specs=[VMEM] * len(outs),
        scratch_shapes=[pltpu.VMEM(weight.shape, jnp.bfloat16)],
        compiler_params=params(10),
        cost_estimate=COST,
        name="layer",
    )(row, weight, cotangent, *flat)


def gradient_kernel(scale, order, aggregated, deltas, *outs):
    product = jnp.dot(aggregated[...], deltas[...], preferred_element_type=jnp.float32) * scale
    for out, chunks in zip(outs, order):
        depth = out.shape[1]
        for n, k in enumerate(chunks):
            out[n] = product[k * depth : (k + 1) * depth, :]


def gradient(scale, order, aggregated, deltas):
    depth = aggregated.shape[0] // sum(len(chunks) for chunks in order)
    outs = [jax.ShapeDtypeStruct((len(chunks), depth, deltas.shape[1]), jnp.float32) for chunks in order]
    return pl.pallas_call(
        functools.partial(gradient_kernel, scale, order),
        out_shape=outs,
        in_specs=[VMEM] * 2,
        out_specs=[VMEM] * len(outs),
        compiler_params=params(6),
        cost_estimate=COST,
        name="weight_gradient",
    )(aggregated, deltas)


def swap(value, axis, k):
    size = lax.axis_size(axis)
    return lax.ppermute(value, axis, [(i, i ^ k) for i in range(size)])


def wide_sum(*values):
    total = values[0].astype(jnp.float32)
    for value in values[1:]:
        total = total + value.astype(jnp.float32)
    return (total.astype(values[0].dtype),)


def after(value, *earlier):
    return lax.optimization_barrier((value, *earlier))[0]


def stack(*values):
    return (jnp.concatenate(values),)


def with_chunk(mine, other, *parts):
    total = functools.reduce(jnp.add, parts)
    high = total.astype(jnp.bfloat16)
    low = (total - high.astype(jnp.float32)).astype(jnp.bfloat16)
    return (jnp.concatenate([mine, other, jnp.concatenate([high, low], axis=1)]),)


def chunk_sum(depth, *values):
    total = None
    for value in values:
        halves = value[-depth:].astype(jnp.float32)
        wide = halves.shape[1] // 2
        chunk = halves[:, :wide] + halves[:, wide:]
        total = chunk if total is None else total + chunk
    return (total,)


def pair_sum(mine, *received):
    return tuple(mine + jnp.concatenate(received))


def row_payloads(depth, chunk, sibling, mine, *received):
    total = (mine.astype(jnp.float32) + jnp.concatenate(received).astype(jnp.float32)).astype(mine.dtype)
    gradient_chunks = jnp.concatenate([chunk.astype(mine.dtype), sibling.astype(mine.dtype)], axis=1)
    parts = [total[first : first + depth] for first in range(0, total.shape[0], depth)]
    return parts[0], *[jnp.concatenate([part, gradient_chunks], axis=1) for part in parts[1:]]


def finish_kernel(row, chunk, sibling, mine, *refs):
    received = refs[:-2]
    grad_features, grad_weight = refs[-2:]
    depth, nodes = mine.shape
    total = mine[...].astype(jnp.float32)
    for part in received:
        total += part[:, :nodes].astype(jnp.float32)
    grad_features[...] = total.astype(mine.dtype)
    wide = grad_weight.shape[1]
    own = [ref[...].astype(mine.dtype) for ref in (chunk, sibling)]
    chunks = own + [part[:, nodes + n * wide : nodes + (n + 1) * wide] for part in received for n in range(2)]
    for k, value in enumerate(chunks):
        first = pl.multiple_of((row[0] ^ k) * depth, depth)
        grad_weight[pl.ds(first, depth), :] = value.astype(jnp.float32)


def finish(row, chunk, sibling, mine, received):
    n_chunks = 2 * (1 + len(received))
    return pl.pallas_call(
        finish_kernel,
        out_shape=[
            jax.ShapeDtypeStruct(mine.shape, mine.dtype),
            jax.ShapeDtypeStruct((n_chunks * chunk.shape[0], chunk.shape[1]), jnp.float32),
        ],
        in_specs=[SMEM] + [VMEM] * (3 + len(received)),
        out_specs=[VMEM] * 2,
        compiler_params=params(8),
        cost_estimate=COST,
        name="finish",
    )(row, chunk, sibling, mine, *received)


def shards_exchanged(features, weight, adj_values, block_rows, block_cols, block_counts, cotangent):
    n_row = lax.axis_size("row")
    n_col = lax.axis_size("col")
    adj = adj_values[0, 0]
    rows = block_rows[0, 0]
    cols = block_cols[0, 0]
    count = block_counts
    size = adj.shape[1]
    nodes = cotangent.shape[0] * n_row * n_col
    row_blocks = cotangent.shape[0] * n_col // size
    col_blocks = features.shape[0] // size
    row = lax.axis_index("row").reshape(1)
    col = lax.axis_index("col").reshape(1)
    own = after(features.T, row, col)

    depth = features.shape[1]
    near = [k for k in range(2, n_row, 2) if k & (k - 1) == 0]
    far = [k for k in range(2, n_row, 2) if k & (k - 1) != 0]
    sibling = swap(own, "row", 1)
    from_near = [swap(own, "row", k) for k in near]
    rows, cols, *halves, tile = fetch(count, rows, cols, own, adj)
    from_near = [after(part, tile) for part in from_near]
    from_far = [swap(half, "row", k) for k in far for half in halves]

    def pass_on(beyond, received):
        return wide_sum(beyond, received[beyond.shape[0] :])

    def forward_pieces(parts, depths):
        outs = forward(col, count, rows, cols, tile, parts, row_blocks, depths, [(0,), (2,), (1, 3)])
        outs = [outs[n : n + 3] for n in range(0, len(outs), 3)]
        return [(kept, beyond, swap(sent, "col", 1)) for kept, beyond, sent in outs]

    def fold(piece, *earlier):
        kept, beyond, received = piece
        received = after(received, *earlier)
        (passed,) = fuse("pass_on", pass_on, beyond, received)
        return [kept, received, swap(passed, "col", 2)]

    n_near = 2 * depth * (1 + len(near))
    cut = n_near // 2 + 16
    parts = [own, sibling] + [piece for part in from_near for piece in (part, swap(part, "row", 1))]
    pieces = forward_pieces(parts, [cut, n_near - cut])
    from_far = [after(part, pieces[0][0]) for part in from_far]
    parts = []
    for n in range(0, len(from_far), 2):
        halves = from_far[n : n + 2]
        parts += halves + [swap(half, "row", 1) for half in halves]
    pieces += forward_pieces(parts, [2 * depth * len(far)])
    sums = []
    for piece in pieces:
        sums.append(fold(piece, *(sums[-1][1:2] if sums else ())))

    evens = tuple(range(0, n_row, 2))
    odds = tuple(range(1, n_row, 2))
    n_all = weight.shape[0]
    cut = n_all // 2 + 16
    cuts = [cut, n_all - cut]
    output, deltas, aggregated, *backs = middle(n_row, row, weight, cotangent, sums, evens + odds, cuts)
    beyond = [swap(back, "col", 2) for back in backs]

    even, *odd = gradient(1.0 / math.sqrt(nodes), [evens, odds[:2], odds[2:]], aggregated, deltas)
    chunk, *sent = fuse("gradient_sum", pair_sum, even, *[swap(part, "row", 1) for part in odd])
    from_rows = [swap(part, "row", k) for part, k in zip(sent, evens[1:])]
    (chunk,) = fuse("chunk_sum", wide_sum, chunk, *from_rows)
    chunks = [chunk, swap(chunk, "col", 2)]

    (large,) = fuse("stack", stack, backs[0], beyond[0])
    (small,) = fuse("with_chunk", with_chunk, backs[1], after(beyond[1], large), *chunks)
    large_received, small_received = swap(large, "col", 1), swap(small, "col", 1)
    (chunk,) = fuse("chunk_sum", functools.partial(chunk_sum, depth), small, small_received)

    mine, *sent = backward(
        col,
        count,
        rows,
        cols,
        tile,
        [*backs, *beyond, after(large_received, chunk), small_received],
        [[(0, 0), (1, 0)], [(4, 0), (5, 0)], [(2, 0), (3, 0)], [(4, cuts[0]), (5, cuts[1])]],
        cuts,
        [n_all // 2] + [n_all // 4] * 2,
        col_blocks,
    )
    from_sibling = [swap(part, "row", 1) for part in sent]
    sibling_chunk = swap(chunk, "row", 1)
    own_sum, *sums = fuse(
        "row_payloads", functools.partial(row_payloads, depth), chunk, sibling_chunk, mine, *from_sibling
    )
    received = [swap(part, "row", k) for part, k in zip(sums, evens[1:])]
    grad_features, grad_weight = finish(row, chunk, sibling_chunk, own_sum, received)
    return output, grad_weight, grad_features.T


def shards_gathered(features, weight, adj_values, block_rows, block_cols, block_counts, cotangent):
    n_row = lax.axis_size("row")
    n_col = lax.axis_size("col")
    adj = adj_values[0, 0]
    rows = block_rows[0, 0]
    cols = block_cols[0, 0]
    count = block_counts
    size = adj.shape[1]
    nodes = cotangent.shape[0] * n_row * n_col
    row_blocks = cotangent.shape[0] * n_col // size
    col_blocks = features.shape[0] // size
    zero = jnp.zeros((1,), jnp.int32)
    panels = lax.all_gather(features.T, "row", axis=0, tiled=True)
    (terms,) = forward(zero, count, rows, cols, adj, [panels], row_blocks, [panels.shape[0]], [(0,)])
    part = lax.psum_scatter(terms, "col", scatter_dimension=1, tiled=True)
    output, deltas, aggregated, back = middle(1, zero, weight, cotangent, [[part]], (0,), [weight.shape[0]])
    slab = lax.all_gather(back, "col", axis=1, tiled=True)
    (column_terms,) = backward(zero, count, rows, cols, adj, [slab], [[(0, 0)]], [slab.shape[0]], [slab.shape[0]], col_blocks)
    grad_features = lax.psum_scatter(column_terms, "row", scatter_dimension=0, tiled=True).T
    (part,) = gradient(1.0 / math.sqrt(nodes), [(0,)], aggregated, deltas)
    grad_weight = lax.psum(part[0], ("row", "col"))
    return output, grad_weight, grad_features


def solution(mesh):
    n_row = mesh.shape["row"]
    n_col = mesh.shape["col"]
    exchanged = n_row == 8 and n_col == 4
    return jax.shard_map(
        shards_exchanged if exchanged else shards_gathered,
        mesh=mesh,
        in_specs=(
            P("col", "row"),
            P(),
            P("row", "col", None, None, None),
            P("row", "col", None),
            P("row", "col", None),
            P("row", "col"),
            P(("row", "col"), None),
        ),
        out_specs=(P(("row", "col"), None), P(), P("col", "row")),
        check_vma=False,
    )
```

profile of v0, /device:TPU:0, one launch (start us, length us, event | category | flops | bytes accessed | tf_op | source)
XLA Modules:
  0.0 96.1 jit_solution(18256063489372674064)
XLA Ops:
  0.6 3.0 %collective-permute-start.1 = (bf16[32,4096]{1,0:T(8,128)(2,1)}, bf16[32,4096]{1,0:T(8,128)(2,1)S(1)}, u32[]{:S(2)}, u32[]{:S(2)}) collective-permute-start(bf16[32,4096]{1,0:T(8,128)(2,1)} %bitcast.7), channel_id=1, source_target_pairs={{0,8},{4,12},{8,0},{12,4},{16,24},{20,28},{24,16},{28,20},{1,9},{5... | collective-permute-start | bytes 786440 | tf_op jit(solution)/shard_map/ppermute | solution.py:292
  3.7 1.5 %collective-permute-start.3 = (bf16[32,4096]{1,0:T(8,128)(2,1)}, bf16[32,4096]{1,0:T(8,128)(2,1)S(1)}, u32[]{:S(2)}, u32[]{:S(2)}) collective-permute-start(bf16[32,4096]{1,0:T(8,128)(2,1)} %bitcast.8), channel_id=1, source_target_pairs={{0,16},{4,20},{8,24},{12,28},{16,0},{20,4},{24,8},{28,12},{1,17},{... | collective-permute-start | bytes 786440 | tf_op jit(solution)/shard_map/ppermute | solution.py:292
  5.8 2.1 %fetch.1 = (s32[96]{0:T(128)S(1)}, s32[96]{0:T(128)S(1)}, bf16[16,4096]{1,0:T(8,128)(2,1)S(1)}, bf16[16,4096]{1,0:T(8,128)(2,1)S(1)}, bf16[96,128,128]{2,1,0:T(8,128)(2,1)S(1)}) custom-call(s32[1,1]{1,0:T(1,128)S(6)} %copy.10.count, s32[96]{0:T(128)} %bitcast.13, s32[96]{0:T(128)} %bitcast.14, bf16[32,4096]{1,0:T(8,128)(2,1)} %bitcast.10, ...), custom_call_target="tpu_custom_call" | custom-call | flops 1 | bytes 1 | tf_op jit(solution)/shard_map/fetch/pallas_call | solution.py:103
  7.9 2.3 %collective-permute-done.1.refs_2_ = bf16[32,4096]{1,0:T(8,128)(2,1)S(1)} collective-permute-done((bf16[32,4096]{1,0:T(8,128)(2,1)}, bf16[32,4096]{1,0:T(8,128)(2,1)S(1)}, u32[]{:S(2)}, u32[]{:S(2)}) %collective-permute-start.1) | collective-permute-done | bytes 262176 | tf_op jit(solution)/shard_map/ppermute | solution.py:292
  10.2 1.5 %collective-permute-done.3.refs_4_ = bf16[32,4096]{1,0:T(8,128)(2,1)S(1)} collective-permute-done((bf16[32,4096]{1,0:T(8,128)(2,1)}, bf16[32,4096]{1,0:T(8,128)(2,1)S(1)}, u32[]{:S(2)}, u32[]{:S(2)}) %collective-permute-start.3) | collective-permute-done | bytes 262176 | tf_op jit(solution)/shard_map/ppermute | solution.py:292
  11.6 1.7 %collective-permute-start.10 = (bf16[16,4096]{1,0:T(8,128)(2,1)S(1)}, bf16[16,4096]{1,0:T(8,128)(2,1)S(1)}, u32[]{:S(2)}, u32[]{:S(2)}) collective-permute-start(bf16[16,4096]{1,0:T(8,128)(2,1)S(1)} %get-tuple-element.62), channel_id=1, source_target_pairs={{0,24},{4,28},{8,16},{12,20},{16,8},{20,12},{24,0},{28,4},{1,25},{... | collective-permute-start | bytes 393224 | tf_op jit(solution)/shard_map/ppermute | solution.py:292
  13.4 1.2 %collective-permute-start.9 = (bf16[16,4096]{1,0:T(8,128)(2,1)S(1)}, bf16[16,4096]{1,0:T(8,128)(2,1)S(1)}, u32[]{:S(2)}, u32[]{:S(2)}) collective-permute-start(bf16[16,4096]{1,0:T(8,128)(2,1)S(1)} %get-tuple-element.60), channel_id=1, source_target_pairs={{0,24},{4,28},{8,16},{12,20},{16,8},{20,12},{24,0},{28,4},{1,25},{... | collective-permute-start | bytes 393224 | tf_op jit(solution)/shard_map/ppermute | solution.py:292
  14.6 4.5 %forward_products.2 = (bf16[112,512]{1,0:T(8,128)(2,1)S(1)}, bf16[112,512]{1,0:T(8,128)(2,1)S(1)}, bf16[224,512]{1,0:T(8,128)(2,1)S(1)}, bf16[80,512]{1,0:T(8,12...) custom-call(s32[1]{0:T(128)} %bitcast.1.place, s32[1,1]{1,0:T(1,128)S(6)} %copy.10.count, ...), custom_call_target="tpu_custom_call" | custom-call | flops 1 | bytes 1 | tf_op jit(solution)/shard_map/forward_products/pallas_call | solution.py:154
  19.1 1.6 %collective-permute-start.5 = (bf16[224,512]{1,0:T(8,128)(2,1)S(1)}, bf16[224,512]{1,0:T(8,128)(2,1)S(1)}, u32[]{:S(2)}, u32[]{:S(2)}) collective-permute-start(bf16[224,512]{1,0:T(8,128)(2,1)S(1)} %get-tuple-element.54), channel_id=1, source_target_pairs={{0,1},{1,0},{2,3},{3,2},{4,5},{5,4},{6,7},{7,6},{8,9},{9,8},{10,11... | collective-permute-start | bytes 688136 | tf_op jit(solution)/shard_map/ppermute | solution.py:292
  21.3 1.6 %collective-permute-start.7 = (bf16[160,512]{1,0:T(8,128)(2,1)S(1)}, bf16[160,512]{1,0:T(8,128)(2,1)S(1)}, u32[]{:S(2)}, u32[]{:S(2)}) collective-permute-start(bf16[160,512]{1,0:T(8,128)(2,1)S(1)} %get-tuple-element.57), channel_id=1, source_target_pairs={{0,1},{1,0},{2,3},{3,2},{4,5},{5,4},{6,7},{7,6},{8,9},{9,8},{10,11... | collective-permute-start | bytes 491528 | tf_op jit(solution)/shard_map/ppermute | solution.py:292
  22.8 3.9 %forward_products.3 = (bf16[64,512]{1,0:T(8,128)(2,1)S(1)}, bf16[64,512]{1,0:T(8,128)(2,1)S(1)}, bf16[128,512]{1,0:T(8,128)(2,1)S(1)}) custom-call(s32[1]{0:T(128)} %bitcast.1.place, s32[1,1]{1,0:T(1,128)S(6)} %copy.10.count, s32[96]{0:T(128)S(1)} %get-tuple-element.48.rows, s32[96]{0:T(128)S(1)} %get-tuple-element.49.cols, ...), custom_call_target="tpu_custom_call" | custom-call | flops 1 | bytes 1 | tf_op jit(solution)/shard_map/forward_products/pallas_call | solution.py:154
  26.7 1.4 %collective-permute-start.13 = (bf16[128,512]{1,0:T(8,128)(2,1)S(1)}, bf16[128,512]{1,0:T(8,128)(2,1)S(1)}, u32[]{:S(2)}, u32[]{:S(2)}) collective-permute-start(bf16[128,512]{1,0:T(8,128)(2,1)S(1)} %get-tuple-element.65), channel_id=1, source_target_pairs={{0,1},{1,0},{2,3},{3,2},{4,5},{5,4},{6,7},{7,6},{8,9},{9,8},{10,11... | collective-permute-start | bytes 393224 | tf_op jit(solution)/shard_map/ppermute | solution.py:292
  28.1 2.7 %collective-permute-start.6 = (bf16[112,512]{1,0:T(8,128)(2,1)S(1)}, bf16[112,512]{1,0:T(8,128)(2,1)S(1)}, u32[]{:S(2)}, u32[]{:S(2)}) collective-permute-start(bf16[112,512]{1,0:T(8,128)(2,1)S(1)} %pass_on.3), channel_id=1, source_target_pairs={{0,2},{1,3},{2,0},{3,1},{4,6},{5,7},{6,4},{7,5},{8,10},{9,11},{10,... | collective-permute-start | bytes 344072 | tf_op jit(solution)/shard_map/ppermute | solution.py:292
  30.8 1.3 %collective-permute-start.8 = (bf16[80,512]{1,0:T(8,128)(2,1)S(1)}, bf16[80,512]{1,0:T(8,128)(2,1)S(1)}, u32[]{:S(2)}, u32[]{:S(2)}) collective-permute-start(bf16[80,512]{1,0:T(8,128)(2,1)S(1)} %pass_on.4), channel_id=1, source_target_pairs={{0,2},{1,3},{2,0},{3,1},{4,6},{5,7},{6,4},{7,5},{8,10},{9,11},{10,... | collective-permute-start | bytes 245768 | tf_op jit(solution)/shard_map/ppermute | solution.py:292
  32.2 1.2 %collective-permute-done.13.refs_1_.refs_7_ = bf16[128,512]{1,0:T(8,128)(2,1)S(1)} collective-permute-done((bf16[128,512]{1,0:T(8,128)(2,1)S(1)}, bf16[128,512]{1,0:T(8,128)(2,1)S(1)}, u32[]{:S(2)}, u32[]{:S(2)}) %collective-permute-start.13) | collective-permute-done | bytes 131104 | tf_op jit(solution)/shard_map/ppermute | solution.py:292
  33.4 2.5 %collective-permute-start.14 = (bf16[64,512]{1,0:T(8,128)(2,1)S(1)}, bf16[64,512]{1,0:T(8,128)(2,1)S(1)}, u32[]{:S(2)}, u32[]{:S(2)}) collective-permute-start(bf16[64,512]{1,0:T(8,128)(2,1)S(1)} %pass_on.5), channel_id=1, source_target_pairs={{0,2},{1,3},{2,0},{3,1},{4,6},{5,7},{6,4},{7,5},{8,10},{9,11},{10,... | collective-permute-start | bytes 196616 | tf_op jit(solution)/shard_map/ppermute | solution.py:292
  35.9 5.4 %collective-permute-done.8.refs_5_ = bf16[80,512]{1,0:T(8,128)(2,1)S(1)} collective-permute-done((bf16[80,512]{1,0:T(8,128)(2,1)S(1)}, bf16[80,512]{1,0:T(8,128)(2,1)S(1)}, u32[]{:S(2)}, u32[]{:S(2)}) %collective-permute-start.8) | collective-permute-done | bytes 81952 | tf_op jit(solution)/shard_map/ppermute | solution.py:292
  43.9 2.9 %collective-permute-start.15 = (bf16[112,512]{1,0:T(8,128)(2,1)S(1)}, bf16[112,512]{1,0:T(8,128)(2,1)S(1)}, u32[]{:S(2)}, u32[]{:S(2)}) collective-permute-start(bf16[112,512]{1,0:T(8,128)(2,1)S(1)} %get-tuple-element.69.refs_0_.refs_1_), channel_id=1, source_target_pairs={{0,2},{1,3},{2,0},{3,1},{4,6},{5,7},{6,4},{7,5},{8,10},{9,11},{10,... | collective-permute-start | bytes 344072 | tf_op jit(solution)/shard_map/ppermute | solution.py:292
  47.3 2.0 %collective-permute-start.20 = (f32[32,256]{1,0:T(8,128)S(1)}, f32[32,256]{1,0:T(8,128)S(1)}, u32[]{:S(2)}, u32[]{:S(2)}) collective-permute-start(f32[32,256]{1,0:T(8,128)S(1)} %get-tuple-element.79), channel_id=1, source_target_pairs={{0,16},{4,20},{8,24},{12,28},{16,0},{20,4},{24,8},{28,12},{1,17},{... | collective-permute-start | bytes 98312 | tf_op jit(solution)/shard_map/ppermute | solution.py:292
  49.3 1.2 %collective-permute-start.21 = (f32[32,256]{1,0:T(8,128)S(1)}, f32[32,256]{1,0:T(8,128)S(1)}, u32[]{:S(2)}, u32[]{:S(2)}) collective-permute-start(f32[32,256]{1,0:T(8,128)S(1)} %get-tuple-element.80), channel_id=1, source_target_pairs={{0,24},{4,28},{8,16},{12,20},{16,8},{20,12},{24,0},{28,4},{1,25},{... | collective-permute-start | bytes 98312 | tf_op jit(solution)/shard_map/ppermute | solution.py:292
  51.2 2.9 %collective-permute-done.21.refs_3_ = f32[32,256]{1,0:T(8,128)S(1)} collective-permute-done((f32[32,256]{1,0:T(8,128)S(1)}, f32[32,256]{1,0:T(8,128)S(1)}, u32[]{:S(2)}, u32[]{:S(2)}) %collective-permute-start.21) | collective-permute-done | bytes 32800 | tf_op jit(solution)/shard_map/ppermute | solution.py:292
  55.1 2.1 %collective-permute-start.25 = (bf16[288,512]{1,0:T(8,128)(2,1)S(1)}, bf16[288,512]{1,0:T(8,128)(2,1)S(1)}, u32[]{:S(2)}, u32[]{:S(2)}) collective-permute-start(bf16[288,512]{1,0:T(8,128)(2,1)S(1)} %stack.1), channel_id=1, source_target_pairs={{0,1},{1,0},{2,3},{3,2},{4,5},{5,4},{6,7},{7,6},{8,9},{9,8},{10,11... | collective-permute-start | bytes 884744 | tf_op jit(solution)/shard_map/ppermute | solution.py:292
  57.2 1.9 %collective-permute-done.22.refs_3_ = f32[32,256]{1,0:T(8,128)S(1)} collective-permute-done((f32[32,256]{1,0:T(8,128)S(1)}, f32[32,256]{1,0:T(8,128)S(1)}, u32[]{:S(2)}, u32[]{:S(2)}) %collective-permute-start.22) | collective-permute-done | bytes 32800 | tf_op jit(solution)/shard_map/ppermute | solution.py:292
  59.1 1.3 %collective-permute-start.23 = (bf16[256,512]{1,0:T(8,128)(2,1)S(1)}, bf16[256,512]{1,0:T(8,128)(2,1)S(1)}, u32[]{:S(2)}, u32[]{:S(2)}) collective-permute-start(bf16[256,512]{1,0:T(8,128)(2,1)S(1)} %with_chunk.1.refs_0_), channel_id=1, source_target_pairs={{0,1},{1,0},{2,3},{3,2},{4,5},{5,4},{6,7},{7,6},{8,9},{9,8},{10,11... | collective-permute-start | bytes 786440 | tf_op jit(solution)/shard_map/ppermute | solution.py:292
  60.4 8.6 %collective-permute-done.23.refs_1_.refs_5_ = bf16[256,512]{1,0:T(8,128)(2,1)S(1)} collective-permute-done((bf16[256,512]{1,0:T(8,128)(2,1)S(1)}, bf16[256,512]{1,0:T(8,128)(2,1)S(1)}, u32[]{:S(2)}, u32[]{:S(2)}) %collective-permute-start.23) | collective-permute-done | bytes 262176 | tf_op jit(solution)/shard_map/ppermute | solution.py:292
  69.0 4.6 %backward_products.1 = (bf16[128,4096]{1,0:T(8,128)(2,1)S(1)}, bf16[64,4096]{1,0:T(8,128)(2,1)S(1)}, bf16[64,4096]{1,0:T(8,128)(2,1)S(1)}) custom-call(s32[1]{0:T(128)} %bitcast.1.place, s32[1,1]{1,0:T(1,128)S(6)} %copy.10.count, s32[96]{0:T(128)S(1)} %get-tuple-element.48.rows, s32[96]{0:T(128)S(1)} %get-tuple-element.49.cols, ...), custom_call_target="tpu_custom_call" | custom-call | flops 1 | bytes 1 | tf_op jit(solution)/shard_map/backward_products/pallas_call | solution.py:197
  74.3 2.1 %collective-permute-done.24.refs_1_.sibling = f32[32,256]{1,0:T(8,128)S(1)} collective-permute-done((f32[32,256]{1,0:T(8,128)S(1)}, f32[32,256]{1,0:T(8,128)S(1)}, u32[]{:S(2)}, u32[]{:S(2)}) %collective-permute-start.24) | collective-permute-done | bytes 32800 | tf_op jit(solution)/shard_map/ppermute | solution.py:292
  77.1 3.1 %collective-permute-start.29 = (bf16[32,4608]{1,0:T(8,128)(2,1)S(1)}, bf16[32,4608]{1,0:T(8,128)(2,1)S(1)}, u32[]{:S(2)}, u32[]{:S(2)}) collective-permute-start(bf16[32,4608]{1,0:T(8,128)(2,1)S(1)} %get-tuple-element.87), channel_id=1, source_target_pairs={{0,16},{4,20},{8,24},{12,28},{16,0},{20,4},{24,8},{28,12},{1,17},{... | collective-permute-start | bytes 884744 | tf_op jit(solution)/shard_map/ppermute | solution.py:292
  80.2 1.4 %collective-permute-start.30 = (bf16[32,4608]{1,0:T(8,128)(2,1)S(1)}, bf16[32,4608]{1,0:T(8,128)(2,1)S(1)}, u32[]{:S(2)}, u32[]{:S(2)}) collective-permute-start(bf16[32,4608]{1,0:T(8,128)(2,1)S(1)} %get-tuple-element.88), channel_id=1, source_target_pairs={{0,24},{4,28},{8,16},{12,20},{16,8},{20,12},{24,0},{28,4},{1,25},{... | collective-permute-start | bytes 884744 | tf_op jit(solution)/shard_map/ppermute | solution.py:292
  81.6 5.1 %collective-permute-done.28.refs_0_ = bf16[32,4608]{1,0:T(8,128)(2,1)S(1)} collective-permute-done((bf16[32,4608]{1,0:T(8,128)(2,1)S(1)}, bf16[32,4608]{1,0:T(8,128)(2,1)S(1)}, u32[]{:S(2)}, u32[]{:S(2)}) %collective-permute-start.28) | collective-permute-done | bytes 294944 | tf_op jit(solution)/shard_map/ppermute | solution.py:292
  86.7 6.6 %collective-permute-done.29.refs_1_ = bf16[32,4608]{1,0:T(8,128)(2,1)S(1)} collective-permute-done((bf16[32,4608]{1,0:T(8,128)(2,1)S(1)}, bf16[32,4608]{1,0:T(8,128)(2,1)S(1)}, u32[]{:S(2)}, u32[]{:S(2)}) %collective-permute-start.29) | collective-permute-done | bytes 294944 | tf_op jit(solution)/shard_map/ppermute | solution.py:292
  93.3 1.8 %collective-permute-done.30.refs_2_ = bf16[32,4608]{1,0:T(8,128)(2,1)S(1)} collective-permute-done((bf16[32,4608]{1,0:T(8,128)(2,1)S(1)}, bf16[32,4608]{1,0:T(8,128)(2,1)S(1)}, u32[]{:S(2)}, u32[]{:S(2)}) %collective-permute-start.30) | collective-permute-done | bytes 294944 | tf_op jit(solution)/shard_map/ppermute | solution.py:292
  (52 shorter events, 7.8 us)
Async XLA Ops:
  0.6 9.5 %collective-permute-start.1 = (bf16[32,4096]{1,0:T(8,128)(2,1)}, bf16[32,4096]{1,0:T(8,128)(2,1)S(1)}, u32[]{:S(2)}, u32[]{:S(2)}) collective-permute-start(bf16[32,4096]{1,0:T(8,128)(2,1)} %bitcast.7), channel_id=1, source_target_pairs={{0,8},{4,12},{8,0},{12,4},{16,24},{20,28},{24,16},{28,20},{1,9},{5... | collective-permute-start | bytes 786440 | tf_op jit(solution)/shard_map/ppermute | solution.py:292
  3.7 8.0 %collective-permute-start.3 = (bf16[32,4096]{1,0:T(8,128)(2,1)}, bf16[32,4096]{1,0:T(8,128)(2,1)S(1)}, u32[]{:S(2)}, u32[]{:S(2)}) collective-permute-start(bf16[32,4096]{1,0:T(8,128)(2,1)} %bitcast.8), channel_id=1, source_target_pairs={{0,16},{4,20},{8,24},{12,28},{16,0},{20,4},{24,8},{28,12},{1,17},{... | collective-permute-start | bytes 786440 | tf_op jit(solution)/shard_map/ppermute | solution.py:292
  5.2 9.4 %collective-permute-start = (bf16[32,4096]{1,0:T(8,128)(2,1)}, bf16[32,4096]{1,0:T(8,128)(2,1)S(1)}, u32[]{:S(2)}, u32[]{:S(2)}) collective-permute-start(bf16[32,4096]{1,0:T(8,128)(2,1)} %bitcast.9), channel_id=1, source_target_pairs={{0,4},{4,0},{8,12},{12,8},{16,20},{20,16},{24,28},{28,24},{1,5},{5... | collective-permute-start | bytes 786440 | tf_op jit(solution)/shard_map/ppermute | solution.py:292
  10.2 4.4 %collective-permute-start.2 = (bf16[32,4096]{1,0:T(8,128)(2,1)S(1)}, bf16[32,4096]{1,0:T(8,128)(2,1)S(1)}, u32[]{:S(2)}, u32[]{:S(2)}) collective-permute-start(bf16[32,4096]{1,0:T(8,128)(2,1)S(1)} %collective-permute-done.1.refs_2_), channel_id=1, source_target_pairs={{0,4},{4,0},{8,12},{12,8},{16,20},{20,16},{24,28},{28,24},{1,5},{5... | collective-permute-start | bytes 786440 | tf_op jit(solution)/shard_map/ppermute | solution.py:292
  11.6 2.9 %collective-permute-start.4 = (bf16[32,4096]{1,0:T(8,128)(2,1)S(1)}, bf16[32,4096]{1,0:T(8,128)(2,1)S(1)}, u32[]{:S(2)}, u32[]{:S(2)}) collective-permute-start(bf16[32,4096]{1,0:T(8,128)(2,1)S(1)} %collective-permute-done.3.refs_4_), channel_id=1, source_target_pairs={{0,4},{4,0},{8,12},{12,8},{16,20},{20,16},{24,28},{28,24},{1,5},{5... | collective-permute-start | bytes 786440 | tf_op jit(solution)/shard_map/ppermute | solution.py:292
  11.6 9.1 %collective-permute-start.10 = (bf16[16,4096]{1,0:T(8,128)(2,1)S(1)}, bf16[16,4096]{1,0:T(8,128)(2,1)S(1)}, u32[]{:S(2)}, u32[]{:S(2)}) collective-permute-start(bf16[16,4096]{1,0:T(8,128)(2,1)S(1)} %get-tuple-element.62), channel_id=1, source_target_pairs={{0,24},{4,28},{8,16},{12,20},{16,8},{20,12},{24,0},{28,4},{1,25},{... | collective-permute-start | bytes 393224 | tf_op jit(solution)/shard_map/ppermute | solution.py:292
  13.4 7.9 %collective-permute-start.9 = (bf16[16,4096]{1,0:T(8,128)(2,1)S(1)}, bf16[16,4096]{1,0:T(8,128)(2,1)S(1)}, u32[]{:S(2)}, u32[]{:S(2)}) collective-permute-start(bf16[16,4096]{1,0:T(8,128)(2,1)S(1)} %get-tuple-element.60), channel_id=1, source_target_pairs={{0,24},{4,28},{8,16},{12,20},{16,8},{20,12},{24,0},{28,4},{1,25},{... | collective-permute-start | bytes 393224 | tf_op jit(solution)/shard_map/ppermute | solution.py:292
  19.1 22.9 %copy-start.1 = (bf16[512,256]{1,0:T(8,128)(2,1)S(1)}, bf16[512,256]{1,0:T(8,128)(2,1)}, u32[]{:S(2)}) copy-start(bf16[512,256]{1,0:T(8,128)(2,1)} %cotangent.1) | copy-start | bytes 786436
  19.1 9.0 %collective-permute-start.5 = (bf16[224,512]{1,0:T(8,128)(2,1)S(1)}, bf16[224,512]{1,0:T(8,128)(2,1)S(1)}, u32[]{:S(2)}, u32[]{:S(2)}) collective-permute-start(bf16[224,512]{1,0:T(8,128)(2,1)S(1)} %get-tuple-element.54), channel_id=1, source_target_pairs={{0,1},{1,0},{2,3},{3,2},{4,5},{5,4},{6,7},{7,6},{8,9},{9,8},{10,11... | collective-permute-start | bytes 688136 | tf_op jit(solution)/shard_map/ppermute | solution.py:292
  20.8 2.1 %collective-permute-start.12 = (bf16[16,4096]{1,0:T(8,128)(2,1)S(1)}, bf16[16,4096]{1,0:T(8,128)(2,1)S(1)}, u32[]{:S(2)}, u32[]{:S(2)}) collective-permute-start(bf16[16,4096]{1,0:T(8,128)(2,1)S(1)} %collective-permute-done.10.refs_1_), channel_id=1, source_target_pairs={{0,4},{4,0},{8,12},{12,8},{16,20},{20,16},{24,28},{28,24},{1,5},{5... | collective-permute-start | bytes 393224 | tf_op jit(solution)/shard_map/ppermute | solution.py:292
  21.2 1.6 %collective-permute-start.11 = (bf16[16,4096]{1,0:T(8,128)(2,1)S(1)}, bf16[16,4096]{1,0:T(8,128)(2,1)S(1)}, u32[]{:S(2)}, u32[]{:S(2)}) collective-permute-start(bf16[16,4096]{1,0:T(8,128)(2,1)S(1)} %collective-permute-done.9.refs_0_), channel_id=1, source_target_pairs={{0,4},{4,0},{8,12},{12,8},{16,20},{20,16},{24,28},{28,24},{1,5},{5... | collective-permute-start | bytes 393224 | tf_op jit(solution)/shard_map/ppermute | solution.py:292
  21.3 9.5 %collective-permute-start.7 = (bf16[160,512]{1,0:T(8,128)(2,1)S(1)}, bf16[160,512]{1,0:T(8,128)(2,1)S(1)}, u32[]{:S(2)}, u32[]{:S(2)}) collective-permute-start(bf16[160,512]{1,0:T(8,128)(2,1)S(1)} %get-tuple-element.57), channel_id=1, source_target_pairs={{0,1},{1,0},{2,3},{3,2},{4,5},{5,4},{6,7},{7,6},{8,9},{9,8},{10,11... | collective-permute-start | bytes 491528 | tf_op jit(solution)/shard_map/ppermute | solution.py:292
  26.7 6.7 %collective-permute-start.13 = (bf16[128,512]{1,0:T(8,128)(2,1)S(1)}, bf16[128,512]{1,0:T(8,128)(2,1)S(1)}, u32[]{:S(2)}, u32[]{:S(2)}) collective-permute-start(bf16[128,512]{1,0:T(8,128)(2,1)S(1)} %get-tuple-element.65), channel_id=1, source_target_pairs={{0,1},{1,0},{2,3},{3,2},{4,5},{5,4},{6,7},{7,6},{8,9},{9,8},{10,11... | collective-permute-start | bytes 393224 | tf_op jit(solution)/shard_map/ppermute | solution.py:292
  28.1 13.8 %collective-permute-start.6 = (bf16[112,512]{1,0:T(8,128)(2,1)S(1)}, bf16[112,512]{1,0:T(8,128)(2,1)S(1)}, u32[]{:S(2)}, u32[]{:S(2)}) collective-permute-start(bf16[112,512]{1,0:T(8,128)(2,1)S(1)} %pass_on.3), channel_id=1, source_target_pairs={{0,2},{1,3},{2,0},{3,1},{4,6},{5,7},{6,4},{7,5},{8,10},{9,11},{10,... | collective-permute-start | bytes 344072 | tf_op jit(solution)/shard_map/ppermute | solution.py:292
  30.8 10.4 %collective-permute-start.8 = (bf16[80,512]{1,0:T(8,128)(2,1)S(1)}, bf16[80,512]{1,0:T(8,128)(2,1)S(1)}, u32[]{:S(2)}, u32[]{:S(2)}) collective-permute-start(bf16[80,512]{1,0:T(8,128)(2,1)S(1)} %pass_on.4), channel_id=1, source_target_pairs={{0,2},{1,3},{2,0},{3,1},{4,6},{5,7},{6,4},{7,5},{8,10},{9,11},{10,... | collective-permute-start | bytes 245768 | tf_op jit(solution)/shard_map/ppermute | solution.py:292
  33.4 8.6 %collective-permute-start.14 = (bf16[64,512]{1,0:T(8,128)(2,1)S(1)}, bf16[64,512]{1,0:T(8,128)(2,1)S(1)}, u32[]{:S(2)}, u32[]{:S(2)}) collective-permute-start(bf16[64,512]{1,0:T(8,128)(2,1)S(1)} %pass_on.5), channel_id=1, source_target_pairs={{0,2},{1,3},{2,0},{3,1},{4,6},{5,7},{6,4},{7,5},{8,10},{9,11},{10,... | collective-permute-start | bytes 196616 | tf_op jit(solution)/shard_map/ppermute | solution.py:292
  43.1 12.0 %collective-permute-start.16 = (bf16[144,512]{1,0:T(8,128)(2,1)S(1)}, bf16[144,512]{1,0:T(8,128)(2,1)S(1)}, u32[]{:S(2)}, u32[]{:S(2)}) collective-permute-start(bf16[144,512]{1,0:T(8,128)(2,1)S(1)} %get-tuple-element.70.refs_0_), channel_id=1, source_target_pairs={{0,2},{1,3},{2,0},{3,1},{4,6},{5,7},{6,4},{7,5},{8,10},{9,11},{10,... | collective-permute-start | bytes 442376 | tf_op jit(solution)/shard_map/ppermute | solution.py:292
  43.3 3.5 %collective-permute-start.17 = (f32[2,32,256]{2,1,0:T(8,128)S(1)}, f32[2,32,256]{2,1,0:T(8,128)S(1)}, u32[]{:S(2)}, u32[]{:S(2)}) collective-permute-start(f32[2,32,256]{2,1,0:T(8,128)S(1)} %get-tuple-element.75), channel_id=1, source_target_pairs={{0,4},{4,0},{8,12},{12,8},{16,20},{20,16},{24,28},{28,24},{1,5},{5... | collective-permute-start | bytes 196616 | tf_op jit(solution)/shard_map/ppermute | solution.py:292
  43.4 3.4 %collective-permute-start.18 = (f32[2,32,256]{2,1,0:T(8,128)S(1)}, f32[2,32,256]{2,1,0:T(8,128)S(1)}, u32[]{:S(2)}, u32[]{:S(2)}) collective-permute-start(f32[2,32,256]{2,1,0:T(8,128)S(1)} %get-tuple-element.76), channel_id=1, source_target_pairs={{0,4},{4,0},{8,12},{12,8},{16,20},{20,16},{24,28},{28,24},{1,5},{5... | collective-permute-start | bytes 196616 | tf_op jit(solution)/shard_map/ppermute | solution.py:292
  43.9 13.3 %collective-permute-start.15 = (bf16[112,512]{1,0:T(8,128)(2,1)S(1)}, bf16[112,512]{1,0:T(8,128)(2,1)S(1)}, u32[]{:S(2)}, u32[]{:S(2)}) collective-permute-start(bf16[112,512]{1,0:T(8,128)(2,1)S(1)} %get-tuple-element.69.refs_0_.refs_1_), channel_id=1, source_target_pairs={{0,2},{1,3},{2,0},{3,1},{4,6},{5,7},{6,4},{7,5},{8,10},{9,11},{10,... | collective-permute-start | bytes 344072 | tf_op jit(solution)/shard_map/ppermute | solution.py:292
  46.9 4.0 %collective-permute-start.19 = (f32[32,256]{1,0:T(8,128)S(1)}, f32[32,256]{1,0:T(8,128)S(1)}, u32[]{:S(2)}, u32[]{:S(2)}) collective-permute-start(f32[32,256]{1,0:T(8,128)S(1)} %get-tuple-element.78), channel_id=1, source_target_pairs={{0,8},{4,12},{8,0},{12,4},{16,24},{20,28},{24,16},{28,20},{1,9},{5... | collective-permute-start | bytes 98312 | tf_op jit(solution)/shard_map/ppermute | solution.py:292
  47.3 3.9 %collective-permute-start.20 = (f32[32,256]{1,0:T(8,128)S(1)}, f32[32,256]{1,0:T(8,128)S(1)}, u32[]{:S(2)}, u32[]{:S(2)}) collective-permute-start(f32[32,256]{1,0:T(8,128)S(1)} %get-tuple-element.79), channel_id=1, source_target_pairs={{0,16},{4,20},{8,24},{12,28},{16,0},{20,4},{24,8},{28,12},{1,17},{... | collective-permute-start | bytes 98312 | tf_op jit(solution)/shard_map/ppermute | solution.py:292
  49.3 4.8 %collective-permute-start.21 = (f32[32,256]{1,0:T(8,128)S(1)}, f32[32,256]{1,0:T(8,128)S(1)}, u32[]{:S(2)}, u32[]{:S(2)}) collective-permute-start(f32[32,256]{1,0:T(8,128)S(1)} %get-tuple-element.80), channel_id=1, source_target_pairs={{0,24},{4,28},{8,16},{12,20},{16,8},{20,12},{24,0},{28,4},{1,25},{... | collective-permute-start | bytes 98312 | tf_op jit(solution)/shard_map/ppermute | solution.py:292
  54.1 5.0 %collective-permute-start.22 = (f32[32,256]{1,0:T(8,128)S(1)}, f32[32,256]{1,0:T(8,128)S(1)}, u32[]{:S(2)}, u32[]{:S(2)}) collective-permute-start(f32[32,256]{1,0:T(8,128)S(1)} %chunk_sum.2.refs_2_), channel_id=1, source_target_pairs={{0,2},{1,3},{2,0},{3,1},{4,6},{5,7},{6,4},{7,5},{8,10},{9,11},{10,... | collective-permute-start | bytes 98312 | tf_op jit(solution)/shard_map/ppermute | solution.py:292
  55.1 13.9 %collective-permute-start.25 = (bf16[288,512]{1,0:T(8,128)(2,1)S(1)}, bf16[288,512]{1,0:T(8,128)(2,1)S(1)}, u32[]{:S(2)}, u32[]{:S(2)}) collective-permute-start(bf16[288,512]{1,0:T(8,128)(2,1)S(1)} %stack.1), channel_id=1, source_target_pairs={{0,1},{1,0},{2,3},{3,2},{4,5},{5,4},{6,7},{7,6},{8,9},{9,8},{10,11... | collective-permute-start | bytes 884744 | tf_op jit(solution)/shard_map/ppermute | solution.py:292
  59.1 9.9 %collective-permute-start.23 = (bf16[256,512]{1,0:T(8,128)(2,1)S(1)}, bf16[256,512]{1,0:T(8,128)(2,1)S(1)}, u32[]{:S(2)}, u32[]{:S(2)}) collective-permute-start(bf16[256,512]{1,0:T(8,128)(2,1)S(1)} %with_chunk.1.refs_0_), channel_id=1, source_target_pairs={{0,1},{1,0},{2,3},{3,2},{4,5},{5,4},{6,7},{7,6},{8,9},{9,8},{10,11... | collective-permute-start | bytes 786440 | tf_op jit(solution)/shard_map/ppermute | solution.py:292
  73.7 2.8 %collective-permute-start.26 = (bf16[64,4096]{1,0:T(8,128)(2,1)S(1)}, bf16[64,4096]{1,0:T(8,128)(2,1)S(1)}, u32[]{:S(2)}, u32[]{:S(2)}) collective-permute-start(bf16[64,4096]{1,0:T(8,128)(2,1)S(1)} %get-tuple-element.83), channel_id=1, source_target_pairs={{0,4},{4,0},{8,12},{12,8},{16,20},{20,16},{24,28},{28,24},{1,5},{5... | collective-permute-start | bytes 1572872 | tf_op jit(solution)/shard_map/ppermute | solution.py:292
  73.7 2.7 %collective-permute-start.27 = (bf16[64,4096]{1,0:T(8,128)(2,1)S(1)}, bf16[64,4096]{1,0:T(8,128)(2,1)S(1)}, u32[]{:S(2)}, u32[]{:S(2)}) collective-permute-start(bf16[64,4096]{1,0:T(8,128)(2,1)S(1)} %get-tuple-element.84), channel_id=1, source_target_pairs={{0,4},{4,0},{8,12},{12,8},{16,20},{20,16},{24,28},{28,24},{1,5},{5... | collective-permute-start | bytes 1572872 | tf_op jit(solution)/shard_map/ppermute | solution.py:292
  74.2 2.2 %collective-permute-start.24 = (f32[32,256]{1,0:T(8,128)S(1)}, f32[32,256]{1,0:T(8,128)S(1)}, u32[]{:S(2)}, u32[]{:S(2)}) collective-permute-start(f32[32,256]{1,0:T(8,128)S(1)} %chunk_sum.3.refs_0_.chunk), channel_id=1, source_target_pairs={{0,4},{4,0},{8,12},{12,8},{16,20},{20,16},{24,28},{28,24},{1,5},{5... | collective-permute-start | bytes 98312 | tf_op jit(solution)/shard_map/ppermute | solution.py:292
  76.7 9.9 %collective-permute-start.28 = (bf16[32,4608]{1,0:T(8,128)(2,1)S(1)}, bf16[32,4608]{1,0:T(8,128)(2,1)S(1)}, u32[]{:S(2)}, u32[]{:S(2)}) collective-permute-start(bf16[32,4608]{1,0:T(8,128)(2,1)S(1)} %get-tuple-element.86), channel_id=1, source_target_pairs={{0,8},{4,12},{8,0},{12,4},{16,24},{20,28},{24,16},{28,20},{1,9},{5... | collective-permute-start | bytes 884744 | tf_op jit(solution)/shard_map/ppermute | solution.py:292
  77.1 16.2 %collective-permute-start.29 = (bf16[32,4608]{1,0:T(8,128)(2,1)S(1)}, bf16[32,4608]{1,0:T(8,128)(2,1)S(1)}, u32[]{:S(2)}, u32[]{:S(2)}) collective-permute-start(bf16[32,4608]{1,0:T(8,128)(2,1)S(1)} %get-tuple-element.87), channel_id=1, source_target_pairs={{0,16},{4,20},{8,24},{12,28},{16,0},{20,4},{24,8},{28,12},{1,17},{... | collective-permute-start | bytes 884744 | tf_op jit(solution)/shard_map/ppermute | solution.py:292
  80.2 14.9 %collective-permute-start.30 = (bf16[32,4608]{1,0:T(8,128)(2,1)S(1)}, bf16[32,4608]{1,0:T(8,128)(2,1)S(1)}, u32[]{:S(2)}, u32[]{:S(2)}) collective-permute-start(bf16[32,4608]{1,0:T(8,128)(2,1)S(1)} %get-tuple-element.88), channel_id=1, source_target_pairs={{0,24},{4,28},{8,16},{12,20},{16,8},{20,12},{24,0},{28,4},{1,25},{... | collective-permute-start | bytes 884744 | tf_op jit(solution)/shard_map/ppermute | solution.py:292
  (2 other events, 36.8 us)
where the time goes:
time: 95.9 us; the launch traced here: 96.1 us
  waiting for transfers between devices  41.4 us (43%)
  starting transfers between devices  35.4 us (37%)
  Pallas kernels  17.8 us (19%)
  between operations  1.45 us (2%)
    ppermute x31, waiting for transfers between devices, swap(): return lax.ppermute(value, axis, [(i, i ^ k) for i in range(size)])  41.4 us
    ppermute x31, starting transfers between devices, swap(): return lax.ppermute(value, axis, [(i, i ^ k) for i in range(size)])  35.4 us
    pallas_call x2, Pallas kernels, forward(): pl.pallas_call(functools.partial(forward_kernel, len(parts), depths, layo...  8.36 us
    pallas_call x1, Pallas kernels, backward(): pl.pallas_call(functools.partial(backward_kernel, spots, depths), out_sha...  4.63 us
    pallas_call x1, Pallas kernels, fetch(): pl.pallas_call(fetch_kernel, out_shape=outs + [jax.ShapeDtypeStruct(tile....  2.06 us
  transfers between devices with their start and end apart: 31, of which 15 were waited for; matrix products, arithmetic and copies ran while one was open for 0% of the time, Pallas kernels for 11%

commit v1 on v0

--- a/solution.py
+++ b/solution.py
@@ -238,6 +238,7 @@
     product = jnp.concatenate(rows)
     first = 0
     for back in backs:
+        first %= product.shape[0]
         back[...] = product[first : first + back.shape[0], :]
         first += back.shape[0]
 
@@ -303,15 +304,11 @@
     return lax.optimization_barrier((value, *earlier))[0]
 
 
-def stack(*values):
-    return (jnp.concatenate(values),)
-
-
-def with_chunk(mine, other, *parts):
+def with_chunk(rows, *parts):
     total = functools.reduce(jnp.add, parts)
     high = total.astype(jnp.bfloat16)
     low = (total - high.astype(jnp.float32)).astype(jnp.bfloat16)
-    return (jnp.concatenate([mine, other, jnp.concatenate([high, low], axis=1)]),)
+    return (jnp.concatenate([rows, jnp.concatenate([high, low], axis=1)]),)
 
 
 def chunk_sum(depth, *values):
@@ -328,43 +325,50 @@
     return tuple(mine + jnp.concatenate(received))
 
 
+def row_sums(depth, mine, *received):
+    total = mine.astype(jnp.float32) + jnp.concatenate(received).astype(jnp.float32)
+    total = jnp.concatenate([total, total[:, :128]], axis=1).astype(mine.dtype)
+    return tuple(total[first : first + depth] for first in range(0, total.shape[0], depth))
+
+
 def row_payloads(depth, chunk, sibling, mine, *received):
-    total = (mine.astype(jnp.float32) + jnp.concatenate(received).astype(jnp.float32)).astype(mine.dtype)
-    gradient_chunks = jnp.concatenate([chunk.astype(mine.dtype), sibling.astype(mine.dtype)], axis=1)
-    parts = [total[first : first + depth] for first in range(0, total.shape[0], depth)]
-    return parts[0], *[jnp.concatenate([part, gradient_chunks], axis=1) for part in parts[1:]]
-
-
-def finish_kernel(row, chunk, sibling, mine, *refs):
-    received = refs[:-2]
+    chunks = jnp.concatenate([chunk.astype(mine.dtype), sibling.astype(mine.dtype)], axis=1)
+    total = mine.astype(jnp.float32) + jnp.concatenate(received).astype(jnp.float32)
+    total = total.astype(mine.dtype)
+    own, *sums = [total[first : first + depth] for first in range(0, total.shape[0], depth)]
+    return chunks, own, *[jnp.concatenate([part, chunks], axis=1) for part in sums]
+
+
+def finish_kernel(keys, row, *refs):
     grad_features, grad_weight = refs[-2:]
-    depth, nodes = mine.shape
-    total = mine[...].astype(jnp.float32)
-    for part in received:
+    parts, chunks = refs[: len(keys)], refs[len(keys) : -2]
+    depth, nodes = grad_features.shape
+    wide = grad_weight.shape[1]
+    total = parts[0][...].astype(jnp.float32)
+    for part in parts[1:]:
         total += part[:, :nodes].astype(jnp.float32)
-    grad_features[...] = total.astype(mine.dtype)
-    wide = grad_weight.shape[1]
-    own = [ref[...].astype(mine.dtype) for ref in (chunk, sibling)]
-    chunks = own + [part[:, nodes + n * wide : nodes + (n + 1) * wide] for part in received for n in range(2)]
-    for k, value in enumerate(chunks):
-        first = pl.multiple_of((row[0] ^ k) * depth, depth)
-        grad_weight[pl.ds(first, depth), :] = value.astype(jnp.float32)
-
-
-def finish(row, chunk, sibling, mine, received):
-    n_chunks = 2 * (1 + len(received))
-    return pl.pallas_call(
-        finish_kernel,
+    grad_features[...] = total.astype(grad_features.dtype)
+    values = [ref[...] for ref in chunks] + [part[:, nodes:] for part in parts[len(chunks) :]]
+    for key, value in zip(keys, values):
+        for k in range(2):
+            first = pl.multiple_of((row[0] ^ (key + k)) * depth, depth)
+            grad_weight[pl.ds(first, depth), :] = value[:, k * wide : (k + 1) * wide].astype(jnp.float32)
+
+
+def finish(row, keys, parts, chunks):
+    depth, nodes = parts[0].shape
+    return pl.pallas_call(
+        functools.partial(finish_kernel, keys),
         out_shape=[
-            jax.ShapeDtypeStruct(mine.shape, mine.dtype),
-            jax.ShapeDtypeStruct((n_chunks * chunk.shape[0], chunk.shape[1]), jnp.float32),
+            jax.ShapeDtypeStruct((depth, nodes), jnp.bfloat16),
+            jax.ShapeDtypeStruct((2 * len(keys) * depth, chunks[0].shape[1] // 2), jnp.float32),
         ],
-        in_specs=[SMEM] + [VMEM] * (3 + len(received)),
+        in_specs=[SMEM] + [VMEM] * (len(parts) + len(chunks)),
         out_specs=[VMEM] * 2,
         compiler_params=params(8),
         cost_estimate=COST,
         name="finish",
-    )(row, chunk, sibling, mine, *received)
+    )(row, *parts, *chunks)
 
 
 def shards_exchanged(features, weight, adj_values, block_rows, block_cols, block_counts, cotangent):
@@ -419,44 +423,50 @@
     for piece in pieces:
         sums.append(fold(piece, *(sums[-1][1:2] if sums else ())))
 
+    groups = [near, [0] + far]
+    order = [k + side for group in groups for side in range(2) for k in group]
+    cuts = [2 * depth * len(group) for group in groups]
+    output, deltas, aggregated, back, *backs = middle(
+        n_row, row, weight, cotangent, sums, order, [sum(cuts)] + cuts
+    )
+    beside = swap(back, "col", 1)
+    beyond = [swap(part, "col", 2) for part in backs]
+
     evens = tuple(range(0, n_row, 2))
     odds = tuple(range(1, n_row, 2))
-    n_all = weight.shape[0]
-    cut = n_all // 2 + 16
-    cuts = [cut, n_all - cut]
-    output, deltas, aggregated, *backs = middle(n_row, row, weight, cotangent, sums, evens + odds, cuts)
-    beyond = [swap(back, "col", 2) for back in backs]
-
     even, *odd = gradient(1.0 / math.sqrt(nodes), [evens, odds[:2], odds[2:]], aggregated, deltas)
     chunk, *sent = fuse("gradient_sum", pair_sum, even, *[swap(part, "row", 1) for part in odd])
     from_rows = [swap(part, "row", k) for part, k in zip(sent, evens[1:])]
-    (chunk,) = fuse("chunk_sum", wide_sum, chunk, *from_rows)
+    (chunk,) = fuse("chunk_sum", wide_sum, after(chunk, beside), *from_rows)
     chunks = [chunk, swap(chunk, "col", 2)]
 
-    (large,) = fuse("stack", stack, backs[0], beyond[0])
-    (small,) = fuse("with_chunk", with_chunk, backs[1], after(beyond[1], large), *chunks)
-    large_received, small_received = swap(large, "col", 1), swap(small, "col", 1)
-    (chunk,) = fuse("chunk_sum", functools.partial(chunk_sum, depth), small, small_received)
-
-    mine, *sent = backward(
-        col,
-        count,
-        rows,
-        cols,
-        tile,
-        [*backs, *beyond, after(large_received, chunk), small_received],
-        [[(0, 0), (1, 0)], [(4, 0), (5, 0)], [(2, 0), (3, 0)], [(4, cuts[0]), (5, cuts[1])]],
-        cuts,
-        [n_all // 2] + [n_all // 4] * 2,
-        col_blocks,
+    beyond[0] = after(beyond[0], chunk)
+    (second,) = fuse("with_chunk", with_chunk, after(beyond[1], beyond[0]), *chunks)
+    received = [swap(beyond[0], "col", 1), swap(second, "col", 1)]
+
+    def columns(n, *earlier):
+        parts = [back, beside, after(beyond[n], *earlier), received[n]]
+        spots = [[(0, n * cuts[0])], [(1, n * cuts[0])], [(2, 0)], [(3, 0)]]
+        out_depths = [cuts[n] // 2] + [cuts[n] // (8 - 4 * n)] * (4 - 2 * n)
+        mine, *sent = backward(
+            col, count, rows, cols, tile, parts, spots, cuts[n : n + 1], out_depths, col_blocks
+        )
+        return [mine] + [swap(part, "row", 1) for part in sent]
+
+    sums = fuse("row_sums", functools.partial(row_sums, depth), *columns(0, second))
+    near_sums = [swap(part, "row", k) for part, k in zip(sums, near)]
+    received[1] = after(received[1], *sums)
+    (chunk,) = fuse("chunk_sum", functools.partial(chunk_sum, depth), second, received[1])
+    mine, *from_sibling = columns(1, chunk)
+    mine = after(mine, *near_sums)
+    chunks, own_sum, *sums = fuse(
+        "row_payloads", functools.partial(row_payloads, depth), chunk, swap(chunk, "row", 1), mine, *from_sibling
     )
-    from_sibling = [swap(part, "row", 1) for part in sent]
-    sibling_chunk = swap(chunk, "row", 1)
-    own_sum, *sums = fuse(
-        "row_payloads", functools.partial(row_payloads, depth), chunk, sibling_chunk, mine, *from_sibling
+    far_sums = [swap(part, "row", k) for part, k in zip(sums, far)]
+    near_chunks = [swap(chunks, "row", k) for k in near]
+    grad_features, grad_weight = finish(
+        row, [0] + near + far, [own_sum] + near_sums + far_sums, [chunks] + near_chunks
     )
-    received = [swap(part, "row", k) for part, k in zip(sums, evens[1:])]
-    grad_features, grad_weight = finish(row, chunk, sibling_chunk, own_sum, received)
     return output, grad_weight, grad_features.T
 
 

time: 95.9 us -> 89.1 us (0.929)
  waiting for transfers between devices: 41.4 us -> 37.4 us
  starting transfers between devices: 35.4 us -> 33.5 us
  Pallas kernels: 17.8 us -> 16.6 us
    ppermute x31 -> x38, waiting for transfers between devices: 41.4 us -> 37.4 us  [swap(): return lax.ppermute(value, axis, [(i, i ^ k) for i in range(size)])]
    ppermute x31 -> x38, starting transfers between devices: 35.4 us -> 33.5 us  [swap(): return lax.ppermute(value, axis, [(i, i ^ k) for i in range(size)])]
    pallas_call x2, Pallas kernels: 8.36 us -> 6.55 us  [forward(): pl.pallas_call(functools.partial(forward_kernel, len(parts), depths, layo...]
    pallas_call x1 -> x2, Pallas kernels: 4.63 us -> 5.47 us  [backward(): pl.pallas_call(functools.partial(backward_kernel, spots, depths), out_sha...]
  transfers between devices with their start and end apart: 31 -> 38, of which waited for: 15 -> 20; matrix products, arithmetic and copies ran while one was open for 0% -> 0% of each run, Pallas kernels for 11% -> 16%
where the time goes in v1:
time: 89.1 us; the launch traced here: 89 us
  waiting for transfers between devices  37.4 us (42%)
  starting transfers between devices  33.5 us (38%)
  Pallas kernels  16.6 us (19%)
  between operations  1.49 us (2%)
    ppermute x38, waiting for transfers between devices, swap(): return lax.ppermute(value, axis, [(i, i ^ k) for i in range(size)])  37.4 us
    ppermute x38, starting transfers between devices, swap(): return lax.ppermute(value, axis, [(i, i ^ k) for i in range(size)])  33.5 us
    pallas_call x2, Pallas kernels, forward(): pl.pallas_call(functools.partial(forward_kernel, len(parts), depths, layo...  6.55 us
    pallas_call x2, Pallas kernels, backward(): pl.pallas_call(functools.partial(backward_kernel, spots, depths), out_sha...  5.47 us
    pallas_call x1, Pallas kernels, fetch(): pl.pallas_call(fetch_kernel, out_shape=outs + [jax.ShapeDtypeStruct(tile....  1.82 us
  transfers between devices with their start and end apart: 38, of which 20 were waited for; matrix products, arithmetic and copies ran while one was open for 0% of the time, Pallas kernels for 16%

profile of v1, /device:TPU:0, one launch (start us, length us, event | category | flops | bytes accessed | tf_op | source)
XLA Modules:
  0.0 89.0 jit_solution(5367048964891279960)
XLA Ops:
  0.6 3.0 %collective-permute-start.1 = (bf16[32,4096]{1,0:T(8,128)(2,1)}, bf16[32,4096]{1,0:T(8,128)(2,1)S(1)}, u32[]{:S(2)}, u32[]{:S(2)}) collective-permute-start(bf16[32,4096]{1,0:T(8,128)(2,1)} %bitcast.7), channel_id=1, source_target_pairs={{0,8},{4,12},{8,0},{12,4},{16,24},{20,28},{24,16},{28,20},{1,9},{5... | collective-permute-start | bytes 786440 | tf_op jit(solution)/shard_map/ppermute | solution.py:293
  3.7 1.5 %collective-permute-start.3 = (bf16[32,4096]{1,0:T(8,128)(2,1)}, bf16[32,4096]{1,0:T(8,128)(2,1)S(1)}, u32[]{:S(2)}, u32[]{:S(2)}) collective-permute-start(bf16[32,4096]{1,0:T(8,128)(2,1)} %bitcast.8), channel_id=1, source_target_pairs={{0,16},{4,20},{8,24},{12,28},{16,0},{20,4},{24,8},{28,12},{1,17},{... | collective-permute-start | bytes 786440 | tf_op jit(solution)/shard_map/ppermute | solution.py:293
  5.8 1.8 %fetch.1 = (s32[96]{0:T(128)S(1)}, s32[96]{0:T(128)S(1)}, bf16[16,4096]{1,0:T(8,128)(2,1)S(1)}, bf16[16,4096]{1,0:T(8,128)(2,1)S(1)}, bf16[96,128,128]{2,1,0:T(8,128)(2,1)S(1)}) custom-call(s32[1,1]{1,0:T(1,128)S(6)} %copy.10.count, s32[96]{0:T(128)} %bitcast.13, s32[96]{0:T(128)} %bitcast.14, bf16[32,4096]{1,0:T(8,128)(2,1)} %bitcast.10, ...), custom_call_target="tpu_custom_call" | custom-call | flops 1 | bytes 1 | tf_op jit(solution)/shard_map/fetch/pallas_call | solution.py:103
  7.7 2.5 %collective-permute-done.1.refs_2_ = bf16[32,4096]{1,0:T(8,128)(2,1)S(1)} collective-permute-done((bf16[32,4096]{1,0:T(8,128)(2,1)}, bf16[32,4096]{1,0:T(8,128)(2,1)S(1)}, u32[]{:S(2)}, u32[]{:S(2)}) %collective-permute-start.1) | collective-permute-done | bytes 262176 | tf_op jit(solution)/shard_map/ppermute | solution.py:293
  10.2 1.5 %collective-permute-done.3.refs_4_ = bf16[32,4096]{1,0:T(8,128)(2,1)S(1)} collective-permute-done((bf16[32,4096]{1,0:T(8,128)(2,1)}, bf16[32,4096]{1,0:T(8,128)(2,1)S(1)}, u32[]{:S(2)}, u32[]{:S(2)}) %collective-permute-start.3) | collective-permute-done | bytes 262176 | tf_op jit(solution)/shard_map/ppermute | solution.py:293
  11.6 1.7 %collective-permute-start.10 = (bf16[16,4096]{1,0:T(8,128)(2,1)S(1)}, bf16[16,4096]{1,0:T(8,128)(2,1)S(1)}, u32[]{:S(2)}, u32[]{:S(2)}) collective-permute-start(bf16[16,4096]{1,0:T(8,128)(2,1)S(1)} %get-tuple-element.74), channel_id=1, source_target_pairs={{0,24},{4,28},{8,16},{12,20},{16,8},{20,12},{24,0},{28,4},{1,25},{... | collective-permute-start | bytes 393224 | tf_op jit(solution)/shard_map/ppermute | solution.py:293
  13.4 1.2 %collective-permute-start.9 = (bf16[16,4096]{1,0:T(8,128)(2,1)S(1)}, bf16[16,4096]{1,0:T(8,128)(2,1)S(1)}, u32[]{:S(2)}, u32[]{:S(2)}) collective-permute-start(bf16[16,4096]{1,0:T(8,128)(2,1)S(1)} %get-tuple-element.72), channel_id=1, source_target_pairs={{0,24},{4,28},{8,16},{12,20},{16,8},{20,12},{24,0},{28,4},{1,25},{... | collective-permute-start | bytes 393224 | tf_op jit(solution)/shard_map/ppermute | solution.py:293
  14.6 3.6 %forward_products.2 = (bf16[112,512]{1,0:T(8,128)(2,1)S(1)}, bf16[112,512]{1,0:T(8,128)(2,1)S(1)}, bf16[224,512]{1,0:T(8,128)(2,1)S(1)}, bf16[80,512]{1,0:T(8,12...) custom-call(s32[1]{0:T(128)} %bitcast.1.place, s32[1,1]{1,0:T(1,128)S(6)} %copy.10.count, ...), custom_call_target="tpu_custom_call" | custom-call | flops 1 | bytes 1 | tf_op jit(solution)/shard_map/forward_products/pallas_call | solution.py:154
  18.2 1.3 %collective-permute-start.5 = (bf16[224,512]{1,0:T(8,128)(2,1)S(1)}, bf16[224,512]{1,0:T(8,128)(2,1)S(1)}, u32[]{:S(2)}, u32[]{:S(2)}) collective-permute-start(bf16[224,512]{1,0:T(8,128)(2,1)S(1)} %get-tuple-element.66), channel_id=1, source_target_pairs={{0,1},{1,0},{2,3},{3,2},{4,5},{5,4},{6,7},{7,6},{8,9},{9,8},{10,11... | collective-permute-start | bytes 688136 | tf_op jit(solution)/shard_map/ppermute | solution.py:293
  19.5 1.2 %collective-permute-start.12 = (bf16[16,4096]{1,0:T(8,128)(2,1)S(1)}, bf16[16,4096]{1,0:T(8,128)(2,1)S(1)}, u32[]{:S(2)}, u32[]{:S(2)}) collective-permute-start(bf16[16,4096]{1,0:T(8,128)(2,1)S(1)} %collective-permute-done.10.refs_1_), channel_id=1, source_target_pairs={{0,4},{4,0},{8,12},{12,8},{16,20},{20,16},{24,28},{28,24},{1,5},{5... | collective-permute-start | bytes 393224 | tf_op jit(solution)/shard_map/ppermute | solution.py:293
  21.3 1.6 %collective-permute-start.7 = (bf16[160,512]{1,0:T(8,128)(2,1)S(1)}, bf16[160,512]{1,0:T(8,128)(2,1)S(1)}, u32[]{:S(2)}, u32[]{:S(2)}) collective-permute-start(bf16[160,512]{1,0:T(8,128)(2,1)S(1)} %get-tuple-element.69), channel_id=1, source_target_pairs={{0,1},{1,0},{2,3},{3,2},{4,5},{5,4},{6,7},{7,6},{8,9},{9,8},{10,11... | collective-permute-start | bytes 491528 | tf_op jit(solution)/shard_map/ppermute | solution.py:293
  22.8 3.0 %forward_products.3 = (bf16[64,512]{1,0:T(8,128)(2,1)S(1)}, bf16[64,512]{1,0:T(8,128)(2,1)S(1)}, bf16[128,512]{1,0:T(8,128)(2,1)S(1)}) custom-call(s32[1]{0:T(128)} %bitcast.1.place, s32[1,1]{1,0:T(1,128)S(6)} %copy.10.count, s32[96]{0:T(128)S(1)} %get-tuple-element.60.rows, s32[96]{0:T(128)S(1)} %get-tuple-element.61.cols, ...), custom_call_target="tpu_custom_call" | custom-call | flops 1 | bytes 1 | tf_op jit(solution)/shard_map/forward_products/pallas_call | solution.py:154
  25.8 1.1 %collective-permute-start.13 = (bf16[128,512]{1,0:T(8,128)(2,1)S(1)}, bf16[128,512]{1,0:T(8,128)(2,1)S(1)}, u32[]{:S(2)}, u32[]{:S(2)}) collective-permute-start(bf16[128,512]{1,0:T(8,128)(2,1)S(1)} %get-tuple-element.77), channel_id=1, source_target_pairs={{0,1},{1,0},{2,3},{3,2},{4,5},{5,4},{6,7},{7,6},{8,9},{9,8},{10,11... | collective-permute-start | bytes 393224 | tf_op jit(solution)/shard_map/ppermute | solution.py:293
  27.0 2.7 %collective-permute-start.6 = (bf16[112,512]{1,0:T(8,128)(2,1)S(1)}, bf16[112,512]{1,0:T(8,128)(2,1)S(1)}, u32[]{:S(2)}, u32[]{:S(2)}) collective-permute-start(bf16[112,512]{1,0:T(8,128)(2,1)S(1)} %pass_on.3), channel_id=1, source_target_pairs={{0,2},{1,3},{2,0},{3,1},{4,6},{5,7},{6,4},{7,5},{8,10},{9,11},{10,... | collective-permute-start | bytes 344072 | tf_op jit(solution)/shard_map/ppermute | solution.py:293
  30.9 3.5 %collective-permute-done.13.refs_1_.refs_7_ = bf16[128,512]{1,0:T(8,128)(2,1)S(1)} collective-permute-done((bf16[128,512]{1,0:T(8,128)(2,1)S(1)}, bf16[128,512]{1,0:T(8,128)(2,1)S(1)}, u32[]{:S(2)}, u32[]{:S(2)}) %collective-permute-start.13) | collective-permute-done | bytes 131104 | tf_op jit(solution)/shard_map/ppermute | solution.py:293
  35.4 5.8 %collective-permute-done.8.refs_5_ = bf16[80,512]{1,0:T(8,128)(2,1)S(1)} collective-permute-done((bf16[80,512]{1,0:T(8,128)(2,1)S(1)}, bf16[80,512]{1,0:T(8,128)(2,1)S(1)}, u32[]{:S(2)}, u32[]{:S(2)}) %collective-permute-start.8) | collective-permute-done | bytes 81952 | tf_op jit(solution)/shard_map/ppermute | solution.py:293
  41.2 1.4 %collective-permute-done.14.refs_8_ = bf16[64,512]{1,0:T(8,128)(2,1)S(1)} collective-permute-done((bf16[64,512]{1,0:T(8,128)(2,1)S(1)}, bf16[64,512]{1,0:T(8,128)(2,1)S(1)}, u32[]{:S(2)}, u32[]{:S(2)}) %collective-permute-start.14) | collective-permute-done | bytes 65568 | tf_op jit(solution)/shard_map/ppermute | solution.py:293
  42.6 1.1 %layer.1 = (bf16[512,256]{1,0:T(8,128)(2,1)}, bf16[512,256]{1,0:T(8,128)(2,1)S(1)}, bf16[256,512]{1,0:T(8,128)(2,1)S(1)}, bf16[256,512]{1,0:T(8,128)(2,1)S(1)}, ...) custom-call(s32[1]{0:T(128)} %bitcast.row, bf16[256,256]{1,0:T(8,128)(2,1)S(1)} %copy-done.2, ...), custom_call_target="tpu_custom_call" | custom-call | flops 1 | bytes 1 | tf_op jit(solution)/shard_map/layer/pallas_call | solution.py:257
  43.7 2.6 %collective-permute-start.16 = (bf16[128,512]{1,0:T(8,128)(2,1)S(1)}, bf16[128,512]{1,0:T(8,128)(2,1)S(1)}, u32[]{:S(2)}, u32[]{:S(2)}) collective-permute-start(bf16[128,512]{1,0:T(8,128)(2,1)S(1)} %get-tuple-element.82), channel_id=1, source_target_pairs={{0,2},{1,3},{2,0},{3,1},{4,6},{5,7},{6,4},{7,5},{8,10},{9,11},{10,... | collective-permute-start | bytes 393224 | tf_op jit(solution)/shard_map/ppermute | solution.py:293
  48.0 1.1 %collective-permute-start.20 = (f32[32,256]{1,0:T(8,128)S(1)}, f32[32,256]{1,0:T(8,128)S(1)}, u32[]{:S(2)}, u32[]{:S(2)}) collective-permute-start(f32[32,256]{1,0:T(8,128)S(1)} %get-tuple-element.91), channel_id=1, source_target_pairs={{0,8},{4,12},{8,0},{12,4},{16,24},{20,28},{24,16},{28,20},{1,9},{5... | collective-permute-start | bytes 98312 | tf_op jit(solution)/shard_map/ppermute | solution.py:293
  49.7 1.8 %collective-permute-start.22 = (f32[32,256]{1,0:T(8,128)S(1)}, f32[32,256]{1,0:T(8,128)S(1)}, u32[]{:S(2)}, u32[]{:S(2)}) collective-permute-start(f32[32,256]{1,0:T(8,128)S(1)} %get-tuple-element.93), channel_id=1, source_target_pairs={{0,24},{4,28},{8,16},{12,20},{16,8},{20,12},{24,0},{28,4},{1,25},{... | collective-permute-start | bytes 98312 | tf_op jit(solution)/shard_map/ppermute | solution.py:293
  51.6 3.3 %collective-permute-done.19.refs_1_ = bf16[256,512]{1,0:T(8,128)(2,1)S(1)} collective-permute-done((bf16[256,512]{1,0:T(8,128)(2,1)S(1)}, bf16[256,512]{1,0:T(8,128)(2,1)S(1)}, u32[]{:S(2)}, u32[]{:S(2)}) %collective-permute-start.19) | collective-permute-done | bytes 262176 | tf_op jit(solution)/shard_map/ppermute | solution.py:293
  54.9 2.2 %collective-permute-start.25 = (bf16[128,512]{1,0:T(8,128)(2,1)S(1)}, bf16[128,512]{1,0:T(8,128)(2,1)S(1)}, u32[]{:S(2)}, u32[]{:S(2)}) collective-permute-start(bf16[128,512]{1,0:T(8,128)(2,1)S(1)} %collective-permute-done.16.refs_2_), channel_id=1, source_target_pairs={{0,1},{1,0},{2,3},{3,2},{4,5},{5,4},{6,7},{7,6},{8,9},{9,8},{10,11... | collective-permute-start | bytes 393224 | tf_op jit(solution)/shard_map/ppermute | solution.py:293
  57.9 5.0 %collective-permute-done.15.refs_0_.refs_2_ = bf16[128,512]{1,0:T(8,128)(2,1)S(1)} collective-permute-done((bf16[128,512]{1,0:T(8,128)(2,1)S(1)}, bf16[128,512]{1,0:T(8,128)(2,1)S(1)}, u32[]{:S(2)}, u32[]{:S(2)}) %collective-permute-start.15) | collective-permute-done | bytes 131104 | tf_op jit(solution)/shard_map/ppermute | solution.py:293
  63.9 2.7 %backward_products.2 = (bf16[64,4096]{1,0:T(8,128)(2,1)S(1)}, bf16[16,4096]{1,0:T(8,128)(2,1)S(1)}, bf16[16,4096]{1,0:T(8,128)(2,1)S(1)}, bf16[16,4096]{1,0:T(8,128)(2,1)S(1)}, bf16[16,4096]{1,0:T(8,128)(2,1)S(1)}) custom-call(s32[1]{0:T(128)} %bitcast.1.place, s32[1,1]{1,0:T(1,128)S(6)} %copy.10.count, s32[96]{0:T(128)S(1)} %get-tuple-element.60.rows, ...), custom_call_target="tpu_custom_call" | custom-call | flops 1 | bytes 1 | tf_op jit(solution)/shard_map/backward_products/pallas_call | solution.py:197
  69.0 1.0 %collective-permute-start.32 = (bf16[32,4224]{1,0:T(8,128)(2,1)S(1)}, bf16[32,4224]{1,0:T(8,128)(2,1)S(1)}, u32[]{:S(2)}, u32[]{:S(2)}) collective-permute-start(bf16[32,4224]{1,0:T(8,128)(2,1)S(1)} %get-tuple-element.103), channel_id=1, source_target_pairs={{0,16},{4,20},{8,24},{12,28},{16,0},{20,4},{24,8},{28,12},{1,17},{... | collective-permute-start | bytes 811016 | tf_op jit(solution)/shard_map/ppermute | solution.py:293
  70.1 2.7 %backward_products.3 = (bf16[64,4096]{1,0:T(8,128)(2,1)S(1)}, bf16[32,4096]{1,0:T(8,128)(2,1)S(1)}, bf16[32,4096]{1,0:T(8,128)(2,1)S(1)}) custom-call(s32[1]{0:T(128)} %bitcast.1.place, s32[1,1]{1,0:T(1,128)S(6)} %copy.10.count, s32[96]{0:T(128)S(1)} %get-tuple-element.60.rows, s32[96]{0:T(128)S(1)} %get-tuple-element.61.cols, ...), custom_call_target="tpu_custom_call" | custom-call | flops 1 | bytes 1 | tf_op jit(solution)/shard_map/backward_products/pallas_call | solution.py:197
  73.5 4.2 %collective-permute-done.31.refs_1_ = bf16[32,4224]{1,0:T(8,128)(2,1)S(1)} collective-permute-done((bf16[32,4224]{1,0:T(8,128)(2,1)S(1)}, bf16[32,4224]{1,0:T(8,128)(2,1)S(1)}, u32[]{:S(2)}, u32[]{:S(2)}) %collective-permute-start.31) | collective-permute-done | bytes 270368 | tf_op jit(solution)/shard_map/ppermute | solution.py:293
  78.0 1.5 %collective-permute-start.35 = (bf16[32,4608]{1,0:T(8,128)(2,1)S(1)}, bf16[32,4608]{1,0:T(8,128)(2,1)S(1)}, u32[]{:S(2)}, u32[]{:S(2)}) collective-permute-start(bf16[32,4608]{1,0:T(8,128)(2,1)S(1)} %get-tuple-element.111), channel_id=1, source_target_pairs={{0,24},{4,28},{8,16},{12,20},{16,8},{20,12},{24,0},{28,4},{1,25},{... | collective-permute-start | bytes 884744 | tf_op jit(solution)/shard_map/ppermute | solution.py:293
  80.2 1.3 %collective-permute-start.37 = (bf16[32,512]{1,0:T(8,128)(2,1)S(1)}, bf16[32,512]{1,0:T(8,128)(2,1)S(1)}, u32[]{:S(2)}, u32[]{:S(2)}) collective-permute-start(bf16[32,512]{1,0:T(8,128)(2,1)S(1)} %get-tuple-element.112.refs_4_), channel_id=1, source_target_pairs={{0,16},{4,20},{8,24},{12,28},{16,0},{20,4},{24,8},{28,12},{1,17},{... | collective-permute-start | bytes 98312 | tf_op jit(solution)/shard_map/ppermute | solution.py:293
  81.5 5.5 %collective-permute-done.36.refs_5_ = bf16[32,512]{1,0:T(8,128)(2,1)S(1)} collective-permute-done((bf16[32,512]{1,0:T(8,128)(2,1)S(1)}, bf16[32,512]{1,0:T(8,128)(2,1)S(1)}, u32[]{:S(2)}, u32[]{:S(2)}) %collective-permute-start.36) | collective-permute-done | bytes 32800 | tf_op jit(solution)/shard_map/ppermute | solution.py:293
  87.0 1.0 %collective-permute-done.37.refs_6_ = bf16[32,512]{1,0:T(8,128)(2,1)S(1)} collective-permute-done((bf16[32,512]{1,0:T(8,128)(2,1)S(1)}, bf16[32,512]{1,0:T(8,128)(2,1)S(1)}, u32[]{:S(2)}, u32[]{:S(2)}) %collective-permute-start.37) | collective-permute-done | bytes 32800 | tf_op jit(solution)/shard_map/ppermute | solution.py:293
  (67 shorter events, 12.0 us)
Async XLA Ops:
  0.6 9.5 %collective-permute-start.1 = (bf16[32,4096]{1,0:T(8,128)(2,1)}, bf16[32,4096]{1,0:T(8,128)(2,1)S(1)}, u32[]{:S(2)}, u32[]{:S(2)}) collective-permute-start(bf16[32,4096]{1,0:T(8,128)(2,1)} %bitcast.7), channel_id=1, source_target_pairs={{0,8},{4,12},{8,0},{12,4},{16,24},{20,28},{24,16},{28,20},{1,9},{5... | collective-permute-start | bytes 786440 | tf_op jit(solution)/shard_map/ppermute | solution.py:293
  3.7 8.0 %collective-permute-start.3 = (bf16[32,4096]{1,0:T(8,128)(2,1)}, bf16[32,4096]{1,0:T(8,128)(2,1)S(1)}, u32[]{:S(2)}, u32[]{:S(2)}) collective-permute-start(bf16[32,4096]{1,0:T(8,128)(2,1)} %bitcast.8), channel_id=1, source_target_pairs={{0,16},{4,20},{8,24},{12,28},{16,0},{20,4},{24,8},{28,12},{1,17},{... | collective-permute-start | bytes 786440 | tf_op jit(solution)/shard_map/ppermute | solution.py:293
  5.2 9.4 %collective-permute-start = (bf16[32,4096]{1,0:T(8,128)(2,1)}, bf16[32,4096]{1,0:T(8,128)(2,1)S(1)}, u32[]{:S(2)}, u32[]{:S(2)}) collective-permute-start(bf16[32,4096]{1,0:T(8,128)(2,1)} %bitcast.9), channel_id=1, source_target_pairs={{0,4},{4,0},{8,12},{12,8},{16,20},{20,16},{24,28},{28,24},{1,5},{5... | collective-permute-start | bytes 786440 | tf_op jit(solution)/shard_map/ppermute | solution.py:293
  10.2 4.4 %collective-permute-start.2 = (bf16[32,4096]{1,0:T(8,128)(2,1)S(1)}, bf16[32,4096]{1,0:T(8,128)(2,1)S(1)}, u32[]{:S(2)}, u32[]{:S(2)}) collective-permute-start(bf16[32,4096]{1,0:T(8,128)(2,1)S(1)} %collective-permute-done.1.refs_2_), channel_id=1, source_target_pairs={{0,4},{4,0},{8,12},{12,8},{16,20},{20,16},{24,28},{28,24},{1,5},{5... | collective-permute-start | bytes 786440 | tf_op jit(solution)/shard_map/ppermute | solution.py:293
  11.6 2.9 %collective-permute-start.4 = (bf16[32,4096]{1,0:T(8,128)(2,1)S(1)}, bf16[32,4096]{1,0:T(8,128)(2,1)S(1)}, u32[]{:S(2)}, u32[]{:S(2)}) collective-permute-start(bf16[32,4096]{1,0:T(8,128)(2,1)S(1)} %collective-permute-done.3.refs_4_), channel_id=1, source_target_pairs={{0,4},{4,0},{8,12},{12,8},{16,20},{20,16},{24,28},{28,24},{1,5},{5... | collective-permute-start | bytes 786440 | tf_op jit(solution)/shard_map/ppermute | solution.py:293
  11.6 7.9 %collective-permute-start.10 = (bf16[16,4096]{1,0:T(8,128)(2,1)S(1)}, bf16[16,4096]{1,0:T(8,128)(2,1)S(1)}, u32[]{:S(2)}, u32[]{:S(2)}) collective-permute-start(bf16[16,4096]{1,0:T(8,128)(2,1)S(1)} %get-tuple-element.74), channel_id=1, source_target_pairs={{0,24},{4,28},{8,16},{12,20},{16,8},{20,12},{24,0},{28,4},{1,25},{... | collective-permute-start | bytes 393224 | tf_op jit(solution)/shard_map/ppermute | solution.py:293
  13.4 7.9 %collective-permute-start.9 = (bf16[16,4096]{1,0:T(8,128)(2,1)S(1)}, bf16[16,4096]{1,0:T(8,128)(2,1)S(1)}, u32[]{:S(2)}, u32[]{:S(2)}) collective-permute-start(bf16[16,4096]{1,0:T(8,128)(2,1)S(1)} %get-tuple-element.72), channel_id=1, source_target_pairs={{0,24},{4,28},{8,16},{12,20},{16,8},{20,12},{24,0},{28,4},{1,25},{... | collective-permute-start | bytes 393224 | tf_op jit(solution)/shard_map/ppermute | solution.py:293
  18.2 8.8 %collective-permute-start.5 = (bf16[224,512]{1,0:T(8,128)(2,1)S(1)}, bf16[224,512]{1,0:T(8,128)(2,1)S(1)}, u32[]{:S(2)}, u32[]{:S(2)}) collective-permute-start(bf16[224,512]{1,0:T(8,128)(2,1)S(1)} %get-tuple-element.66), channel_id=1, source_target_pairs={{0,1},{1,0},{2,3},{3,2},{4,5},{5,4},{6,7},{7,6},{8,9},{9,8},{10,11... | collective-permute-start | bytes 688136 | tf_op jit(solution)/shard_map/ppermute | solution.py:293
  19.5 3.3 %collective-permute-start.12 = (bf16[16,4096]{1,0:T(8,128)(2,1)S(1)}, bf16[16,4096]{1,0:T(8,128)(2,1)S(1)}, u32[]{:S(2)}, u32[]{:S(2)}) collective-permute-start(bf16[16,4096]{1,0:T(8,128)(2,1)S(1)} %collective-permute-done.10.refs_1_), channel_id=1, source_target_pairs={{0,4},{4,0},{8,12},{12,8},{16,20},{20,16},{24,28},{28,24},{1,5},{5... | collective-permute-start | bytes 393224 | tf_op jit(solution)/shard_map/ppermute | solution.py:293
  21.2 1.6 %collective-permute-start.11 = (bf16[16,4096]{1,0:T(8,128)(2,1)S(1)}, bf16[16,4096]{1,0:T(8,128)(2,1)S(1)}, u32[]{:S(2)}, u32[]{:S(2)}) collective-permute-start(bf16[16,4096]{1,0:T(8,128)(2,1)S(1)} %collective-permute-done.9.refs_0_), channel_id=1, source_target_pairs={{0,4},{4,0},{8,12},{12,8},{16,20},{20,16},{24,28},{28,24},{1,5},{5... | collective-permute-start | bytes 393224 | tf_op jit(solution)/shard_map/ppermute | solution.py:293
  21.3 8.9 %collective-permute-start.7 = (bf16[160,512]{1,0:T(8,128)(2,1)S(1)}, bf16[160,512]{1,0:T(8,128)(2,1)S(1)}, u32[]{:S(2)}, u32[]{:S(2)}) collective-permute-start(bf16[160,512]{1,0:T(8,128)(2,1)S(1)} %get-tuple-element.69), channel_id=1, source_target_pairs={{0,1},{1,0},{2,3},{3,2},{4,5},{5,4},{6,7},{7,6},{8,9},{9,8},{10,11... | collective-permute-start | bytes 491528 | tf_op jit(solution)/shard_map/ppermute | solution.py:293
  25.8 8.6 %collective-permute-start.13 = (bf16[128,512]{1,0:T(8,128)(2,1)S(1)}, bf16[128,512]{1,0:T(8,128)(2,1)S(1)}, u32[]{:S(2)}, u32[]{:S(2)}) collective-permute-start(bf16[128,512]{1,0:T(8,128)(2,1)S(1)} %get-tuple-element.77), channel_id=1, source_target_pairs={{0,1},{1,0},{2,3},{3,2},{4,5},{5,4},{6,7},{7,6},{8,9},{9,8},{10,11... | collective-permute-start | bytes 393224 | tf_op jit(solution)/shard_map/ppermute | solution.py:293
  27.0 15.6 %collective-permute-start.6 = (bf16[112,512]{1,0:T(8,128)(2,1)S(1)}, bf16[112,512]{1,0:T(8,128)(2,1)S(1)}, u32[]{:S(2)}, u32[]{:S(2)}) collective-permute-start(bf16[112,512]{1,0:T(8,128)(2,1)S(1)} %pass_on.3), channel_id=1, source_target_pairs={{0,2},{1,3},{2,0},{3,1},{4,6},{5,7},{6,4},{7,5},{8,10},{9,11},{10,... | collective-permute-start | bytes 344072 | tf_op jit(solution)/shard_map/ppermute | solution.py:293
  30.2 11.0 %collective-permute-start.8 = (bf16[80,512]{1,0:T(8,128)(2,1)S(1)}, bf16[80,512]{1,0:T(8,128)(2,1)S(1)}, u32[]{:S(2)}, u32[]{:S(2)}) collective-permute-start(bf16[80,512]{1,0:T(8,128)(2,1)S(1)} %pass_on.4), channel_id=1, source_target_pairs={{0,2},{1,3},{2,0},{3,1},{4,6},{5,7},{6,4},{7,5},{8,10},{9,11},{10,... | collective-permute-start | bytes 245768 | tf_op jit(solution)/shard_map/ppermute | solution.py:293
  34.5 8.1 %collective-permute-start.14 = (bf16[64,512]{1,0:T(8,128)(2,1)S(1)}, bf16[64,512]{1,0:T(8,128)(2,1)S(1)}, u32[]{:S(2)}, u32[]{:S(2)}) collective-permute-start(bf16[64,512]{1,0:T(8,128)(2,1)S(1)} %pass_on.5), channel_id=1, source_target_pairs={{0,2},{1,3},{2,0},{3,1},{4,6},{5,7},{6,4},{7,5},{8,10},{9,11},{10,... | collective-permute-start | bytes 196616 | tf_op jit(solution)/shard_map/ppermute | solution.py:293
  43.7 11.1 %collective-permute-start.19 = (bf16[256,512]{1,0:T(8,128)(2,1)S(1)}, bf16[256,512]{1,0:T(8,128)(2,1)S(1)}, u32[]{:S(2)}, u32[]{:S(2)}) collective-permute-start(bf16[256,512]{1,0:T(8,128)(2,1)S(1)} %get-tuple-element.89.refs_0_), channel_id=1, source_target_pairs={{0,1},{1,0},{2,3},{3,2},{4,5},{5,4},{6,7},{7,6},{8,9},{9,8},{10,11... | collective-permute-start | bytes 786440 | tf_op jit(solution)/shard_map/ppermute | solution.py:293
  43.7 11.2 %collective-permute-start.16 = (bf16[128,512]{1,0:T(8,128)(2,1)S(1)}, bf16[128,512]{1,0:T(8,128)(2,1)S(1)}, u32[]{:S(2)}, u32[]{:S(2)}) collective-permute-start(bf16[128,512]{1,0:T(8,128)(2,1)S(1)} %get-tuple-element.82), channel_id=1, source_target_pairs={{0,2},{1,3},{2,0},{3,1},{4,6},{5,7},{6,4},{7,5},{8,10},{9,11},{10,... | collective-permute-start | bytes 393224 | tf_op jit(solution)/shard_map/ppermute | solution.py:293
  48.0 6.8 %collective-permute-start.20 = (f32[32,256]{1,0:T(8,128)S(1)}, f32[32,256]{1,0:T(8,128)S(1)}, u32[]{:S(2)}, u32[]{:S(2)}) collective-permute-start(f32[32,256]{1,0:T(8,128)S(1)} %get-tuple-element.91), channel_id=1, source_target_pairs={{0,8},{4,12},{8,0},{12,4},{16,24},{20,28},{24,16},{28,20},{1,9},{5... | collective-permute-start | bytes 98312 | tf_op jit(solution)/shard_map/ppermute | solution.py:293
  49.1 5.8 %collective-permute-start.21 = (f32[32,256]{1,0:T(8,128)S(1)}, f32[32,256]{1,0:T(8,128)S(1)}, u32[]{:S(2)}, u32[]{:S(2)}) collective-permute-start(f32[32,256]{1,0:T(8,128)S(1)} %get-tuple-element.92), channel_id=1, source_target_pairs={{0,16},{4,20},{8,24},{12,28},{16,0},{20,4},{24,8},{28,12},{1,17},{... | collective-permute-start | bytes 98312 | tf_op jit(solution)/shard_map/ppermute | solution.py:293
  49.7 5.1 %collective-permute-start.22 = (f32[32,256]{1,0:T(8,128)S(1)}, f32[32,256]{1,0:T(8,128)S(1)}, u32[]{:S(2)}, u32[]{:S(2)}) collective-permute-start(f32[32,256]{1,0:T(8,128)S(1)} %get-tuple-element.93), channel_id=1, source_target_pairs={{0,24},{4,28},{8,16},{12,20},{16,8},{20,12},{24,0},{28,4},{1,25},{... | collective-permute-start | bytes 98312 | tf_op jit(solution)/shard_map/ppermute | solution.py:293
  54.8 8.1 %collective-permute-start.15 = (bf16[128,512]{1,0:T(8,128)(2,1)S(1)}, bf16[128,512]{1,0:T(8,128)(2,1)S(1)}, u32[]{:S(2)}, u32[]{:S(2)}) collective-permute-start(bf16[128,512]{1,0:T(8,128)(2,1)S(1)} %get-tuple-element.81), channel_id=1, source_target_pairs={{0,2},{1,3},{2,0},{3,1},{4,6},{5,7},{6,4},{7,5},{8,10},{9,11},{10,... | collective-permute-start | bytes 393224 | tf_op jit(solution)/shard_map/ppermute | solution.py:293
  54.9 9.1 %collective-permute-start.25 = (bf16[128,512]{1,0:T(8,128)(2,1)S(1)}, bf16[128,512]{1,0:T(8,128)(2,1)S(1)}, u32[]{:S(2)}, u32[]{:S(2)}) collective-permute-start(bf16[128,512]{1,0:T(8,128)(2,1)S(1)} %collective-permute-done.16.refs_2_), channel_id=1, source_target_pairs={{0,1},{1,0},{2,3},{3,2},{4,5},{5,4},{6,7},{7,6},{8,9},{9,8},{10,11... | collective-permute-start | bytes 393224 | tf_op jit(solution)/shard_map/ppermute | solution.py:293
  57.1 6.5 %collective-permute-start.23 = (f32[32,256]{1,0:T(8,128)S(1)}, f32[32,256]{1,0:T(8,128)S(1)}, u32[]{:S(2)}, u32[]{:S(2)}) collective-permute-start(f32[32,256]{1,0:T(8,128)S(1)} %chunk_sum.2.refs_1_), channel_id=1, source_target_pairs={{0,2},{1,3},{2,0},{3,1},{4,6},{5,7},{6,4},{7,5},{8,10},{9,11},{10,... | collective-permute-start | bytes 98312 | tf_op jit(solution)/shard_map/ppermute | solution.py:293
  63.6 6.4 %collective-permute-start.24 = (bf16[160,512]{1,0:T(8,128)(2,1)S(1)}, bf16[160,512]{1,0:T(8,128)(2,1)S(1)}, u32[]{:S(2)}, u32[]{:S(2)}) collective-permute-start(bf16[160,512]{1,0:T(8,128)(2,1)S(1)} %with_chunk.1.refs_0_), channel_id=1, source_target_pairs={{0,1},{1,0},{2,3},{3,2},{4,5},{5,4},{6,7},{7,6},{8,9},{9,8},{10,11... | collective-permute-start | bytes 491528 | tf_op jit(solution)/shard_map/ppermute | solution.py:293
  69.0 8.8 %collective-permute-start.31 = (bf16[32,4224]{1,0:T(8,128)(2,1)S(1)}, bf16[32,4224]{1,0:T(8,128)(2,1)S(1)}, u32[]{:S(2)}, u32[]{:S(2)}) collective-permute-start(bf16[32,4224]{1,0:T(8,128)(2,1)S(1)} %get-tuple-element.102), channel_id=1, source_target_pairs={{0,8},{4,12},{8,0},{12,4},{16,24},{20,28},{24,16},{28,20},{1,9},{5... | collective-permute-start | bytes 811016 | tf_op jit(solution)/shard_map/ppermute | solution.py:293
  69.0 8.8 %collective-permute-start.32 = (bf16[32,4224]{1,0:T(8,128)(2,1)S(1)}, bf16[32,4224]{1,0:T(8,128)(2,1)S(1)}, u32[]{:S(2)}, u32[]{:S(2)}) collective-permute-start(bf16[32,4224]{1,0:T(8,128)(2,1)S(1)} %get-tuple-element.103), channel_id=1, source_target_pairs={{0,16},{4,20},{8,24},{12,28},{16,0},{20,4},{24,8},{28,12},{1,17},{... | collective-permute-start | bytes 811016 | tf_op jit(solution)/shard_map/ppermute | solution.py:293
  72.8 5.0 %collective-permute-start.33 = (bf16[32,4096]{1,0:T(8,128)(2,1)S(1)}, bf16[32,4096]{1,0:T(8,128)(2,1)S(1)}, u32[]{:S(2)}, u32[]{:S(2)}) collective-permute-start(bf16[32,4096]{1,0:T(8,128)(2,1)S(1)} %get-tuple-element.108), channel_id=1, source_target_pairs={{0,4},{4,0},{8,12},{12,8},{16,20},{20,16},{24,28},{28,24},{1,5},{5... | collective-permute-start | bytes 786440 | tf_op jit(solution)/shard_map/ppermute | solution.py:293
  72.9 4.9 %collective-permute-start.34 = (bf16[32,4096]{1,0:T(8,128)(2,1)S(1)}, bf16[32,4096]{1,0:T(8,128)(2,1)S(1)}, u32[]{:S(2)}, u32[]{:S(2)}) collective-permute-start(bf16[32,4096]{1,0:T(8,128)(2,1)S(1)} %get-tuple-element.109), channel_id=1, source_target_pairs={{0,4},{4,0},{8,12},{12,8},{16,20},{20,16},{24,28},{28,24},{1,5},{5... | collective-permute-start | bytes 786440 | tf_op jit(solution)/shard_map/ppermute | solution.py:293
  73.4 4.4 %collective-permute-start.30 = (f32[32,256]{1,0:T(8,128)S(1)}, f32[32,256]{1,0:T(8,128)S(1)}, u32[]{:S(2)}, u32[]{:S(2)}) collective-permute-start(f32[32,256]{1,0:T(8,128)S(1)} %chunk_sum.3.refs_0_), channel_id=1, source_target_pairs={{0,4},{4,0},{8,12},{12,8},{16,20},{20,16},{24,28},{28,24},{1,5},{5... | collective-permute-start | bytes 98312 | tf_op jit(solution)/shard_map/ppermute | solution.py:293
  78.0 10.1 %collective-permute-start.35 = (bf16[32,4608]{1,0:T(8,128)(2,1)S(1)}, bf16[32,4608]{1,0:T(8,128)(2,1)S(1)}, u32[]{:S(2)}, u32[]{:S(2)}) collective-permute-start(bf16[32,4608]{1,0:T(8,128)(2,1)S(1)} %get-tuple-element.111), channel_id=1, source_target_pairs={{0,24},{4,28},{8,16},{12,20},{16,8},{20,12},{24,0},{28,4},{1,25},{... | collective-permute-start | bytes 884744 | tf_op jit(solution)/shard_map/ppermute | solution.py:293
  79.4 7.6 %collective-permute-start.36 = (bf16[32,512]{1,0:T(8,128)(2,1)S(1)}, bf16[32,512]{1,0:T(8,128)(2,1)S(1)}, u32[]{:S(2)}, u32[]{:S(2)}) collective-permute-start(bf16[32,512]{1,0:T(8,128)(2,1)S(1)} %get-tuple-element.112.refs_4_), channel_id=1, source_target_pairs={{0,8},{4,12},{8,0},{12,4},{16,24},{20,28},{24,16},{28,20},{1,9},{5... | collective-permute-start | bytes 98312 | tf_op jit(solution)/shard_map/ppermute | solution.py:293
  80.2 7.9 %collective-permute-start.37 = (bf16[32,512]{1,0:T(8,128)(2,1)S(1)}, bf16[32,512]{1,0:T(8,128)(2,1)S(1)}, u32[]{:S(2)}, u32[]{:S(2)}) collective-permute-start(bf16[32,512]{1,0:T(8,128)(2,1)S(1)} %get-tuple-element.112.refs_4_), channel_id=1, source_target_pairs={{0,16},{4,20},{8,24},{12,28},{16,0},{20,4},{24,8},{28,12},{1,17},{... | collective-permute-start | bytes 98312 | tf_op jit(solution)/shard_map/ppermute | solution.py:293
  (9 other events, 71.2 us)

commit v2 on v1

--- a/solution.py
+++ b/solution.py
@@ -116,9 +116,10 @@
 
 
 def forward_kernel(n_parts, depths, layout, place, count, rows, cols, adj, *refs):
-    parts = refs[:n_parts]
-    outs = refs[n_parts:-2]
+    parts, refs = refs[:n_parts], refs[n_parts:]
     source, total = refs[-2:]
+    outs = refs[-2 - len(depths) * len(layout) : -2]
+    carried = refs[: len(refs) - 2 - len(outs)]
     size = adj.shape[1]
     row = 0
     for part in parts:
@@ -128,33 +129,38 @@
         row += depth
     product_loop(count[0, 0], cols, rows, adj, source, total, NT)
     blocks = outs[0].shape[1] // size
+    ahead = carried[0].shape[0] // len(layout[0]) if carried else 0
     outs = iter(outs)
     row = 0
     for depth in depths:
-        for chunks in layout:
+        for m, chunks in enumerate(layout):
             out = next(outs)
             for n, k in enumerate(chunks):
+                begin = n * (ahead + depth)
+                if ahead:
+                    out[begin : begin + ahead, :] = carried[m][n * ahead : (n + 1) * ahead, :]
                 first = (place[0] ^ k) * blocks
                 for i in range(blocks):
-                    out[n * depth : (n + 1) * depth, i * size : (i + 1) * size] = total[
+                    out[begin + ahead : begin + ahead + depth, i * size : (i + 1) * size] = total[
                         first + i, row : row + depth, :
                     ].astype(out.dtype)
         row += depth
 
 
-def forward(place, count, rows, cols, adj, parts, row_blocks, depths, layout):
+def forward(place, count, rows, cols, adj, parts, row_blocks, depths, layout, carried=()):
     size = adj.shape[1]
     col_blocks = parts[0].shape[1] // size
     wide = row_blocks * size // sum(len(chunks) for chunks in layout)
+    ahead = carried[0].shape[0] // len(layout[0]) if carried else 0
     outs = [
-        jax.ShapeDtypeStruct((len(chunks) * depth, wide), jnp.bfloat16)
+        jax.ShapeDtypeStruct((len(chunks) * (ahead + depth), wide), jnp.bfloat16)
         for depth in depths
         for chunks in layout
     ]
     return pl.pallas_call(
         functools.partial(forward_kernel, len(parts), depths, layout),
         out_shape=outs,
-        in_specs=[SMEM] * 4 + [VMEM] * (1 + len(parts)),
+        in_specs=[SMEM] * 4 + [VMEM] * (1 + len(parts) + len(carried)),
         out_specs=[VMEM] * len(outs),
         scratch_shapes=[
             pltpu.VMEM((col_blocks, sum(depths), size), jnp.bfloat16),
@@ -163,7 +169,7 @@
         compiler_params=params(14),
         cost_estimate=COST,
         name="forward_products",
-    )(place, count, rows, cols, adj, *parts)
+    )(place, count, rows, cols, adj, *parts, *carried)
 
 
 def backward_kernel(spots, depths, place, count, rows, cols, adj, *refs):
@@ -212,7 +218,7 @@
 def middle_kernel(sizes, order, n_sum, n_row, row, weight, cotangent, *refs):
     terms = refs[: n_sum * len(sizes)]
     outs = refs[n_sum * len(sizes) : -1]
-    output, deltas, aggregated, *backs = outs
+    output, deltas, aggregated, back = outs
     ordered = refs[-1]
     depth = weight.shape[0] // n_row
     for j in range(n_row):
@@ -233,17 +239,11 @@
     delta = (cotangent[...].astype(jnp.float32) * slopes).astype(jnp.bfloat16)
     deltas[...] = delta
     product = lax.dot_general(ordered[...], delta, NT, preferred_element_type=jnp.float32)
-    product = product.astype(jnp.bfloat16)
-    rows = [product[k * depth : (k + 1) * depth, :] for k in order]
-    product = jnp.concatenate(rows)
-    first = 0
-    for back in backs:
-        first %= product.shape[0]
-        back[...] = product[first : first + back.shape[0], :]
-        first += back.shape[0]
-
-
-def middle(n_row, row, weight, cotangent, pieces, order, depths):
+    for n, k in enumerate(order):
+        back[n * depth : (n + 1) * depth, :] = product[k * depth : (k + 1) * depth, :].astype(jnp.bfloat16)
+
+
+def middle(n_row, row, weight, cotangent, pieces, order):
     sizes = [piece[0].shape[0] for piece in pieces]
     nodes = cotangent.shape[0]
     features = weight.shape[0]
@@ -252,7 +252,8 @@
         shape((nodes, features), jnp.bfloat16),
         shape((nodes, features), jnp.bfloat16),
         shape((features, nodes), jnp.bfloat16),
-    ] + [shape((depth, nodes), jnp.bfloat16) for depth in depths]
+        shape((features, nodes), jnp.bfloat16),
+    ]
     flat = [term for piece in pieces for term in piece]
     return pl.pallas_call(
         functools.partial(middle_kernel, sizes, order, len(pieces[0]), n_row),
@@ -304,11 +305,11 @@
     return lax.optimization_barrier((value, *earlier))[0]
 
 
-def with_chunk(rows, *parts):
+def with_chunk(first, rows, *parts):
     total = functools.reduce(jnp.add, parts)
     high = total.astype(jnp.bfloat16)
     low = (total - high.astype(jnp.float32)).astype(jnp.bfloat16)
-    return (jnp.concatenate([rows, jnp.concatenate([high, low], axis=1)]),)
+    return (jnp.concatenate([rows[first:], jnp.concatenate([high, low], axis=1)]),)
 
 
 def chunk_sum(depth, *values):
@@ -321,34 +322,61 @@
     return (total,)
 
 
-def pair_sum(mine, *received):
-    return tuple(mine + jnp.concatenate(received))
-
-
-def row_sums(depth, mine, *received):
-    total = mine.astype(jnp.float32) + jnp.concatenate(received).astype(jnp.float32)
-    total = jnp.concatenate([total, total[:, :128]], axis=1).astype(mine.dtype)
-    return tuple(total[first : first + depth] for first in range(0, total.shape[0], depth))
-
-
-def row_payloads(depth, chunk, sibling, mine, *received):
-    chunks = jnp.concatenate([chunk.astype(mine.dtype), sibling.astype(mine.dtype)], axis=1)
+def halves_sum(mine, *received):
+    total = mine + jnp.concatenate(received)
+    half = total.shape[0] // 2
+    return total[:half], total[half:]
+
+
+def far_sums(depth, mine, *received):
     total = mine.astype(jnp.float32) + jnp.concatenate(received).astype(jnp.float32)
     total = total.astype(mine.dtype)
-    own, *sums = [total[first : first + depth] for first in range(0, total.shape[0], depth)]
-    return chunks, own, *[jnp.concatenate([part, chunks], axis=1) for part in sums]
+    own, far = total[:depth], total[depth:]
+    return own, jnp.concatenate([far, far[:, :128]], axis=1)
+
+
+def near_kernel(row, chunk, sibling, half_way, mine, *refs):
+    received, (chunks, *sums) = refs[: -1 - 2], refs[-1 - 2 :]
+    depth = half_way.shape[0]
+    nodes = mine.shape[1]
+    for k, ref in enumerate((chunk, sibling)):
+        wide = ref.shape[1]
+        chunks[:, k * wide : (k + 1) * wide] = ref[...].astype(chunks.dtype)
+    passed = half_way[:, :nodes].astype(jnp.float32)
+    odd = row[0] % 2
+    for n, out in enumerate(sums):
+        total = mine[n * depth : (n + 1) * depth, :].astype(jnp.float32) + received[n][...].astype(jnp.float32)
+        total += jnp.where(odd == 1 - n, passed, 0.0)
+        out[:, :nodes] = total.astype(out.dtype)
+        out[:, nodes:] = chunks[...]
+
+
+def near_payloads(row, chunk, sibling, half_way, mine, received):
+    depth, nodes = received[0].shape
+    wide = 2 * chunk.shape[1]
+    shape = jax.ShapeDtypeStruct
+    return pl.pallas_call(
+        near_kernel,
+        out_shape=[shape((depth, wide), mine.dtype)]
+        + [shape((depth, nodes + wide), mine.dtype)] * len(received),
+        in_specs=[SMEM] + [VMEM] * (4 + len(received)),
+        out_specs=[VMEM] * (1 + len(received)),
+        compiler_params=params(8),
+        cost_estimate=COST,
+        name="near_payloads",
+    )(row, chunk, sibling, half_way, mine, *received)
 
 
 def finish_kernel(keys, row, *refs):
     grad_features, grad_weight = refs[-2:]
-    parts, chunks = refs[: len(keys)], refs[len(keys) : -2]
     depth, nodes = grad_features.shape
     wide = grad_weight.shape[1]
+    parts = [ref for ref in refs[:-2] if ref.shape[1] >= nodes]
+    values = [ref[...] for ref in refs[:-2] if ref.shape[1] < nodes] + [part[:, nodes:] for part in parts[1:]]
     total = parts[0][...].astype(jnp.float32)
     for part in parts[1:]:
         total += part[:, :nodes].astype(jnp.float32)
     grad_features[...] = total.astype(grad_features.dtype)
-    values = [ref[...] for ref in chunks] + [part[:, nodes:] for part in parts[len(chunks) :]]
     for key, value in zip(keys, values):
         for k in range(2):
             first = pl.multiple_of((row[0] ^ (key + k)) * depth, depth)
@@ -398,75 +426,68 @@
     def pass_on(beyond, received):
         return wide_sum(beyond, received[beyond.shape[0] :])
 
-    def forward_pieces(parts, depths):
-        outs = forward(col, count, rows, cols, tile, parts, row_blocks, depths, [(0,), (2,), (1, 3)])
-        outs = [outs[n : n + 3] for n in range(0, len(outs), 3)]
-        return [(kept, beyond, swap(sent, "col", 1)) for kept, beyond, sent in outs]
-
-    def fold(piece, *earlier):
-        kept, beyond, received = piece
-        received = after(received, *earlier)
+    layout = [(0,), (2,), (1, 3)]
+
+    def fold(kept, beyond, received):
         (passed,) = fuse("pass_on", pass_on, beyond, received)
         return [kept, received, swap(passed, "col", 2)]
 
     n_near = 2 * depth * (1 + len(near))
-    cut = n_near // 2 + 16
+    cut = n_near * 5 // 6
     parts = [own, sibling] + [piece for part in from_near for piece in (part, swap(part, "row", 1))]
-    pieces = forward_pieces(parts, [cut, n_near - cut])
-    from_far = [after(part, pieces[0][0]) for part in from_far]
+    kept, beyond, sent, *carried = forward(
+        col, count, rows, cols, tile, parts, row_blocks, [cut, n_near - cut], layout
+    )
+    received = swap(sent, "col", 1)
+    from_far = [after(part, kept) for part in from_far]
     parts = []
     for n in range(0, len(from_far), 2):
         halves = from_far[n : n + 2]
         parts += halves + [swap(half, "row", 1) for half in halves]
-    pieces += forward_pieces(parts, [2 * depth * len(far)])
-    sums = []
-    for piece in pieces:
-        sums.append(fold(piece, *(sums[-1][1:2] if sums else ())))
-
-    groups = [near, [0] + far]
+    far_piece = forward(
+        col, count, rows, cols, tile, parts, row_blocks, [2 * depth * len(far)], layout, carried
+    )
+    far_received = swap(far_piece[2], "col", 1)
+    first = fold(kept, beyond, after(received, far_piece[0]))
+    second = fold(*far_piece[:2], after(far_received, first[1]))
+    sums = [first, second]
+
+    groups = [[0] + far, near]
     order = [k + side for group in groups for side in range(2) for k in group]
     cuts = [2 * depth * len(group) for group in groups]
-    output, deltas, aggregated, back, *backs = middle(
-        n_row, row, weight, cotangent, sums, order, [sum(cuts)] + cuts
-    )
+    output, deltas, aggregated, back = middle(n_row, row, weight, cotangent, sums, order)
     beside = swap(back, "col", 1)
-    beyond = [swap(part, "col", 2) for part in backs]
-
-    evens = tuple(range(0, n_row, 2))
-    odds = tuple(range(1, n_row, 2))
-    even, *odd = gradient(1.0 / math.sqrt(nodes), [evens, odds[:2], odds[2:]], aggregated, deltas)
-    chunk, *sent = fuse("gradient_sum", pair_sum, even, *[swap(part, "row", 1) for part in odd])
-    from_rows = [swap(part, "row", k) for part, k in zip(sent, evens[1:])]
-    (chunk,) = fuse("chunk_sum", wide_sum, after(chunk, beside), *from_rows)
+    beyond = swap(back, "col", 2)
+
+    even, *odd = gradient(1.0 / math.sqrt(nodes), [(0, 4, 2, 6), (1, 5), (3, 7)], aggregated, deltas)
+    even, sent = fuse("gradient_sum", halves_sum, even, *[swap(part, "row", 1) for part in odd])
+    even, sent = fuse("gradient_sum", halves_sum, even, swap(sent, "row", 2))
+    (chunk,) = fuse("gradient_sum", lambda a, b: ((a + b)[0],), after(even, beside), swap(sent, "row", 4))
     chunks = [chunk, swap(chunk, "col", 2)]
 
-    beyond[0] = after(beyond[0], chunk)
-    (second,) = fuse("with_chunk", with_chunk, after(beyond[1], beyond[0]), *chunks)
-    received = [swap(beyond[0], "col", 1), swap(second, "col", 1)]
+    cut = cuts[0]
+    (first,) = fuse("first_rows", lambda rows: (rows[:cut],), after(beyond, *chunks))
+    (second,) = fuse("with_chunk", functools.partial(with_chunk, cut), after(beyond, first), *chunks)
+    received = [swap(first, "col", 1), swap(second, "col", 1)]
 
     def columns(n, *earlier):
-        parts = [back, beside, after(beyond[n], *earlier), received[n]]
-        spots = [[(0, n * cuts[0])], [(1, n * cuts[0])], [(2, 0)], [(3, 0)]]
+        parts = [back, beside, after(beyond, *earlier), received[n]]
+        spots = [[(part, n * cut)] for part in range(3)] + [[(3, 0)]]
         out_depths = [cuts[n] // 2] + [cuts[n] // (8 - 4 * n)] * (4 - 2 * n)
         mine, *sent = backward(
             col, count, rows, cols, tile, parts, spots, cuts[n : n + 1], out_depths, col_blocks
         )
         return [mine] + [swap(part, "row", 1) for part in sent]
 
-    sums = fuse("row_sums", functools.partial(row_sums, depth), *columns(0, second))
-    near_sums = [swap(part, "row", k) for part, k in zip(sums, near)]
-    received[1] = after(received[1], *sums)
+    own_sum, far_sum = fuse("far_sums", functools.partial(far_sums, depth), *columns(0, second))
+    half_way = lax.ppermute(far_sum, "row", [(i, i ^ (4 if i % 2 else 2)) for i in range(n_row)])
+    received[1] = after(received[1], far_sum)
     (chunk,) = fuse("chunk_sum", functools.partial(chunk_sum, depth), second, received[1])
     mine, *from_sibling = columns(1, chunk)
-    mine = after(mine, *near_sums)
-    chunks, own_sum, *sums = fuse(
-        "row_payloads", functools.partial(row_payloads, depth), chunk, swap(chunk, "row", 1), mine, *from_sibling
-    )
-    far_sums = [swap(part, "row", k) for part, k in zip(sums, far)]
-    near_chunks = [swap(chunks, "row", k) for k in near]
-    grad_features, grad_weight = finish(
-        row, [0] + near + far, [own_sum] + near_sums + far_sums, [chunks] + near_chunks
-    )
+    chunks, *near_sums = near_payloads(row, chunk, swap(chunk, "row", 1), half_way, mine, from_sibling)
+    near_sums = [swap(part, "row", k) for part, k in zip(near_sums, near)]
+    far_chunks = [swap(chunks, "row", k) for k in far]
+    grad_features, grad_weight = finish(row, [0] + far + near, [own_sum] + near_sums, [chunks] + far_chunks)
     return output, grad_weight, grad_features.T
 
 
@@ -485,7 +506,7 @@
     panels = lax.all_gather(features.T, "row", axis=0, tiled=True)
     (terms,) = forward(zero, count, rows, cols, adj, [panels], row_blocks, [panels.shape[0]], [(0,)])
     part = lax.psum_scatter(terms, "col", scatter_dimension=1, tiled=True)
-    output, deltas, aggregated, back = middle(1, zero, weight, cotangent, [[part]], (0,), [weight.shape[0]])
+    output, deltas, aggregated, back = middle(1, zero, weight, cotangent, [[part]], (0,))
     slab = lax.all_gather(back, "col", axis=1, tiled=True)
     (column_terms,) = backward(zero, count, rows, cols, adj, [slab], [[(0, 0)]], [slab.shape[0]], [slab.shape[0]], col_blocks)
     grad_features = lax.psum_scatter(column_terms, "row", scatter_dimension=0, tiled=True).T

time: 89.1 us -> 92 us (1.033)
  Pallas kernels: 16.6 us -> 21.4 us
  starting transfers between devices: 33.5 us -> 29 us
  waiting for transfers between devices: 37.4 us -> 40.2 us
    ppermute x38 -> x32, starting transfers between devices: 33.5 us -> 27.5 us  [swap(): return lax.ppermute(value, axis, [(i, i ^ k) for i in range(size)])]
    ppermute x38 -> x32, waiting for transfers between devices: 37.4 us -> 40.2 us  [swap(): return lax.ppermute(value, axis, [(i, i ^ k) for i in range(size)])]
    pallas_call x2, Pallas kernels: 6.55 us -> 8.96 us  [forward(): pl.pallas_call(functools.partial(forward_kernel, len(parts), depths, layo...]
    pallas_call x2, Pallas kernels: 5.47 us -> 7.35 us  [backward(): pl.pallas_call(functools.partial(backward_kernel, spots, depths), out_sha...]
    ppermute x0 -> x1, starting transfers between devices: none -> 1.5 us  [shards_exchanged(): lax.ppermute(far_sum, 'row', [(i, i ^ (4 if i % 2 else 2)) for i in range...]
  transfers between devices with their start and end apart: 38 -> 33, of which waited for: 20 -> 21; matrix products, arithmetic and copies ran while one was open for 0% -> 0% of each run, Pallas kernels for 16% -> 21%
where the time goes in v2:
time: 92 us; the launch traced here: 92.1 us
  waiting for transfers between devices  40.2 us (44%)
  starting transfers between devices  29 us (32%)
  Pallas kernels  21.4 us (23%)
  between operations  1.49 us (2%)
    ppermute x32, waiting for transfers between devices, swap(): return lax.ppermute(value, axis, [(i, i ^ k) for i in range(size)])  40.2 us
    ppermute x32, starting transfers between devices, swap(): return lax.ppermute(value, axis, [(i, i ^ k) for i in range(size)])  27.5 us
    pallas_call x2, Pallas kernels, forward(): pl.pallas_call(functools.partial(forward_kernel, len(parts), depths, layo...  8.96 us
    pallas_call x2, Pallas kernels, backward(): pl.pallas_call(functools.partial(backward_kernel, spots, depths), out_sha...  7.35 us
    pallas_call x1, Pallas kernels, fetch(): pl.pallas_call(fetch_kernel, out_shape=outs + [jax.ShapeDtypeStruct(tile....  2.14 us
  transfers between devices with their start and end apart: 33, of which 21 were waited for; matrix products, arithmetic and copies ran while one was open for 0% of the time, Pallas kernels for 21%

profile of v2, /device:TPU:0, one launch (start us, length us, event | category | flops | bytes accessed | tf_op | source)
XLA Modules:
  0.0 92.1 jit_solution(17753116423572285165)
XLA Ops:
  0.6 3.0 %collective-permute-start.1 = (bf16[32,4096]{1,0:T(8,128)(2,1)}, bf16[32,4096]{1,0:T(8,128)(2,1)S(1)}, u32[]{:S(2)}, u32[]{:S(2)}) collective-permute-start(bf16[32,4096]{1,0:T(8,128)(2,1)} %bitcast.7), channel_id=1, source_target_pairs={{0,8},{4,12},{8,0},{12,4},{16,24},{20,28},{24,16},{28,20},{1,9},{5... | collective-permute-start | bytes 786440 | tf_op jit(solution)/shard_map/ppermute | solution.py:294
  3.7 1.5 %collective-permute-start.3 = (bf16[32,4096]{1,0:T(8,128)(2,1)}, bf16[32,4096]{1,0:T(8,128)(2,1)S(1)}, u32[]{:S(2)}, u32[]{:S(2)}) collective-permute-start(bf16[32,4096]{1,0:T(8,128)(2,1)} %bitcast.8), channel_id=1, source_target_pairs={{0,16},{4,20},{8,24},{12,28},{16,0},{20,4},{24,8},{28,12},{1,17},{... | collective-permute-start | bytes 786440 | tf_op jit(solution)/shard_map/ppermute | solution.py:294
  5.8 2.1 %fetch.1 = (s32[96]{0:T(128)S(1)}, s32[96]{0:T(128)S(1)}, bf16[16,4096]{1,0:T(8,128)(2,1)S(1)}, bf16[16,4096]{1,0:T(8,128)(2,1)S(1)}, bf16[96,128,128]{2,1,0:T(8,128)(2,1)S(1)}) custom-call(s32[1,1]{1,0:T(1,128)S(6)} %copy.10.count, s32[96]{0:T(128)} %bitcast.13, s32[96]{0:T(128)} %bitcast.14, bf16[32,4096]{1,0:T(8,128)(2,1)} %bitcast.10, ...), custom_call_target="tpu_custom_call" | custom-call | flops 1 | bytes 1 | tf_op jit(solution)/shard_map/fetch/pallas_call | solution.py:103
  8.0 2.2 %collective-permute-done.1.refs_2_ = bf16[32,4096]{1,0:T(8,128)(2,1)S(1)} collective-permute-done((bf16[32,4096]{1,0:T(8,128)(2,1)}, bf16[32,4096]{1,0:T(8,128)(2,1)S(1)}, u32[]{:S(2)}, u32[]{:S(2)}) %collective-permute-start.1) | collective-permute-done | bytes 262176 | tf_op jit(solution)/shard_map/ppermute | solution.py:294
  10.2 1.5 %collective-permute-done.3.refs_4_ = bf16[32,4096]{1,0:T(8,128)(2,1)S(1)} collective-permute-done((bf16[32,4096]{1,0:T(8,128)(2,1)}, bf16[32,4096]{1,0:T(8,128)(2,1)S(1)}, u32[]{:S(2)}, u32[]{:S(2)}) %collective-permute-start.3) | collective-permute-done | bytes 262176 | tf_op jit(solution)/shard_map/ppermute | solution.py:294
  11.6 1.7 %collective-permute-start.7 = (bf16[16,4096]{1,0:T(8,128)(2,1)S(1)}, bf16[16,4096]{1,0:T(8,128)(2,1)S(1)}, u32[]{:S(2)}, u32[]{:S(2)}) collective-permute-start(bf16[16,4096]{1,0:T(8,128)(2,1)S(1)} %get-tuple-element.66), channel_id=1, source_target_pairs={{0,24},{4,28},{8,16},{12,20},{16,8},{20,12},{24,0},{28,4},{1,25},{... | collective-permute-start | bytes 393224 | tf_op jit(solution)/shard_map/ppermute | solution.py:294
  13.4 1.2 %collective-permute-start.6 = (bf16[16,4096]{1,0:T(8,128)(2,1)S(1)}, bf16[16,4096]{1,0:T(8,128)(2,1)S(1)}, u32[]{:S(2)}, u32[]{:S(2)}) collective-permute-start(bf16[16,4096]{1,0:T(8,128)(2,1)S(1)} %get-tuple-element.64), channel_id=1, source_target_pairs={{0,24},{4,28},{8,16},{12,20},{16,8},{20,12},{24,0},{28,4},{1,25},{... | collective-permute-start | bytes 393224 | tf_op jit(solution)/shard_map/ppermute | solution.py:294
  14.6 4.8 %forward_products.2 = (bf16[160,512]{1,0:T(8,128)(2,1)S(1)}, bf16[160,512]{1,0:T(8,128)(2,1)S(1)}, bf16[320,512]{1,0:T(8,128)(2,1)S(1)}, bf16[32,512]{1,0:T(8,12...) custom-call(s32[1]{0:T(128)} %bitcast.1.place, s32[1,1]{1,0:T(1,128)S(6)} %copy.10.count, ...), custom_call_target="tpu_custom_call" | custom-call | flops 1 | bytes 1 | tf_op jit(solution)/shard_map/forward_products/pallas_call | solution.py:160
  19.4 1.6 %collective-permute-start.5 = (bf16[320,512]{1,0:T(8,128)(2,1)S(1)}, bf16[320,512]{1,0:T(8,128)(2,1)S(1)}, u32[]{:S(2)}, u32[]{:S(2)}) collective-permute-start(bf16[320,512]{1,0:T(8,128)(2,1)S(1)} %get-tuple-element.63), channel_id=1, source_target_pairs={{0,1},{1,0},{2,3},{3,2},{4,5},{5,4},{6,7},{7,6},{8,9},{9,8},{10,11... | collective-permute-start | bytes 983048 | tf_op jit(solution)/shard_map/ppermute | solution.py:294
  21.6 0.8 collective-permute-done.9.refs_3_
  22.6 4.2 %forward_products.3 = (bf16[96,512]{1,0:T(8,128)(2,1)S(1)}, bf16[96,512]{1,0:T(8,128)(2,1)S(1)}, bf16[192,512]{1,0:T(8,128)(2,1)S(1)}) custom-call(s32[1]{0:T(128)} %bitcast.1.place, s32[1,1]{1,0:T(1,128)S(6)} %copy.10.count, s32[96]{0:T(128)S(1)} %get-tuple-element.57.rows, s32[96]{0:T(128)S(1)} %get-tuple-element.58.cols, ...), custom_call_target="tpu_custom_call" | custom-call | flops 1 | bytes 1 | tf_op jit(solution)/shard_map/forward_products/pallas_call | solution.py:160
  26.8 1.6 %collective-permute-start.11 = (bf16[192,512]{1,0:T(8,128)(2,1)S(1)}, bf16[192,512]{1,0:T(8,128)(2,1)S(1)}, u32[]{:S(2)}, u32[]{:S(2)}) collective-permute-start(bf16[192,512]{1,0:T(8,128)(2,1)S(1)} %get-tuple-element.74), channel_id=1, source_target_pairs={{0,1},{1,0},{2,3},{3,2},{4,5},{5,4},{6,7},{7,6},{8,9},{9,8},{10,11... | collective-permute-start | bytes 589832 | tf_op jit(solution)/shard_map/ppermute | solution.py:294
  28.5 2.4 %collective-permute-start.10 = (bf16[160,512]{1,0:T(8,128)(2,1)S(1)}, bf16[160,512]{1,0:T(8,128)(2,1)S(1)}, u32[]{:S(2)}, u32[]{:S(2)}) collective-permute-start(bf16[160,512]{1,0:T(8,128)(2,1)S(1)} %pass_on.2), channel_id=1, source_target_pairs={{0,2},{1,3},{2,0},{3,1},{4,6},{5,7},{6,4},{7,5},{8,10},{9,11},{10,... | collective-permute-start | bytes 491528 | tf_op jit(solution)/shard_map/ppermute | solution.py:294
  30.8 6.1 %collective-permute-done.11.refs_1_.refs_4_ = bf16[192,512]{1,0:T(8,128)(2,1)S(1)} collective-permute-done((bf16[192,512]{1,0:T(8,128)(2,1)S(1)}, bf16[192,512]{1,0:T(8,128)(2,1)S(1)}, u32[]{:S(2)}, u32[]{:S(2)}) %collective-permute-start.11) | collective-permute-done | bytes 196640 | tf_op jit(solution)/shard_map/ppermute | solution.py:294
  37.1 5.6 %collective-permute-done.12.refs_5_ = bf16[96,512]{1,0:T(8,128)(2,1)S(1)} collective-permute-done((bf16[96,512]{1,0:T(8,128)(2,1)S(1)}, bf16[96,512]{1,0:T(8,128)(2,1)S(1)}, u32[]{:S(2)}, u32[]{:S(2)}) %collective-permute-start.12) | collective-permute-done | bytes 98336 | tf_op jit(solution)/shard_map/ppermute | solution.py:294
  42.7 1.1 %layer.1 = (bf16[512,256]{1,0:T(8,128)(2,1)}, bf16[512,256]{1,0:T(8,128)(2,1)S(1)}, bf16[256,512]{1,0:T(8,128)(2,1)S(1)}, bf16[256,512]{1,0:T(8,128)(2,1)S(1)}) custom-call(s32[1]{0:T(128)} %bitcast.row, bf16[256,256]{1,0:T(8,128)(2,1)S(1)} %copy-done.2, bf16[512,256]{1,0:T(8,128)(2,1)S(1)} %copy-done.1, bf16[160,512]{1,0:T(8,128)(2,1)S(1)} %get-tuple-element.62.refs_0_, ...), custom_call_target="tpu_custom_call" | custom-call | flops 1 | bytes 1 | tf_op jit(solution)/shard_map/layer/pallas_call | solution.py:258
  43.8 2.6 %collective-permute-start.14 = (bf16[256,512]{1,0:T(8,128)(2,1)S(1)}, bf16[256,512]{1,0:T(8,128)(2,1)S(1)}, u32[]{:S(2)}, u32[]{:S(2)}) collective-permute-start(bf16[256,512]{1,0:T(8,128)(2,1)S(1)} %get-tuple-element.78.refs_0_), channel_id=1, source_target_pairs={{0,2},{1,3},{2,0},{3,1},{4,6},{5,7},{6,4},{7,5},{8,10},{9,11},{10,... | collective-permute-start | bytes 786440 | tf_op jit(solution)/shard_map/ppermute | solution.py:294
  48.6 4.0 %collective-permute-done.17.refs_1_ = f32[2,32,256]{2,1,0:T(8,128)S(1)} collective-permute-done((f32[2,32,256]{2,1,0:T(8,128)S(1)}, f32[2,32,256]{2,1,0:T(8,128)S(1)}, u32[]{:S(2)}, u32[]{:S(2)}) %collective-permute-start.17) | collective-permute-done | bytes 65568 | tf_op jit(solution)/shard_map/ppermute | solution.py:294
  52.6 2.9 %collective-permute-start.18 = (f32[1,32,256]{2,1,0:T(8,128)S(1)}, f32[1,32,256]{2,1,0:T(8,128)S(1)}, u32[]{:S(2)}, u32[]{:S(2)}) collective-permute-start(f32[1,32,256]{2,1,0:T(8,128)S(1)} %get-tuple-element.88), channel_id=1, source_target_pairs={{0,16},{4,20},{8,24},{12,28},{16,0},{20,4},{24,8},{28,12},{1,17},{... | collective-permute-start | bytes 98312 | tf_op jit(solution)/shard_map/ppermute | solution.py:294
  56.2 1.2 %collective-permute-done.18.refs_1_ = f32[1,32,256]{2,1,0:T(8,128)S(1)} collective-permute-done((f32[1,32,256]{2,1,0:T(8,128)S(1)}, f32[1,32,256]{2,1,0:T(8,128)S(1)}, u32[]{:S(2)}, u32[]{:S(2)}) %collective-permute-start.18) | collective-permute-done | bytes 32800 | tf_op jit(solution)/shard_map/ppermute | solution.py:294
  57.4 4.8 %collective-permute-done.19.refs_2_ = f32[32,256]{1,0:T(8,128)S(1)} collective-permute-done((f32[32,256]{1,0:T(8,128)S(1)}, f32[32,256]{1,0:T(8,128)S(1)}, u32[]{:S(2)}, u32[]{:S(2)}) %collective-permute-start.19) | collective-permute-done | bytes 32800 | tf_op jit(solution)/shard_map/ppermute | solution.py:294
  62.3 2.1 %collective-permute-start.25 = (bf16[160,512]{1,0:T(8,128)(2,1)S(1)}, bf16[160,512]{1,0:T(8,128)(2,1)S(1)}, u32[]{:S(2)}, u32[]{:S(2)}) collective-permute-start(bf16[160,512]{1,0:T(8,128)(2,1)S(1)} %with_chunk.1.refs_0_), channel_id=1, source_target_pairs={{0,1},{1,0},{2,3},{3,2},{4,5},{5,4},{6,7},{7,6},{8,9},{9,8},{10,11... | collective-permute-start | bytes 491528 | tf_op jit(solution)/shard_map/ppermute | solution.py:294
  64.4 3.1 %collective-permute-done.20.refs_3_ = bf16[128,512]{1,0:T(8,128)(2,1)S(1)} collective-permute-done((bf16[128,512]{1,0:T(8,128)(2,1)S(1)}, bf16[128,512]{1,0:T(8,128)(2,1)S(1)}, u32[]{:S(2)}, u32[]{:S(2)}) %collective-permute-start.20) | collective-permute-done | bytes 131104 | tf_op jit(solution)/shard_map/ppermute | solution.py:294
  67.5 3.7 %backward_products.2 = (bf16[64,4096]{1,0:T(8,128)(2,1)S(1)}, bf16[16,4096]{1,0:T(8,128)(2,1)S(1)}, bf16[16,4096]{1,0:T(8,128)(2,1)S(1)}, bf16[16,4096]{1,0:T(8,128)(2,1)S(1)}, bf16[16,4096]{1,0:T(8,128)(2,1)S(1)}) custom-call(s32[1]{0:T(128)} %bitcast.1.place, s32[1,1]{1,0:T(1,128)S(6)} %copy.10.count, s32[96]{0:T(128)S(1)} %get-tuple-element.57.rows, ...), custom_call_target="tpu_custom_call" | custom-call | flops 1 | bytes 1 | tf_op jit(solution)/shard_map/backward_products/pallas_call | solution.py:203
  73.5 1.5 %collective-permute-start.27 = (bf16[32,4224]{1,0:T(8,128)(2,1)S(1)}, bf16[32,4224]{1,0:T(8,128)(2,1)S(1)}, u32[]{:S(2)}, u32[]{:S(2)}) collective-permute-start(bf16[32,4224]{1,0:T(8,128)(2,1)S(1)} %get-tuple-element.98), channel_id=1, source_target_pairs={{0,8},{4,20},{8,0},{12,28},{16,24},{20,4},{24,16},{28,12},{1,9},{5... | collective-permute-start | bytes 811016 | tf_op jit(solution)/shard_map/ppermute | solution.py:483
  75.0 3.6 %backward_products.3 = (bf16[64,4096]{1,0:T(8,128)(2,1)S(1)}, bf16[32,4096]{1,0:T(8,128)(2,1)S(1)}, bf16[32,4096]{1,0:T(8,128)(2,1)S(1)}) custom-call(s32[1]{0:T(128)} %bitcast.1.place, s32[1,1]{1,0:T(1,128)S(6)} %copy.10.count, s32[96]{0:T(128)S(1)} %get-tuple-element.57.rows, s32[96]{0:T(128)S(1)} %get-tuple-element.58.cols, ...), custom_call_target="tpu_custom_call" | custom-call | flops 1 | bytes 1 | tf_op jit(solution)/shard_map/backward_products/pallas_call | solution.py:203
  79.3 1.4 %collective-permute-done.26.sibling = f32[32,256]{1,0:T(8,128)S(1)} collective-permute-done((f32[32,256]{1,0:T(8,128)S(1)}, f32[32,256]{1,0:T(8,128)S(1)}, u32[]{:S(2)}, u32[]{:S(2)}) %collective-permute-start.26) | collective-permute-done | bytes 32800 | tf_op jit(solution)/shard_map/ppermute | solution.py:294
  81.1 0.8 collective-permute-start.30
  81.9 1.4 %collective-permute-start.31 = (bf16[32,4608]{1,0:T(8,128)(2,1)S(1)}, bf16[32,4608]{1,0:T(8,128)(2,1)S(1)}, u32[]{:S(2)}, u32[]{:S(2)}) collective-permute-start(bf16[32,4608]{1,0:T(8,128)(2,1)S(1)} %get-tuple-element.105), channel_id=1, source_target_pairs={{0,16},{4,20},{8,24},{12,28},{16,0},{20,4},{24,8},{28,12},{1,17},{... | collective-permute-start | bytes 884744 | tf_op jit(solution)/shard_map/ppermute | solution.py:294
  83.3 1.4 %collective-permute-start.32 = (bf16[32,512]{1,0:T(8,128)(2,1)S(1)}, bf16[32,512]{1,0:T(8,128)(2,1)S(1)}, u32[]{:S(2)}, u32[]{:S(2)}) collective-permute-start(bf16[32,512]{1,0:T(8,128)(2,1)S(1)} %get-tuple-element.106.refs_3_), channel_id=1, source_target_pairs={{0,24},{4,28},{8,16},{12,20},{16,8},{20,12},{24,0},{28,4},{1,25},{... | collective-permute-start | bytes 98312 | tf_op jit(solution)/shard_map/ppermute | solution.py:294
  84.7 6.3 %collective-permute-done.32.refs_4_ = bf16[32,512]{1,0:T(8,128)(2,1)S(1)} collective-permute-done((bf16[32,512]{1,0:T(8,128)(2,1)S(1)}, bf16[32,512]{1,0:T(8,128)(2,1)S(1)}, u32[]{:S(2)}, u32[]{:S(2)}) %collective-permute-start.32) | collective-permute-done | bytes 32800 | tf_op jit(solution)/shard_map/ppermute | solution.py:294
  91.2 0.9 finish.1
  (58 shorter events, 7.5 us)
Async XLA Ops:
  0.6 9.5 %collective-permute-start.1 = (bf16[32,4096]{1,0:T(8,128)(2,1)}, bf16[32,4096]{1,0:T(8,128)(2,1)S(1)}, u32[]{:S(2)}, u32[]{:S(2)}) collective-permute-start(bf16[32,4096]{1,0:T(8,128)(2,1)} %bitcast.7), channel_id=1, source_target_pairs={{0,8},{4,12},{8,0},{12,4},{16,24},{20,28},{24,16},{28,20},{1,9},{5... | collective-permute-start | bytes 786440 | tf_op jit(solution)/shard_map/ppermute | solution.py:294
  3.7 8.0 %collective-permute-start.3 = (bf16[32,4096]{1,0:T(8,128)(2,1)}, bf16[32,4096]{1,0:T(8,128)(2,1)S(1)}, u32[]{:S(2)}, u32[]{:S(2)}) collective-permute-start(bf16[32,4096]{1,0:T(8,128)(2,1)} %bitcast.8), channel_id=1, source_target_pairs={{0,16},{4,20},{8,24},{12,28},{16,0},{20,4},{24,8},{28,12},{1,17},{... | collective-permute-start | bytes 786440 | tf_op jit(solution)/shard_map/ppermute | solution.py:294
  5.2 9.4 %collective-permute-start = (bf16[32,4096]{1,0:T(8,128)(2,1)}, bf16[32,4096]{1,0:T(8,128)(2,1)S(1)}, u32[]{:S(2)}, u32[]{:S(2)}) collective-permute-start(bf16[32,4096]{1,0:T(8,128)(2,1)} %bitcast.9), channel_id=1, source_target_pairs={{0,4},{4,0},{8,12},{12,8},{16,20},{20,16},{24,28},{28,24},{1,5},{5... | collective-permute-start | bytes 786440 | tf_op jit(solution)/shard_map/ppermute | solution.py:294
  10.2 4.4 %collective-permute-start.2 = (bf16[32,4096]{1,0:T(8,128)(2,1)S(1)}, bf16[32,4096]{1,0:T(8,128)(2,1)S(1)}, u32[]{:S(2)}, u32[]{:S(2)}) collective-permute-start(bf16[32,4096]{1,0:T(8,128)(2,1)S(1)} %collective-permute-done.1.refs_2_), channel_id=1, source_target_pairs={{0,4},{4,0},{8,12},{12,8},{16,20},{20,16},{24,28},{28,24},{1,5},{5... | collective-permute-start | bytes 786440 | tf_op jit(solution)/shard_map/ppermute | solution.py:294
  11.6 2.9 %collective-permute-start.4 = (bf16[32,4096]{1,0:T(8,128)(2,1)S(1)}, bf16[32,4096]{1,0:T(8,128)(2,1)S(1)}, u32[]{:S(2)}, u32[]{:S(2)}) collective-permute-start(bf16[32,4096]{1,0:T(8,128)(2,1)S(1)} %collective-permute-done.3.refs_4_), channel_id=1, source_target_pairs={{0,4},{4,0},{8,12},{12,8},{16,20},{20,16},{24,28},{28,24},{1,5},{5... | collective-permute-start | bytes 786440 | tf_op jit(solution)/shard_map/ppermute | solution.py:294
  11.6 9.4 %collective-permute-start.7 = (bf16[16,4096]{1,0:T(8,128)(2,1)S(1)}, bf16[16,4096]{1,0:T(8,128)(2,1)S(1)}, u32[]{:S(2)}, u32[]{:S(2)}) collective-permute-start(bf16[16,4096]{1,0:T(8,128)(2,1)S(1)} %get-tuple-element.66), channel_id=1, source_target_pairs={{0,24},{4,28},{8,16},{12,20},{16,8},{20,12},{24,0},{28,4},{1,25},{... | collective-permute-start | bytes 393224 | tf_op jit(solution)/shard_map/ppermute | solution.py:294
  13.4 7.9 %collective-permute-start.6 = (bf16[16,4096]{1,0:T(8,128)(2,1)S(1)}, bf16[16,4096]{1,0:T(8,128)(2,1)S(1)}, u32[]{:S(2)}, u32[]{:S(2)}) collective-permute-start(bf16[16,4096]{1,0:T(8,128)(2,1)S(1)} %get-tuple-element.64), channel_id=1, source_target_pairs={{0,24},{4,28},{8,16},{12,20},{16,8},{20,12},{24,0},{28,4},{1,25},{... | collective-permute-start | bytes 393224 | tf_op jit(solution)/shard_map/ppermute | solution.py:294
  19.4 9.0 %collective-permute-start.5 = (bf16[320,512]{1,0:T(8,128)(2,1)S(1)}, bf16[320,512]{1,0:T(8,128)(2,1)S(1)}, u32[]{:S(2)}, u32[]{:S(2)}) collective-permute-start(bf16[320,512]{1,0:T(8,128)(2,1)S(1)} %get-tuple-element.63), channel_id=1, source_target_pairs={{0,1},{1,0},{2,3},{3,2},{4,5},{5,4},{6,7},{7,6},{8,9},{9,8},{10,11... | collective-permute-start | bytes 983048 | tf_op jit(solution)/shard_map/ppermute | solution.py:294
  21.1 1.3 %collective-permute-start.9 = (bf16[16,4096]{1,0:T(8,128)(2,1)S(1)}, bf16[16,4096]{1,0:T(8,128)(2,1)S(1)}, u32[]{:S(2)}, u32[]{:S(2)}) collective-permute-start(bf16[16,4096]{1,0:T(8,128)(2,1)S(1)} %collective-permute-done.7.refs_1_), channel_id=1, source_target_pairs={{0,4},{4,0},{8,12},{12,8},{16,20},{20,16},{24,28},{28,24},{1,5},{5... | collective-permute-start | bytes 393224 | tf_op jit(solution)/shard_map/ppermute | solution.py:294
  21.2 1.4 %collective-permute-start.8 = (bf16[16,4096]{1,0:T(8,128)(2,1)S(1)}, bf16[16,4096]{1,0:T(8,128)(2,1)S(1)}, u32[]{:S(2)}, u32[]{:S(2)}) collective-permute-start(bf16[16,4096]{1,0:T(8,128)(2,1)S(1)} %collective-permute-done.6.refs_0_), channel_id=1, source_target_pairs={{0,4},{4,0},{8,12},{12,8},{16,20},{20,16},{24,28},{28,24},{1,5},{5... | collective-permute-start | bytes 393224 | tf_op jit(solution)/shard_map/ppermute | solution.py:294
  26.8 10.1 %collective-permute-start.11 = (bf16[192,512]{1,0:T(8,128)(2,1)S(1)}, bf16[192,512]{1,0:T(8,128)(2,1)S(1)}, u32[]{:S(2)}, u32[]{:S(2)}) collective-permute-start(bf16[192,512]{1,0:T(8,128)(2,1)S(1)} %get-tuple-element.74), channel_id=1, source_target_pairs={{0,1},{1,0},{2,3},{3,2},{4,5},{5,4},{6,7},{7,6},{8,9},{9,8},{10,11... | collective-permute-start | bytes 589832 | tf_op jit(solution)/shard_map/ppermute | solution.py:294
  28.5 14.2 %collective-permute-start.10 = (bf16[160,512]{1,0:T(8,128)(2,1)S(1)}, bf16[160,512]{1,0:T(8,128)(2,1)S(1)}, u32[]{:S(2)}, u32[]{:S(2)}) collective-permute-start(bf16[160,512]{1,0:T(8,128)(2,1)S(1)} %pass_on.2), channel_id=1, source_target_pairs={{0,2},{1,3},{2,0},{3,1},{4,6},{5,7},{6,4},{7,5},{8,10},{9,11},{10,... | collective-permute-start | bytes 491528 | tf_op jit(solution)/shard_map/ppermute | solution.py:294
  36.9 5.7 %collective-permute-start.12 = (bf16[96,512]{1,0:T(8,128)(2,1)S(1)}, bf16[96,512]{1,0:T(8,128)(2,1)S(1)}, u32[]{:S(2)}, u32[]{:S(2)}) collective-permute-start(bf16[96,512]{1,0:T(8,128)(2,1)S(1)} %pass_on.3), channel_id=1, source_target_pairs={{0,2},{1,3},{2,0},{3,1},{4,6},{5,7},{6,4},{7,5},{8,10},{9,11},{10,... | collective-permute-start | bytes 294920 | tf_op jit(solution)/shard_map/ppermute | solution.py:294
  43.8 12.4 %collective-permute-start.13 = (bf16[256,512]{1,0:T(8,128)(2,1)S(1)}, bf16[256,512]{1,0:T(8,128)(2,1)S(1)}, u32[]{:S(2)}, u32[]{:S(2)}) collective-permute-start(bf16[256,512]{1,0:T(8,128)(2,1)S(1)} %get-tuple-element.78.refs_0_), channel_id=1, source_target_pairs={{0,1},{1,0},{2,3},{3,2},{4,5},{5,4},{6,7},{7,6},{8,9},{9,8},{10,11... | collective-permute-start | bytes 786440 | tf_op jit(solution)/shard_map/ppermute | solution.py:294
  43.8 13.6 %collective-permute-start.14 = (bf16[256,512]{1,0:T(8,128)(2,1)S(1)}, bf16[256,512]{1,0:T(8,128)(2,1)S(1)}, u32[]{:S(2)}, u32[]{:S(2)}) collective-permute-start(bf16[256,512]{1,0:T(8,128)(2,1)S(1)} %get-tuple-element.78.refs_0_), channel_id=1, source_target_pairs={{0,2},{1,3},{2,0},{3,1},{4,6},{5,7},{6,4},{7,5},{8,10},{9,11},{10,... | collective-permute-start | bytes 786440 | tf_op jit(solution)/shard_map/ppermute | solution.py:294
  46.7 1.4 %collective-permute-start.16 = (f32[2,32,256]{2,1,0:T(8,128)S(1)}, f32[2,32,256]{2,1,0:T(8,128)S(1)}, u32[]{:S(2)}, u32[]{:S(2)}) collective-permute-start(f32[2,32,256]{2,1,0:T(8,128)S(1)} %get-tuple-element.83), channel_id=1, source_target_pairs={{0,4},{4,0},{8,12},{12,8},{16,20},{20,16},{24,28},{28,24},{1,5},{5... | collective-permute-start | bytes 196616 | tf_op jit(solution)/shard_map/ppermute | solution.py:294
  48.2 4.4 %collective-permute-start.17 = (f32[2,32,256]{2,1,0:T(8,128)S(1)}, f32[2,32,256]{2,1,0:T(8,128)S(1)}, u32[]{:S(2)}, u32[]{:S(2)}) collective-permute-start(f32[2,32,256]{2,1,0:T(8,128)S(1)} %get-tuple-element.85), channel_id=1, source_target_pairs={{0,8},{4,12},{8,0},{12,4},{16,24},{20,28},{24,16},{28,20},{1,9},{5... | collective-permute-start | bytes 196616 | tf_op jit(solution)/shard_map/ppermute | solution.py:294
  52.6 4.8 %collective-permute-start.18 = (f32[1,32,256]{2,1,0:T(8,128)S(1)}, f32[1,32,256]{2,1,0:T(8,128)S(1)}, u32[]{:S(2)}, u32[]{:S(2)}) collective-permute-start(f32[1,32,256]{2,1,0:T(8,128)S(1)} %get-tuple-element.88), channel_id=1, source_target_pairs={{0,16},{4,20},{8,24},{12,28},{16,0},{20,4},{24,8},{28,12},{1,17},{... | collective-permute-start | bytes 98312 | tf_op jit(solution)/shard_map/ppermute | solution.py:294
  57.4 4.8 %collective-permute-start.19 = (f32[32,256]{1,0:T(8,128)S(1)}, f32[32,256]{1,0:T(8,128)S(1)}, u32[]{:S(2)}, u32[]{:S(2)}) collective-permute-start(f32[32,256]{1,0:T(8,128)S(1)} %gradient_sum.5.refs_1_), channel_id=1, source_target_pairs={{0,2},{1,3},{2,0},{3,1},{4,6},{5,7},{6,4},{7,5},{8,10},{9,11},{10,... | collective-permute-start | bytes 98312 | tf_op jit(solution)/shard_map/ppermute | solution.py:294
  62.2 5.3 %collective-permute-start.20 = (bf16[128,512]{1,0:T(8,128)(2,1)S(1)}, bf16[128,512]{1,0:T(8,128)(2,1)S(1)}, u32[]{:S(2)}, u32[]{:S(2)}) collective-permute-start(bf16[128,512]{1,0:T(8,128)(2,1)S(1)} %first_rows.1), channel_id=1, source_target_pairs={{0,1},{1,0},{2,3},{3,2},{4,5},{5,4},{6,7},{7,6},{8,9},{9,8},{10,11... | collective-permute-start | bytes 393224 | tf_op jit(solution)/shard_map/ppermute | solution.py:294
  62.3 12.6 %collective-permute-start.25 = (bf16[160,512]{1,0:T(8,128)(2,1)S(1)}, bf16[160,512]{1,0:T(8,128)(2,1)S(1)}, u32[]{:S(2)}, u32[]{:S(2)}) collective-permute-start(bf16[160,512]{1,0:T(8,128)(2,1)S(1)} %with_chunk.1.refs_0_), channel_id=1, source_target_pairs={{0,1},{1,0},{2,3},{3,2},{4,5},{5,4},{6,7},{7,6},{8,9},{9,8},{10,11... | collective-permute-start | bytes 491528 | tf_op jit(solution)/shard_map/ppermute | solution.py:294
  71.2 1.4 %collective-permute-start.21 = (bf16[16,4096]{1,0:T(8,128)(2,1)S(1)}, bf16[16,4096]{1,0:T(8,128)(2,1)S(1)}, u32[]{:S(2)}, u32[]{:S(2)}) collective-permute-start(bf16[16,4096]{1,0:T(8,128)(2,1)S(1)} %get-tuple-element.93), channel_id=1, source_target_pairs={{0,4},{4,0},{8,12},{12,8},{16,20},{20,16},{24,28},{28,24},{1,5},{5... | collective-permute-start | bytes 393224 | tf_op jit(solution)/shard_map/ppermute | solution.py:294
  71.3 1.5 %collective-permute-start.22 = (bf16[16,4096]{1,0:T(8,128)(2,1)S(1)}, bf16[16,4096]{1,0:T(8,128)(2,1)S(1)}, u32[]{:S(2)}, u32[]{:S(2)}) collective-permute-start(bf16[16,4096]{1,0:T(8,128)(2,1)S(1)} %get-tuple-element.94), channel_id=1, source_target_pairs={{0,4},{4,0},{8,12},{12,8},{16,20},{20,16},{24,28},{28,24},{1,5},{5... | collective-permute-start | bytes 393224 | tf_op jit(solution)/shard_map/ppermute | solution.py:294
  71.8 1.3 %collective-permute-start.23 = (bf16[16,4096]{1,0:T(8,128)(2,1)S(1)}, bf16[16,4096]{1,0:T(8,128)(2,1)S(1)}, u32[]{:S(2)}, u32[]{:S(2)}) collective-permute-start(bf16[16,4096]{1,0:T(8,128)(2,1)S(1)} %get-tuple-element.95), channel_id=1, source_target_pairs={{0,4},{4,0},{8,12},{12,8},{16,20},{20,16},{24,28},{28,24},{1,5},{5... | collective-permute-start | bytes 393224 | tf_op jit(solution)/shard_map/ppermute | solution.py:294
  71.9 1.5 %collective-permute-start.24 = (bf16[16,4096]{1,0:T(8,128)(2,1)S(1)}, bf16[16,4096]{1,0:T(8,128)(2,1)S(1)}, u32[]{:S(2)}, u32[]{:S(2)}) collective-permute-start(bf16[16,4096]{1,0:T(8,128)(2,1)S(1)} %get-tuple-element.96), channel_id=1, source_target_pairs={{0,4},{4,0},{8,12},{12,8},{16,20},{20,16},{24,28},{28,24},{1,5},{5... | collective-permute-start | bytes 393224 | tf_op jit(solution)/shard_map/ppermute | solution.py:294
  73.5 7.2 %collective-permute-start.27 = (bf16[32,4224]{1,0:T(8,128)(2,1)S(1)}, bf16[32,4224]{1,0:T(8,128)(2,1)S(1)}, u32[]{:S(2)}, u32[]{:S(2)}) collective-permute-start(bf16[32,4224]{1,0:T(8,128)(2,1)S(1)} %get-tuple-element.98), channel_id=1, source_target_pairs={{0,8},{4,20},{8,0},{12,28},{16,24},{20,4},{24,16},{28,12},{1,9},{5... | collective-permute-start | bytes 811016 | tf_op jit(solution)/shard_map/ppermute | solution.py:483
  78.6 2.0 %collective-permute-start.28 = (bf16[32,4096]{1,0:T(8,128)(2,1)S(1)}, bf16[32,4096]{1,0:T(8,128)(2,1)S(1)}, u32[]{:S(2)}, u32[]{:S(2)}) collective-permute-start(bf16[32,4096]{1,0:T(8,128)(2,1)S(1)} %get-tuple-element.102), channel_id=1, source_target_pairs={{0,4},{4,0},{8,12},{12,8},{16,20},{20,16},{24,28},{28,24},{1,5},{5... | collective-permute-start | bytes 786440 | tf_op jit(solution)/shard_map/ppermute | solution.py:294
  78.7 1.9 %collective-permute-start.29 = (bf16[32,4096]{1,0:T(8,128)(2,1)S(1)}, bf16[32,4096]{1,0:T(8,128)(2,1)S(1)}, u32[]{:S(2)}, u32[]{:S(2)}) collective-permute-start(bf16[32,4096]{1,0:T(8,128)(2,1)S(1)} %get-tuple-element.103), channel_id=1, source_target_pairs={{0,4},{4,0},{8,12},{12,8},{16,20},{20,16},{24,28},{28,24},{1,5},{5... | collective-permute-start | bytes 786440 | tf_op jit(solution)/shard_map/ppermute | solution.py:294
  79.2 1.4 %collective-permute-start.26 = (f32[32,256]{1,0:T(8,128)S(1)}, f32[32,256]{1,0:T(8,128)S(1)}, u32[]{:S(2)}, u32[]{:S(2)}) collective-permute-start(f32[32,256]{1,0:T(8,128)S(1)} %chunk_sum.1.chunk), channel_id=1, source_target_pairs={{0,4},{4,0},{8,12},{12,8},{16,20},{20,16},{24,28},{28,24},{1,5},{5... | collective-permute-start | bytes 98312 | tf_op jit(solution)/shard_map/ppermute | solution.py:294
  81.1 9.9 %collective-permute-start.30 = (bf16[32,4608]{1,0:T(8,128)(2,1)S(1)}, bf16[32,4608]{1,0:T(8,128)(2,1)S(1)}, u32[]{:S(2)}, u32[]{:S(2)}) collective-permute-start(bf16[32,4608]{1,0:T(8,128)(2,1)S(1)} %get-tuple-element.104), channel_id=1, source_target_pairs={{0,8},{4,12},{8,0},{12,4},{16,24},{20,28},{24,16},{28,20},{1,9},{5... | collective-permute-start | bytes 884744 | tf_op jit(solution)/shard_map/ppermute | solution.py:294
  81.9 9.3 %collective-permute-start.31 = (bf16[32,4608]{1,0:T(8,128)(2,1)S(1)}, bf16[32,4608]{1,0:T(8,128)(2,1)S(1)}, u32[]{:S(2)}, u32[]{:S(2)}) collective-permute-start(bf16[32,4608]{1,0:T(8,128)(2,1)S(1)} %get-tuple-element.105), channel_id=1, source_target_pairs={{0,16},{4,20},{8,24},{12,28},{16,0},{20,4},{24,8},{28,12},{1,17},{... | collective-permute-start | bytes 884744 | tf_op jit(solution)/shard_map/ppermute | solution.py:294
  83.3 7.7 %collective-permute-start.32 = (bf16[32,512]{1,0:T(8,128)(2,1)S(1)}, bf16[32,512]{1,0:T(8,128)(2,1)S(1)}, u32[]{:S(2)}, u32[]{:S(2)}) collective-permute-start(bf16[32,512]{1,0:T(8,128)(2,1)S(1)} %get-tuple-element.106.refs_3_), channel_id=1, source_target_pairs={{0,24},{4,28},{8,16},{12,20},{16,8},{20,12},{24,0},{28,4},{1,25},{... | collective-permute-start | bytes 98312 | tf_op jit(solution)/shard_map/ppermute | solution.py:294
  (4 other events, 61.8 us)

commit v3 on v2

--- a/solution.py
+++ b/solution.py
@@ -218,7 +218,7 @@
 def middle_kernel(sizes, order, n_sum, n_row, row, weight, cotangent, *refs):
     terms = refs[: n_sum * len(sizes)]
     outs = refs[n_sum * len(sizes) : -1]
-    output, deltas, aggregated, back = outs
+    output, deltas, aggregated, *backs = outs
     ordered = refs[-1]
     depth = weight.shape[0] // n_row
     for j in range(n_row):
@@ -239,11 +239,15 @@
     delta = (cotangent[...].astype(jnp.float32) * slopes).astype(jnp.bfloat16)
     deltas[...] = delta
     product = lax.dot_general(ordered[...], delta, NT, preferred_element_type=jnp.float32)
-    for n, k in enumerate(order):
-        back[n * depth : (n + 1) * depth, :] = product[k * depth : (k + 1) * depth, :].astype(jnp.bfloat16)
-
-
-def middle(n_row, row, weight, cotangent, pieces, order):
+    product = jnp.concatenate([product[k * depth : (k + 1) * depth, :] for k in order]).astype(jnp.bfloat16)
+    first = 0
+    for back in backs:
+        first %= product.shape[0]
+        back[...] = product[first : first + back.shape[0], :]
+        first += back.shape[0]
+
+
+def middle(n_row, row, weight, cotangent, pieces, order, depths):
     sizes = [piece[0].shape[0] for piece in pieces]
     nodes = cotangent.shape[0]
     features = weight.shape[0]
@@ -252,8 +256,7 @@
         shape((nodes, features), jnp.bfloat16),
         shape((nodes, features), jnp.bfloat16),
         shape((features, nodes), jnp.bfloat16),
-        shape((features, nodes), jnp.bfloat16),
-    ]
+    ] + [shape((depth, nodes), jnp.bfloat16) for depth in depths]
     flat = [term for piece in pieces for term in piece]
     return pl.pallas_call(
         functools.partial(middle_kernel, sizes, order, len(pieces[0]), n_row),
@@ -305,11 +308,11 @@
     return lax.optimization_barrier((value, *earlier))[0]
 
 
-def with_chunk(first, rows, *parts):
+def with_chunk(rows, *parts):
     total = functools.reduce(jnp.add, parts)
     high = total.astype(jnp.bfloat16)
     low = (total - high.astype(jnp.float32)).astype(jnp.bfloat16)
-    return (jnp.concatenate([rows[first:], jnp.concatenate([high, low], axis=1)]),)
+    return (jnp.concatenate([rows, jnp.concatenate([high, low], axis=1)]),)
 
 
 def chunk_sum(depth, *values):
@@ -455,27 +458,37 @@
     groups = [[0] + far, near]
     order = [k + side for group in groups for side in range(2) for k in group]
     cuts = [2 * depth * len(group) for group in groups]
-    output, deltas, aggregated, back = middle(n_row, row, weight, cotangent, sums, order)
+    ahead = depth // 2
+    output, deltas, aggregated, back, *backs = middle(
+        n_row, row, weight, cotangent, sums, order, [sum(cuts), cuts[0] + ahead, cuts[1] - ahead]
+    )
     beside = swap(back, "col", 1)
-    beyond = swap(back, "col", 2)
+    beyond = [swap(part, "col", 2) for part in backs]
 
     even, *odd = gradient(1.0 / math.sqrt(nodes), [(0, 4, 2, 6), (1, 5), (3, 7)], aggregated, deltas)
     even, sent = fuse("gradient_sum", halves_sum, even, *[swap(part, "row", 1) for part in odd])
     even, sent = fuse("gradient_sum", halves_sum, even, swap(sent, "row", 2))
-    (chunk,) = fuse("gradient_sum", lambda a, b: ((a + b)[0],), after(even, beside), swap(sent, "row", 4))
+    beyond[0] = after(beyond[0], sent)
+    even = after(even, beyond[1])
+    (chunk,) = fuse("gradient_sum", lambda a, b: ((a + b)[0],), even, swap(sent, "row", 4))
     chunks = [chunk, swap(chunk, "col", 2)]
 
-    cut = cuts[0]
-    (first,) = fuse("first_rows", lambda rows: (rows[:cut],), after(beyond, *chunks))
-    (second,) = fuse("with_chunk", functools.partial(with_chunk, cut), after(beyond, first), *chunks)
-    received = [swap(first, "col", 1), swap(second, "col", 1)]
+    (second,) = fuse("with_chunk", with_chunk, beyond[1], *chunks)
+    received = [swap(beyond[0], "col", 1), swap(second, "col", 1)]
 
     def columns(n, *earlier):
-        parts = [back, beside, after(beyond, *earlier), received[n]]
-        spots = [[(part, n * cut)] for part in range(3)] + [[(3, 0)]]
+        parts = [back, beside, after(beyond[0], *earlier), received[0], beyond[1], received[1]]
+        if n == 0:
+            depths = cuts[:1]
+            parts = parts[:4]
+            spots = [[(part, 0)] for part in range(4)]
+        else:
+            depths = [ahead, cuts[1] - ahead]
+            spots = [[(part, cuts[0]), (part, cuts[0] + ahead)] for part in range(2)]
+            spots += [[(part, cuts[0]), (part + 2, 0)] for part in (2, 3)]
         out_depths = [cuts[n] // 2] + [cuts[n] // (8 - 4 * n)] * (4 - 2 * n)
         mine, *sent = backward(
-            col, count, rows, cols, tile, parts, spots, cuts[n : n + 1], out_depths, col_blocks
+            col, count, rows, cols, tile, parts, spots, depths, out_depths, col_blocks
         )
         return [mine] + [swap(part, "row", 1) for part in sent]
 
@@ -506,7 +519,7 @@
     panels = lax.all_gather(features.T, "row", axis=0, tiled=True)
     (terms,) = forward(zero, count, rows, cols, adj, [panels], row_blocks, [panels.shape[0]], [(0,)])
     part = lax.psum_scatter(terms, "col", scatter_dimension=1, tiled=True)
-    output, deltas, aggregated, back = middle(1, zero, weight, cotangent, [[part]], (0,))
+    output, deltas, aggregated, back = middle(1, zero, weight, cotangent, [[part]], (0,), [weight.shape[0]])
     slab = lax.all_gather(back, "col", axis=1, tiled=True)
     (column_terms,) = backward(zero, count, rows, cols, adj, [slab], [[(0, 0)]], [slab.shape[0]], [slab.shape[0]], col_blocks)
     grad_features = lax.psum_scatter(column_terms, "row", scatter_dimension=0, tiled=True).T

time: 92 us -> 88.8 us (0.965)
  starting transfers between devices: 29 us -> 40.7 us
  Pallas kernels: 21.4 us -> 12.3 us
  waiting for transfers between devices: 40.2 us -> 35.1 us
    ppermute x32 -> x33, starting transfers between devices: 27.5 us -> 39.8 us  [swap(): return lax.ppermute(value, axis, [(i, i ^ k) for i in range(size)])]
    ppermute x32 -> x33, waiting for transfers between devices: 40.2 us -> 35.1 us  [swap(): return lax.ppermute(value, axis, [(i, i ^ k) for i in range(size)])]
    pallas_call x2, Pallas kernels: 8.96 us -> 4.16 us  [forward(): pl.pallas_call(functools.partial(forward_kernel, len(parts), depths, layo...]
    pallas_call x2, Pallas kernels: 7.35 us -> 3.66 us  [backward(): pl.pallas_call(functools.partial(backward_kernel, spots, depths), out_sha...]
  transfers between devices with their start and end apart: 33 -> 34, of which waited for: 21 -> 20; matrix products, arithmetic and copies ran while one was open for 0% -> 0% of each run, Pallas kernels for 21% -> 11%
where the time goes in v3:
time: 88.8 us; the launch traced here: 89.6 us
  starting transfers between devices  40.7 us (46%)
  waiting for transfers between devices  35.1 us (40%)
  Pallas kernels  12.3 us (14%)
  between operations  1.46 us (2%)
    ppermute x33, starting transfers between devices, swap(): return lax.ppermute(value, axis, [(i, i ^ k) for i in range(size)])  39.8 us
    ppermute x33, waiting for transfers between devices, swap(): return lax.ppermute(value, axis, [(i, i ^ k) for i in range(size)])  35.1 us
    pallas_call x2, Pallas kernels, forward(): pl.pallas_call(functools.partial(forward_kernel, len(parts), depths, layo...  4.16 us
    pallas_call x2, Pallas kernels, backward(): pl.pallas_call(functools.partial(backward_kernel, spots, depths), out_sha...  3.66 us
  transfers between devices with their start and end apart: 34, of which 20 were waited for; matrix products, arithmetic and copies ran while one was open for 0% of the time, Pallas kernels for 11%

profile of v3, /device:TPU:0, one launch (start us, length us, event | category | flops | bytes accessed | tf_op | source)
XLA Modules:
  0.0 89.6 jit_solution(16017173252393898323)
XLA Ops:
  0.6 3.0 %collective-permute-start.1 = (bf16[32,4096]{1,0:T(8,128)(2,1)}, bf16[32,4096]{1,0:T(8,128)(2,1)S(1)}, u32[]{:S(2)}, u32[]{:S(2)}) collective-permute-start(bf16[32,4096]{1,0:T(8,128)(2,1)} %bitcast.7), channel_id=1, source_target_pairs={{0,8},{4,12},{8,0},{12,4},{16,24},{20,28},{24,16},{28,20},{1,9},{5... | collective-permute-start | bytes 786440 | tf_op jit(solution)/shard_map/ppermute | solution.py:297
  3.7 1.5 %collective-permute-start.3 = (bf16[32,4096]{1,0:T(8,128)(2,1)}, bf16[32,4096]{1,0:T(8,128)(2,1)S(1)}, u32[]{:S(2)}, u32[]{:S(2)}) collective-permute-start(bf16[32,4096]{1,0:T(8,128)(2,1)} %bitcast.8), channel_id=1, source_target_pairs={{0,16},{4,20},{8,24},{12,28},{16,0},{20,4},{24,8},{28,12},{1,17},{... | collective-permute-start | bytes 786440 | tf_op jit(solution)/shard_map/ppermute | solution.py:297
  5.8 1.5 %fetch.1 = (s32[96]{0:T(128)S(1)}, s32[96]{0:T(128)S(1)}, bf16[16,4096]{1,0:T(8,128)(2,1)S(1)}, bf16[16,4096]{1,0:T(8,128)(2,1)S(1)}, bf16[96,128,128]{2,1,0:T(8,128)(2,1)S(1)}) custom-call(s32[1,1]{1,0:T(1,128)S(6)} %copy.10.count, s32[96]{0:T(128)} %bitcast.13, s32[96]{0:T(128)} %bitcast.14, bf16[32,4096]{1,0:T(8,128)(2,1)} %bitcast.10, ...), custom_call_target="tpu_custom_call" | custom-call | flops 1 | bytes 1 | tf_op jit(solution)/shard_map/fetch/pallas_call | solution.py:103
  7.3 2.8 %collective-permute-done.1.refs_2_ = bf16[32,4096]{1,0:T(8,128)(2,1)S(1)} collective-permute-done((bf16[32,4096]{1,0:T(8,128)(2,1)}, bf16[32,4096]{1,0:T(8,128)(2,1)S(1)}, u32[]{:S(2)}, u32[]{:S(2)}) %collective-permute-start.1) | collective-permute-done | bytes 262176 | tf_op jit(solution)/shard_map/ppermute | solution.py:297
  10.2 1.5 %collective-permute-done.3.refs_4_ = bf16[32,4096]{1,0:T(8,128)(2,1)S(1)} collective-permute-done((bf16[32,4096]{1,0:T(8,128)(2,1)}, bf16[32,4096]{1,0:T(8,128)(2,1)S(1)}, u32[]{:S(2)}, u32[]{:S(2)}) %collective-permute-start.3) | collective-permute-done | bytes 262176 | tf_op jit(solution)/shard_map/ppermute | solution.py:297
  11.6 1.7 %collective-permute-start.7 = (bf16[16,4096]{1,0:T(8,128)(2,1)S(1)}, bf16[16,4096]{1,0:T(8,128)(2,1)S(1)}, u32[]{:S(2)}, u32[]{:S(2)}) collective-permute-start(bf16[16,4096]{1,0:T(8,128)(2,1)S(1)} %get-tuple-element.67), channel_id=1, source_target_pairs={{0,24},{4,28},{8,16},{12,20},{16,8},{20,12},{24,0},{28,4},{1,25},{... | collective-permute-start | bytes 393224 | tf_op jit(solution)/shard_map/ppermute | solution.py:297
  13.4 1.2 %collective-permute-start.6 = (bf16[16,4096]{1,0:T(8,128)(2,1)S(1)}, bf16[16,4096]{1,0:T(8,128)(2,1)S(1)}, u32[]{:S(2)}, u32[]{:S(2)}) collective-permute-start(bf16[16,4096]{1,0:T(8,128)(2,1)S(1)} %get-tuple-element.65), channel_id=1, source_target_pairs={{0,24},{4,28},{8,16},{12,20},{16,8},{20,12},{24,0},{28,4},{1,25},{... | collective-permute-start | bytes 393224 | tf_op jit(solution)/shard_map/ppermute | solution.py:297
  14.6 2.3 %forward_products.2 = (bf16[160,512]{1,0:T(8,128)(2,1)S(1)}, bf16[160,512]{1,0:T(8,128)(2,1)S(1)}, bf16[320,512]{1,0:T(8,128)(2,1)S(1)}, bf16[32,512]{1,0:T(8,12...) custom-call(s32[1]{0:T(128)} %bitcast.1.place, s32[1,1]{1,0:T(1,128)S(6)} %copy.10.count, ...), custom_call_target="tpu_custom_call" | custom-call | flops 1 | bytes 1 | tf_op jit(solution)/shard_map/forward_products/pallas_call | solution.py:160
  16.9 1.6 %collective-permute-start.5 = (bf16[320,512]{1,0:T(8,128)(2,1)S(1)}, bf16[320,512]{1,0:T(8,128)(2,1)S(1)}, u32[]{:S(2)}, u32[]{:S(2)}) collective-permute-start(bf16[320,512]{1,0:T(8,128)(2,1)S(1)} %get-tuple-element.64), channel_id=1, source_target_pairs={{0,1},{1,0},{2,3},{3,2},{4,5},{5,4},{6,7},{7,6},{8,9},{9,8},{10,11... | collective-permute-start | bytes 983048 | tf_op jit(solution)/shard_map/ppermute | solution.py:297
  18.8 1.9 %collective-permute-start.9 = (bf16[16,4096]{1,0:T(8,128)(2,1)S(1)}, bf16[16,4096]{1,0:T(8,128)(2,1)S(1)}, u32[]{:S(2)}, u32[]{:S(2)}) collective-permute-start(bf16[16,4096]{1,0:T(8,128)(2,1)S(1)} %collective-permute-done.7.refs_1_), channel_id=1, source_target_pairs={{0,4},{4,0},{8,12},{12,8},{16,20},{20,16},{24,28},{28,24},{1,5},{5... | collective-permute-start | bytes 393224 | tf_op jit(solution)/shard_map/ppermute | solution.py:297
  22.6 1.9 %forward_products.3 = (bf16[96,512]{1,0:T(8,128)(2,1)S(1)}, bf16[96,512]{1,0:T(8,128)(2,1)S(1)}, bf16[192,512]{1,0:T(8,128)(2,1)S(1)}) custom-call(s32[1]{0:T(128)} %bitcast.1.place, s32[1,1]{1,0:T(1,128)S(6)} %copy.10.count, s32[96]{0:T(128)S(1)} %get-tuple-element.58.rows, s32[96]{0:T(128)S(1)} %get-tuple-element.59.cols, ...), custom_call_target="tpu_custom_call" | custom-call | flops 1 | bytes 1 | tf_op jit(solution)/shard_map/forward_products/pallas_call | solution.py:160
  24.5 1.6 %collective-permute-start.11 = (bf16[192,512]{1,0:T(8,128)(2,1)S(1)}, bf16[192,512]{1,0:T(8,128)(2,1)S(1)}, u32[]{:S(2)}, u32[]{:S(2)}) collective-permute-start(bf16[192,512]{1,0:T(8,128)(2,1)S(1)} %get-tuple-element.75), channel_id=1, source_target_pairs={{0,1},{1,0},{2,3},{3,2},{4,5},{5,4},{6,7},{7,6},{8,9},{9,8},{10,11... | collective-permute-start | bytes 589832 | tf_op jit(solution)/shard_map/ppermute | solution.py:297
  26.2 3.2 %collective-permute-start.10 = (bf16[160,512]{1,0:T(8,128)(2,1)S(1)}, bf16[160,512]{1,0:T(8,128)(2,1)S(1)}, u32[]{:S(2)}, u32[]{:S(2)}) collective-permute-start(bf16[160,512]{1,0:T(8,128)(2,1)S(1)} %pass_on.2), channel_id=1, source_target_pairs={{0,2},{1,3},{2,0},{3,1},{4,6},{5,7},{6,4},{7,5},{8,10},{9,11},{10,... | collective-permute-start | bytes 491528 | tf_op jit(solution)/shard_map/ppermute | solution.py:297
  29.4 1.6 %collective-permute-done.11.refs_1_.refs_4_ = bf16[192,512]{1,0:T(8,128)(2,1)S(1)} collective-permute-done((bf16[192,512]{1,0:T(8,128)(2,1)S(1)}, bf16[192,512]{1,0:T(8,128)(2,1)S(1)}, u32[]{:S(2)}, u32[]{:S(2)}) %collective-permute-start.11) | collective-permute-done | bytes 196640 | tf_op jit(solution)/shard_map/ppermute | solution.py:297
  31.0 3.1 %collective-permute-start.12 = (bf16[96,512]{1,0:T(8,128)(2,1)S(1)}, bf16[96,512]{1,0:T(8,128)(2,1)S(1)}, u32[]{:S(2)}, u32[]{:S(2)}) collective-permute-start(bf16[96,512]{1,0:T(8,128)(2,1)S(1)} %pass_on.3), channel_id=1, source_target_pairs={{0,2},{1,3},{2,0},{3,1},{4,6},{5,7},{6,4},{7,5},{8,10},{9,11},{10,... | collective-permute-start | bytes 294920 | tf_op jit(solution)/shard_map/ppermute | solution.py:297
  34.1 8.1 %collective-permute-done.12.refs_5_ = bf16[96,512]{1,0:T(8,128)(2,1)S(1)} collective-permute-done((bf16[96,512]{1,0:T(8,128)(2,1)S(1)}, bf16[96,512]{1,0:T(8,128)(2,1)S(1)}, u32[]{:S(2)}, u32[]{:S(2)}) %collective-permute-start.12) | collective-permute-done | bytes 98336 | tf_op jit(solution)/shard_map/ppermute | solution.py:297
  42.2 1.1 %layer.1 = (bf16[512,256]{1,0:T(8,128)(2,1)}, bf16[512,256]{1,0:T(8,128)(2,1)S(1)}, bf16[256,512]{1,0:T(8,128)(2,1)S(1)}, bf16[256,512]{1,0:T(8,128)(2,1)S(1)}, ...) custom-call(s32[1]{0:T(128)} %bitcast.row, bf16[256,256]{1,0:T(8,128)(2,1)S(1)} %copy-done.2, ...), custom_call_target="tpu_custom_call" | custom-call | flops 1 | bytes 1 | tf_op jit(solution)/shard_map/layer/pallas_call | solution.py:261
  44.2 3.7 %collective-permute-start.13 = (bf16[256,512]{1,0:T(8,128)(2,1)S(1)}, bf16[256,512]{1,0:T(8,128)(2,1)S(1)}, u32[]{:S(2)}, u32[]{:S(2)}) collective-permute-start(bf16[256,512]{1,0:T(8,128)(2,1)S(1)} %get-tuple-element.79.refs_0_), channel_id=1, source_target_pairs={{0,1},{1,0},{2,3},{3,2},{4,5},{5,4},{6,7},{7,6},{8,9},{9,8},{10,11... | collective-permute-start | bytes 786440 | tf_op jit(solution)/shard_map/ppermute | solution.py:297
  48.8 3.4 %collective-permute-done.17.refs_1_ = f32[2,32,256]{2,1,0:T(8,128)S(1)} collective-permute-done((f32[2,32,256]{2,1,0:T(8,128)S(1)}, f32[2,32,256]{2,1,0:T(8,128)S(1)}, u32[]{:S(2)}, u32[]{:S(2)}) %collective-permute-start.17) | collective-permute-done | bytes 65568 | tf_op jit(solution)/shard_map/ppermute | solution.py:297
  52.3 1.7 %collective-permute-done.14.refs_2_ = bf16[144,512]{1,0:T(8,128)(2,1)S(1)} collective-permute-done((bf16[144,512]{1,0:T(8,128)(2,1)S(1)}, bf16[144,512]{1,0:T(8,128)(2,1)S(1)}, u32[]{:S(2)}, u32[]{:S(2)}) %collective-permute-start.14) | collective-permute-done | bytes 147488 | tf_op jit(solution)/shard_map/ppermute | solution.py:297
  54.0 2.8 %collective-permute-start.19 = (f32[1,32,256]{2,1,0:T(8,128)S(1)}, f32[1,32,256]{2,1,0:T(8,128)S(1)}, u32[]{:S(2)}, u32[]{:S(2)}) collective-permute-start(f32[1,32,256]{2,1,0:T(8,128)S(1)} %get-tuple-element.88), channel_id=1, source_target_pairs={{0,16},{4,20},{8,24},{12,28},{16,0},{20,4},{24,8},{28,12},{1,17},{... | collective-permute-start | bytes 98312 | tf_op jit(solution)/shard_map/ppermute | solution.py:297
  57.0 1.7 %collective-permute-done.19.refs_1_ = f32[1,32,256]{2,1,0:T(8,128)S(1)} collective-permute-done((f32[1,32,256]{2,1,0:T(8,128)S(1)}, f32[1,32,256]{2,1,0:T(8,128)S(1)}, u32[]{:S(2)}, u32[]{:S(2)}) %collective-permute-start.19) | collective-permute-done | bytes 32800 | tf_op jit(solution)/shard_map/ppermute | solution.py:297
  58.7 1.8 %collective-permute-start.20 = (f32[32,256]{1,0:T(8,128)S(1)}, f32[32,256]{1,0:T(8,128)S(1)}, u32[]{:S(2)}, u32[]{:S(2)}) collective-permute-start(f32[32,256]{1,0:T(8,128)S(1)} %gradient_sum.5.refs_1_), channel_id=1, source_target_pairs={{0,2},{1,3},{2,0},{3,1},{4,6},{5,7},{6,4},{7,5},{8,10},{9,11},{10,... | collective-permute-start | bytes 98312 | tf_op jit(solution)/shard_map/ppermute | solution.py:297
  60.5 3.0 %collective-permute-done.20.refs_2_ = f32[32,256]{1,0:T(8,128)S(1)} collective-permute-done((f32[32,256]{1,0:T(8,128)S(1)}, f32[32,256]{1,0:T(8,128)S(1)}, u32[]{:S(2)}, u32[]{:S(2)}) %collective-permute-start.20) | collective-permute-done | bytes 32800 | tf_op jit(solution)/shard_map/ppermute | solution.py:297
  63.5 1.7 %collective-permute-start.26 = (bf16[144,512]{1,0:T(8,128)(2,1)S(1)}, bf16[144,512]{1,0:T(8,128)(2,1)S(1)}, u32[]{:S(2)}, u32[]{:S(2)}) collective-permute-start(bf16[144,512]{1,0:T(8,128)(2,1)S(1)} %with_chunk.1.refs_0_), channel_id=1, source_target_pairs={{0,1},{1,0},{2,3},{3,2},{4,5},{5,4},{6,7},{7,6},{8,9},{9,8},{10,11... | collective-permute-start | bytes 442376 | tf_op jit(solution)/shard_map/ppermute | solution.py:297
  65.2 1.8 %backward_products.2 = (bf16[64,4096]{1,0:T(8,128)(2,1)S(1)}, bf16[16,4096]{1,0:T(8,128)(2,1)S(1)}, bf16[16,4096]{1,0:T(8,128)(2,1)S(1)}, bf16[16,4096]{1,0:T(8,128)(2,1)S(1)}, bf16[16,4096]{1,0:T(8,128)(2,1)S(1)}) custom-call(s32[1]{0:T(128)} %bitcast.1.place, s32[1,1]{1,0:T(1,128)S(6)} %copy.10.count, s32[96]{0:T(128)S(1)} %get-tuple-element.58.rows, ...), custom_call_target="tpu_custom_call" | custom-call | flops 1 | bytes 1 | tf_op jit(solution)/shard_map/backward_products/pallas_call | solution.py:203
  70.3 1.8 %backward_products.3 = (bf16[64,4096]{1,0:T(8,128)(2,1)S(1)}, bf16[32,4096]{1,0:T(8,128)(2,1)S(1)}, bf16[32,4096]{1,0:T(8,128)(2,1)S(1)}) custom-call(s32[1]{0:T(128)} %bitcast.1.place, s32[1,1]{1,0:T(1,128)S(6)} %copy.10.count, s32[96]{0:T(128)S(1)} %get-tuple-element.58.rows, s32[96]{0:T(128)S(1)} %get-tuple-element.59.cols, ...), custom_call_target="tpu_custom_call" | custom-call | flops 1 | bytes 1 | tf_op jit(solution)/shard_map/backward_products/pallas_call | solution.py:203
  72.2 4.2 %collective-permute-start.29 = (bf16[32,4096]{1,0:T(8,128)(2,1)S(1)}, bf16[32,4096]{1,0:T(8,128)(2,1)S(1)}, u32[]{:S(2)}, u32[]{:S(2)}) collective-permute-start(bf16[32,4096]{1,0:T(8,128)(2,1)S(1)} %get-tuple-element.104), channel_id=1, source_target_pairs={{0,4},{4,0},{8,12},{12,8},{16,20},{20,16},{24,28},{28,24},{1,5},{5... | collective-permute-start | bytes 786440 | tf_op jit(solution)/shard_map/ppermute | solution.py:297
  76.8 1.1 %collective-permute-done.27.sibling = f32[32,256]{1,0:T(8,128)S(1)} collective-permute-done((f32[32,256]{1,0:T(8,128)S(1)}, f32[32,256]{1,0:T(8,128)S(1)}, u32[]{:S(2)}, u32[]{:S(2)}) %collective-permute-start.27) | collective-permute-done | bytes 32800 | tf_op jit(solution)/shard_map/ppermute | solution.py:297
  78.4 1.8 %collective-permute-start.32 = (bf16[32,4608]{1,0:T(8,128)(2,1)S(1)}, bf16[32,4608]{1,0:T(8,128)(2,1)S(1)}, u32[]{:S(2)}, u32[]{:S(2)}) collective-permute-start(bf16[32,4608]{1,0:T(8,128)(2,1)S(1)} %get-tuple-element.107), channel_id=1, source_target_pairs={{0,16},{4,20},{8,24},{12,28},{16,0},{20,4},{24,8},{28,12},{1,17},{... | collective-permute-start | bytes 884744 | tf_op jit(solution)/shard_map/ppermute | solution.py:297
  80.3 1.7 %collective-permute-start.33 = (bf16[32,512]{1,0:T(8,128)(2,1)S(1)}, bf16[32,512]{1,0:T(8,128)(2,1)S(1)}, u32[]{:S(2)}, u32[]{:S(2)}) collective-permute-start(bf16[32,512]{1,0:T(8,128)(2,1)S(1)} %get-tuple-element.108.refs_3_), channel_id=1, source_target_pairs={{0,24},{4,28},{8,16},{12,20},{16,8},{20,12},{24,0},{28,4},{1,25},{... | collective-permute-start | bytes 98312 | tf_op jit(solution)/shard_map/ppermute | solution.py:297
  81.9 6.8 %collective-permute-done.33.refs_4_ = bf16[32,512]{1,0:T(8,128)(2,1)S(1)} collective-permute-done((bf16[32,512]{1,0:T(8,128)(2,1)S(1)}, bf16[32,512]{1,0:T(8,128)(2,1)S(1)}, u32[]{:S(2)}, u32[]{:S(2)}) %collective-permute-start.33) | collective-permute-done | bytes 32800 | tf_op jit(solution)/shard_map/ppermute | solution.py:297
  (59 shorter events, 9.5 us)
Async XLA Ops:
  0.6 9.5 %collective-permute-start.1 = (bf16[32,4096]{1,0:T(8,128)(2,1)}, bf16[32,4096]{1,0:T(8,128)(2,1)S(1)}, u32[]{:S(2)}, u32[]{:S(2)}) collective-permute-start(bf16[32,4096]{1,0:T(8,128)(2,1)} %bitcast.7), channel_id=1, source_target_pairs={{0,8},{4,12},{8,0},{12,4},{16,24},{20,28},{24,16},{28,20},{1,9},{5... | collective-permute-start | bytes 786440 | tf_op jit(solution)/shard_map/ppermute | solution.py:297
  3.7 8.0 %collective-permute-start.3 = (bf16[32,4096]{1,0:T(8,128)(2,1)}, bf16[32,4096]{1,0:T(8,128)(2,1)S(1)}, u32[]{:S(2)}, u32[]{:S(2)}) collective-permute-start(bf16[32,4096]{1,0:T(8,128)(2,1)} %bitcast.8), channel_id=1, source_target_pairs={{0,16},{4,20},{8,24},{12,28},{16,0},{20,4},{24,8},{28,12},{1,17},{... | collective-permute-start | bytes 786440 | tf_op jit(solution)/shard_map/ppermute | solution.py:297
  5.2 9.4 %collective-permute-start = (bf16[32,4096]{1,0:T(8,128)(2,1)}, bf16[32,4096]{1,0:T(8,128)(2,1)S(1)}, u32[]{:S(2)}, u32[]{:S(2)}) collective-permute-start(bf16[32,4096]{1,0:T(8,128)(2,1)} %bitcast.9), channel_id=1, source_target_pairs={{0,4},{4,0},{8,12},{12,8},{16,20},{20,16},{24,28},{28,24},{1,5},{5... | collective-permute-start | bytes 786440 | tf_op jit(solution)/shard_map/ppermute | solution.py:297
  10.2 4.4 %collective-permute-start.2 = (bf16[32,4096]{1,0:T(8,128)(2,1)S(1)}, bf16[32,4096]{1,0:T(8,128)(2,1)S(1)}, u32[]{:S(2)}, u32[]{:S(2)}) collective-permute-start(bf16[32,4096]{1,0:T(8,128)(2,1)S(1)} %collective-permute-done.1.refs_2_), channel_id=1, source_target_pairs={{0,4},{4,0},{8,12},{12,8},{16,20},{20,16},{24,28},{28,24},{1,5},{5... | collective-permute-start | bytes 786440 | tf_op jit(solution)/shard_map/ppermute | solution.py:297
  11.6 2.9 %collective-permute-start.4 = (bf16[32,4096]{1,0:T(8,128)(2,1)S(1)}, bf16[32,4096]{1,0:T(8,128)(2,1)S(1)}, u32[]{:S(2)}, u32[]{:S(2)}) collective-permute-start(bf16[32,4096]{1,0:T(8,128)(2,1)S(1)} %collective-permute-done.3.refs_4_), channel_id=1, source_target_pairs={{0,4},{4,0},{8,12},{12,8},{16,20},{20,16},{24,28},{28,24},{1,5},{5... | collective-permute-start | bytes 786440 | tf_op jit(solution)/shard_map/ppermute | solution.py:297
  11.6 7.2 %collective-permute-start.7 = (bf16[16,4096]{1,0:T(8,128)(2,1)S(1)}, bf16[16,4096]{1,0:T(8,128)(2,1)S(1)}, u32[]{:S(2)}, u32[]{:S(2)}) collective-permute-start(bf16[16,4096]{1,0:T(8,128)(2,1)S(1)} %get-tuple-element.67), channel_id=1, source_target_pairs={{0,24},{4,28},{8,16},{12,20},{16,8},{20,12},{24,0},{28,4},{1,25},{... | collective-permute-start | bytes 393224 | tf_op jit(solution)/shard_map/ppermute | solution.py:297
  13.4 7.9 %collective-permute-start.6 = (bf16[16,4096]{1,0:T(8,128)(2,1)S(1)}, bf16[16,4096]{1,0:T(8,128)(2,1)S(1)}, u32[]{:S(2)}, u32[]{:S(2)}) collective-permute-start(bf16[16,4096]{1,0:T(8,128)(2,1)S(1)} %get-tuple-element.65), channel_id=1, source_target_pairs={{0,24},{4,28},{8,16},{12,20},{16,8},{20,12},{24,0},{28,4},{1,25},{... | collective-permute-start | bytes 393224 | tf_op jit(solution)/shard_map/ppermute | solution.py:297
  16.9 9.3 %collective-permute-start.5 = (bf16[320,512]{1,0:T(8,128)(2,1)S(1)}, bf16[320,512]{1,0:T(8,128)(2,1)S(1)}, u32[]{:S(2)}, u32[]{:S(2)}) collective-permute-start(bf16[320,512]{1,0:T(8,128)(2,1)S(1)} %get-tuple-element.64), channel_id=1, source_target_pairs={{0,1},{1,0},{2,3},{3,2},{4,5},{5,4},{6,7},{7,6},{8,9},{9,8},{10,11... | collective-permute-start | bytes 983048 | tf_op jit(solution)/shard_map/ppermute | solution.py:297
  18.8 2.9 %collective-permute-start.9 = (bf16[16,4096]{1,0:T(8,128)(2,1)S(1)}, bf16[16,4096]{1,0:T(8,128)(2,1)S(1)}, u32[]{:S(2)}, u32[]{:S(2)}) collective-permute-start(bf16[16,4096]{1,0:T(8,128)(2,1)S(1)} %collective-permute-done.7.refs_1_), channel_id=1, source_target_pairs={{0,4},{4,0},{8,12},{12,8},{16,20},{20,16},{24,28},{28,24},{1,5},{5... | collective-permute-start | bytes 393224 | tf_op jit(solution)/shard_map/ppermute | solution.py:297
  24.5 6.5 %collective-permute-start.11 = (bf16[192,512]{1,0:T(8,128)(2,1)S(1)}, bf16[192,512]{1,0:T(8,128)(2,1)S(1)}, u32[]{:S(2)}, u32[]{:S(2)}) collective-permute-start(bf16[192,512]{1,0:T(8,128)(2,1)S(1)} %get-tuple-element.75), channel_id=1, source_target_pairs={{0,1},{1,0},{2,3},{3,2},{4,5},{5,4},{6,7},{7,6},{8,9},{9,8},{10,11... | collective-permute-start | bytes 589832 | tf_op jit(solution)/shard_map/ppermute | solution.py:297
  26.2 16.0 %collective-permute-start.10 = (bf16[160,512]{1,0:T(8,128)(2,1)S(1)}, bf16[160,512]{1,0:T(8,128)(2,1)S(1)}, u32[]{:S(2)}, u32[]{:S(2)}) collective-permute-start(bf16[160,512]{1,0:T(8,128)(2,1)S(1)} %pass_on.2), channel_id=1, source_target_pairs={{0,2},{1,3},{2,0},{3,1},{4,6},{5,7},{6,4},{7,5},{8,10},{9,11},{10,... | collective-permute-start | bytes 491528 | tf_op jit(solution)/shard_map/ppermute | solution.py:297
  31.0 11.2 %collective-permute-start.12 = (bf16[96,512]{1,0:T(8,128)(2,1)S(1)}, bf16[96,512]{1,0:T(8,128)(2,1)S(1)}, u32[]{:S(2)}, u32[]{:S(2)}) collective-permute-start(bf16[96,512]{1,0:T(8,128)(2,1)S(1)} %pass_on.3), channel_id=1, source_target_pairs={{0,2},{1,3},{2,0},{3,1},{4,6},{5,7},{6,4},{7,5},{8,10},{9,11},{10,... | collective-permute-start | bytes 294920 | tf_op jit(solution)/shard_map/ppermute | solution.py:297
  43.4 10.6 %collective-permute-start.14 = (bf16[144,512]{1,0:T(8,128)(2,1)S(1)}, bf16[144,512]{1,0:T(8,128)(2,1)S(1)}, u32[]{:S(2)}, u32[]{:S(2)}) collective-permute-start(bf16[144,512]{1,0:T(8,128)(2,1)S(1)} %get-tuple-element.80), channel_id=1, source_target_pairs={{0,2},{1,3},{2,0},{3,1},{4,6},{5,7},{6,4},{7,5},{8,10},{9,11},{10,... | collective-permute-start | bytes 442376 | tf_op jit(solution)/shard_map/ppermute | solution.py:297
  43.6 4.3 %collective-permute-start.15 = (f32[2,32,256]{2,1,0:T(8,128)S(1)}, f32[2,32,256]{2,1,0:T(8,128)S(1)}, u32[]{:S(2)}, u32[]{:S(2)}) collective-permute-start(f32[2,32,256]{2,1,0:T(8,128)S(1)} %get-tuple-element.84), channel_id=1, source_target_pairs={{0,4},{4,0},{8,12},{12,8},{16,20},{20,16},{24,28},{28,24},{1,5},{5... | collective-permute-start | bytes 196616 | tf_op jit(solution)/shard_map/ppermute | solution.py:297
  43.8 4.1 %collective-permute-start.16 = (f32[2,32,256]{2,1,0:T(8,128)S(1)}, f32[2,32,256]{2,1,0:T(8,128)S(1)}, u32[]{:S(2)}, u32[]{:S(2)}) collective-permute-start(f32[2,32,256]{2,1,0:T(8,128)S(1)} %get-tuple-element.85), channel_id=1, source_target_pairs={{0,4},{4,0},{8,12},{12,8},{16,20},{20,16},{24,28},{28,24},{1,5},{5... | collective-permute-start | bytes 196616 | tf_op jit(solution)/shard_map/ppermute | solution.py:297
  44.2 21.0 %collective-permute-start.13 = (bf16[256,512]{1,0:T(8,128)(2,1)S(1)}, bf16[256,512]{1,0:T(8,128)(2,1)S(1)}, u32[]{:S(2)}, u32[]{:S(2)}) collective-permute-start(bf16[256,512]{1,0:T(8,128)(2,1)S(1)} %get-tuple-element.79.refs_0_), channel_id=1, source_target_pairs={{0,1},{1,0},{2,3},{3,2},{4,5},{5,4},{6,7},{7,6},{8,9},{9,8},{10,11... | collective-permute-start | bytes 786440 | tf_op jit(solution)/shard_map/ppermute | solution.py:297
  47.9 4.3 %collective-permute-start.17 = (f32[2,32,256]{2,1,0:T(8,128)S(1)}, f32[2,32,256]{2,1,0:T(8,128)S(1)}, u32[]{:S(2)}, u32[]{:S(2)}) collective-permute-start(f32[2,32,256]{2,1,0:T(8,128)S(1)} %get-tuple-element.87), channel_id=1, source_target_pairs={{0,8},{4,12},{8,0},{12,4},{16,24},{20,28},{24,16},{28,20},{1,9},{5... | collective-permute-start | bytes 196616 | tf_op jit(solution)/shard_map/ppermute | solution.py:297
  48.0 9.0 %collective-permute-start.18 = (bf16[112,512]{1,0:T(8,128)(2,1)S(1)}, bf16[112,512]{1,0:T(8,128)(2,1)S(1)}, u32[]{:S(2)}, u32[]{:S(2)}) collective-permute-start(bf16[112,512]{1,0:T(8,128)(2,1)S(1)} %get-tuple-element.90), channel_id=1, source_target_pairs={{0,2},{1,3},{2,0},{3,1},{4,6},{5,7},{6,4},{7,5},{8,10},{9,11},{10,... | collective-permute-start | bytes 344072 | tf_op jit(solution)/shard_map/ppermute | solution.py:297
  54.0 11.2 %collective-permute-start.21 = (bf16[144,512]{1,0:T(8,128)(2,1)S(1)}, bf16[144,512]{1,0:T(8,128)(2,1)S(1)}, u32[]{:S(2)}, u32[]{:S(2)}) collective-permute-start(bf16[144,512]{1,0:T(8,128)(2,1)S(1)} %collective-permute-done.14.refs_2_), channel_id=1, source_target_pairs={{0,1},{1,0},{2,3},{3,2},{4,5},{5,4},{6,7},{7,6},{8,9},{9,8},{10,11... | collective-permute-start | bytes 442376 | tf_op jit(solution)/shard_map/ppermute | solution.py:297
  54.0 4.7 %collective-permute-start.19 = (f32[1,32,256]{2,1,0:T(8,128)S(1)}, f32[1,32,256]{2,1,0:T(8,128)S(1)}, u32[]{:S(2)}, u32[]{:S(2)}) collective-permute-start(f32[1,32,256]{2,1,0:T(8,128)S(1)} %get-tuple-element.88), channel_id=1, source_target_pairs={{0,16},{4,20},{8,24},{12,28},{16,0},{20,4},{24,8},{28,12},{1,17},{... | collective-permute-start | bytes 98312 | tf_op jit(solution)/shard_map/ppermute | solution.py:297
  58.7 4.8 %collective-permute-start.20 = (f32[32,256]{1,0:T(8,128)S(1)}, f32[32,256]{1,0:T(8,128)S(1)}, u32[]{:S(2)}, u32[]{:S(2)}) collective-permute-start(f32[32,256]{1,0:T(8,128)S(1)} %gradient_sum.5.refs_1_), channel_id=1, source_target_pairs={{0,2},{1,3},{2,0},{3,1},{4,6},{5,7},{6,4},{7,5},{8,10},{9,11},{10,... | collective-permute-start | bytes 98312 | tf_op jit(solution)/shard_map/ppermute | solution.py:297
  63.5 6.8 %collective-permute-start.26 = (bf16[144,512]{1,0:T(8,128)(2,1)S(1)}, bf16[144,512]{1,0:T(8,128)(2,1)S(1)}, u32[]{:S(2)}, u32[]{:S(2)}) collective-permute-start(bf16[144,512]{1,0:T(8,128)(2,1)S(1)} %with_chunk.1.refs_0_), channel_id=1, source_target_pairs={{0,1},{1,0},{2,3},{3,2},{4,5},{5,4},{6,7},{7,6},{8,9},{9,8},{10,11... | collective-permute-start | bytes 442376 | tf_op jit(solution)/shard_map/ppermute | solution.py:297
  67.0 1.4 %collective-permute-start.22 = (bf16[16,4096]{1,0:T(8,128)(2,1)S(1)}, bf16[16,4096]{1,0:T(8,128)(2,1)S(1)}, u32[]{:S(2)}, u32[]{:S(2)}) collective-permute-start(bf16[16,4096]{1,0:T(8,128)(2,1)S(1)} %get-tuple-element.95), channel_id=1, source_target_pairs={{0,4},{4,0},{8,12},{12,8},{16,20},{20,16},{24,28},{28,24},{1,5},{5... | collective-permute-start | bytes 393224 | tf_op jit(solution)/shard_map/ppermute | solution.py:297
  67.1 1.5 %collective-permute-start.23 = (bf16[16,4096]{1,0:T(8,128)(2,1)S(1)}, bf16[16,4096]{1,0:T(8,128)(2,1)S(1)}, u32[]{:S(2)}, u32[]{:S(2)}) collective-permute-start(bf16[16,4096]{1,0:T(8,128)(2,1)S(1)} %get-tuple-element.96), channel_id=1, source_target_pairs={{0,4},{4,0},{8,12},{12,8},{16,20},{20,16},{24,28},{28,24},{1,5},{5... | collective-permute-start | bytes 393224 | tf_op jit(solution)/shard_map/ppermute | solution.py:297
  67.7 1.5 %collective-permute-start.25 = (bf16[16,4096]{1,0:T(8,128)(2,1)S(1)}, bf16[16,4096]{1,0:T(8,128)(2,1)S(1)}, u32[]{:S(2)}, u32[]{:S(2)}) collective-permute-start(bf16[16,4096]{1,0:T(8,128)(2,1)S(1)} %get-tuple-element.98), channel_id=1, source_target_pairs={{0,4},{4,0},{8,12},{12,8},{16,20},{20,16},{24,28},{28,24},{1,5},{5... | collective-permute-start | bytes 393224 | tf_op jit(solution)/shard_map/ppermute | solution.py:297
  69.3 8.6 %collective-permute-start.28 = (bf16[32,4224]{1,0:T(8,128)(2,1)S(1)}, bf16[32,4224]{1,0:T(8,128)(2,1)S(1)}, u32[]{:S(2)}, u32[]{:S(2)}) collective-permute-start(bf16[32,4224]{1,0:T(8,128)(2,1)S(1)} %get-tuple-element.100), channel_id=1, source_target_pairs={{0,8},{4,20},{8,0},{12,28},{16,24},{20,4},{24,16},{28,12},{1,9},{5... | collective-permute-start | bytes 811016 | tf_op jit(solution)/shard_map/ppermute | solution.py:496
  72.2 5.8 %collective-permute-start.29 = (bf16[32,4096]{1,0:T(8,128)(2,1)S(1)}, bf16[32,4096]{1,0:T(8,128)(2,1)S(1)}, u32[]{:S(2)}, u32[]{:S(2)}) collective-permute-start(bf16[32,4096]{1,0:T(8,128)(2,1)S(1)} %get-tuple-element.104), channel_id=1, source_target_pairs={{0,4},{4,0},{8,12},{12,8},{16,20},{20,16},{24,28},{28,24},{1,5},{5... | collective-permute-start | bytes 786440 | tf_op jit(solution)/shard_map/ppermute | solution.py:297
  76.3 1.6 %collective-permute-start.30 = (bf16[32,4096]{1,0:T(8,128)(2,1)S(1)}, bf16[32,4096]{1,0:T(8,128)(2,1)S(1)}, u32[]{:S(2)}, u32[]{:S(2)}) collective-permute-start(bf16[32,4096]{1,0:T(8,128)(2,1)S(1)} %get-tuple-element.105), channel_id=1, source_target_pairs={{0,4},{4,0},{8,12},{12,8},{16,20},{20,16},{24,28},{28,24},{1,5},{5... | collective-permute-start | bytes 786440 | tf_op jit(solution)/shard_map/ppermute | solution.py:297
  76.4 1.5 %collective-permute-start.27 = (f32[32,256]{1,0:T(8,128)S(1)}, f32[32,256]{1,0:T(8,128)S(1)}, u32[]{:S(2)}, u32[]{:S(2)}) collective-permute-start(f32[32,256]{1,0:T(8,128)S(1)} %chunk_sum.1.chunk), channel_id=1, source_target_pairs={{0,4},{4,0},{8,12},{12,8},{16,20},{20,16},{24,28},{28,24},{1,5},{5... | collective-permute-start | bytes 98312 | tf_op jit(solution)/shard_map/ppermute | solution.py:297
  78.4 10.4 %collective-permute-start.31 = (bf16[32,4608]{1,0:T(8,128)(2,1)S(1)}, bf16[32,4608]{1,0:T(8,128)(2,1)S(1)}, u32[]{:S(2)}, u32[]{:S(2)}) collective-permute-start(bf16[32,4608]{1,0:T(8,128)(2,1)S(1)} %get-tuple-element.106), channel_id=1, source_target_pairs={{0,8},{4,12},{8,0},{12,4},{16,24},{20,28},{24,16},{28,20},{1,9},{5... | collective-permute-start | bytes 884744 | tf_op jit(solution)/shard_map/ppermute | solution.py:297
  78.4 10.3 %collective-permute-start.32 = (bf16[32,4608]{1,0:T(8,128)(2,1)S(1)}, bf16[32,4608]{1,0:T(8,128)(2,1)S(1)}, u32[]{:S(2)}, u32[]{:S(2)}) collective-permute-start(bf16[32,4608]{1,0:T(8,128)(2,1)S(1)} %get-tuple-element.107), channel_id=1, source_target_pairs={{0,16},{4,20},{8,24},{12,28},{16,0},{20,4},{24,8},{28,12},{1,17},{... | collective-permute-start | bytes 884744 | tf_op jit(solution)/shard_map/ppermute | solution.py:297
  80.3 8.4 %collective-permute-start.33 = (bf16[32,512]{1,0:T(8,128)(2,1)S(1)}, bf16[32,512]{1,0:T(8,128)(2,1)S(1)}, u32[]{:S(2)}, u32[]{:S(2)}) collective-permute-start(bf16[32,512]{1,0:T(8,128)(2,1)S(1)} %get-tuple-element.108.refs_3_), channel_id=1, source_target_pairs={{0,24},{4,28},{8,16},{12,20},{16,8},{20,12},{24,0},{28,4},{1,25},{... | collective-permute-start | bytes 98312 | tf_op jit(solution)/shard_map/ppermute | solution.py:297
  (5 other events, 67.3 us)

commit v4 on v3

--- a/solution.py
+++ b/solution.py
@@ -459,16 +459,17 @@
     order = [k + side for group in groups for side in range(2) for k in group]
     cuts = [2 * depth * len(group) for group in groups]
     ahead = depth // 2
-    output, deltas, aggregated, back, *backs = middle(
-        n_row, row, weight, cotangent, sums, order, [sum(cuts), cuts[0] + ahead, cuts[1] - ahead]
+    output, deltas, aggregated, *backs = middle(
+        n_row, row, weight, cotangent, sums, order, [cuts[0] + ahead, cuts[1] - ahead]
     )
-    beside = swap(back, "col", 1)
+    beside = [swap(backs[0], "col", 1)]
     beyond = [swap(part, "col", 2) for part in backs]
 
     even, *odd = gradient(1.0 / math.sqrt(nodes), [(0, 4, 2, 6), (1, 5), (3, 7)], aggregated, deltas)
     even, sent = fuse("gradient_sum", halves_sum, even, *[swap(part, "row", 1) for part in odd])
-    even, sent = fuse("gradient_sum", halves_sum, even, swap(sent, "row", 2))
+    even, sent = fuse("gradient_sum", halves_sum, after(even, beside[0]), swap(sent, "row", 2))
     beyond[0] = after(beyond[0], sent)
+    beside.append(swap(after(backs[1], beyond[0]), "col", 1))
     even = after(even, beyond[1])
     (chunk,) = fuse("gradient_sum", lambda a, b: ((a + b)[0],), even, swap(sent, "row", 4))
     chunks = [chunk, swap(chunk, "col", 2)]
@@ -477,22 +478,21 @@
     received = [swap(beyond[0], "col", 1), swap(second, "col", 1)]
 
     def columns(n, *earlier):
-        parts = [back, beside, after(beyond[0], *earlier), received[0], beyond[1], received[1]]
+        parts = [backs[0], beside[0], after(beyond[0], *earlier), received[0]]
         if n == 0:
             depths = cuts[:1]
-            parts = parts[:4]
             spots = [[(part, 0)] for part in range(4)]
         else:
             depths = [ahead, cuts[1] - ahead]
-            spots = [[(part, cuts[0]), (part, cuts[0] + ahead)] for part in range(2)]
-            spots += [[(part, cuts[0]), (part + 2, 0)] for part in (2, 3)]
+            parts += [backs[1], beside[1], beyond[1], received[1]]
+            spots = [[(part, cuts[0]), (part + 4, 0)] for part in range(4)]
         out_depths = [cuts[n] // 2] + [cuts[n] // (8 - 4 * n)] * (4 - 2 * n)
         mine, *sent = backward(
             col, count, rows, cols, tile, parts, spots, depths, out_depths, col_blocks
         )
         return [mine] + [swap(part, "row", 1) for part in sent]
 
-    own_sum, far_sum = fuse("far_sums", functools.partial(far_sums, depth), *columns(0, second))
+    own_sum, far_sum = fuse("far_sums", functools.partial(far_sums, depth), *columns(0, second, beside[1]))
     half_way = lax.ppermute(far_sum, "row", [(i, i ^ (4 if i % 2 else 2)) for i in range(n_row)])
     received[1] = after(received[1], far_sum)
     (chunk,) = fuse("chunk_sum", functools.partial(chunk_sum, depth), second, received[1])

time: 88.8 us -> 90.4 us (1.018); the launches traced: 89.6 us -> 90.1 us
  starting transfers between devices: 40.7 us -> 27.8 us
  waiting for transfers between devices: 35.1 us -> 45.1 us
  Pallas kernels: 12.3 us -> 15.7 us
    ppermute x33 -> x34, starting transfers between devices: 39.8 us -> 27.7 us  [swap(): return lax.ppermute(value, axis, [(i, i ^ k) for i in range(size)])]
    ppermute x33 -> x34, waiting for transfers between devices: 35.1 us -> 44.1 us  [swap(): return lax.ppermute(value, axis, [(i, i ^ k) for i in range(size)])]
    pallas_call x2, Pallas kernels: 4.16 us -> 5.95 us  [forward(): pl.pallas_call(functools.partial(forward_kernel, len(parts), depths, layo...]
    pallas_call x2, Pallas kernels: 3.66 us -> 5.05 us  [backward(): pl.pallas_call(functools.partial(backward_kernel, spots, depths), out_sha...]
    ppermute x1, waiting for transfers between devices: 0.01 us -> 1.03 us  [shards_exchanged(): lax.ppermute(far_sum, 'row', [(i, i ^ (4 if i % 2 else 2)) for i in range...]
    ppermute x1, starting transfers between devices: 0.98 us -> 0.07 us  [shards_exchanged(): lax.ppermute(far_sum, 'row', [(i, i ^ (4 if i % 2 else 2)) for i in range...]
  transfers between devices with their start and end apart: 34 -> 35, of which waited for: 20 -> 23; matrix products, arithmetic and copies ran while one was open for 0% -> 0% of each run, Pallas kernels for 11% -> 15%
where the time goes in v4:
time: 90.4 us; the launch traced here: 90.1 us
  waiting for transfers between devices  45.1 us (50%)
  starting transfers between devices  27.8 us (31%)
  Pallas kernels  15.7 us (17%)
  between operations  1.49 us (2%)
    ppermute x34, waiting for transfers between devices, swap(): return lax.ppermute(value, axis, [(i, i ^ k) for i in range(size)])  44.1 us
    ppermute x34, starting transfers between devices, swap(): return lax.ppermute(value, axis, [(i, i ^ k) for i in range(size)])  27.7 us
    pallas_call x2, Pallas kernels, forward(): pl.pallas_call(functools.partial(forward_kernel, len(parts), depths, layo...  5.95 us
    pallas_call x2, Pallas kernels, backward(): pl.pallas_call(functools.partial(backward_kernel, spots, depths), out_sha...  5.05 us
  transfers between devices with their start and end apart: 35, of which 23 were waited for; matrix products, arithmetic and copies ran while one was open for 0% of the time, Pallas kernels for 15%

profile of v4, /device:TPU:0, one launch (start us, length us, event | category | flops | bytes accessed | tf_op | source)
XLA Modules:
  0.0 90.1 jit_solution(3711559224637716305)
XLA Ops:
  0.6 3.0 %collective-permute-start.1 = (bf16[32,4096]{1,0:T(8,128)(2,1)}, bf16[32,4096]{1,0:T(8,128)(2,1)S(1)}, u32[]{:S(2)}, u32[]{:S(2)}) collective-permute-start(bf16[32,4096]{1,0:T(8,128)(2,1)} %bitcast.7), channel_id=1, source_target_pairs={{0,8},{4,12},{8,0},{12,4},{16,24},{20,28},{24,16},{28,20},{1,9},{5... | collective-permute-start | bytes 786440 | tf_op jit(solution)/shard_map/ppermute | solution.py:297
  3.7 1.5 %collective-permute-start.3 = (bf16[32,4096]{1,0:T(8,128)(2,1)}, bf16[32,4096]{1,0:T(8,128)(2,1)S(1)}, u32[]{:S(2)}, u32[]{:S(2)}) collective-permute-start(bf16[32,4096]{1,0:T(8,128)(2,1)} %bitcast.8), channel_id=1, source_target_pairs={{0,16},{4,20},{8,24},{12,28},{16,0},{20,4},{24,8},{28,12},{1,17},{... | collective-permute-start | bytes 786440 | tf_op jit(solution)/shard_map/ppermute | solution.py:297
  5.8 1.7 %fetch.1 = (s32[96]{0:T(128)S(1)}, s32[96]{0:T(128)S(1)}, bf16[16,4096]{1,0:T(8,128)(2,1)S(1)}, bf16[16,4096]{1,0:T(8,128)(2,1)S(1)}, bf16[96,128,128]{2,1,0:T(8,128)(2,1)S(1)}) custom-call(s32[1,1]{1,0:T(1,128)S(6)} %copy.10.count, s32[96]{0:T(128)} %bitcast.13, s32[96]{0:T(128)} %bitcast.14, bf16[32,4096]{1,0:T(8,128)(2,1)} %bitcast.10, ...), custom_call_target="tpu_custom_call" | custom-call | flops 1 | bytes 1 | tf_op jit(solution)/shard_map/fetch/pallas_call | solution.py:103
  7.6 2.6 %collective-permute-done.1.refs_2_ = bf16[32,4096]{1,0:T(8,128)(2,1)S(1)} collective-permute-done((bf16[32,4096]{1,0:T(8,128)(2,1)}, bf16[32,4096]{1,0:T(8,128)(2,1)S(1)}, u32[]{:S(2)}, u32[]{:S(2)}) %collective-permute-start.1) | collective-permute-done | bytes 262176 | tf_op jit(solution)/shard_map/ppermute | solution.py:297
  10.2 1.5 %collective-permute-done.3.refs_4_ = bf16[32,4096]{1,0:T(8,128)(2,1)S(1)} collective-permute-done((bf16[32,4096]{1,0:T(8,128)(2,1)}, bf16[32,4096]{1,0:T(8,128)(2,1)S(1)}, u32[]{:S(2)}, u32[]{:S(2)}) %collective-permute-start.3) | collective-permute-done | bytes 262176 | tf_op jit(solution)/shard_map/ppermute | solution.py:297
  11.6 1.7 %collective-permute-start.7 = (bf16[16,4096]{1,0:T(8,128)(2,1)S(1)}, bf16[16,4096]{1,0:T(8,128)(2,1)S(1)}, u32[]{:S(2)}, u32[]{:S(2)}) collective-permute-start(bf16[16,4096]{1,0:T(8,128)(2,1)S(1)} %get-tuple-element.68), channel_id=1, source_target_pairs={{0,24},{4,28},{8,16},{12,20},{16,8},{20,12},{24,0},{28,4},{1,25},{... | collective-permute-start | bytes 393224 | tf_op jit(solution)/shard_map/ppermute | solution.py:297
  13.4 1.2 %collective-permute-start.6 = (bf16[16,4096]{1,0:T(8,128)(2,1)S(1)}, bf16[16,4096]{1,0:T(8,128)(2,1)S(1)}, u32[]{:S(2)}, u32[]{:S(2)}) collective-permute-start(bf16[16,4096]{1,0:T(8,128)(2,1)S(1)} %get-tuple-element.66), channel_id=1, source_target_pairs={{0,24},{4,28},{8,16},{12,20},{16,8},{20,12},{24,0},{28,4},{1,25},{... | collective-permute-start | bytes 393224 | tf_op jit(solution)/shard_map/ppermute | solution.py:297
  14.6 3.2 %forward_products.2 = (bf16[160,512]{1,0:T(8,128)(2,1)S(1)}, bf16[160,512]{1,0:T(8,128)(2,1)S(1)}, bf16[320,512]{1,0:T(8,128)(2,1)S(1)}, bf16[32,512]{1,0:T(8,12...) custom-call(s32[1]{0:T(128)} %bitcast.1.place, s32[1,1]{1,0:T(1,128)S(6)} %copy.10.count, ...), custom_call_target="tpu_custom_call" | custom-call | flops 1 | bytes 1 | tf_op jit(solution)/shard_map/forward_products/pallas_call | solution.py:160
  17.8 1.6 %collective-permute-start.5 = (bf16[320,512]{1,0:T(8,128)(2,1)S(1)}, bf16[320,512]{1,0:T(8,128)(2,1)S(1)}, u32[]{:S(2)}, u32[]{:S(2)}) collective-permute-start(bf16[320,512]{1,0:T(8,128)(2,1)S(1)} %get-tuple-element.65), channel_id=1, source_target_pairs={{0,1},{1,0},{2,3},{3,2},{4,5},{5,4},{6,7},{7,6},{8,9},{9,8},{10,11... | collective-permute-start | bytes 983048 | tf_op jit(solution)/shard_map/ppermute | solution.py:297
  19.5 1.8 %collective-permute-done.6.refs_0_ = bf16[16,4096]{1,0:T(8,128)(2,1)S(1)} collective-permute-done((bf16[16,4096]{1,0:T(8,128)(2,1)S(1)}, bf16[16,4096]{1,0:T(8,128)(2,1)S(1)}, u32[]{:S(2)}, u32[]{:S(2)}) %collective-permute-start.6) | collective-permute-done | bytes 131104 | tf_op jit(solution)/shard_map/ppermute | solution.py:297
  21.3 1.3 %collective-permute-done.8.refs_2_ = bf16[16,4096]{1,0:T(8,128)(2,1)S(1)} collective-permute-done((bf16[16,4096]{1,0:T(8,128)(2,1)S(1)}, bf16[16,4096]{1,0:T(8,128)(2,1)S(1)}, u32[]{:S(2)}, u32[]{:S(2)}) %collective-permute-start.8) | collective-permute-done | bytes 131104 | tf_op jit(solution)/shard_map/ppermute | solution.py:297
  22.6 2.7 %forward_products.3 = (bf16[96,512]{1,0:T(8,128)(2,1)S(1)}, bf16[96,512]{1,0:T(8,128)(2,1)S(1)}, bf16[192,512]{1,0:T(8,128)(2,1)S(1)}) custom-call(s32[1]{0:T(128)} %bitcast.1.place, s32[1,1]{1,0:T(1,128)S(6)} %copy.10.count, s32[96]{0:T(128)S(1)} %get-tuple-element.59.rows, s32[96]{0:T(128)S(1)} %get-tuple-element.60.cols, ...), custom_call_target="tpu_custom_call" | custom-call | flops 1 | bytes 1 | tf_op jit(solution)/shard_map/forward_products/pallas_call | solution.py:160
  25.3 1.6 %collective-permute-start.11 = (bf16[192,512]{1,0:T(8,128)(2,1)S(1)}, bf16[192,512]{1,0:T(8,128)(2,1)S(1)}, u32[]{:S(2)}, u32[]{:S(2)}) collective-permute-start(bf16[192,512]{1,0:T(8,128)(2,1)S(1)} %get-tuple-element.76), channel_id=1, source_target_pairs={{0,1},{1,0},{2,3},{3,2},{4,5},{5,4},{6,7},{7,6},{8,9},{9,8},{10,11... | collective-permute-start | bytes 589832 | tf_op jit(solution)/shard_map/ppermute | solution.py:297
  27.7 2.8 %collective-permute-start.10 = (bf16[160,512]{1,0:T(8,128)(2,1)S(1)}, bf16[160,512]{1,0:T(8,128)(2,1)S(1)}, u32[]{:S(2)}, u32[]{:S(2)}) collective-permute-start(bf16[160,512]{1,0:T(8,128)(2,1)S(1)} %pass_on.2), channel_id=1, source_target_pairs={{0,2},{1,3},{2,0},{3,1},{4,6},{5,7},{6,4},{7,5},{8,10},{9,11},{10,... | collective-permute-start | bytes 491528 | tf_op jit(solution)/shard_map/ppermute | solution.py:297
  30.5 5.5 %collective-permute-done.11.refs_1_.refs_4_ = bf16[192,512]{1,0:T(8,128)(2,1)S(1)} collective-permute-done((bf16[192,512]{1,0:T(8,128)(2,1)S(1)}, bf16[192,512]{1,0:T(8,128)(2,1)S(1)}, u32[]{:S(2)}, u32[]{:S(2)}) %collective-permute-start.11) | collective-permute-done | bytes 196640 | tf_op jit(solution)/shard_map/ppermute | solution.py:297
  36.1 6.6 %collective-permute-done.12.refs_5_ = bf16[96,512]{1,0:T(8,128)(2,1)S(1)} collective-permute-done((bf16[96,512]{1,0:T(8,128)(2,1)S(1)}, bf16[96,512]{1,0:T(8,128)(2,1)S(1)}, u32[]{:S(2)}, u32[]{:S(2)}) %collective-permute-start.12) | collective-permute-done | bytes 98336 | tf_op jit(solution)/shard_map/ppermute | solution.py:297
  42.7 1.1 %layer.1 = (bf16[512,256]{1,0:T(8,128)(2,1)}, bf16[512,256]{1,0:T(8,128)(2,1)S(1)}, bf16[256,512]{1,0:T(8,128)(2,1)S(1)}, bf16[144,512]{1,0:T(8,128)(2,1)S(1)}, bf16[112,512]{1,0:T(8,128)(2,1)S(1)}) custom-call(s32[1]{0:T(128)} %bitcast.row, bf16[256,256]{1,0:T(8,128)(2,1)S(1)} %copy-done.2, bf16[512,256]{1,0:T(8,128)(2,1)S(1)} %copy-done.1, ...), custom_call_target="tpu_custom_call" | custom-call | flops 1 | bytes 1 | tf_op jit(solution)/shard_map/layer/pallas_call | solution.py:261
  44.0 3.4 %collective-permute-start.14 = (bf16[144,512]{1,0:T(8,128)(2,1)S(1)}, bf16[144,512]{1,0:T(8,128)(2,1)S(1)}, u32[]{:S(2)}, u32[]{:S(2)}) collective-permute-start(bf16[144,512]{1,0:T(8,128)(2,1)S(1)} %get-tuple-element.80.refs_0_), channel_id=1, source_target_pairs={{0,2},{1,3},{2,0},{3,1},{4,6},{5,7},{6,4},{7,5},{8,10},{9,11},{10,... | collective-permute-start | bytes 442376 | tf_op jit(solution)/shard_map/ppermute | solution.py:297
  49.3 3.0 %collective-permute-done.13.refs_1_ = bf16[144,512]{1,0:T(8,128)(2,1)S(1)} collective-permute-done((bf16[144,512]{1,0:T(8,128)(2,1)S(1)}, bf16[144,512]{1,0:T(8,128)(2,1)S(1)}, u32[]{:S(2)}, u32[]{:S(2)}) %collective-permute-start.13) | collective-permute-done | bytes 147488 | tf_op jit(solution)/shard_map/ppermute | solution.py:297
  52.3 1.3 %collective-permute-done.17.refs_1_ = f32[2,32,256]{2,1,0:T(8,128)S(1)} collective-permute-done((f32[2,32,256]{2,1,0:T(8,128)S(1)}, f32[2,32,256]{2,1,0:T(8,128)S(1)}, u32[]{:S(2)}, u32[]{:S(2)}) %collective-permute-start.17) | collective-permute-done | bytes 65568 | tf_op jit(solution)/shard_map/ppermute | solution.py:297
  53.6 3.0 %collective-permute-done.14.refs_2_ = bf16[144,512]{1,0:T(8,128)(2,1)S(1)} collective-permute-done((bf16[144,512]{1,0:T(8,128)(2,1)S(1)}, bf16[144,512]{1,0:T(8,128)(2,1)S(1)}, u32[]{:S(2)}, u32[]{:S(2)}) %collective-permute-start.14) | collective-permute-done | bytes 147488 | tf_op jit(solution)/shard_map/ppermute | solution.py:297
  56.6 2.0 %collective-permute-start.21 = (bf16[112,512]{1,0:T(8,128)(2,1)S(1)}, bf16[112,512]{1,0:T(8,128)(2,1)S(1)}, u32[]{:S(2)}, u32[]{:S(2)}) collective-permute-start(bf16[112,512]{1,0:T(8,128)(2,1)S(1)} %get-tuple-element.94.refs_4_), channel_id=1, source_target_pairs={{0,1},{1,0},{2,3},{3,2},{4,5},{5,4},{6,7},{7,6},{8,9},{9,8},{10,11... | collective-permute-start | bytes 344072 | tf_op jit(solution)/shard_map/ppermute | solution.py:297
  58.7 3.9 %collective-permute-done.19.refs_1_ = f32[1,32,256]{2,1,0:T(8,128)S(1)} collective-permute-done((f32[1,32,256]{2,1,0:T(8,128)S(1)}, f32[1,32,256]{2,1,0:T(8,128)S(1)}, u32[]{:S(2)}, u32[]{:S(2)}) %collective-permute-start.19) | collective-permute-done | bytes 32800 | tf_op jit(solution)/shard_map/ppermute | solution.py:297
  62.6 1.1 %collective-permute-start.20 = (f32[32,256]{1,0:T(8,128)S(1)}, f32[32,256]{1,0:T(8,128)S(1)}, u32[]{:S(2)}, u32[]{:S(2)}) collective-permute-start(f32[32,256]{1,0:T(8,128)S(1)} %gradient_sum.5.refs_1_), channel_id=1, source_target_pairs={{0,2},{1,3},{2,0},{3,1},{4,6},{5,7},{6,4},{7,5},{8,10},{9,11},{10,... | collective-permute-start | bytes 98312 | tf_op jit(solution)/shard_map/ppermute | solution.py:297
  63.7 3.7 %collective-permute-done.20.refs_2_ = f32[32,256]{1,0:T(8,128)S(1)} collective-permute-done((f32[32,256]{1,0:T(8,128)S(1)}, f32[32,256]{1,0:T(8,128)S(1)}, u32[]{:S(2)}, u32[]{:S(2)}) %collective-permute-start.20) | collective-permute-done | bytes 32800 | tf_op jit(solution)/shard_map/ppermute | solution.py:297
  67.6 2.5 %backward_products.2 = (bf16[64,4096]{1,0:T(8,128)(2,1)S(1)}, bf16[16,4096]{1,0:T(8,128)(2,1)S(1)}, bf16[16,4096]{1,0:T(8,128)(2,1)S(1)}, bf16[16,4096]{1,0:T(8,128)(2,1)S(1)}, bf16[16,4096]{1,0:T(8,128)(2,1)S(1)}) custom-call(s32[1]{0:T(128)} %bitcast.1.place, s32[1,1]{1,0:T(1,128)S(6)} %copy.10.count, s32[96]{0:T(128)S(1)} %get-tuple-element.59.rows, ...), custom_call_target="tpu_custom_call" | custom-call | flops 1 | bytes 1 | tf_op jit(solution)/shard_map/backward_products/pallas_call | solution.py:203
  72.6 2.5 %backward_products.3 = (bf16[64,4096]{1,0:T(8,128)(2,1)S(1)}, bf16[32,4096]{1,0:T(8,128)(2,1)S(1)}, bf16[32,4096]{1,0:T(8,128)(2,1)S(1)}) custom-call(s32[1]{0:T(128)} %bitcast.1.place, s32[1,1]{1,0:T(1,128)S(6)} %copy.10.count, s32[96]{0:T(128)S(1)} %get-tuple-element.59.rows, s32[96]{0:T(128)S(1)} %get-tuple-element.60.cols, ...), custom_call_target="tpu_custom_call" | custom-call | flops 1 | bytes 1 | tf_op jit(solution)/shard_map/backward_products/pallas_call | solution.py:203
  75.1 1.2 %collective-permute-start.30 = (bf16[32,4096]{1,0:T(8,128)(2,1)S(1)}, bf16[32,4096]{1,0:T(8,128)(2,1)S(1)}, u32[]{:S(2)}, u32[]{:S(2)}) collective-permute-start(bf16[32,4096]{1,0:T(8,128)(2,1)S(1)} %get-tuple-element.106), channel_id=1, source_target_pairs={{0,4},{4,0},{8,12},{12,8},{16,20},{20,16},{24,28},{28,24},{1,5},{5... | collective-permute-start | bytes 786440 | tf_op jit(solution)/shard_map/ppermute | solution.py:297
  76.9 1.1 %collective-permute-done.28.sibling = f32[32,256]{1,0:T(8,128)S(1)} collective-permute-done((f32[32,256]{1,0:T(8,128)S(1)}, f32[32,256]{1,0:T(8,128)S(1)}, u32[]{:S(2)}, u32[]{:S(2)}) %collective-permute-start.28) | collective-permute-done | bytes 32800 | tf_op jit(solution)/shard_map/ppermute | solution.py:297
  79.5 1.6 %collective-permute-start.33 = (bf16[32,4608]{1,0:T(8,128)(2,1)S(1)}, bf16[32,4608]{1,0:T(8,128)(2,1)S(1)}, u32[]{:S(2)}, u32[]{:S(2)}) collective-permute-start(bf16[32,4608]{1,0:T(8,128)(2,1)S(1)} %get-tuple-element.109), channel_id=1, source_target_pairs={{0,16},{4,20},{8,24},{12,28},{16,0},{20,4},{24,8},{28,12},{1,17},{... | collective-permute-start | bytes 884744 | tf_op jit(solution)/shard_map/ppermute | solution.py:297
  81.0 1.9 %collective-permute-start.34 = (bf16[32,512]{1,0:T(8,128)(2,1)S(1)}, bf16[32,512]{1,0:T(8,128)(2,1)S(1)}, u32[]{:S(2)}, u32[]{:S(2)}) collective-permute-start(bf16[32,512]{1,0:T(8,128)(2,1)S(1)} %get-tuple-element.110.refs_3_), channel_id=1, source_target_pairs={{0,24},{4,28},{8,16},{12,20},{16,8},{20,12},{24,0},{28,4},{1,25},{... | collective-permute-start | bytes 98312 | tf_op jit(solution)/shard_map/ppermute | solution.py:297
  83.0 6.2 %collective-permute-done.34.refs_4_ = bf16[32,512]{1,0:T(8,128)(2,1)S(1)} collective-permute-done((bf16[32,512]{1,0:T(8,128)(2,1)S(1)}, bf16[32,512]{1,0:T(8,128)(2,1)S(1)}, u32[]{:S(2)}, u32[]{:S(2)}) %collective-permute-start.34) | collective-permute-done | bytes 32800 | tf_op jit(solution)/shard_map/ppermute | solution.py:297
  (61 shorter events, 8.6 us)
Async XLA Ops:
  0.6 9.5 %collective-permute-start.1 = (bf16[32,4096]{1,0:T(8,128)(2,1)}, bf16[32,4096]{1,0:T(8,128)(2,1)S(1)}, u32[]{:S(2)}, u32[]{:S(2)}) collective-permute-start(bf16[32,4096]{1,0:T(8,128)(2,1)} %bitcast.7), channel_id=1, source_target_pairs={{0,8},{4,12},{8,0},{12,4},{16,24},{20,28},{24,16},{28,20},{1,9},{5... | collective-permute-start | bytes 786440 | tf_op jit(solution)/shard_map/ppermute | solution.py:297
  3.7 8.0 %collective-permute-start.3 = (bf16[32,4096]{1,0:T(8,128)(2,1)}, bf16[32,4096]{1,0:T(8,128)(2,1)S(1)}, u32[]{:S(2)}, u32[]{:S(2)}) collective-permute-start(bf16[32,4096]{1,0:T(8,128)(2,1)} %bitcast.8), channel_id=1, source_target_pairs={{0,16},{4,20},{8,24},{12,28},{16,0},{20,4},{24,8},{28,12},{1,17},{... | collective-permute-start | bytes 786440 | tf_op jit(solution)/shard_map/ppermute | solution.py:297
  5.2 9.4 %collective-permute-start = (bf16[32,4096]{1,0:T(8,128)(2,1)}, bf16[32,4096]{1,0:T(8,128)(2,1)S(1)}, u32[]{:S(2)}, u32[]{:S(2)}) collective-permute-start(bf16[32,4096]{1,0:T(8,128)(2,1)} %bitcast.9), channel_id=1, source_target_pairs={{0,4},{4,0},{8,12},{12,8},{16,20},{20,16},{24,28},{28,24},{1,5},{5... | collective-permute-start | bytes 786440 | tf_op jit(solution)/shard_map/ppermute | solution.py:297
  10.2 4.4 %collective-permute-start.2 = (bf16[32,4096]{1,0:T(8,128)(2,1)S(1)}, bf16[32,4096]{1,0:T(8,128)(2,1)S(1)}, u32[]{:S(2)}, u32[]{:S(2)}) collective-permute-start(bf16[32,4096]{1,0:T(8,128)(2,1)S(1)} %collective-permute-done.1.refs_2_), channel_id=1, source_target_pairs={{0,4},{4,0},{8,12},{12,8},{16,20},{20,16},{24,28},{28,24},{1,5},{5... | collective-permute-start | bytes 786440 | tf_op jit(solution)/shard_map/ppermute | solution.py:297
  11.6 2.9 %collective-permute-start.4 = (bf16[32,4096]{1,0:T(8,128)(2,1)S(1)}, bf16[32,4096]{1,0:T(8,128)(2,1)S(1)}, u32[]{:S(2)}, u32[]{:S(2)}) collective-permute-start(bf16[32,4096]{1,0:T(8,128)(2,1)S(1)} %collective-permute-done.3.refs_4_), channel_id=1, source_target_pairs={{0,4},{4,0},{8,12},{12,8},{16,20},{20,16},{24,28},{28,24},{1,5},{5... | collective-permute-start | bytes 786440 | tf_op jit(solution)/shard_map/ppermute | solution.py:297
  11.6 7.9 %collective-permute-start.7 = (bf16[16,4096]{1,0:T(8,128)(2,1)S(1)}, bf16[16,4096]{1,0:T(8,128)(2,1)S(1)}, u32[]{:S(2)}, u32[]{:S(2)}) collective-permute-start(bf16[16,4096]{1,0:T(8,128)(2,1)S(1)} %get-tuple-element.68), channel_id=1, source_target_pairs={{0,24},{4,28},{8,16},{12,20},{16,8},{20,12},{24,0},{28,4},{1,25},{... | collective-permute-start | bytes 393224 | tf_op jit(solution)/shard_map/ppermute | solution.py:297
  13.4 7.9 %collective-permute-start.6 = (bf16[16,4096]{1,0:T(8,128)(2,1)S(1)}, bf16[16,4096]{1,0:T(8,128)(2,1)S(1)}, u32[]{:S(2)}, u32[]{:S(2)}) collective-permute-start(bf16[16,4096]{1,0:T(8,128)(2,1)S(1)} %get-tuple-element.66), channel_id=1, source_target_pairs={{0,24},{4,28},{8,16},{12,20},{16,8},{20,12},{24,0},{28,4},{1,25},{... | collective-permute-start | bytes 393224 | tf_op jit(solution)/shard_map/ppermute | solution.py:297
  17.8 9.8 %collective-permute-start.5 = (bf16[320,512]{1,0:T(8,128)(2,1)S(1)}, bf16[320,512]{1,0:T(8,128)(2,1)S(1)}, u32[]{:S(2)}, u32[]{:S(2)}) collective-permute-start(bf16[320,512]{1,0:T(8,128)(2,1)S(1)} %get-tuple-element.65), channel_id=1, source_target_pairs={{0,1},{1,0},{2,3},{3,2},{4,5},{5,4},{6,7},{7,6},{8,9},{9,8},{10,11... | collective-permute-start | bytes 983048 | tf_op jit(solution)/shard_map/ppermute | solution.py:297
  19.5 1.8 %collective-permute-start.9 = (bf16[16,4096]{1,0:T(8,128)(2,1)S(1)}, bf16[16,4096]{1,0:T(8,128)(2,1)S(1)}, u32[]{:S(2)}, u32[]{:S(2)}) collective-permute-start(bf16[16,4096]{1,0:T(8,128)(2,1)S(1)} %collective-permute-done.7.refs_1_), channel_id=1, source_target_pairs={{0,4},{4,0},{8,12},{12,8},{16,20},{20,16},{24,28},{28,24},{1,5},{5... | collective-permute-start | bytes 393224 | tf_op jit(solution)/shard_map/ppermute | solution.py:297
  25.3 10.7 %collective-permute-start.11 = (bf16[192,512]{1,0:T(8,128)(2,1)S(1)}, bf16[192,512]{1,0:T(8,128)(2,1)S(1)}, u32[]{:S(2)}, u32[]{:S(2)}) collective-permute-start(bf16[192,512]{1,0:T(8,128)(2,1)S(1)} %get-tuple-element.76), channel_id=1, source_target_pairs={{0,1},{1,0},{2,3},{3,2},{4,5},{5,4},{6,7},{7,6},{8,9},{9,8},{10,11... | collective-permute-start | bytes 589832 | tf_op jit(solution)/shard_map/ppermute | solution.py:297
  27.7 15.0 %collective-permute-start.10 = (bf16[160,512]{1,0:T(8,128)(2,1)S(1)}, bf16[160,512]{1,0:T(8,128)(2,1)S(1)}, u32[]{:S(2)}, u32[]{:S(2)}) collective-permute-start(bf16[160,512]{1,0:T(8,128)(2,1)S(1)} %pass_on.2), channel_id=1, source_target_pairs={{0,2},{1,3},{2,0},{3,1},{4,6},{5,7},{6,4},{7,5},{8,10},{9,11},{10,... | collective-permute-start | bytes 491528 | tf_op jit(solution)/shard_map/ppermute | solution.py:297
  36.0 6.7 %collective-permute-start.12 = (bf16[96,512]{1,0:T(8,128)(2,1)S(1)}, bf16[96,512]{1,0:T(8,128)(2,1)S(1)}, u32[]{:S(2)}, u32[]{:S(2)}) collective-permute-start(bf16[96,512]{1,0:T(8,128)(2,1)S(1)} %pass_on.3), channel_id=1, source_target_pairs={{0,2},{1,3},{2,0},{3,1},{4,6},{5,7},{6,4},{7,5},{8,10},{9,11},{10,... | collective-permute-start | bytes 294920 | tf_op jit(solution)/shard_map/ppermute | solution.py:297
  43.8 8.5 %collective-permute-start.13 = (bf16[144,512]{1,0:T(8,128)(2,1)S(1)}, bf16[144,512]{1,0:T(8,128)(2,1)S(1)}, u32[]{:S(2)}, u32[]{:S(2)}) collective-permute-start(bf16[144,512]{1,0:T(8,128)(2,1)S(1)} %get-tuple-element.80.refs_0_), channel_id=1, source_target_pairs={{0,1},{1,0},{2,3},{3,2},{4,5},{5,4},{6,7},{7,6},{8,9},{9,8},{10,11... | collective-permute-start | bytes 442376 | tf_op jit(solution)/shard_map/ppermute | solution.py:297
  44.0 12.6 %collective-permute-start.14 = (bf16[144,512]{1,0:T(8,128)(2,1)S(1)}, bf16[144,512]{1,0:T(8,128)(2,1)S(1)}, u32[]{:S(2)}, u32[]{:S(2)}) collective-permute-start(bf16[144,512]{1,0:T(8,128)(2,1)S(1)} %get-tuple-element.80.refs_0_), channel_id=1, source_target_pairs={{0,2},{1,3},{2,0},{3,1},{4,6},{5,7},{6,4},{7,5},{8,10},{9,11},{10,... | collective-permute-start | bytes 442376 | tf_op jit(solution)/shard_map/ppermute | solution.py:297
  47.7 1.4 %collective-permute-start.16 = (f32[2,32,256]{2,1,0:T(8,128)S(1)}, f32[2,32,256]{2,1,0:T(8,128)S(1)}, u32[]{:S(2)}, u32[]{:S(2)}) collective-permute-start(f32[2,32,256]{2,1,0:T(8,128)S(1)} %get-tuple-element.85), channel_id=1, source_target_pairs={{0,4},{4,0},{8,12},{12,8},{16,20},{20,16},{24,28},{28,24},{1,5},{5... | collective-permute-start | bytes 196616 | tf_op jit(solution)/shard_map/ppermute | solution.py:297
  49.2 4.4 %collective-permute-start.17 = (f32[2,32,256]{2,1,0:T(8,128)S(1)}, f32[2,32,256]{2,1,0:T(8,128)S(1)}, u32[]{:S(2)}, u32[]{:S(2)}) collective-permute-start(f32[2,32,256]{2,1,0:T(8,128)S(1)} %get-tuple-element.88), channel_id=1, source_target_pairs={{0,8},{4,12},{8,0},{12,4},{16,24},{20,28},{24,16},{28,20},{1,9},{5... | collective-permute-start | bytes 196616 | tf_op jit(solution)/shard_map/ppermute | solution.py:297
  49.2 9.5 %collective-permute-start.18 = (bf16[112,512]{1,0:T(8,128)(2,1)S(1)}, bf16[112,512]{1,0:T(8,128)(2,1)S(1)}, u32[]{:S(2)}, u32[]{:S(2)}) collective-permute-start(bf16[112,512]{1,0:T(8,128)(2,1)S(1)} %get-tuple-element.94.refs_4_), channel_id=1, source_target_pairs={{0,2},{1,3},{2,0},{3,1},{4,6},{5,7},{6,4},{7,5},{8,10},{9,11},{10,... | collective-permute-start | bytes 344072 | tf_op jit(solution)/shard_map/ppermute | solution.py:297
  56.6 11.0 %collective-permute-start.22 = (bf16[144,512]{1,0:T(8,128)(2,1)S(1)}, bf16[144,512]{1,0:T(8,128)(2,1)S(1)}, u32[]{:S(2)}, u32[]{:S(2)}) collective-permute-start(bf16[144,512]{1,0:T(8,128)(2,1)S(1)} %collective-permute-done.14.refs_2_), channel_id=1, source_target_pairs={{0,1},{1,0},{2,3},{3,2},{4,5},{5,4},{6,7},{7,6},{8,9},{9,8},{10,11... | collective-permute-start | bytes 442376 | tf_op jit(solution)/shard_map/ppermute | solution.py:297
  56.6 11.0 %collective-permute-start.21 = (bf16[112,512]{1,0:T(8,128)(2,1)S(1)}, bf16[112,512]{1,0:T(8,128)(2,1)S(1)}, u32[]{:S(2)}, u32[]{:S(2)}) collective-permute-start(bf16[112,512]{1,0:T(8,128)(2,1)S(1)} %get-tuple-element.94.refs_4_), channel_id=1, source_target_pairs={{0,1},{1,0},{2,3},{3,2},{4,5},{5,4},{6,7},{7,6},{8,9},{9,8},{10,11... | collective-permute-start | bytes 344072 | tf_op jit(solution)/shard_map/ppermute | solution.py:297
  58.6 3.9 %collective-permute-start.19 = (f32[1,32,256]{2,1,0:T(8,128)S(1)}, f32[1,32,256]{2,1,0:T(8,128)S(1)}, u32[]{:S(2)}, u32[]{:S(2)}) collective-permute-start(f32[1,32,256]{2,1,0:T(8,128)S(1)} %get-tuple-element.89), channel_id=1, source_target_pairs={{0,16},{4,20},{8,24},{12,28},{16,0},{20,4},{24,8},{28,12},{1,17},{... | collective-permute-start | bytes 98312 | tf_op jit(solution)/shard_map/ppermute | solution.py:297
  62.6 4.8 %collective-permute-start.20 = (f32[32,256]{1,0:T(8,128)S(1)}, f32[32,256]{1,0:T(8,128)S(1)}, u32[]{:S(2)}, u32[]{:S(2)}) collective-permute-start(f32[32,256]{1,0:T(8,128)S(1)} %gradient_sum.5.refs_1_), channel_id=1, source_target_pairs={{0,2},{1,3},{2,0},{3,1},{4,6},{5,7},{6,4},{7,5},{8,10},{9,11},{10,... | collective-permute-start | bytes 98312 | tf_op jit(solution)/shard_map/ppermute | solution.py:297
  67.4 5.2 %collective-permute-start.27 = (bf16[144,512]{1,0:T(8,128)(2,1)S(1)}, bf16[144,512]{1,0:T(8,128)(2,1)S(1)}, u32[]{:S(2)}, u32[]{:S(2)}) collective-permute-start(bf16[144,512]{1,0:T(8,128)(2,1)S(1)} %with_chunk.1.refs_0_), channel_id=1, source_target_pairs={{0,1},{1,0},{2,3},{3,2},{4,5},{5,4},{6,7},{7,6},{8,9},{9,8},{10,11... | collective-permute-start | bytes 442376 | tf_op jit(solution)/shard_map/ppermute | solution.py:297
  70.2 1.4 %collective-permute-start.23 = (bf16[16,4096]{1,0:T(8,128)(2,1)S(1)}, bf16[16,4096]{1,0:T(8,128)(2,1)S(1)}, u32[]{:S(2)}, u32[]{:S(2)}) collective-permute-start(bf16[16,4096]{1,0:T(8,128)(2,1)S(1)} %get-tuple-element.97), channel_id=1, source_target_pairs={{0,4},{4,0},{8,12},{12,8},{16,20},{20,16},{24,28},{28,24},{1,5},{5... | collective-permute-start | bytes 393224 | tf_op jit(solution)/shard_map/ppermute | solution.py:297
  70.3 1.5 %collective-permute-start.24 = (bf16[16,4096]{1,0:T(8,128)(2,1)S(1)}, bf16[16,4096]{1,0:T(8,128)(2,1)S(1)}, u32[]{:S(2)}, u32[]{:S(2)}) collective-permute-start(bf16[16,4096]{1,0:T(8,128)(2,1)S(1)} %get-tuple-element.98), channel_id=1, source_target_pairs={{0,4},{4,0},{8,12},{12,8},{16,20},{20,16},{24,28},{28,24},{1,5},{5... | collective-permute-start | bytes 393224 | tf_op jit(solution)/shard_map/ppermute | solution.py:297
  70.8 1.5 %collective-permute-start.26 = (bf16[16,4096]{1,0:T(8,128)(2,1)S(1)}, bf16[16,4096]{1,0:T(8,128)(2,1)S(1)}, u32[]{:S(2)}, u32[]{:S(2)}) collective-permute-start(bf16[16,4096]{1,0:T(8,128)(2,1)S(1)} %get-tuple-element.100), channel_id=1, source_target_pairs={{0,4},{4,0},{8,12},{12,8},{16,20},{20,16},{24,28},{28,24},{1,5},{5... | collective-permute-start | bytes 393224 | tf_op jit(solution)/shard_map/ppermute | solution.py:297
  72.5 6.5 %collective-permute-start.29 = (bf16[32,4224]{1,0:T(8,128)(2,1)S(1)}, bf16[32,4224]{1,0:T(8,128)(2,1)S(1)}, u32[]{:S(2)}, u32[]{:S(2)}) collective-permute-start(bf16[32,4224]{1,0:T(8,128)(2,1)S(1)} %get-tuple-element.102), channel_id=1, source_target_pairs={{0,8},{4,20},{8,0},{12,28},{16,24},{20,4},{24,16},{28,12},{1,9},{5... | collective-permute-start | bytes 811016 | tf_op jit(solution)/shard_map/ppermute | solution.py:496
  75.1 2.8 %collective-permute-start.30 = (bf16[32,4096]{1,0:T(8,128)(2,1)S(1)}, bf16[32,4096]{1,0:T(8,128)(2,1)S(1)}, u32[]{:S(2)}, u32[]{:S(2)}) collective-permute-start(bf16[32,4096]{1,0:T(8,128)(2,1)S(1)} %get-tuple-element.106), channel_id=1, source_target_pairs={{0,4},{4,0},{8,12},{12,8},{16,20},{20,16},{24,28},{28,24},{1,5},{5... | collective-permute-start | bytes 786440 | tf_op jit(solution)/shard_map/ppermute | solution.py:297
  76.4 1.6 %collective-permute-start.31 = (bf16[32,4096]{1,0:T(8,128)(2,1)S(1)}, bf16[32,4096]{1,0:T(8,128)(2,1)S(1)}, u32[]{:S(2)}, u32[]{:S(2)}) collective-permute-start(bf16[32,4096]{1,0:T(8,128)(2,1)S(1)} %get-tuple-element.107), channel_id=1, source_target_pairs={{0,4},{4,0},{8,12},{12,8},{16,20},{20,16},{24,28},{28,24},{1,5},{5... | collective-permute-start | bytes 786440 | tf_op jit(solution)/shard_map/ppermute | solution.py:297
  76.4 1.5 %collective-permute-start.28 = (f32[32,256]{1,0:T(8,128)S(1)}, f32[32,256]{1,0:T(8,128)S(1)}, u32[]{:S(2)}, u32[]{:S(2)}) collective-permute-start(f32[32,256]{1,0:T(8,128)S(1)} %chunk_sum.1.chunk), channel_id=1, source_target_pairs={{0,4},{4,0},{8,12},{12,8},{16,20},{20,16},{24,28},{28,24},{1,5},{5... | collective-permute-start | bytes 98312 | tf_op jit(solution)/shard_map/ppermute | solution.py:297
  79.4 9.8 %collective-permute-start.32 = (bf16[32,4608]{1,0:T(8,128)(2,1)S(1)}, bf16[32,4608]{1,0:T(8,128)(2,1)S(1)}, u32[]{:S(2)}, u32[]{:S(2)}) collective-permute-start(bf16[32,4608]{1,0:T(8,128)(2,1)S(1)} %get-tuple-element.108), channel_id=1, source_target_pairs={{0,8},{4,12},{8,0},{12,4},{16,24},{20,28},{24,16},{28,20},{1,9},{5... | collective-permute-start | bytes 884744 | tf_op jit(solution)/shard_map/ppermute | solution.py:297
  79.5 9.7 %collective-permute-start.33 = (bf16[32,4608]{1,0:T(8,128)(2,1)S(1)}, bf16[32,4608]{1,0:T(8,128)(2,1)S(1)}, u32[]{:S(2)}, u32[]{:S(2)}) collective-permute-start(bf16[32,4608]{1,0:T(8,128)(2,1)S(1)} %get-tuple-element.109), channel_id=1, source_target_pairs={{0,16},{4,20},{8,24},{12,28},{16,0},{20,4},{24,8},{28,12},{1,17},{... | collective-permute-start | bytes 884744 | tf_op jit(solution)/shard_map/ppermute | solution.py:297
  81.0 8.1 %collective-permute-start.34 = (bf16[32,512]{1,0:T(8,128)(2,1)S(1)}, bf16[32,512]{1,0:T(8,128)(2,1)S(1)}, u32[]{:S(2)}, u32[]{:S(2)}) collective-permute-start(bf16[32,512]{1,0:T(8,128)(2,1)S(1)} %get-tuple-element.110.refs_3_), channel_id=1, source_target_pairs={{0,24},{4,28},{8,16},{12,20},{16,8},{20,12},{24,0},{28,4},{1,25},{... | collective-permute-start | bytes 98312 | tf_op jit(solution)/shard_map/ppermute | solution.py:297
  (6 other events, 67.6 us)

commit v5 on v3

--- a/solution.py
+++ b/solution.py
@@ -46,32 +46,73 @@
     return math.gcd(slots, 8)
 
 
-def product_loop(count, source_ids, target_ids, adj, source, total, dims):
-    turn = turn_of(adj.shape[0])
+def list_size(slots, groups):
+    return (slots + groups) // 2 + 8
+
+
+def pair_up(count, ids, groups, pending, lists, base):
+    size = list_size(ids.shape[0], groups)
+    for group in range(groups):
+        pending[group] = -1
+
+    def visit(slot, entries):
+        group = ids[slot]
+        partner = pending[group]
+        found = partner >= 0
+        lists[base + entries] = partner
+        lists[base + size + entries] = slot
+        pending[group] = jnp.where(found, -1, slot)
+        return entries + jnp.where(found, 1, 0)
+
+    def leave(group, entries):
+        slot = pending[group]
+        lists[base + entries] = slot
+        lists[base + size + entries] = slot
+        return entries + jnp.where(slot >= 0, 1, 0)
+
+    pairs = lax.fori_loop(0, count, visit, 0)
+    lists[base + 2 * size] = lax.fori_loop(0, groups, leave, pairs)
+    lists[base + 2 * size + 1] = pairs
+
+
+def lists_size(slots, groups):
+    return sum(2 * list_size(slots, n) + 2 for n in groups)
+
+
+def product_loop(lists, base, groups, source_ids, target_ids, adj, source, total, dims, axis):
+    size = list_size(adj.shape[0], groups)
+    width = adj.shape[1]
     spare = total.shape[0] - 1
+    turn = 4
+    entries = lists[base + 2 * size]
+    pairs = lists[base + 2 * size + 1]
     total[...] = jnp.zeros_like(total)
 
     def step(index, carry):
-        first = index * turn
         for k in range(turn):
-            slot = first + k
+            n = index * turn + k
+            first = jnp.where(n < entries, lists[base + n], 0)
+            second = jnp.where(n < pairs, lists[base + size + n], first)
+            blocks = jnp.concatenate([adj[first], adj[second]], axis=axis)
             product = lax.dot_general(
-                source[source_ids[slot]], adj[slot], dims, preferred_element_type=jnp.float32
+                source[source_ids[first]], blocks, dims, preferred_element_type=jnp.float32
             )
-            target = jnp.where(slot < count, target_ids[slot], spare)
-            total[target] += product
+            total[jnp.where(n < entries, target_ids[first], spare)] += product[:, :width]
+            total[jnp.where(n < pairs, target_ids[second], spare)] += product[:, width:]
         return carry
 
-    lax.fori_loop(0, (count + turn - 1) // turn, step, 0)
-
-
-def fetch_kernel(count, rows, cols, features, tile, *refs):
-    outs, (sem, small_sem) = refs[:5], refs[5:]
+    lax.fori_loop(0, (entries + turn - 1) // turn, step, 0)
+
+
+def fetch_kernel(groups, count, rows, cols, features, tile, *refs):
+    outs, lists = refs[:5], refs[5]
+    row_ids, col_ids, pending, sem, small_sem = refs[6:]
     half = features.shape[0] // 2
-    sources = (rows, cols, features.at[pl.ds(0, half)], features.at[pl.ds(half, half)])
+    sources = (rows, cols, rows, cols, features.at[pl.ds(0, half)], features.at[pl.ds(half, half)])
+    targets = (row_ids, col_ids, *outs[:4])
     small = [
         pltpu.make_async_copy(source, target, small_sem.at[n])
-        for n, (source, target) in enumerate(zip(sources, outs))
+        for n, (source, target) in enumerate(zip(sources, targets))
     ]
     for copy in small:
         copy.start()
@@ -91,23 +132,53 @@
 
     turns = (count[0, 0] + turn - 1) // turn
     lax.fori_loop(0, turns, begin, 0)
+    for copy in small[:2]:
+        copy.wait()
+    list_pairs(groups, count[0, 0], row_ids, col_ids, pending, lists)
     lax.fori_loop(0, turns, wait, 0)
-    for copy in small:
+    for copy in small[2:]:
         copy.wait()
 
 
-def fetch(count, rows, cols, features, tile):
+def list_pairs(groups, count, rows, cols, pending, lists):
+    pair_up(count, cols, groups[0], pending, lists, 0)
+    pair_up(count, rows, groups[1], pending, lists, 2 * list_size(rows.shape[0], groups[0]) + 2)
+
+
+def pairs_kernel(groups, count, rows, cols, lists, pending):
+    list_pairs(groups, count[0, 0], rows, cols, pending, lists)
+
+
+def pair_lists(groups, count, rows, cols):
+    return pl.pallas_call(
+        functools.partial(pairs_kernel, groups),
+        out_shape=jax.ShapeDtypeStruct((lists_size(rows.shape[0], groups),), jnp.int32),
+        in_specs=[SMEM] * 3,
+        out_specs=SMEM,
+        scratch_shapes=[pltpu.SMEM((max(groups),), jnp.int32)],
+        compiler_params=params(4),
+        cost_estimate=COST,
+        name="pair_lists",
+    )(count, rows, cols)
+
+
+def fetch(groups, count, rows, cols, features, tile):
     arrays = (rows, cols, features, tile)
     half = jax.ShapeDtypeStruct((features.shape[0] // 2, features.shape[1]), features.dtype)
     outs = [jax.ShapeDtypeStruct(array.shape, array.dtype) for array in (rows, cols)] + [half] * 2
-    return pl.pallas_call(
-        fetch_kernel,
-        out_shape=outs + [jax.ShapeDtypeStruct(tile.shape, tile.dtype)],
+    outs.append(jax.ShapeDtypeStruct(tile.shape, tile.dtype))
+    outs.append(jax.ShapeDtypeStruct((lists_size(rows.shape[0], groups),), jnp.int32))
+    return pl.pallas_call(
+        functools.partial(fetch_kernel, groups),
+        out_shape=outs,
         in_specs=[SMEM] + [HBM] * 4,
-        out_specs=[VMEM] * 5,
+        out_specs=[VMEM] * 5 + [SMEM],
         scratch_shapes=[
+            pltpu.SMEM(rows.shape, rows.dtype),
+            pltpu.SMEM(cols.shape, cols.dtype),
+            pltpu.SMEM((max(groups),), jnp.int32),
             pltpu.SemaphoreType.DMA((tile.shape[0] // turn_of(tile.shape[0]),)),
-            pltpu.SemaphoreType.DMA((4,)),
+            pltpu.SemaphoreType.DMA((6,)),
         ],
         compiler_params=params(4),
         cost_estimate=COST,
@@ -115,7 +186,7 @@
     )(count, *[pltpu.with_memory_space_constraint(array, pltpu.HBM) for array in arrays])
 
 
-def forward_kernel(n_parts, depths, layout, place, count, rows, cols, adj, *refs):
+def forward_kernel(n_parts, depths, layout, place, lists, rows, cols, adj, *refs):
     parts, refs = refs[:n_parts], refs[n_parts:]
     source, total = refs[-2:]
     outs = refs[-2 - len(depths) * len(layout) : -2]
@@ -127,7 +198,7 @@
         for c in range(source.shape[0]):
             source[c, row : row + depth, :] = part[:, c * size : (c + 1) * size]
         row += depth
-    product_loop(count[0, 0], cols, rows, adj, source, total, NT)
+    product_loop(lists, 0, source.shape[0], cols, rows, adj, source, total, NT, 0)
     blocks = outs[0].shape[1] // size
     ahead = carried[0].shape[0] // len(layout[0]) if carried else 0
     outs = iter(outs)
@@ -147,7 +218,7 @@
         row += depth
 
 
-def forward(place, count, rows, cols, adj, parts, row_blocks, depths, layout, carried=()):
+def forward(place, lists, rows, cols, adj, parts, row_blocks, depths, layout, carried=()):
     size = adj.shape[1]
     col_blocks = parts[0].shape[1] // size
     wide = row_blocks * size // sum(len(chunks) for chunks in layout)
@@ -169,10 +240,10 @@
         compiler_params=params(14),
         cost_estimate=COST,
         name="forward_products",
-    )(place, count, rows, cols, adj, *parts, *carried)
-
-
-def backward_kernel(spots, depths, place, count, rows, cols, adj, *refs):
+    )(place, lists, rows, cols, adj, *parts, *carried)
+
+
+def backward_kernel(spots, depths, place, lists, rows, cols, adj, *refs):
     n_parts = 1 + max(part for places in spots for part, _ in places)
     parts = refs[:n_parts]
     outs = refs[n_parts:-2]
@@ -188,7 +259,8 @@
                     offset : offset + depth, i * size : (i + 1) * size
                 ]
             row += depth
-    product_loop(count[0, 0], rows, cols, adj, source, total, NN)
+    base = 2 * list_size(adj.shape[0], total.shape[0] - 1) + 2
+    product_loop(lists, base, source.shape[0], rows, cols, adj, source, total, NN, 1)
     row = 0
     for out in outs:
         depth = out.shape[0]
@@ -197,7 +269,7 @@
         row += depth
 
 
-def backward(place, count, rows, cols, adj, parts, spots, depths, out_depths, col_blocks):
+def backward(place, lists, rows, cols, adj, parts, spots, depths, out_depths, col_blocks):
     size = adj.shape[1]
     row_blocks = len(spots) * parts[0].shape[1] // size
     return pl.pallas_call(
@@ -212,7 +284,7 @@
         compiler_params=params(14),
         cost_estimate=COST,
         name="backward_products",
-    )(place, count, rows, cols, adj, *parts)
+    )(place, lists, rows, cols, adj, *parts)
 
 
 def middle_kernel(sizes, order, n_sum, n_row, row, weight, cotangent, *refs):
@@ -422,7 +494,7 @@
     far = [k for k in range(2, n_row, 2) if k & (k - 1) != 0]
     sibling = swap(own, "row", 1)
     from_near = [swap(own, "row", k) for k in near]
-    rows, cols, *halves, tile = fetch(count, rows, cols, own, adj)
+    rows, cols, *halves, tile, lists = fetch((col_blocks, row_blocks), count, rows, cols, own, adj)
     from_near = [after(part, tile) for part in from_near]
     from_far = [swap(half, "row", k) for k in far for half in halves]
 
@@ -439,7 +511,7 @@
     cut = n_near * 5 // 6
     parts = [own, sibling] + [piece for part in from_near for piece in (part, swap(part, "row", 1))]
     kept, beyond, sent, *carried = forward(
-        col, count, rows, cols, tile, parts, row_blocks, [cut, n_near - cut], layout
+        col, lists, rows, cols, tile, parts, row_blocks, [cut, n_near - cut], layout
     )
     received = swap(sent, "col", 1)
     from_far = [after(part, kept) for part in from_far]
@@ -448,7 +520,7 @@
         halves = from_far[n : n + 2]
         parts += halves + [swap(half, "row", 1) for half in halves]
     far_piece = forward(
-        col, count, rows, cols, tile, parts, row_blocks, [2 * depth * len(far)], layout, carried
+        col, lists, rows, cols, tile, parts, row_blocks, [2 * depth * len(far)], layout, carried
     )
     far_received = swap(far_piece[2], "col", 1)
     first = fold(kept, beyond, after(received, far_piece[0]))
@@ -488,7 +560,7 @@
             spots += [[(part, cuts[0]), (part + 2, 0)] for part in (2, 3)]
         out_depths = [cuts[n] // 2] + [cuts[n] // (8 - 4 * n)] * (4 - 2 * n)
         mine, *sent = backward(
-            col, count, rows, cols, tile, parts, spots, depths, out_depths, col_blocks
+            col, lists, rows, cols, tile, parts, spots, depths, out_depths, col_blocks
         )
         return [mine] + [swap(part, "row", 1) for part in sent]
 
@@ -516,12 +588,13 @@
     row_blocks = cotangent.shape[0] * n_col // size
     col_blocks = features.shape[0] // size
     zero = jnp.zeros((1,), jnp.int32)
+    lists = pair_lists((col_blocks, row_blocks), count, rows, cols)
     panels = lax.all_gather(features.T, "row", axis=0, tiled=True)
-    (terms,) = forward(zero, count, rows, cols, adj, [panels], row_blocks, [panels.shape[0]], [(0,)])
+    (terms,) = forward(zero, lists, rows, cols, adj, [panels], row_blocks, [panels.shape[0]], [(0,)])
     part = lax.psum_scatter(terms, "col", scatter_dimension=1, tiled=True)
     output, deltas, aggregated, back = middle(1, zero, weight, cotangent, [[part]], (0,), [weight.shape[0]])
     slab = lax.all_gather(back, "col", axis=1, tiled=True)
-    (column_terms,) = backward(zero, count, rows, cols, adj, [slab], [[(0, 0)]], [slab.shape[0]], [slab.shape[0]], col_blocks)
+    (column_terms,) = backward(zero, lists, rows, cols, adj, [slab], [[(0, 0)]], [slab.shape[0]], [slab.shape[0]], col_blocks)
     grad_features = lax.psum_scatter(column_terms, "row", scatter_dimension=0, tiled=True).T
     (part,) = gradient(1.0 / math.sqrt(nodes), [(0,)], aggregated, deltas)
     grad_weight = lax.psum(part[0], ("row", "col"))

time: 88.8 us -> 90.2 us (1.016)
  Pallas kernels: 12.3 us -> 24 us
  starting transfers between devices: 40.7 us -> 30.2 us
    ppermute x33, starting transfers between devices: 39.8 us -> 30.1 us  [swap(): return lax.ppermute(value, axis, [(i, i ^ k) for i in range(size)])]
    pallas_call x2, Pallas kernels: 4.16 us -> 8.58 us  [forward(): pl.pallas_call(functools.partial(forward_kernel, len(parts), depths, layo...]
    pallas_call x2, Pallas kernels: 3.66 us -> 8.05 us  [backward(): pl.pallas_call(functools.partial(backward_kernel, spots, depths), out_sha...]
    pallas_call x1, Pallas kernels: 1.5 us -> 4.42 us  [fetch(): pl.pallas_call(functools.partial(fetch_kernel, groups), out_shape=outs, i...]
    ppermute x1, starting transfers between devices: 0.98 us -> 0.07 us  [shards_exchanged(): lax.ppermute(far_sum, 'row', [(i, i ^ (4 if i % 2 else 2)) for i in range...]
  transfers between devices with their start and end apart: 34 -> 34, of which waited for: 20 -> 20; matrix products, arithmetic and copies ran while one was open for 0% -> 0% of each run, Pallas kernels for 11% -> 24%
where the time goes in v5:
time: 90.2 us; the launch traced here: 90.3 us
  waiting for transfers between devices  34.6 us (38%)
  starting transfers between devices  30.2 us (33%)
  Pallas kernels  24 us (27%)
  between operations  1.49 us (2%)
    ppermute x33, waiting for transfers between devices, swap(): return lax.ppermute(value, axis, [(i, i ^ k) for i in range(size)])  34.3 us
    ppermute x33, starting transfers between devices, swap(): return lax.ppermute(value, axis, [(i, i ^ k) for i in range(size)])  30.1 us
    pallas_call x2, Pallas kernels, forward(): pl.pallas_call(functools.partial(forward_kernel, len(parts), depths, layo...  8.58 us
    pallas_call x2, Pallas kernels, backward(): pl.pallas_call(functools.partial(backward_kernel, spots, depths), out_sha...  8.05 us
    pallas_call x1, Pallas kernels, fetch(): pl.pallas_call(functools.partial(fetch_kernel, groups), out_shape=outs, i...  4.42 us
  transfers between devices with their start and end apart: 34, of which 20 were waited for; matrix products, arithmetic and copies ran while one was open for 0% of the time, Pallas kernels for 24%

profile of v5, /device:TPU:0, one launch (start us, length us, event | category | flops | bytes accessed | tf_op | source)
XLA Modules:
  0.0 90.3 jit_solution(9414295888349746158)
XLA Ops:
  0.6 3.0 %collective-permute-start.1 = (bf16[32,4096]{1,0:T(8,128)(2,1)}, bf16[32,4096]{1,0:T(8,128)(2,1)S(1)}, u32[]{:S(2)}, u32[]{:S(2)}) collective-permute-start(bf16[32,4096]{1,0:T(8,128)(2,1)} %bitcast.7), channel_id=1, source_target_pairs={{0,8},{4,12},{8,0},{12,4},{16,24},{20,28},{24,16},{28,20},{1,9},{5... | collective-permute-start | bytes 786440 | tf_op jit(solution)/shard_map/ppermute | solution.py:369
  3.7 1.5 %collective-permute-start.3 = (bf16[32,4096]{1,0:T(8,128)(2,1)}, bf16[32,4096]{1,0:T(8,128)(2,1)S(1)}, u32[]{:S(2)}, u32[]{:S(2)}) collective-permute-start(bf16[32,4096]{1,0:T(8,128)(2,1)} %bitcast.8), channel_id=1, source_target_pairs={{0,16},{4,20},{8,24},{12,28},{16,0},{20,4},{24,8},{28,12},{1,17},{... | collective-permute-start | bytes 786440 | tf_op jit(solution)/shard_map/ppermute | solution.py:369
  5.8 4.4 %fetch.1 = (s32[96]{0:T(128)S(1)}, s32[96]{0:T(128)S(1)}, bf16[16,4096]{1,0:T(8,128)(2,1)S(1)}, bf16[16,4096]{1,0:T(8,128)(2,1)S(1)}, bf16[96,128,128]{2,1,0:T(8,128)(2,1)S(1)}, /*index=5*/s32[276]{0:T(512)S(1)}) custom-call(s32[1,1]{1,0:T(1,128)S(6)} %copy.10.count, s32[96]{0:T(128)} %bitcast.13, s32[96]{0:T(128)} %bitcast.14, bf16[32,4096]{1,0:T(8,128)(2,1)} %bitcast.10, ...), custom_call_target="tpu_custom_call" | custom-call | flops 1 | bytes 1 | tf_op jit(solution)/shard_map/fetch/pallas_call | solution.py:171
  10.8 0.8 collective-permute-done.3.refs_4_
  11.6 1.7 %collective-permute-start.7 = (bf16[16,4096]{1,0:T(8,128)(2,1)S(1)}, bf16[16,4096]{1,0:T(8,128)(2,1)S(1)}, u32[]{:S(2)}, u32[]{:S(2)}) collective-permute-start(bf16[16,4096]{1,0:T(8,128)(2,1)S(1)} %get-tuple-element.69), channel_id=1, source_target_pairs={{0,24},{4,28},{8,16},{12,20},{16,8},{20,12},{24,0},{28,4},{1,25},{... | collective-permute-start | bytes 393224 | tf_op jit(solution)/shard_map/ppermute | solution.py:369
  13.4 1.2 %collective-permute-start.6 = (bf16[16,4096]{1,0:T(8,128)(2,1)S(1)}, bf16[16,4096]{1,0:T(8,128)(2,1)S(1)}, u32[]{:S(2)}, u32[]{:S(2)}) collective-permute-start(bf16[16,4096]{1,0:T(8,128)(2,1)S(1)} %get-tuple-element.67), channel_id=1, source_target_pairs={{0,24},{4,28},{8,16},{12,20},{16,8},{20,12},{24,0},{28,4},{1,25},{... | collective-permute-start | bytes 393224 | tf_op jit(solution)/shard_map/ppermute | solution.py:369
  14.6 4.9 %forward_products.2 = (bf16[160,512]{1,0:T(8,128)(2,1)S(1)}, bf16[160,512]{1,0:T(8,128)(2,1)S(1)}, bf16[320,512]{1,0:T(8,128)(2,1)S(1)}, bf16[32,512]{1,0:T(8,12...) custom-call(s32[1]{0:T(128)} %bitcast.1.place, s32[276]{0:T(512)S(1)} %get-tuple-element.59.lists, ...), custom_call_target="tpu_custom_call" | custom-call | flops 1 | bytes 1 | tf_op jit(solution)/shard_map/forward_products/pallas_call | solution.py:231
  19.5 1.3 %collective-permute-start.5 = (bf16[320,512]{1,0:T(8,128)(2,1)S(1)}, bf16[320,512]{1,0:T(8,128)(2,1)S(1)}, u32[]{:S(2)}, u32[]{:S(2)}) collective-permute-start(bf16[320,512]{1,0:T(8,128)(2,1)S(1)} %get-tuple-element.66), channel_id=1, source_target_pairs={{0,1},{1,0},{2,3},{3,2},{4,5},{5,4},{6,7},{7,6},{8,9},{9,8},{10,11... | collective-permute-start | bytes 983048 | tf_op jit(solution)/shard_map/ppermute | solution.py:369
  21.4 0.8 collective-permute-done.9.refs_3_
  22.6 3.7 %forward_products.3 = (bf16[96,512]{1,0:T(8,128)(2,1)S(1)}, bf16[96,512]{1,0:T(8,128)(2,1)S(1)}, bf16[192,512]{1,0:T(8,128)(2,1)S(1)}) custom-call(s32[1]{0:T(128)} %bitcast.1.place, s32[276]{0:T(512)S(1)} %get-tuple-element.59.lists, s32[96]{0:T(128)S(1)} %get-tuple-element.60.rows, s32[96]{0:T(128)S(1)} %get-tuple-element.61.cols, ...), custom_call_target="tpu_custom_call" | custom-call | flops 1 | bytes 1 | tf_op jit(solution)/shard_map/forward_products/pallas_call | solution.py:231
  26.3 1.4 %collective-permute-start.11 = (bf16[192,512]{1,0:T(8,128)(2,1)S(1)}, bf16[192,512]{1,0:T(8,128)(2,1)S(1)}, u32[]{:S(2)}, u32[]{:S(2)}) collective-permute-start(bf16[192,512]{1,0:T(8,128)(2,1)S(1)} %get-tuple-element.77), channel_id=1, source_target_pairs={{0,1},{1,0},{2,3},{3,2},{4,5},{5,4},{6,7},{7,6},{8,9},{9,8},{10,11... | collective-permute-start | bytes 589832 | tf_op jit(solution)/shard_map/ppermute | solution.py:369
  27.7 1.7 %collective-permute-done.5.refs_1_ = bf16[320,512]{1,0:T(8,128)(2,1)S(1)} collective-permute-done((bf16[320,512]{1,0:T(8,128)(2,1)S(1)}, bf16[320,512]{1,0:T(8,128)(2,1)S(1)}, u32[]{:S(2)}, u32[]{:S(2)}) %collective-permute-start.5) | collective-permute-done | bytes 327712 | tf_op jit(solution)/shard_map/ppermute | solution.py:369
  29.5 2.3 %collective-permute-start.10 = (bf16[160,512]{1,0:T(8,128)(2,1)S(1)}, bf16[160,512]{1,0:T(8,128)(2,1)S(1)}, u32[]{:S(2)}, u32[]{:S(2)}) collective-permute-start(bf16[160,512]{1,0:T(8,128)(2,1)S(1)} %pass_on.2), channel_id=1, source_target_pairs={{0,2},{1,3},{2,0},{3,1},{4,6},{5,7},{6,4},{7,5},{8,10},{9,11},{10,... | collective-permute-start | bytes 491528 | tf_op jit(solution)/shard_map/ppermute | solution.py:369
  31.8 5.3 %collective-permute-done.11.refs_1_.refs_4_ = bf16[192,512]{1,0:T(8,128)(2,1)S(1)} collective-permute-done((bf16[192,512]{1,0:T(8,128)(2,1)S(1)}, bf16[192,512]{1,0:T(8,128)(2,1)S(1)}, u32[]{:S(2)}, u32[]{:S(2)}) %collective-permute-start.11) | collective-permute-done | bytes 196640 | tf_op jit(solution)/shard_map/ppermute | solution.py:369
  37.4 6.3 %collective-permute-done.12.refs_5_ = bf16[96,512]{1,0:T(8,128)(2,1)S(1)} collective-permute-done((bf16[96,512]{1,0:T(8,128)(2,1)S(1)}, bf16[96,512]{1,0:T(8,128)(2,1)S(1)}, u32[]{:S(2)}, u32[]{:S(2)}) %collective-permute-start.12) | collective-permute-done | bytes 98336 | tf_op jit(solution)/shard_map/ppermute | solution.py:369
  43.8 1.1 %layer.1 = (bf16[512,256]{1,0:T(8,128)(2,1)}, bf16[512,256]{1,0:T(8,128)(2,1)S(1)}, bf16[256,512]{1,0:T(8,128)(2,1)S(1)}, bf16[256,512]{1,0:T(8,128)(2,1)S(1)}, ...) custom-call(s32[1]{0:T(128)} %bitcast.row, bf16[256,256]{1,0:T(8,128)(2,1)S(1)} %copy-done.2, ...), custom_call_target="tpu_custom_call" | custom-call | flops 1 | bytes 1 | tf_op jit(solution)/shard_map/layer/pallas_call | solution.py:333
  45.7 3.2 %collective-permute-start.13 = (bf16[256,512]{1,0:T(8,128)(2,1)S(1)}, bf16[256,512]{1,0:T(8,128)(2,1)S(1)}, u32[]{:S(2)}, u32[]{:S(2)}) collective-permute-start(bf16[256,512]{1,0:T(8,128)(2,1)S(1)} %get-tuple-element.81.refs_0_), channel_id=1, source_target_pairs={{0,1},{1,0},{2,3},{3,2},{4,5},{5,4},{6,7},{7,6},{8,9},{9,8},{10,11... | collective-permute-start | bytes 786440 | tf_op jit(solution)/shard_map/ppermute | solution.py:369
  49.0 0.7 collective-permute-start.18
  49.7 3.5 %collective-permute-done.17.refs_1_ = f32[2,32,256]{2,1,0:T(8,128)S(1)} collective-permute-done((f32[2,32,256]{2,1,0:T(8,128)S(1)}, f32[2,32,256]{2,1,0:T(8,128)S(1)}, u32[]{:S(2)}, u32[]{:S(2)}) %collective-permute-start.17) | collective-permute-done | bytes 65568 | tf_op jit(solution)/shard_map/ppermute | solution.py:369
  53.2 1.0 %collective-permute-done.14.refs_2_ = bf16[144,512]{1,0:T(8,128)(2,1)S(1)} collective-permute-done((bf16[144,512]{1,0:T(8,128)(2,1)S(1)}, bf16[144,512]{1,0:T(8,128)(2,1)S(1)}, u32[]{:S(2)}, u32[]{:S(2)}) %collective-permute-start.14) | collective-permute-done | bytes 147488 | tf_op jit(solution)/shard_map/ppermute | solution.py:369
  54.3 1.4 %collective-permute-start.19 = (f32[1,32,256]{2,1,0:T(8,128)S(1)}, f32[1,32,256]{2,1,0:T(8,128)S(1)}, u32[]{:S(2)}, u32[]{:S(2)}) collective-permute-start(f32[1,32,256]{2,1,0:T(8,128)S(1)} %get-tuple-element.90), channel_id=1, source_target_pairs={{0,16},{4,20},{8,24},{12,28},{16,0},{20,4},{24,8},{28,12},{1,17},{... | collective-permute-start | bytes 98312 | tf_op jit(solution)/shard_map/ppermute | solution.py:369
  55.7 2.3 %collective-permute-done.18.refs_0_.refs_4_ = bf16[112,512]{1,0:T(8,128)(2,1)S(1)} collective-permute-done((bf16[112,512]{1,0:T(8,128)(2,1)S(1)}, bf16[112,512]{1,0:T(8,128)(2,1)S(1)}, u32[]{:S(2)}, u32[]{:S(2)}) %collective-permute-start.18) | collective-permute-done | bytes 114720 | tf_op jit(solution)/shard_map/ppermute | solution.py:369
  58.2 3.2 %collective-permute-start.20 = (f32[32,256]{1,0:T(8,128)S(1)}, f32[32,256]{1,0:T(8,128)S(1)}, u32[]{:S(2)}, u32[]{:S(2)}) collective-permute-start(f32[32,256]{1,0:T(8,128)S(1)} %gradient_sum.5.refs_1_), channel_id=1, source_target_pairs={{0,2},{1,3},{2,0},{3,1},{4,6},{5,7},{6,4},{7,5},{8,10},{9,11},{10,... | collective-permute-start | bytes 98312 | tf_op jit(solution)/shard_map/ppermute | solution.py:369
  61.5 2.0 %collective-permute-done.20.refs_2_ = f32[32,256]{1,0:T(8,128)S(1)} collective-permute-done((f32[32,256]{1,0:T(8,128)S(1)}, f32[32,256]{1,0:T(8,128)S(1)}, u32[]{:S(2)}, u32[]{:S(2)}) %collective-permute-start.20) | collective-permute-done | bytes 32800 | tf_op jit(solution)/shard_map/ppermute | solution.py:369
  63.5 1.7 %collective-permute-start.26 = (bf16[144,512]{1,0:T(8,128)(2,1)S(1)}, bf16[144,512]{1,0:T(8,128)(2,1)S(1)}, u32[]{:S(2)}, u32[]{:S(2)}) collective-permute-start(bf16[144,512]{1,0:T(8,128)(2,1)S(1)} %with_chunk.1.refs_0_), channel_id=1, source_target_pairs={{0,1},{1,0},{2,3},{3,2},{4,5},{5,4},{6,7},{7,6},{8,9},{9,8},{10,11... | collective-permute-start | bytes 442376 | tf_op jit(solution)/shard_map/ppermute | solution.py:369
  65.4 4.0 %backward_products.2 = (bf16[64,4096]{1,0:T(8,128)(2,1)S(1)}, bf16[16,4096]{1,0:T(8,128)(2,1)S(1)}, bf16[16,4096]{1,0:T(8,128)(2,1)S(1)}, bf16[16,4096]{1,0:T(8,128)(2,1)S(1)}, bf16[16,4096]{1,0:T(8,128)(2,1)S(1)}) custom-call(s32[1]{0:T(128)} %bitcast.1.place, s32[276]{0:T(512)S(1)} %get-tuple-element.59.lists, s32[96]{0:T(128)S(1)} %get-tuple-element.60.rows, ...), custom_call_target="tpu_custom_call" | custom-call | flops 1 | bytes 1 | tf_op jit(solution)/shard_map/backward_products/pallas_call | solution.py:275
  71.7 4.0 %backward_products.3 = (bf16[64,4096]{1,0:T(8,128)(2,1)S(1)}, bf16[32,4096]{1,0:T(8,128)(2,1)S(1)}, bf16[32,4096]{1,0:T(8,128)(2,1)S(1)}) custom-call(s32[1]{0:T(128)} %bitcast.1.place, s32[276]{0:T(512)S(1)} %get-tuple-element.59.lists, s32[96]{0:T(128)S(1)} %get-tuple-element.60.rows, s32[96]{0:T(128)S(1)} %get-tuple-element.61.cols, ...), custom_call_target="tpu_custom_call" | custom-call | flops 1 | bytes 1 | tf_op jit(solution)/shard_map/backward_products/pallas_call | solution.py:275
  76.8 1.1 %collective-permute-done.27.sibling = f32[32,256]{1,0:T(8,128)S(1)} collective-permute-done((f32[32,256]{1,0:T(8,128)S(1)}, f32[32,256]{1,0:T(8,128)S(1)}, u32[]{:S(2)}, u32[]{:S(2)}) %collective-permute-start.27) | collective-permute-done | bytes 32800 | tf_op jit(solution)/shard_map/ppermute | solution.py:369
  78.9 1.2 %collective-permute-start.32 = (bf16[32,4608]{1,0:T(8,128)(2,1)S(1)}, bf16[32,4608]{1,0:T(8,128)(2,1)S(1)}, u32[]{:S(2)}, u32[]{:S(2)}) collective-permute-start(bf16[32,4608]{1,0:T(8,128)(2,1)S(1)} %get-tuple-element.109), channel_id=1, source_target_pairs={{0,16},{4,20},{8,24},{12,28},{16,0},{20,4},{24,8},{28,12},{1,17},{... | collective-permute-start | bytes 884744 | tf_op jit(solution)/shard_map/ppermute | solution.py:369
  80.1 2.1 %collective-permute-start.33 = (bf16[32,512]{1,0:T(8,128)(2,1)S(1)}, bf16[32,512]{1,0:T(8,128)(2,1)S(1)}, u32[]{:S(2)}, u32[]{:S(2)}) collective-permute-start(bf16[32,512]{1,0:T(8,128)(2,1)S(1)} %get-tuple-element.110.refs_3_), channel_id=1, source_target_pairs={{0,24},{4,28},{8,16},{12,20},{16,8},{20,12},{24,0},{28,4},{1,25},{... | collective-permute-start | bytes 98312 | tf_op jit(solution)/shard_map/ppermute | solution.py:369
  82.2 7.3 %collective-permute-done.33.refs_4_ = bf16[32,512]{1,0:T(8,128)(2,1)S(1)} collective-permute-done((bf16[32,512]{1,0:T(8,128)(2,1)S(1)}, bf16[32,512]{1,0:T(8,128)(2,1)S(1)}, u32[]{:S(2)}, u32[]{:S(2)}) %collective-permute-start.33) | collective-permute-done | bytes 32800 | tf_op jit(solution)/shard_map/ppermute | solution.py:369
  89.4 0.9 finish.1
  (59 shorter events, 7.6 us)
Async XLA Ops:
  0.6 9.6 %collective-permute-start.1 = (bf16[32,4096]{1,0:T(8,128)(2,1)}, bf16[32,4096]{1,0:T(8,128)(2,1)S(1)}, u32[]{:S(2)}, u32[]{:S(2)}) collective-permute-start(bf16[32,4096]{1,0:T(8,128)(2,1)} %bitcast.7), channel_id=1, source_target_pairs={{0,8},{4,12},{8,0},{12,4},{16,24},{20,28},{24,16},{28,20},{1,9},{5... | collective-permute-start | bytes 786440 | tf_op jit(solution)/shard_map/ppermute | solution.py:369
  3.7 8.0 %collective-permute-start.3 = (bf16[32,4096]{1,0:T(8,128)(2,1)}, bf16[32,4096]{1,0:T(8,128)(2,1)S(1)}, u32[]{:S(2)}, u32[]{:S(2)}) collective-permute-start(bf16[32,4096]{1,0:T(8,128)(2,1)} %bitcast.8), channel_id=1, source_target_pairs={{0,16},{4,20},{8,24},{12,28},{16,0},{20,4},{24,8},{28,12},{1,17},{... | collective-permute-start | bytes 786440 | tf_op jit(solution)/shard_map/ppermute | solution.py:369
  5.2 9.4 %collective-permute-start = (bf16[32,4096]{1,0:T(8,128)(2,1)}, bf16[32,4096]{1,0:T(8,128)(2,1)S(1)}, u32[]{:S(2)}, u32[]{:S(2)}) collective-permute-start(bf16[32,4096]{1,0:T(8,128)(2,1)} %bitcast.9), channel_id=1, source_target_pairs={{0,4},{4,0},{8,12},{12,8},{16,20},{20,16},{24,28},{28,24},{1,5},{5... | collective-permute-start | bytes 786440 | tf_op jit(solution)/shard_map/ppermute | solution.py:369
  10.3 4.3 %collective-permute-start.2 = (bf16[32,4096]{1,0:T(8,128)(2,1)S(1)}, bf16[32,4096]{1,0:T(8,128)(2,1)S(1)}, u32[]{:S(2)}, u32[]{:S(2)}) collective-permute-start(bf16[32,4096]{1,0:T(8,128)(2,1)S(1)} %collective-permute-done.1.refs_2_), channel_id=1, source_target_pairs={{0,4},{4,0},{8,12},{12,8},{16,20},{20,16},{24,28},{28,24},{1,5},{5... | collective-permute-start | bytes 786440 | tf_op jit(solution)/shard_map/ppermute | solution.py:369
  11.6 2.9 %collective-permute-start.4 = (bf16[32,4096]{1,0:T(8,128)(2,1)S(1)}, bf16[32,4096]{1,0:T(8,128)(2,1)S(1)}, u32[]{:S(2)}, u32[]{:S(2)}) collective-permute-start(bf16[32,4096]{1,0:T(8,128)(2,1)S(1)} %collective-permute-done.3.refs_4_), channel_id=1, source_target_pairs={{0,4},{4,0},{8,12},{12,8},{16,20},{20,16},{24,28},{28,24},{1,5},{5... | collective-permute-start | bytes 786440 | tf_op jit(solution)/shard_map/ppermute | solution.py:369
  11.6 9.2 %collective-permute-start.7 = (bf16[16,4096]{1,0:T(8,128)(2,1)S(1)}, bf16[16,4096]{1,0:T(8,128)(2,1)S(1)}, u32[]{:S(2)}, u32[]{:S(2)}) collective-permute-start(bf16[16,4096]{1,0:T(8,128)(2,1)S(1)} %get-tuple-element.69), channel_id=1, source_target_pairs={{0,24},{4,28},{8,16},{12,20},{16,8},{20,12},{24,0},{28,4},{1,25},{... | collective-permute-start | bytes 393224 | tf_op jit(solution)/shard_map/ppermute | solution.py:369
  13.4 7.9 %collective-permute-start.6 = (bf16[16,4096]{1,0:T(8,128)(2,1)S(1)}, bf16[16,4096]{1,0:T(8,128)(2,1)S(1)}, u32[]{:S(2)}, u32[]{:S(2)}) collective-permute-start(bf16[16,4096]{1,0:T(8,128)(2,1)S(1)} %get-tuple-element.67), channel_id=1, source_target_pairs={{0,24},{4,28},{8,16},{12,20},{16,8},{20,12},{24,0},{28,4},{1,25},{... | collective-permute-start | bytes 393224 | tf_op jit(solution)/shard_map/ppermute | solution.py:369
  19.5 9.9 %collective-permute-start.5 = (bf16[320,512]{1,0:T(8,128)(2,1)S(1)}, bf16[320,512]{1,0:T(8,128)(2,1)S(1)}, u32[]{:S(2)}, u32[]{:S(2)}) collective-permute-start(bf16[320,512]{1,0:T(8,128)(2,1)S(1)} %get-tuple-element.66), channel_id=1, source_target_pairs={{0,1},{1,0},{2,3},{3,2},{4,5},{5,4},{6,7},{7,6},{8,9},{9,8},{10,11... | collective-permute-start | bytes 983048 | tf_op jit(solution)/shard_map/ppermute | solution.py:369
  20.9 1.3 %collective-permute-start.9 = (bf16[16,4096]{1,0:T(8,128)(2,1)S(1)}, bf16[16,4096]{1,0:T(8,128)(2,1)S(1)}, u32[]{:S(2)}, u32[]{:S(2)}) collective-permute-start(bf16[16,4096]{1,0:T(8,128)(2,1)S(1)} %collective-permute-done.7.refs_1_), channel_id=1, source_target_pairs={{0,4},{4,0},{8,12},{12,8},{16,20},{20,16},{24,28},{28,24},{1,5},{5... | collective-permute-start | bytes 393224 | tf_op jit(solution)/shard_map/ppermute | solution.py:369
  26.3 10.9 %collective-permute-start.11 = (bf16[192,512]{1,0:T(8,128)(2,1)S(1)}, bf16[192,512]{1,0:T(8,128)(2,1)S(1)}, u32[]{:S(2)}, u32[]{:S(2)}) collective-permute-start(bf16[192,512]{1,0:T(8,128)(2,1)S(1)} %get-tuple-element.77), channel_id=1, source_target_pairs={{0,1},{1,0},{2,3},{3,2},{4,5},{5,4},{6,7},{7,6},{8,9},{9,8},{10,11... | collective-permute-start | bytes 589832 | tf_op jit(solution)/shard_map/ppermute | solution.py:369
  29.5 14.2 %collective-permute-start.10 = (bf16[160,512]{1,0:T(8,128)(2,1)S(1)}, bf16[160,512]{1,0:T(8,128)(2,1)S(1)}, u32[]{:S(2)}, u32[]{:S(2)}) collective-permute-start(bf16[160,512]{1,0:T(8,128)(2,1)S(1)} %pass_on.2), channel_id=1, source_target_pairs={{0,2},{1,3},{2,0},{3,1},{4,6},{5,7},{6,4},{7,5},{8,10},{9,11},{10,... | collective-permute-start | bytes 491528 | tf_op jit(solution)/shard_map/ppermute | solution.py:369
  37.2 6.6 %collective-permute-start.12 = (bf16[96,512]{1,0:T(8,128)(2,1)S(1)}, bf16[96,512]{1,0:T(8,128)(2,1)S(1)}, u32[]{:S(2)}, u32[]{:S(2)}) collective-permute-start(bf16[96,512]{1,0:T(8,128)(2,1)S(1)} %pass_on.3), channel_id=1, source_target_pairs={{0,2},{1,3},{2,0},{3,1},{4,6},{5,7},{6,4},{7,5},{8,10},{9,11},{10,... | collective-permute-start | bytes 294920 | tf_op jit(solution)/shard_map/ppermute | solution.py:369
  44.9 9.3 %collective-permute-start.14 = (bf16[144,512]{1,0:T(8,128)(2,1)S(1)}, bf16[144,512]{1,0:T(8,128)(2,1)S(1)}, u32[]{:S(2)}, u32[]{:S(2)}) collective-permute-start(bf16[144,512]{1,0:T(8,128)(2,1)S(1)} %get-tuple-element.82), channel_id=1, source_target_pairs={{0,2},{1,3},{2,0},{3,1},{4,6},{5,7},{6,4},{7,5},{8,10},{9,11},{10,... | collective-permute-start | bytes 442376 | tf_op jit(solution)/shard_map/ppermute | solution.py:369
  45.1 3.8 %collective-permute-start.15 = (f32[2,32,256]{2,1,0:T(8,128)S(1)}, f32[2,32,256]{2,1,0:T(8,128)S(1)}, u32[]{:S(2)}, u32[]{:S(2)}) collective-permute-start(f32[2,32,256]{2,1,0:T(8,128)S(1)} %get-tuple-element.86), channel_id=1, source_target_pairs={{0,4},{4,0},{8,12},{12,8},{16,20},{20,16},{24,28},{28,24},{1,5},{5... | collective-permute-start | bytes 196616 | tf_op jit(solution)/shard_map/ppermute | solution.py:369
  45.2 3.7 %collective-permute-start.16 = (f32[2,32,256]{2,1,0:T(8,128)S(1)}, f32[2,32,256]{2,1,0:T(8,128)S(1)}, u32[]{:S(2)}, u32[]{:S(2)}) collective-permute-start(f32[2,32,256]{2,1,0:T(8,128)S(1)} %get-tuple-element.87), channel_id=1, source_target_pairs={{0,4},{4,0},{8,12},{12,8},{16,20},{20,16},{24,28},{28,24},{1,5},{5... | collective-permute-start | bytes 196616 | tf_op jit(solution)/shard_map/ppermute | solution.py:369
  45.7 19.5 %collective-permute-start.13 = (bf16[256,512]{1,0:T(8,128)(2,1)S(1)}, bf16[256,512]{1,0:T(8,128)(2,1)S(1)}, u32[]{:S(2)}, u32[]{:S(2)}) collective-permute-start(bf16[256,512]{1,0:T(8,128)(2,1)S(1)} %get-tuple-element.81.refs_0_), channel_id=1, source_target_pairs={{0,1},{1,0},{2,3},{3,2},{4,5},{5,4},{6,7},{7,6},{8,9},{9,8},{10,11... | collective-permute-start | bytes 786440 | tf_op jit(solution)/shard_map/ppermute | solution.py:369
  48.9 4.3 %collective-permute-start.17 = (f32[2,32,256]{2,1,0:T(8,128)S(1)}, f32[2,32,256]{2,1,0:T(8,128)S(1)}, u32[]{:S(2)}, u32[]{:S(2)}) collective-permute-start(f32[2,32,256]{2,1,0:T(8,128)S(1)} %get-tuple-element.89), channel_id=1, source_target_pairs={{0,8},{4,12},{8,0},{12,4},{16,24},{20,28},{24,16},{28,20},{1,9},{5... | collective-permute-start | bytes 196616 | tf_op jit(solution)/shard_map/ppermute | solution.py:369
  49.0 9.0 %collective-permute-start.18 = (bf16[112,512]{1,0:T(8,128)(2,1)S(1)}, bf16[112,512]{1,0:T(8,128)(2,1)S(1)}, u32[]{:S(2)}, u32[]{:S(2)}) collective-permute-start(bf16[112,512]{1,0:T(8,128)(2,1)S(1)} %get-tuple-element.92), channel_id=1, source_target_pairs={{0,2},{1,3},{2,0},{3,1},{4,6},{5,7},{6,4},{7,5},{8,10},{9,11},{10,... | collective-permute-start | bytes 344072 | tf_op jit(solution)/shard_map/ppermute | solution.py:369
  54.2 11.2 %collective-permute-start.21 = (bf16[144,512]{1,0:T(8,128)(2,1)S(1)}, bf16[144,512]{1,0:T(8,128)(2,1)S(1)}, u32[]{:S(2)}, u32[]{:S(2)}) collective-permute-start(bf16[144,512]{1,0:T(8,128)(2,1)S(1)} %collective-permute-done.14.refs_2_), channel_id=1, source_target_pairs={{0,1},{1,0},{2,3},{3,2},{4,5},{5,4},{6,7},{7,6},{8,9},{9,8},{10,11... | collective-permute-start | bytes 442376 | tf_op jit(solution)/shard_map/ppermute | solution.py:369
  54.3 3.9 %collective-permute-start.19 = (f32[1,32,256]{2,1,0:T(8,128)S(1)}, f32[1,32,256]{2,1,0:T(8,128)S(1)}, u32[]{:S(2)}, u32[]{:S(2)}) collective-permute-start(f32[1,32,256]{2,1,0:T(8,128)S(1)} %get-tuple-element.90), channel_id=1, source_target_pairs={{0,16},{4,20},{8,24},{12,28},{16,0},{20,4},{24,8},{28,12},{1,17},{... | collective-permute-start | bytes 98312 | tf_op jit(solution)/shard_map/ppermute | solution.py:369
  58.2 5.3 %collective-permute-start.20 = (f32[32,256]{1,0:T(8,128)S(1)}, f32[32,256]{1,0:T(8,128)S(1)}, u32[]{:S(2)}, u32[]{:S(2)}) collective-permute-start(f32[32,256]{1,0:T(8,128)S(1)} %gradient_sum.5.refs_1_), channel_id=1, source_target_pairs={{0,2},{1,3},{2,0},{3,1},{4,6},{5,7},{6,4},{7,5},{8,10},{9,11},{10,... | collective-permute-start | bytes 98312 | tf_op jit(solution)/shard_map/ppermute | solution.py:369
  63.5 8.2 %collective-permute-start.26 = (bf16[144,512]{1,0:T(8,128)(2,1)S(1)}, bf16[144,512]{1,0:T(8,128)(2,1)S(1)}, u32[]{:S(2)}, u32[]{:S(2)}) collective-permute-start(bf16[144,512]{1,0:T(8,128)(2,1)S(1)} %with_chunk.1.refs_0_), channel_id=1, source_target_pairs={{0,1},{1,0},{2,3},{3,2},{4,5},{5,4},{6,7},{7,6},{8,9},{9,8},{10,11... | collective-permute-start | bytes 442376 | tf_op jit(solution)/shard_map/ppermute | solution.py:369
  69.4 1.4 %collective-permute-start.22 = (bf16[16,4096]{1,0:T(8,128)(2,1)S(1)}, bf16[16,4096]{1,0:T(8,128)(2,1)S(1)}, u32[]{:S(2)}, u32[]{:S(2)}) collective-permute-start(bf16[16,4096]{1,0:T(8,128)(2,1)S(1)} %get-tuple-element.97), channel_id=1, source_target_pairs={{0,4},{4,0},{8,12},{12,8},{16,20},{20,16},{24,28},{28,24},{1,5},{5... | collective-permute-start | bytes 393224 | tf_op jit(solution)/shard_map/ppermute | solution.py:369
  69.5 1.5 %collective-permute-start.23 = (bf16[16,4096]{1,0:T(8,128)(2,1)S(1)}, bf16[16,4096]{1,0:T(8,128)(2,1)S(1)}, u32[]{:S(2)}, u32[]{:S(2)}) collective-permute-start(bf16[16,4096]{1,0:T(8,128)(2,1)S(1)} %get-tuple-element.98), channel_id=1, source_target_pairs={{0,4},{4,0},{8,12},{12,8},{16,20},{20,16},{24,28},{28,24},{1,5},{5... | collective-permute-start | bytes 393224 | tf_op jit(solution)/shard_map/ppermute | solution.py:369
  70.0 1.5 %collective-permute-start.25 = (bf16[16,4096]{1,0:T(8,128)(2,1)S(1)}, bf16[16,4096]{1,0:T(8,128)(2,1)S(1)}, u32[]{:S(2)}, u32[]{:S(2)}) collective-permute-start(bf16[16,4096]{1,0:T(8,128)(2,1)S(1)} %get-tuple-element.100), channel_id=1, source_target_pairs={{0,4},{4,0},{8,12},{12,8},{16,20},{20,16},{24,28},{28,24},{1,5},{5... | collective-permute-start | bytes 393224 | tf_op jit(solution)/shard_map/ppermute | solution.py:369
  71.6 6.5 %collective-permute-start.28 = (bf16[32,4224]{1,0:T(8,128)(2,1)S(1)}, bf16[32,4224]{1,0:T(8,128)(2,1)S(1)}, u32[]{:S(2)}, u32[]{:S(2)}) collective-permute-start(bf16[32,4224]{1,0:T(8,128)(2,1)S(1)} %get-tuple-element.102), channel_id=1, source_target_pairs={{0,8},{4,20},{8,0},{12,28},{16,24},{20,4},{24,16},{28,12},{1,9},{5... | collective-permute-start | bytes 811016 | tf_op jit(solution)/shard_map/ppermute | solution.py:568
  75.8 2.1 %collective-permute-start.29 = (bf16[32,4096]{1,0:T(8,128)(2,1)S(1)}, bf16[32,4096]{1,0:T(8,128)(2,1)S(1)}, u32[]{:S(2)}, u32[]{:S(2)}) collective-permute-start(bf16[32,4096]{1,0:T(8,128)(2,1)S(1)} %get-tuple-element.106), channel_id=1, source_target_pairs={{0,4},{4,0},{8,12},{12,8},{16,20},{20,16},{24,28},{28,24},{1,5},{5... | collective-permute-start | bytes 786440 | tf_op jit(solution)/shard_map/ppermute | solution.py:369
  76.3 1.6 %collective-permute-start.30 = (bf16[32,4096]{1,0:T(8,128)(2,1)S(1)}, bf16[32,4096]{1,0:T(8,128)(2,1)S(1)}, u32[]{:S(2)}, u32[]{:S(2)}) collective-permute-start(bf16[32,4096]{1,0:T(8,128)(2,1)S(1)} %get-tuple-element.107), channel_id=1, source_target_pairs={{0,4},{4,0},{8,12},{12,8},{16,20},{20,16},{24,28},{28,24},{1,5},{5... | collective-permute-start | bytes 786440 | tf_op jit(solution)/shard_map/ppermute | solution.py:369
  76.4 1.5 %collective-permute-start.27 = (f32[32,256]{1,0:T(8,128)S(1)}, f32[32,256]{1,0:T(8,128)S(1)}, u32[]{:S(2)}, u32[]{:S(2)}) collective-permute-start(f32[32,256]{1,0:T(8,128)S(1)} %chunk_sum.1.chunk), channel_id=1, source_target_pairs={{0,4},{4,0},{8,12},{12,8},{16,20},{20,16},{24,28},{28,24},{1,5},{5... | collective-permute-start | bytes 98312 | tf_op jit(solution)/shard_map/ppermute | solution.py:369
  78.6 10.8 %collective-permute-start.31 = (bf16[32,4608]{1,0:T(8,128)(2,1)S(1)}, bf16[32,4608]{1,0:T(8,128)(2,1)S(1)}, u32[]{:S(2)}, u32[]{:S(2)}) collective-permute-start(bf16[32,4608]{1,0:T(8,128)(2,1)S(1)} %get-tuple-element.108), channel_id=1, source_target_pairs={{0,8},{4,12},{8,0},{12,4},{16,24},{20,28},{24,16},{28,20},{1,9},{5... | collective-permute-start | bytes 884744 | tf_op jit(solution)/shard_map/ppermute | solution.py:369
  78.9 10.5 %collective-permute-start.32 = (bf16[32,4608]{1,0:T(8,128)(2,1)S(1)}, bf16[32,4608]{1,0:T(8,128)(2,1)S(1)}, u32[]{:S(2)}, u32[]{:S(2)}) collective-permute-start(bf16[32,4608]{1,0:T(8,128)(2,1)S(1)} %get-tuple-element.109), channel_id=1, source_target_pairs={{0,16},{4,20},{8,24},{12,28},{16,0},{20,4},{24,8},{28,12},{1,17},{... | collective-permute-start | bytes 884744 | tf_op jit(solution)/shard_map/ppermute | solution.py:369
  80.1 9.3 %collective-permute-start.33 = (bf16[32,512]{1,0:T(8,128)(2,1)S(1)}, bf16[32,512]{1,0:T(8,128)(2,1)S(1)}, u32[]{:S(2)}, u32[]{:S(2)}) collective-permute-start(bf16[32,512]{1,0:T(8,128)(2,1)S(1)} %get-tuple-element.110.refs_3_), channel_id=1, source_target_pairs={{0,24},{4,28},{8,16},{12,20},{16,8},{20,12},{24,0},{28,4},{1,25},{... | collective-permute-start | bytes 98312 | tf_op jit(solution)/shard_map/ppermute | solution.py:369
  (5 other events, 65.2 us)

commit v6 on v5

--- a/solution.py
+++ b/solution.py
@@ -380,10 +380,9 @@
     return lax.optimization_barrier((value, *earlier))[0]
 
 
-def with_chunk(rows, *parts):
-    total = functools.reduce(jnp.add, parts)
-    high = total.astype(jnp.bfloat16)
-    low = (total - high.astype(jnp.float32)).astype(jnp.bfloat16)
+def with_chunk(rows, chunk):
+    high = chunk.astype(jnp.bfloat16)
+    low = (chunk - high.astype(jnp.float32)).astype(jnp.bfloat16)
     return (jnp.concatenate([rows, jnp.concatenate([high, low], axis=1)]),)
 
 
@@ -543,9 +542,7 @@
     beyond[0] = after(beyond[0], sent)
     even = after(even, beyond[1])
     (chunk,) = fuse("gradient_sum", lambda a, b: ((a + b)[0],), even, swap(sent, "row", 4))
-    chunks = [chunk, swap(chunk, "col", 2)]
-
-    (second,) = fuse("with_chunk", with_chunk, beyond[1], *chunks)
+    (second,) = fuse("with_chunk", with_chunk, beyond[1], chunk)
     received = [swap(beyond[0], "col", 1), swap(second, "col", 1)]
 
     def columns(n, *earlier):
@@ -566,9 +563,9 @@
 
     own_sum, far_sum = fuse("far_sums", functools.partial(far_sums, depth), *columns(0, second))
     half_way = lax.ppermute(far_sum, "row", [(i, i ^ (4 if i % 2 else 2)) for i in range(n_row)])
-    received[1] = after(received[1], far_sum)
     (chunk,) = fuse("chunk_sum", functools.partial(chunk_sum, depth), second, received[1])
-    mine, *from_sibling = columns(1, chunk)
+    (chunk,) = fuse("chunk_sum", wide_sum, chunk, swap(chunk, "col", 2))
+    mine, *from_sibling = columns(1, chunk, far_sum)
     chunks, *near_sums = near_payloads(row, chunk, swap(chunk, "row", 1), half_way, mine, from_sibling)
     near_sums = [swap(part, "row", k) for part, k in zip(near_sums, near)]
     far_chunks = [swap(chunks, "row", k) for k in far]

time: 90.2 us -> 90 us (level)
  Pallas kernels: 24 us -> 17.4 us
  starting transfers between devices: 30.2 us -> 36.8 us
    ppermute x33, starting transfers between devices: 30.1 us -> 34.1 us  [swap(): return lax.ppermute(value, axis, [(i, i ^ k) for i in range(size)])]
    pallas_call x2, Pallas kernels: 8.05 us -> 5.18 us  [backward(): pl.pallas_call(functools.partial(backward_kernel, spots, depths), out_sha...]
    ppermute x1, starting transfers between devices: 0.07 us -> 2.77 us  [shards_exchanged(): lax.ppermute(far_sum, 'row', [(i, i ^ (4 if i % 2 else 2)) for i in range...]
    pallas_call x2, Pallas kernels: 8.58 us -> 5.98 us  [forward(): pl.pallas_call(functools.partial(forward_kernel, len(parts), depths, layo...]
    pallas_call x1, Pallas kernels: 4.42 us -> 3.28 us  [fetch(): pl.pallas_call(functools.partial(fetch_kernel, groups), out_shape=outs, i...]
  transfers between devices with their start and end apart: 34 -> 34, of which waited for: 20 -> 20; matrix products, arithmetic and copies ran while one was open for 0% -> 0% of each run, Pallas kernels for 24% -> 17%
where the time goes in v6:
time: 90 us; the launch traced here: 90.5 us
  starting transfers between devices  36.8 us (41%)
  waiting for transfers between devices  34.8 us (39%)
  Pallas kernels  17.4 us (19%)
  between operations  1.48 us (2%)
    ppermute x33, waiting for transfers between devices, swap(): return lax.ppermute(value, axis, [(i, i ^ k) for i in range(size)])  34.8 us
    ppermute x33, starting transfers between devices, swap(): return lax.ppermute(value, axis, [(i, i ^ k) for i in range(size)])  34.1 us
    pallas_call x2, Pallas kernels, forward(): pl.pallas_call(functools.partial(forward_kernel, len(parts), depths, layo...  5.98 us
    pallas_call x2, Pallas kernels, backward(): pl.pallas_call(functools.partial(backward_kernel, spots, depths), out_sha...  5.18 us
    pallas_call x1, Pallas kernels, fetch(): pl.pallas_call(functools.partial(fetch_kernel, groups), out_shape=outs, i...  3.28 us
    ppermute x1, starting transfers between devices, shards_exchanged(): lax.ppermute(far_sum, 'row', [(i, i ^ (4 if i % 2 else 2)) for i in range...  2.77 us
  transfers between devices with their start and end apart: 34, of which 20 were waited for; matrix products, arithmetic and copies ran while one was open for 0% of the time, Pallas kernels for 17%

profile of v6, /device:TPU:0, one launch (start us, length us, event | category | flops | bytes accessed | tf_op | source)
XLA Modules:
  0.0 90.5 jit_solution(16106570683187193927)
XLA Ops:
  0.6 3.0 %collective-permute-start.1 = (bf16[32,4096]{1,0:T(8,128)(2,1)}, bf16[32,4096]{1,0:T(8,128)(2,1)S(1)}, u32[]{:S(2)}, u32[]{:S(2)}) collective-permute-start(bf16[32,4096]{1,0:T(8,128)(2,1)} %bitcast.7), channel_id=1, source_target_pairs={{0,8},{4,12},{8,0},{12,4},{16,24},{20,28},{24,16},{28,20},{1,9},{5... | collective-permute-start | bytes 786440 | tf_op jit(solution)/shard_map/ppermute | solution.py:369
  3.7 1.5 %collective-permute-start.3 = (bf16[32,4096]{1,0:T(8,128)(2,1)}, bf16[32,4096]{1,0:T(8,128)(2,1)S(1)}, u32[]{:S(2)}, u32[]{:S(2)}) collective-permute-start(bf16[32,4096]{1,0:T(8,128)(2,1)} %bitcast.8), channel_id=1, source_target_pairs={{0,16},{4,20},{8,24},{12,28},{16,0},{20,4},{24,8},{28,12},{1,17},{... | collective-permute-start | bytes 786440 | tf_op jit(solution)/shard_map/ppermute | solution.py:369
  5.8 3.3 %fetch.1 = (s32[96]{0:T(128)S(1)}, s32[96]{0:T(128)S(1)}, bf16[16,4096]{1,0:T(8,128)(2,1)S(1)}, bf16[16,4096]{1,0:T(8,128)(2,1)S(1)}, bf16[96,128,128]{2,1,0:T(8,128)(2,1)S(1)}, /*index=5*/s32[276]{0:T(512)S(1)}) custom-call(s32[1,1]{1,0:T(1,128)S(6)} %copy.10.count, s32[96]{0:T(128)} %bitcast.13, s32[96]{0:T(128)} %bitcast.14, bf16[32,4096]{1,0:T(8,128)(2,1)} %bitcast.10, ...), custom_call_target="tpu_custom_call" | custom-call | flops 1 | bytes 1 | tf_op jit(solution)/shard_map/fetch/pallas_call | solution.py:171
  9.1 1.1 %collective-permute-done.1.refs_2_ = bf16[32,4096]{1,0:T(8,128)(2,1)S(1)} collective-permute-done((bf16[32,4096]{1,0:T(8,128)(2,1)}, bf16[32,4096]{1,0:T(8,128)(2,1)S(1)}, u32[]{:S(2)}, u32[]{:S(2)}) %collective-permute-start.1) | collective-permute-done | bytes 262176 | tf_op jit(solution)/shard_map/ppermute | solution.py:369
  10.2 1.5 %collective-permute-done.3.refs_4_ = bf16[32,4096]{1,0:T(8,128)(2,1)S(1)} collective-permute-done((bf16[32,4096]{1,0:T(8,128)(2,1)}, bf16[32,4096]{1,0:T(8,128)(2,1)S(1)}, u32[]{:S(2)}, u32[]{:S(2)}) %collective-permute-start.3) | collective-permute-done | bytes 262176 | tf_op jit(solution)/shard_map/ppermute | solution.py:369
  11.6 1.7 %collective-permute-start.7 = (bf16[16,4096]{1,0:T(8,128)(2,1)S(1)}, bf16[16,4096]{1,0:T(8,128)(2,1)S(1)}, u32[]{:S(2)}, u32[]{:S(2)}) collective-permute-start(bf16[16,4096]{1,0:T(8,128)(2,1)S(1)} %get-tuple-element.68), channel_id=1, source_target_pairs={{0,24},{4,28},{8,16},{12,20},{16,8},{20,12},{24,0},{28,4},{1,25},{... | collective-permute-start | bytes 393224 | tf_op jit(solution)/shard_map/ppermute | solution.py:369
  13.4 1.2 %collective-permute-start.6 = (bf16[16,4096]{1,0:T(8,128)(2,1)S(1)}, bf16[16,4096]{1,0:T(8,128)(2,1)S(1)}, u32[]{:S(2)}, u32[]{:S(2)}) collective-permute-start(bf16[16,4096]{1,0:T(8,128)(2,1)S(1)} %get-tuple-element.66), channel_id=1, source_target_pairs={{0,24},{4,28},{8,16},{12,20},{16,8},{20,12},{24,0},{28,4},{1,25},{... | collective-permute-start | bytes 393224 | tf_op jit(solution)/shard_map/ppermute | solution.py:369
  14.6 3.4 %forward_products.2 = (bf16[160,512]{1,0:T(8,128)(2,1)S(1)}, bf16[160,512]{1,0:T(8,128)(2,1)S(1)}, bf16[320,512]{1,0:T(8,128)(2,1)S(1)}, bf16[32,512]{1,0:T(8,12...) custom-call(s32[1]{0:T(128)} %bitcast.1.place, s32[276]{0:T(512)S(1)} %get-tuple-element.58.lists, ...), custom_call_target="tpu_custom_call" | custom-call | flops 1 | bytes 1 | tf_op jit(solution)/shard_map/forward_products/pallas_call | solution.py:231
  18.0 1.9 %collective-permute-start.5 = (bf16[320,512]{1,0:T(8,128)(2,1)S(1)}, bf16[320,512]{1,0:T(8,128)(2,1)S(1)}, u32[]{:S(2)}, u32[]{:S(2)}) collective-permute-start(bf16[320,512]{1,0:T(8,128)(2,1)S(1)} %get-tuple-element.65), channel_id=1, source_target_pairs={{0,1},{1,0},{2,3},{3,2},{4,5},{5,4},{6,7},{7,6},{8,9},{9,8},{10,11... | collective-permute-start | bytes 983048 | tf_op jit(solution)/shard_map/ppermute | solution.py:369
  20.0 1.3 %collective-permute-done.6.refs_0_ = bf16[16,4096]{1,0:T(8,128)(2,1)S(1)} collective-permute-done((bf16[16,4096]{1,0:T(8,128)(2,1)S(1)}, bf16[16,4096]{1,0:T(8,128)(2,1)S(1)}, u32[]{:S(2)}, u32[]{:S(2)}) %collective-permute-start.6) | collective-permute-done | bytes 131104 | tf_op jit(solution)/shard_map/ppermute | solution.py:369
  21.3 1.3 %collective-permute-done.8.refs_2_ = bf16[16,4096]{1,0:T(8,128)(2,1)S(1)} collective-permute-done((bf16[16,4096]{1,0:T(8,128)(2,1)S(1)}, bf16[16,4096]{1,0:T(8,128)(2,1)S(1)}, u32[]{:S(2)}, u32[]{:S(2)}) %collective-permute-start.8) | collective-permute-done | bytes 131104 | tf_op jit(solution)/shard_map/ppermute | solution.py:369
  22.6 2.6 %forward_products.3 = (bf16[96,512]{1,0:T(8,128)(2,1)S(1)}, bf16[96,512]{1,0:T(8,128)(2,1)S(1)}, bf16[192,512]{1,0:T(8,128)(2,1)S(1)}) custom-call(s32[1]{0:T(128)} %bitcast.1.place, s32[276]{0:T(512)S(1)} %get-tuple-element.58.lists, s32[96]{0:T(128)S(1)} %get-tuple-element.59.rows, s32[96]{0:T(128)S(1)} %get-tuple-element.60.cols, ...), custom_call_target="tpu_custom_call" | custom-call | flops 1 | bytes 1 | tf_op jit(solution)/shard_map/forward_products/pallas_call | solution.py:231
  25.2 1.9 %collective-permute-start.11 = (bf16[192,512]{1,0:T(8,128)(2,1)S(1)}, bf16[192,512]{1,0:T(8,128)(2,1)S(1)}, u32[]{:S(2)}, u32[]{:S(2)}) collective-permute-start(bf16[192,512]{1,0:T(8,128)(2,1)S(1)} %get-tuple-element.76), channel_id=1, source_target_pairs={{0,1},{1,0},{2,3},{3,2},{4,5},{5,4},{6,7},{7,6},{8,9},{9,8},{10,11... | collective-permute-start | bytes 589832 | tf_op jit(solution)/shard_map/ppermute | solution.py:369
  27.7 2.4 %collective-permute-start.10 = (bf16[160,512]{1,0:T(8,128)(2,1)S(1)}, bf16[160,512]{1,0:T(8,128)(2,1)S(1)}, u32[]{:S(2)}, u32[]{:S(2)}) collective-permute-start(bf16[160,512]{1,0:T(8,128)(2,1)S(1)} %pass_on.2), channel_id=1, source_target_pairs={{0,2},{1,3},{2,0},{3,1},{4,6},{5,7},{6,4},{7,5},{8,10},{9,11},{10,... | collective-permute-start | bytes 491528 | tf_op jit(solution)/shard_map/ppermute | solution.py:369
  30.1 5.6 %collective-permute-done.11.refs_1_.refs_4_ = bf16[192,512]{1,0:T(8,128)(2,1)S(1)} collective-permute-done((bf16[192,512]{1,0:T(8,128)(2,1)S(1)}, bf16[192,512]{1,0:T(8,128)(2,1)S(1)}, u32[]{:S(2)}, u32[]{:S(2)}) %collective-permute-start.11) | collective-permute-done | bytes 196640 | tf_op jit(solution)/shard_map/ppermute | solution.py:369
  35.8 5.9 %collective-permute-done.12.refs_5_ = bf16[96,512]{1,0:T(8,128)(2,1)S(1)} collective-permute-done((bf16[96,512]{1,0:T(8,128)(2,1)S(1)}, bf16[96,512]{1,0:T(8,128)(2,1)S(1)}, u32[]{:S(2)}, u32[]{:S(2)}) %collective-permute-start.12) | collective-permute-done | bytes 98336 | tf_op jit(solution)/shard_map/ppermute | solution.py:369
  41.7 1.1 %layer.1 = (bf16[512,256]{1,0:T(8,128)(2,1)}, bf16[512,256]{1,0:T(8,128)(2,1)S(1)}, bf16[256,512]{1,0:T(8,128)(2,1)S(1)}, bf16[256,512]{1,0:T(8,128)(2,1)S(1)}, ...) custom-call(s32[1]{0:T(128)} %bitcast.row, bf16[256,256]{1,0:T(8,128)(2,1)S(1)} %copy-done.2, ...), custom_call_target="tpu_custom_call" | custom-call | flops 1 | bytes 1 | tf_op jit(solution)/shard_map/layer/pallas_call | solution.py:333
  43.7 3.7 %collective-permute-start.13 = (bf16[256,512]{1,0:T(8,128)(2,1)S(1)}, bf16[256,512]{1,0:T(8,128)(2,1)S(1)}, u32[]{:S(2)}, u32[]{:S(2)}) collective-permute-start(bf16[256,512]{1,0:T(8,128)(2,1)S(1)} %get-tuple-element.80.refs_0_), channel_id=1, source_target_pairs={{0,1},{1,0},{2,3},{3,2},{4,5},{5,4},{6,7},{7,6},{8,9},{9,8},{10,11... | collective-permute-start | bytes 786440 | tf_op jit(solution)/shard_map/ppermute | solution.py:369
  47.4 1.6 %collective-permute-start.17 = (f32[2,32,256]{2,1,0:T(8,128)S(1)}, f32[2,32,256]{2,1,0:T(8,128)S(1)}, u32[]{:S(2)}, u32[]{:S(2)}) collective-permute-start(f32[2,32,256]{2,1,0:T(8,128)S(1)} %get-tuple-element.88), channel_id=1, source_target_pairs={{0,8},{4,12},{8,0},{12,4},{16,24},{20,28},{24,16},{28,20},{1,9},{5... | collective-permute-start | bytes 196616 | tf_op jit(solution)/shard_map/ppermute | solution.py:369
  49.1 1.1 %collective-permute-start.18 = (bf16[112,512]{1,0:T(8,128)(2,1)S(1)}, bf16[112,512]{1,0:T(8,128)(2,1)S(1)}, u32[]{:S(2)}, u32[]{:S(2)}) collective-permute-start(bf16[112,512]{1,0:T(8,128)(2,1)S(1)} %get-tuple-element.91), channel_id=1, source_target_pairs={{0,2},{1,3},{2,0},{3,1},{4,6},{5,7},{6,4},{7,5},{8,10},{9,11},{10,... | collective-permute-start | bytes 344072 | tf_op jit(solution)/shard_map/ppermute | solution.py:369
  50.2 1.6 %collective-permute-done.17.refs_1_ = f32[2,32,256]{2,1,0:T(8,128)S(1)} collective-permute-done((f32[2,32,256]{2,1,0:T(8,128)S(1)}, f32[2,32,256]{2,1,0:T(8,128)S(1)}, u32[]{:S(2)}, u32[]{:S(2)}) %collective-permute-start.17) | collective-permute-done | bytes 65568 | tf_op jit(solution)/shard_map/ppermute | solution.py:369
  52.8 3.0 %collective-permute-start.19 = (f32[1,32,256]{2,1,0:T(8,128)S(1)}, f32[1,32,256]{2,1,0:T(8,128)S(1)}, u32[]{:S(2)}, u32[]{:S(2)}) collective-permute-start(f32[1,32,256]{2,1,0:T(8,128)S(1)} %get-tuple-element.89), channel_id=1, source_target_pairs={{0,16},{4,20},{8,24},{12,28},{16,0},{20,4},{24,8},{28,12},{1,17},{... | collective-permute-start | bytes 98312 | tf_op jit(solution)/shard_map/ppermute | solution.py:369
  56.5 1.2 %collective-permute-done.19.refs_1_ = f32[1,32,256]{2,1,0:T(8,128)S(1)} collective-permute-done((f32[1,32,256]{2,1,0:T(8,128)S(1)}, f32[1,32,256]{2,1,0:T(8,128)S(1)}, u32[]{:S(2)}, u32[]{:S(2)}) %collective-permute-start.19) | collective-permute-done | bytes 32800 | tf_op jit(solution)/shard_map/ppermute | solution.py:369
  57.8 2.1 %collective-permute-start.25 = (bf16[144,512]{1,0:T(8,128)(2,1)S(1)}, bf16[144,512]{1,0:T(8,128)(2,1)S(1)}, u32[]{:S(2)}, u32[]{:S(2)}) collective-permute-start(bf16[144,512]{1,0:T(8,128)(2,1)S(1)} %with_chunk.1.refs_0_), channel_id=1, source_target_pairs={{0,1},{1,0},{2,3},{3,2},{4,5},{5,4},{6,7},{7,6},{8,9},{9,8},{10,11... | collective-permute-start | bytes 442376 | tf_op jit(solution)/shard_map/ppermute | solution.py:369
  59.9 2.7 %collective-permute-done.20.refs_3_ = bf16[144,512]{1,0:T(8,128)(2,1)S(1)} collective-permute-done((bf16[144,512]{1,0:T(8,128)(2,1)S(1)}, bf16[144,512]{1,0:T(8,128)(2,1)S(1)}, u32[]{:S(2)}, u32[]{:S(2)}) %collective-permute-start.20) | collective-permute-done | bytes 147488 | tf_op jit(solution)/shard_map/ppermute | solution.py:369
  62.6 2.6 %backward_products.2 = (bf16[64,4096]{1,0:T(8,128)(2,1)S(1)}, bf16[16,4096]{1,0:T(8,128)(2,1)S(1)}, bf16[16,4096]{1,0:T(8,128)(2,1)S(1)}, bf16[16,4096]{1,0:T(8,128)(2,1)S(1)}, bf16[16,4096]{1,0:T(8,128)(2,1)S(1)}) custom-call(s32[1]{0:T(128)} %bitcast.1.place, s32[276]{0:T(512)S(1)} %get-tuple-element.58.lists, s32[96]{0:T(128)S(1)} %get-tuple-element.59.rows, ...), custom_call_target="tpu_custom_call" | custom-call | flops 1 | bytes 1 | tf_op jit(solution)/shard_map/backward_products/pallas_call | solution.py:275
  67.5 2.8 %collective-permute-start.28 = (bf16[32,4224]{1,0:T(8,128)(2,1)S(1)}, bf16[32,4224]{1,0:T(8,128)(2,1)S(1)}, u32[]{:S(2)}, u32[]{:S(2)}) collective-permute-start(bf16[32,4224]{1,0:T(8,128)(2,1)S(1)} %get-tuple-element.101), channel_id=1, source_target_pairs={{0,8},{4,20},{8,0},{12,28},{16,24},{20,4},{24,16},{28,12},{1,9},{5... | collective-permute-start | bytes 811016 | tf_op jit(solution)/shard_map/ppermute | solution.py:565
  71.2 2.6 %backward_products.3 = (bf16[64,4096]{1,0:T(8,128)(2,1)S(1)}, bf16[32,4096]{1,0:T(8,128)(2,1)S(1)}, bf16[32,4096]{1,0:T(8,128)(2,1)S(1)}) custom-call(s32[1]{0:T(128)} %bitcast.1.place, s32[276]{0:T(512)S(1)} %get-tuple-element.58.lists, s32[96]{0:T(128)S(1)} %get-tuple-element.59.rows, s32[96]{0:T(128)S(1)} %get-tuple-element.60.cols, ...), custom_call_target="tpu_custom_call" | custom-call | flops 1 | bytes 1 | tf_op jit(solution)/shard_map/backward_products/pallas_call | solution.py:275
  74.5 1.4 %collective-permute-done.27.sibling = f32[32,256]{1,0:T(8,128)S(1)} collective-permute-done((f32[32,256]{1,0:T(8,128)S(1)}, f32[32,256]{1,0:T(8,128)S(1)}, u32[]{:S(2)}, u32[]{:S(2)}) %collective-permute-start.27) | collective-permute-done | bytes 32800 | tf_op jit(solution)/shard_map/ppermute | solution.py:369
  76.3 3.5 %collective-permute-start.31 = (bf16[32,4608]{1,0:T(8,128)(2,1)S(1)}, bf16[32,4608]{1,0:T(8,128)(2,1)S(1)}, u32[]{:S(2)}, u32[]{:S(2)}) collective-permute-start(bf16[32,4608]{1,0:T(8,128)(2,1)S(1)} %get-tuple-element.106), channel_id=1, source_target_pairs={{0,8},{4,12},{8,0},{12,4},{16,24},{20,28},{24,16},{28,20},{1,9},{5... | collective-permute-start | bytes 884744 | tf_op jit(solution)/shard_map/ppermute | solution.py:369
  80.5 1.4 %collective-permute-start.33 = (bf16[32,512]{1,0:T(8,128)(2,1)S(1)}, bf16[32,512]{1,0:T(8,128)(2,1)S(1)}, u32[]{:S(2)}, u32[]{:S(2)}) collective-permute-start(bf16[32,512]{1,0:T(8,128)(2,1)S(1)} %get-tuple-element.108.refs_3_), channel_id=1, source_target_pairs={{0,24},{4,28},{8,16},{12,20},{16,8},{20,12},{24,0},{28,4},{1,25},{... | collective-permute-start | bytes 98312 | tf_op jit(solution)/shard_map/ppermute | solution.py:369
  81.9 7.7 %collective-permute-done.33.refs_4_ = bf16[32,512]{1,0:T(8,128)(2,1)S(1)} collective-permute-done((bf16[32,512]{1,0:T(8,128)(2,1)S(1)}, bf16[32,512]{1,0:T(8,128)(2,1)S(1)}, u32[]{:S(2)}, u32[]{:S(2)}) %collective-permute-start.33) | collective-permute-done | bytes 32800 | tf_op jit(solution)/shard_map/ppermute | solution.py:369
  (60 shorter events, 9.4 us)
Async XLA Ops:
  0.6 9.5 %collective-permute-start.1 = (bf16[32,4096]{1,0:T(8,128)(2,1)}, bf16[32,4096]{1,0:T(8,128)(2,1)S(1)}, u32[]{:S(2)}, u32[]{:S(2)}) collective-permute-start(bf16[32,4096]{1,0:T(8,128)(2,1)} %bitcast.7), channel_id=1, source_target_pairs={{0,8},{4,12},{8,0},{12,4},{16,24},{20,28},{24,16},{28,20},{1,9},{5... | collective-permute-start | bytes 786440 | tf_op jit(solution)/shard_map/ppermute | solution.py:369
  3.7 8.0 %collective-permute-start.3 = (bf16[32,4096]{1,0:T(8,128)(2,1)}, bf16[32,4096]{1,0:T(8,128)(2,1)S(1)}, u32[]{:S(2)}, u32[]{:S(2)}) collective-permute-start(bf16[32,4096]{1,0:T(8,128)(2,1)} %bitcast.8), channel_id=1, source_target_pairs={{0,16},{4,20},{8,24},{12,28},{16,0},{20,4},{24,8},{28,12},{1,17},{... | collective-permute-start | bytes 786440 | tf_op jit(solution)/shard_map/ppermute | solution.py:369
  5.2 9.4 %collective-permute-start = (bf16[32,4096]{1,0:T(8,128)(2,1)}, bf16[32,4096]{1,0:T(8,128)(2,1)S(1)}, u32[]{:S(2)}, u32[]{:S(2)}) collective-permute-start(bf16[32,4096]{1,0:T(8,128)(2,1)} %bitcast.9), channel_id=1, source_target_pairs={{0,4},{4,0},{8,12},{12,8},{16,20},{20,16},{24,28},{28,24},{1,5},{5... | collective-permute-start | bytes 786440 | tf_op jit(solution)/shard_map/ppermute | solution.py:369
  10.2 4.4 %collective-permute-start.2 = (bf16[32,4096]{1,0:T(8,128)(2,1)S(1)}, bf16[32,4096]{1,0:T(8,128)(2,1)S(1)}, u32[]{:S(2)}, u32[]{:S(2)}) collective-permute-start(bf16[32,4096]{1,0:T(8,128)(2,1)S(1)} %collective-permute-done.1.refs_2_), channel_id=1, source_target_pairs={{0,4},{4,0},{8,12},{12,8},{16,20},{20,16},{24,28},{28,24},{1,5},{5... | collective-permute-start | bytes 786440 | tf_op jit(solution)/shard_map/ppermute | solution.py:369
  11.6 2.9 %collective-permute-start.4 = (bf16[32,4096]{1,0:T(8,128)(2,1)S(1)}, bf16[32,4096]{1,0:T(8,128)(2,1)S(1)}, u32[]{:S(2)}, u32[]{:S(2)}) collective-permute-start(bf16[32,4096]{1,0:T(8,128)(2,1)S(1)} %collective-permute-done.3.refs_4_), channel_id=1, source_target_pairs={{0,4},{4,0},{8,12},{12,8},{16,20},{20,16},{24,28},{28,24},{1,5},{5... | collective-permute-start | bytes 786440 | tf_op jit(solution)/shard_map/ppermute | solution.py:369
  11.6 8.3 %collective-permute-start.7 = (bf16[16,4096]{1,0:T(8,128)(2,1)S(1)}, bf16[16,4096]{1,0:T(8,128)(2,1)S(1)}, u32[]{:S(2)}, u32[]{:S(2)}) collective-permute-start(bf16[16,4096]{1,0:T(8,128)(2,1)S(1)} %get-tuple-element.68), channel_id=1, source_target_pairs={{0,24},{4,28},{8,16},{12,20},{16,8},{20,12},{24,0},{28,4},{1,25},{... | collective-permute-start | bytes 393224 | tf_op jit(solution)/shard_map/ppermute | solution.py:369
  13.4 7.9 %collective-permute-start.6 = (bf16[16,4096]{1,0:T(8,128)(2,1)S(1)}, bf16[16,4096]{1,0:T(8,128)(2,1)S(1)}, u32[]{:S(2)}, u32[]{:S(2)}) collective-permute-start(bf16[16,4096]{1,0:T(8,128)(2,1)S(1)} %get-tuple-element.66), channel_id=1, source_target_pairs={{0,24},{4,28},{8,16},{12,20},{16,8},{20,12},{24,0},{28,4},{1,25},{... | collective-permute-start | bytes 393224 | tf_op jit(solution)/shard_map/ppermute | solution.py:369
  18.0 9.6 %collective-permute-start.5 = (bf16[320,512]{1,0:T(8,128)(2,1)S(1)}, bf16[320,512]{1,0:T(8,128)(2,1)S(1)}, u32[]{:S(2)}, u32[]{:S(2)}) collective-permute-start(bf16[320,512]{1,0:T(8,128)(2,1)S(1)} %get-tuple-element.65), channel_id=1, source_target_pairs={{0,1},{1,0},{2,3},{3,2},{4,5},{5,4},{6,7},{7,6},{8,9},{9,8},{10,11... | collective-permute-start | bytes 983048 | tf_op jit(solution)/shard_map/ppermute | solution.py:369
  20.0 1.3 %collective-permute-start.9 = (bf16[16,4096]{1,0:T(8,128)(2,1)S(1)}, bf16[16,4096]{1,0:T(8,128)(2,1)S(1)}, u32[]{:S(2)}, u32[]{:S(2)}) collective-permute-start(bf16[16,4096]{1,0:T(8,128)(2,1)S(1)} %collective-permute-done.7.refs_1_), channel_id=1, source_target_pairs={{0,4},{4,0},{8,12},{12,8},{16,20},{20,16},{24,28},{28,24},{1,5},{5... | collective-permute-start | bytes 393224 | tf_op jit(solution)/shard_map/ppermute | solution.py:369
  25.2 10.5 %collective-permute-start.11 = (bf16[192,512]{1,0:T(8,128)(2,1)S(1)}, bf16[192,512]{1,0:T(8,128)(2,1)S(1)}, u32[]{:S(2)}, u32[]{:S(2)}) collective-permute-start(bf16[192,512]{1,0:T(8,128)(2,1)S(1)} %get-tuple-element.76), channel_id=1, source_target_pairs={{0,1},{1,0},{2,3},{3,2},{4,5},{5,4},{6,7},{7,6},{8,9},{9,8},{10,11... | collective-permute-start | bytes 589832 | tf_op jit(solution)/shard_map/ppermute | solution.py:369
  27.7 14.0 %collective-permute-start.10 = (bf16[160,512]{1,0:T(8,128)(2,1)S(1)}, bf16[160,512]{1,0:T(8,128)(2,1)S(1)}, u32[]{:S(2)}, u32[]{:S(2)}) collective-permute-start(bf16[160,512]{1,0:T(8,128)(2,1)S(1)} %pass_on.2), channel_id=1, source_target_pairs={{0,2},{1,3},{2,0},{3,1},{4,6},{5,7},{6,4},{7,5},{8,10},{9,11},{10,... | collective-permute-start | bytes 491528 | tf_op jit(solution)/shard_map/ppermute | solution.py:369
  35.7 6.0 %collective-permute-start.12 = (bf16[96,512]{1,0:T(8,128)(2,1)S(1)}, bf16[96,512]{1,0:T(8,128)(2,1)S(1)}, u32[]{:S(2)}, u32[]{:S(2)}) collective-permute-start(bf16[96,512]{1,0:T(8,128)(2,1)S(1)} %pass_on.3), channel_id=1, source_target_pairs={{0,2},{1,3},{2,0},{3,1},{4,6},{5,7},{6,4},{7,5},{8,10},{9,11},{10,... | collective-permute-start | bytes 294920 | tf_op jit(solution)/shard_map/ppermute | solution.py:369
  42.9 9.2 %collective-permute-start.14 = (bf16[144,512]{1,0:T(8,128)(2,1)S(1)}, bf16[144,512]{1,0:T(8,128)(2,1)S(1)}, u32[]{:S(2)}, u32[]{:S(2)}) collective-permute-start(bf16[144,512]{1,0:T(8,128)(2,1)S(1)} %get-tuple-element.81), channel_id=1, source_target_pairs={{0,2},{1,3},{2,0},{3,1},{4,6},{5,7},{6,4},{7,5},{8,10},{9,11},{10,... | collective-permute-start | bytes 442376 | tf_op jit(solution)/shard_map/ppermute | solution.py:369
  43.1 4.3 %collective-permute-start.15 = (f32[2,32,256]{2,1,0:T(8,128)S(1)}, f32[2,32,256]{2,1,0:T(8,128)S(1)}, u32[]{:S(2)}, u32[]{:S(2)}) collective-permute-start(f32[2,32,256]{2,1,0:T(8,128)S(1)} %get-tuple-element.85), channel_id=1, source_target_pairs={{0,4},{4,0},{8,12},{12,8},{16,20},{20,16},{24,28},{28,24},{1,5},{5... | collective-permute-start | bytes 196616 | tf_op jit(solution)/shard_map/ppermute | solution.py:369
  43.2 4.2 %collective-permute-start.16 = (f32[2,32,256]{2,1,0:T(8,128)S(1)}, f32[2,32,256]{2,1,0:T(8,128)S(1)}, u32[]{:S(2)}, u32[]{:S(2)}) collective-permute-start(f32[2,32,256]{2,1,0:T(8,128)S(1)} %get-tuple-element.86), channel_id=1, source_target_pairs={{0,4},{4,0},{8,12},{12,8},{16,20},{20,16},{24,28},{28,24},{1,5},{5... | collective-permute-start | bytes 196616 | tf_op jit(solution)/shard_map/ppermute | solution.py:369
  43.7 16.2 %collective-permute-start.13 = (bf16[256,512]{1,0:T(8,128)(2,1)S(1)}, bf16[256,512]{1,0:T(8,128)(2,1)S(1)}, u32[]{:S(2)}, u32[]{:S(2)}) collective-permute-start(bf16[256,512]{1,0:T(8,128)(2,1)S(1)} %get-tuple-element.80.refs_0_), channel_id=1, source_target_pairs={{0,1},{1,0},{2,3},{3,2},{4,5},{5,4},{6,7},{7,6},{8,9},{9,8},{10,11... | collective-permute-start | bytes 786440 | tf_op jit(solution)/shard_map/ppermute | solution.py:369
  47.4 4.3 %collective-permute-start.17 = (f32[2,32,256]{2,1,0:T(8,128)S(1)}, f32[2,32,256]{2,1,0:T(8,128)S(1)}, u32[]{:S(2)}, u32[]{:S(2)}) collective-permute-start(f32[2,32,256]{2,1,0:T(8,128)S(1)} %get-tuple-element.88), channel_id=1, source_target_pairs={{0,8},{4,12},{8,0},{12,4},{16,24},{20,28},{24,16},{28,20},{1,9},{5... | collective-permute-start | bytes 196616 | tf_op jit(solution)/shard_map/ppermute | solution.py:369
  49.1 7.5 %collective-permute-start.18 = (bf16[112,512]{1,0:T(8,128)(2,1)S(1)}, bf16[112,512]{1,0:T(8,128)(2,1)S(1)}, u32[]{:S(2)}, u32[]{:S(2)}) collective-permute-start(bf16[112,512]{1,0:T(8,128)(2,1)S(1)} %get-tuple-element.91), channel_id=1, source_target_pairs={{0,2},{1,3},{2,0},{3,1},{4,6},{5,7},{6,4},{7,5},{8,10},{9,11},{10,... | collective-permute-start | bytes 344072 | tf_op jit(solution)/shard_map/ppermute | solution.py:369
  52.0 10.6 %collective-permute-start.20 = (bf16[144,512]{1,0:T(8,128)(2,1)S(1)}, bf16[144,512]{1,0:T(8,128)(2,1)S(1)}, u32[]{:S(2)}, u32[]{:S(2)}) collective-permute-start(bf16[144,512]{1,0:T(8,128)(2,1)S(1)} %collective-permute-done.14.refs_2_), channel_id=1, source_target_pairs={{0,1},{1,0},{2,3},{3,2},{4,5},{5,4},{6,7},{7,6},{8,9},{9,8},{10,11... | collective-permute-start | bytes 442376 | tf_op jit(solution)/shard_map/ppermute | solution.py:369
  52.8 4.9 %collective-permute-start.19 = (f32[1,32,256]{2,1,0:T(8,128)S(1)}, f32[1,32,256]{2,1,0:T(8,128)S(1)}, u32[]{:S(2)}, u32[]{:S(2)}) collective-permute-start(f32[1,32,256]{2,1,0:T(8,128)S(1)} %get-tuple-element.89), channel_id=1, source_target_pairs={{0,16},{4,20},{8,24},{12,28},{16,0},{20,4},{24,8},{28,12},{1,17},{... | collective-permute-start | bytes 98312 | tf_op jit(solution)/shard_map/ppermute | solution.py:369
  57.8 8.5 %collective-permute-start.25 = (bf16[144,512]{1,0:T(8,128)(2,1)S(1)}, bf16[144,512]{1,0:T(8,128)(2,1)S(1)}, u32[]{:S(2)}, u32[]{:S(2)}) collective-permute-start(bf16[144,512]{1,0:T(8,128)(2,1)S(1)} %with_chunk.1.refs_0_), channel_id=1, source_target_pairs={{0,1},{1,0},{2,3},{3,2},{4,5},{5,4},{6,7},{7,6},{8,9},{9,8},{10,11... | collective-permute-start | bytes 442376 | tf_op jit(solution)/shard_map/ppermute | solution.py:369
  65.2 1.4 %collective-permute-start.21 = (bf16[16,4096]{1,0:T(8,128)(2,1)S(1)}, bf16[16,4096]{1,0:T(8,128)(2,1)S(1)}, u32[]{:S(2)}, u32[]{:S(2)}) collective-permute-start(bf16[16,4096]{1,0:T(8,128)(2,1)S(1)} %get-tuple-element.96), channel_id=1, source_target_pairs={{0,4},{4,0},{8,12},{12,8},{16,20},{20,16},{24,28},{28,24},{1,5},{5... | collective-permute-start | bytes 393224 | tf_op jit(solution)/shard_map/ppermute | solution.py:369
  65.3 1.5 %collective-permute-start.22 = (bf16[16,4096]{1,0:T(8,128)(2,1)S(1)}, bf16[16,4096]{1,0:T(8,128)(2,1)S(1)}, u32[]{:S(2)}, u32[]{:S(2)}) collective-permute-start(bf16[16,4096]{1,0:T(8,128)(2,1)S(1)} %get-tuple-element.97), channel_id=1, source_target_pairs={{0,4},{4,0},{8,12},{12,8},{16,20},{20,16},{24,28},{28,24},{1,5},{5... | collective-permute-start | bytes 393224 | tf_op jit(solution)/shard_map/ppermute | solution.py:369
  65.9 1.5 %collective-permute-start.24 = (bf16[16,4096]{1,0:T(8,128)(2,1)S(1)}, bf16[16,4096]{1,0:T(8,128)(2,1)S(1)}, u32[]{:S(2)}, u32[]{:S(2)}) collective-permute-start(bf16[16,4096]{1,0:T(8,128)(2,1)S(1)} %get-tuple-element.99), channel_id=1, source_target_pairs={{0,4},{4,0},{8,12},{12,8},{16,20},{20,16},{24,28},{28,24},{1,5},{5... | collective-permute-start | bytes 393224 | tf_op jit(solution)/shard_map/ppermute | solution.py:369
  66.3 4.9 %collective-permute-start.26 = (f32[32,256]{1,0:T(8,128)S(1)}, f32[32,256]{1,0:T(8,128)S(1)}, u32[]{:S(2)}, u32[]{:S(2)}) collective-permute-start(f32[32,256]{1,0:T(8,128)S(1)} %chunk_sum.2.refs_0_), channel_id=1, source_target_pairs={{0,2},{1,3},{2,0},{3,1},{4,6},{5,7},{6,4},{7,5},{8,10},{9,11},{10,... | collective-permute-start | bytes 98312 | tf_op jit(solution)/shard_map/ppermute | solution.py:369
  67.5 8.4 %collective-permute-start.28 = (bf16[32,4224]{1,0:T(8,128)(2,1)S(1)}, bf16[32,4224]{1,0:T(8,128)(2,1)S(1)}, u32[]{:S(2)}, u32[]{:S(2)}) collective-permute-start(bf16[32,4224]{1,0:T(8,128)(2,1)S(1)} %get-tuple-element.101), channel_id=1, source_target_pairs={{0,8},{4,20},{8,0},{12,28},{16,24},{20,4},{24,16},{28,12},{1,9},{5... | collective-permute-start | bytes 811016 | tf_op jit(solution)/shard_map/ppermute | solution.py:565
  73.8 2.0 %collective-permute-start.29 = (bf16[32,4096]{1,0:T(8,128)(2,1)S(1)}, bf16[32,4096]{1,0:T(8,128)(2,1)S(1)}, u32[]{:S(2)}, u32[]{:S(2)}) collective-permute-start(bf16[32,4096]{1,0:T(8,128)(2,1)S(1)} %get-tuple-element.104), channel_id=1, source_target_pairs={{0,4},{4,0},{8,12},{12,8},{16,20},{20,16},{24,28},{28,24},{1,5},{5... | collective-permute-start | bytes 786440 | tf_op jit(solution)/shard_map/ppermute | solution.py:369
  73.9 1.9 %collective-permute-start.30 = (bf16[32,4096]{1,0:T(8,128)(2,1)S(1)}, bf16[32,4096]{1,0:T(8,128)(2,1)S(1)}, u32[]{:S(2)}, u32[]{:S(2)}) collective-permute-start(bf16[32,4096]{1,0:T(8,128)(2,1)S(1)} %get-tuple-element.105), channel_id=1, source_target_pairs={{0,4},{4,0},{8,12},{12,8},{16,20},{20,16},{24,28},{28,24},{1,5},{5... | collective-permute-start | bytes 786440 | tf_op jit(solution)/shard_map/ppermute | solution.py:369
  74.4 1.4 %collective-permute-start.27 = (f32[32,256]{1,0:T(8,128)S(1)}, f32[32,256]{1,0:T(8,128)S(1)}, u32[]{:S(2)}, u32[]{:S(2)}) collective-permute-start(f32[32,256]{1,0:T(8,128)S(1)} %chunk_sum.3.chunk), channel_id=1, source_target_pairs={{0,4},{4,0},{8,12},{12,8},{16,20},{20,16},{24,28},{28,24},{1,5},{5... | collective-permute-start | bytes 98312 | tf_op jit(solution)/shard_map/ppermute | solution.py:369
  76.3 13.3 %collective-permute-start.31 = (bf16[32,4608]{1,0:T(8,128)(2,1)S(1)}, bf16[32,4608]{1,0:T(8,128)(2,1)S(1)}, u32[]{:S(2)}, u32[]{:S(2)}) collective-permute-start(bf16[32,4608]{1,0:T(8,128)(2,1)S(1)} %get-tuple-element.106), channel_id=1, source_target_pairs={{0,8},{4,12},{8,0},{12,4},{16,24},{20,28},{24,16},{28,20},{1,9},{5... | collective-permute-start | bytes 884744 | tf_op jit(solution)/shard_map/ppermute | solution.py:369
  79.8 9.8 %collective-permute-start.32 = (bf16[32,4608]{1,0:T(8,128)(2,1)S(1)}, bf16[32,4608]{1,0:T(8,128)(2,1)S(1)}, u32[]{:S(2)}, u32[]{:S(2)}) collective-permute-start(bf16[32,4608]{1,0:T(8,128)(2,1)S(1)} %get-tuple-element.107), channel_id=1, source_target_pairs={{0,16},{4,20},{8,24},{12,28},{16,0},{20,4},{24,8},{28,12},{1,17},{... | collective-permute-start | bytes 884744 | tf_op jit(solution)/shard_map/ppermute | solution.py:369
  80.5 9.1 %collective-permute-start.33 = (bf16[32,512]{1,0:T(8,128)(2,1)S(1)}, bf16[32,512]{1,0:T(8,128)(2,1)S(1)}, u32[]{:S(2)}, u32[]{:S(2)}) collective-permute-start(bf16[32,512]{1,0:T(8,128)(2,1)S(1)} %get-tuple-element.108.refs_3_), channel_id=1, source_target_pairs={{0,24},{4,28},{8,16},{12,20},{16,8},{20,12},{24,0},{28,4},{1,25},{... | collective-permute-start | bytes 98312 | tf_op jit(solution)/shard_map/ppermute | solution.py:369
  (5 other events, 64.1 us)

commit v7 on v3

--- a/solution.py
+++ b/solution.py
@@ -308,10 +308,9 @@
     return lax.optimization_barrier((value, *earlier))[0]
 
 
-def with_chunk(rows, *parts):
-    total = functools.reduce(jnp.add, parts)
-    high = total.astype(jnp.bfloat16)
-    low = (total - high.astype(jnp.float32)).astype(jnp.bfloat16)
+def with_chunk(rows, chunk):
+    high = chunk.astype(jnp.bfloat16)
+    low = (chunk - high.astype(jnp.float32)).astype(jnp.bfloat16)
     return (jnp.concatenate([rows, jnp.concatenate([high, low], axis=1)]),)
 
 
@@ -469,11 +468,9 @@
     even, sent = fuse("gradient_sum", halves_sum, even, *[swap(part, "row", 1) for part in odd])
     even, sent = fuse("gradient_sum", halves_sum, even, swap(sent, "row", 2))
     beyond[0] = after(beyond[0], sent)
-    even = after(even, beyond[1])
+    even = after(even, beyond[1], beside)
     (chunk,) = fuse("gradient_sum", lambda a, b: ((a + b)[0],), even, swap(sent, "row", 4))
-    chunks = [chunk, swap(chunk, "col", 2)]
-
-    (second,) = fuse("with_chunk", with_chunk, beyond[1], *chunks)
+    (second,) = fuse("with_chunk", with_chunk, beyond[1], chunk)
     received = [swap(beyond[0], "col", 1), swap(second, "col", 1)]
 
     def columns(n, *earlier):
@@ -494,9 +491,9 @@
 
     own_sum, far_sum = fuse("far_sums", functools.partial(far_sums, depth), *columns(0, second))
     half_way = lax.ppermute(far_sum, "row", [(i, i ^ (4 if i % 2 else 2)) for i in range(n_row)])
-    received[1] = after(received[1], far_sum)
     (chunk,) = fuse("chunk_sum", functools.partial(chunk_sum, depth), second, received[1])
-    mine, *from_sibling = columns(1, chunk)
+    (chunk,) = fuse("chunk_sum", wide_sum, chunk, swap(chunk, "col", 2))
+    mine, *from_sibling = columns(1, chunk, far_sum)
     chunks, *near_sums = near_payloads(row, chunk, swap(chunk, "row", 1), half_way, mine, from_sibling)
     near_sums = [swap(part, "row", k) for part, k in zip(near_sums, near)]
     far_chunks = [swap(chunks, "row", k) for k in far]

time: 88.8 us -> 89.1 us (level)
  starting transfers between devices: 40.7 us -> 31.6 us
  Pallas kernels: 12.3 us -> 20.2 us
    ppermute x33, starting transfers between devices: 39.8 us -> 29.6 us  [swap(): return lax.ppermute(value, axis, [(i, i ^ k) for i in range(size)])]
    pallas_call x2, Pallas kernels: 4.16 us -> 8.36 us  [forward(): pl.pallas_call(functools.partial(forward_kernel, len(parts), depths, layo...]
    pallas_call x2, Pallas kernels: 3.66 us -> 6.82 us  [backward(): pl.pallas_call(functools.partial(backward_kernel, spots, depths), out_sha...]
    ppermute x1, starting transfers between devices: 0.98 us -> 1.92 us  [shards_exchanged(): lax.ppermute(far_sum, 'row', [(i, i ^ (4 if i % 2 else 2)) for i in range...]
  transfers between devices with their start and end apart: 34 -> 34, of which waited for: 20 -> 21; matrix products, arithmetic and copies ran while one was open for 0% -> 0% of each run, Pallas kernels for 11% -> 20%
where the time goes in v7:
time: 89.1 us
  waiting for transfers between devices  35.8 us (40%)
  starting transfers between devices  31.6 us (35%)
  Pallas kernels  20.2 us (23%)
  between operations  1.5 us (2%)
    ppermute x33, waiting for transfers between devices, swap(): return lax.ppermute(value, axis, [(i, i ^ k) for i in range(size)])  35.8 us
    ppermute x33, starting transfers between devices, swap(): return lax.ppermute(value, axis, [(i, i ^ k) for i in range(size)])  29.6 us
    pallas_call x2, Pallas kernels, forward(): pl.pallas_call(functools.partial(forward_kernel, len(parts), depths, layo...  8.36 us
    pallas_call x2, Pallas kernels, backward(): pl.pallas_call(functools.partial(backward_kernel, spots, depths), out_sha...  6.82 us
    pallas_call x1, Pallas kernels, fetch(): pl.pallas_call(fetch_kernel, out_shape=outs + [jax.ShapeDtypeStruct(tile....  2.06 us
    ppermute x1, starting transfers between devices, shards_exchanged(): lax.ppermute(far_sum, 'row', [(i, i ^ (4 if i % 2 else 2)) for i in range...  1.92 us
  transfers between devices with their start and end apart: 34, of which 21 were waited for; matrix products, arithmetic and copies ran while one was open for 0% of the time, Pallas kernels for 20%

profile of v7, /device:TPU:0, one launch (start us, length us, event | category | flops | bytes accessed | tf_op | source)
XLA Modules:
  0.0 89.1 jit_solution(8749358819527323324)
XLA Ops:
  0.6 3.0 %collective-permute-start.1 = (bf16[32,4096]{1,0:T(8,128)(2,1)}, bf16[32,4096]{1,0:T(8,128)(2,1)S(1)}, u32[]{:S(2)}, u32[]{:S(2)}) collective-permute-start(bf16[32,4096]{1,0:T(8,128)(2,1)} %bitcast.7), channel_id=1, source_target_pairs={{0,8},{4,12},{8,0},{12,4},{16,24},{20,28},{24,16},{28,20},{1,9},{5... | collective-permute-start | bytes 786440 | tf_op jit(solution)/shard_map/ppermute | solution.py:297
  3.7 1.5 %collective-permute-start.3 = (bf16[32,4096]{1,0:T(8,128)(2,1)}, bf16[32,4096]{1,0:T(8,128)(2,1)S(1)}, u32[]{:S(2)}, u32[]{:S(2)}) collective-permute-start(bf16[32,4096]{1,0:T(8,128)(2,1)} %bitcast.8), channel_id=1, source_target_pairs={{0,16},{4,20},{8,24},{12,28},{16,0},{20,4},{24,8},{28,12},{1,17},{... | collective-permute-start | bytes 786440 | tf_op jit(solution)/shard_map/ppermute | solution.py:297
  5.8 2.1 %fetch.1 = (s32[96]{0:T(128)S(1)}, s32[96]{0:T(128)S(1)}, bf16[16,4096]{1,0:T(8,128)(2,1)S(1)}, bf16[16,4096]{1,0:T(8,128)(2,1)S(1)}, bf16[96,128,128]{2,1,0:T(8,128)(2,1)S(1)}) custom-call(s32[1,1]{1,0:T(1,128)S(6)} %copy.10.count, s32[96]{0:T(128)} %bitcast.13, s32[96]{0:T(128)} %bitcast.14, bf16[32,4096]{1,0:T(8,128)(2,1)} %bitcast.10, ...), custom_call_target="tpu_custom_call" | custom-call | flops 1 | bytes 1 | tf_op jit(solution)/shard_map/fetch/pallas_call | solution.py:103
  7.9 2.3 %collective-permute-done.1.refs_2_ = bf16[32,4096]{1,0:T(8,128)(2,1)S(1)} collective-permute-done((bf16[32,4096]{1,0:T(8,128)(2,1)}, bf16[32,4096]{1,0:T(8,128)(2,1)S(1)}, u32[]{:S(2)}, u32[]{:S(2)}) %collective-permute-start.1) | collective-permute-done | bytes 262176 | tf_op jit(solution)/shard_map/ppermute | solution.py:297
  10.2 1.5 %collective-permute-done.3.refs_4_ = bf16[32,4096]{1,0:T(8,128)(2,1)S(1)} collective-permute-done((bf16[32,4096]{1,0:T(8,128)(2,1)}, bf16[32,4096]{1,0:T(8,128)(2,1)S(1)}, u32[]{:S(2)}, u32[]{:S(2)}) %collective-permute-start.3) | collective-permute-done | bytes 262176 | tf_op jit(solution)/shard_map/ppermute | solution.py:297
  11.6 1.7 %collective-permute-start.7 = (bf16[16,4096]{1,0:T(8,128)(2,1)S(1)}, bf16[16,4096]{1,0:T(8,128)(2,1)S(1)}, u32[]{:S(2)}, u32[]{:S(2)}) collective-permute-start(bf16[16,4096]{1,0:T(8,128)(2,1)S(1)} %get-tuple-element.66), channel_id=1, source_target_pairs={{0,24},{4,28},{8,16},{12,20},{16,8},{20,12},{24,0},{28,4},{1,25},{... | collective-permute-start | bytes 393224 | tf_op jit(solution)/shard_map/ppermute | solution.py:297
  13.4 1.2 %collective-permute-start.6 = (bf16[16,4096]{1,0:T(8,128)(2,1)S(1)}, bf16[16,4096]{1,0:T(8,128)(2,1)S(1)}, u32[]{:S(2)}, u32[]{:S(2)}) collective-permute-start(bf16[16,4096]{1,0:T(8,128)(2,1)S(1)} %get-tuple-element.64), channel_id=1, source_target_pairs={{0,24},{4,28},{8,16},{12,20},{16,8},{20,12},{24,0},{28,4},{1,25},{... | collective-permute-start | bytes 393224 | tf_op jit(solution)/shard_map/ppermute | solution.py:297
  14.6 4.5 %forward_products.2 = (bf16[160,512]{1,0:T(8,128)(2,1)S(1)}, bf16[160,512]{1,0:T(8,128)(2,1)S(1)}, bf16[320,512]{1,0:T(8,128)(2,1)S(1)}, bf16[32,512]{1,0:T(8,12...) custom-call(s32[1]{0:T(128)} %bitcast.1.place, s32[1,1]{1,0:T(1,128)S(6)} %copy.10.count, ...), custom_call_target="tpu_custom_call" | custom-call | flops 1 | bytes 1 | tf_op jit(solution)/shard_map/forward_products/pallas_call | solution.py:160
  19.1 2.0 %collective-permute-start.5 = (bf16[320,512]{1,0:T(8,128)(2,1)S(1)}, bf16[320,512]{1,0:T(8,128)(2,1)S(1)}, u32[]{:S(2)}, u32[]{:S(2)}) collective-permute-start(bf16[320,512]{1,0:T(8,128)(2,1)S(1)} %get-tuple-element.63), channel_id=1, source_target_pairs={{0,1},{1,0},{2,3},{3,2},{4,5},{5,4},{6,7},{7,6},{8,9},{9,8},{10,11... | collective-permute-start | bytes 983048 | tf_op jit(solution)/shard_map/ppermute | solution.py:297
  21.6 0.8 collective-permute-done.9.refs_3_
  22.6 3.9 %forward_products.3 = (bf16[96,512]{1,0:T(8,128)(2,1)S(1)}, bf16[96,512]{1,0:T(8,128)(2,1)S(1)}, bf16[192,512]{1,0:T(8,128)(2,1)S(1)}) custom-call(s32[1]{0:T(128)} %bitcast.1.place, s32[1,1]{1,0:T(1,128)S(6)} %copy.10.count, s32[96]{0:T(128)S(1)} %get-tuple-element.57.rows, s32[96]{0:T(128)S(1)} %get-tuple-element.58.cols, ...), custom_call_target="tpu_custom_call" | custom-call | flops 1 | bytes 1 | tf_op jit(solution)/shard_map/forward_products/pallas_call | solution.py:160
  26.5 1.9 %collective-permute-start.11 = (bf16[192,512]{1,0:T(8,128)(2,1)S(1)}, bf16[192,512]{1,0:T(8,128)(2,1)S(1)}, u32[]{:S(2)}, u32[]{:S(2)}) collective-permute-start(bf16[192,512]{1,0:T(8,128)(2,1)S(1)} %get-tuple-element.74), channel_id=1, source_target_pairs={{0,1},{1,0},{2,3},{3,2},{4,5},{5,4},{6,7},{7,6},{8,9},{9,8},{10,11... | collective-permute-start | bytes 589832 | tf_op jit(solution)/shard_map/ppermute | solution.py:297
  28.5 2.7 %collective-permute-start.10 = (bf16[160,512]{1,0:T(8,128)(2,1)S(1)}, bf16[160,512]{1,0:T(8,128)(2,1)S(1)}, u32[]{:S(2)}, u32[]{:S(2)}) collective-permute-start(bf16[160,512]{1,0:T(8,128)(2,1)S(1)} %pass_on.2), channel_id=1, source_target_pairs={{0,2},{1,3},{2,0},{3,1},{4,6},{5,7},{6,4},{7,5},{8,10},{9,11},{10,... | collective-permute-start | bytes 491528 | tf_op jit(solution)/shard_map/ppermute | solution.py:297
  31.1 5.8 %collective-permute-done.11.refs_1_.refs_4_ = bf16[192,512]{1,0:T(8,128)(2,1)S(1)} collective-permute-done((bf16[192,512]{1,0:T(8,128)(2,1)S(1)}, bf16[192,512]{1,0:T(8,128)(2,1)S(1)}, u32[]{:S(2)}, u32[]{:S(2)}) %collective-permute-start.11) | collective-permute-done | bytes 196640 | tf_op jit(solution)/shard_map/ppermute | solution.py:297
  37.4 5.6 %collective-permute-done.12.refs_5_ = bf16[96,512]{1,0:T(8,128)(2,1)S(1)} collective-permute-done((bf16[96,512]{1,0:T(8,128)(2,1)S(1)}, bf16[96,512]{1,0:T(8,128)(2,1)S(1)}, u32[]{:S(2)}, u32[]{:S(2)}) %collective-permute-start.12) | collective-permute-done | bytes 98336 | tf_op jit(solution)/shard_map/ppermute | solution.py:297
  43.0 1.1 %layer.1 = (bf16[512,256]{1,0:T(8,128)(2,1)}, bf16[512,256]{1,0:T(8,128)(2,1)S(1)}, bf16[256,512]{1,0:T(8,128)(2,1)S(1)}, bf16[256,512]{1,0:T(8,128)(2,1)S(1)}, ...) custom-call(s32[1]{0:T(128)} %bitcast.row, bf16[256,256]{1,0:T(8,128)(2,1)S(1)} %copy-done.2, ...), custom_call_target="tpu_custom_call" | custom-call | flops 1 | bytes 1 | tf_op jit(solution)/shard_map/layer/pallas_call | solution.py:261
  44.1 2.7 %collective-permute-start.14 = (bf16[144,512]{1,0:T(8,128)(2,1)S(1)}, bf16[144,512]{1,0:T(8,128)(2,1)S(1)}, u32[]{:S(2)}, u32[]{:S(2)}) collective-permute-start(bf16[144,512]{1,0:T(8,128)(2,1)S(1)} %get-tuple-element.79), channel_id=1, source_target_pairs={{0,2},{1,3},{2,0},{3,1},{4,6},{5,7},{6,4},{7,5},{8,10},{9,11},{10,... | collective-permute-start | bytes 442376 | tf_op jit(solution)/shard_map/ppermute | solution.py:297
  48.6 1.8 %collective-permute-start.17 = (f32[2,32,256]{2,1,0:T(8,128)S(1)}, f32[2,32,256]{2,1,0:T(8,128)S(1)}, u32[]{:S(2)}, u32[]{:S(2)}) collective-permute-start(f32[2,32,256]{2,1,0:T(8,128)S(1)} %get-tuple-element.86), channel_id=1, source_target_pairs={{0,8},{4,12},{8,0},{12,4},{16,24},{20,28},{24,16},{28,20},{1,9},{5... | collective-permute-start | bytes 196616 | tf_op jit(solution)/shard_map/ppermute | solution.py:297
  50.5 2.6 %collective-permute-done.17.refs_1_ = f32[2,32,256]{2,1,0:T(8,128)S(1)} collective-permute-done((f32[2,32,256]{2,1,0:T(8,128)S(1)}, f32[2,32,256]{2,1,0:T(8,128)S(1)}, u32[]{:S(2)}, u32[]{:S(2)}) %collective-permute-start.17) | collective-permute-done | bytes 65568 | tf_op jit(solution)/shard_map/ppermute | solution.py:297
  53.1 4.2 %collective-permute-start.20 = (bf16[144,512]{1,0:T(8,128)(2,1)S(1)}, bf16[144,512]{1,0:T(8,128)(2,1)S(1)}, u32[]{:S(2)}, u32[]{:S(2)}) collective-permute-start(bf16[144,512]{1,0:T(8,128)(2,1)S(1)} %collective-permute-done.14.refs_2_), channel_id=1, source_target_pairs={{0,1},{1,0},{2,3},{3,2},{4,5},{5,4},{6,7},{7,6},{8,9},{9,8},{10,11... | collective-permute-start | bytes 442376 | tf_op jit(solution)/shard_map/ppermute | solution.py:297
  57.3 2.8 %collective-permute-done.18.refs_0_.refs_4_ = bf16[112,512]{1,0:T(8,128)(2,1)S(1)} collective-permute-done((bf16[112,512]{1,0:T(8,128)(2,1)S(1)}, bf16[112,512]{1,0:T(8,128)(2,1)S(1)}, u32[]{:S(2)}, u32[]{:S(2)}) %collective-permute-start.18) | collective-permute-done | bytes 114720 | tf_op jit(solution)/shard_map/ppermute | solution.py:297
  60.2 1.1 %collective-permute-done.19.refs_1_ = f32[1,32,256]{2,1,0:T(8,128)S(1)} collective-permute-done((f32[1,32,256]{2,1,0:T(8,128)S(1)}, f32[1,32,256]{2,1,0:T(8,128)S(1)}, u32[]{:S(2)}, u32[]{:S(2)}) %collective-permute-start.19) | collective-permute-done | bytes 32800 | tf_op jit(solution)/shard_map/ppermute | solution.py:297
  61.4 3.4 %backward_products.2 = (bf16[64,4096]{1,0:T(8,128)(2,1)S(1)}, bf16[16,4096]{1,0:T(8,128)(2,1)S(1)}, bf16[16,4096]{1,0:T(8,128)(2,1)S(1)}, bf16[16,4096]{1,0:T(8,128)(2,1)S(1)}, bf16[16,4096]{1,0:T(8,128)(2,1)S(1)}) custom-call(s32[1]{0:T(128)} %bitcast.1.place, s32[1,1]{1,0:T(1,128)S(6)} %copy.10.count, s32[96]{0:T(128)S(1)} %get-tuple-element.57.rows, ...), custom_call_target="tpu_custom_call" | custom-call | flops 1 | bytes 1 | tf_op jit(solution)/shard_map/backward_products/pallas_call | solution.py:203
  67.1 1.9 %collective-permute-start.28 = (bf16[32,4224]{1,0:T(8,128)(2,1)S(1)}, bf16[32,4224]{1,0:T(8,128)(2,1)S(1)}, u32[]{:S(2)}, u32[]{:S(2)}) collective-permute-start(bf16[32,4224]{1,0:T(8,128)(2,1)S(1)} %get-tuple-element.99), channel_id=1, source_target_pairs={{0,8},{4,20},{8,0},{12,28},{16,24},{20,4},{24,16},{28,12},{1,9},{5... | collective-permute-start | bytes 811016 | tf_op jit(solution)/shard_map/ppermute | solution.py:493
  69.0 2.7 %collective-permute-done.26.refs_1_ = f32[32,256]{1,0:T(8,128)S(1)} collective-permute-done((f32[32,256]{1,0:T(8,128)S(1)}, f32[32,256]{1,0:T(8,128)S(1)}, u32[]{:S(2)}, u32[]{:S(2)}) %collective-permute-start.26) | collective-permute-done | bytes 32800 | tf_op jit(solution)/shard_map/ppermute | solution.py:297
  71.7 3.4 %backward_products.3 = (bf16[64,4096]{1,0:T(8,128)(2,1)S(1)}, bf16[32,4096]{1,0:T(8,128)(2,1)S(1)}, bf16[32,4096]{1,0:T(8,128)(2,1)S(1)}) custom-call(s32[1]{0:T(128)} %bitcast.1.place, s32[1,1]{1,0:T(1,128)S(6)} %copy.10.count, s32[96]{0:T(128)S(1)} %get-tuple-element.57.rows, s32[96]{0:T(128)S(1)} %get-tuple-element.58.cols, ...), custom_call_target="tpu_custom_call" | custom-call | flops 1 | bytes 1 | tf_op jit(solution)/shard_map/backward_products/pallas_call | solution.py:203
  75.8 1.4 %collective-permute-done.27.sibling = f32[32,256]{1,0:T(8,128)S(1)} collective-permute-done((f32[32,256]{1,0:T(8,128)S(1)}, f32[32,256]{1,0:T(8,128)S(1)}, u32[]{:S(2)}, u32[]{:S(2)}) %collective-permute-start.27) | collective-permute-done | bytes 32800 | tf_op jit(solution)/shard_map/ppermute | solution.py:297
  77.6 1.1 %collective-permute-start.31 = (bf16[32,4608]{1,0:T(8,128)(2,1)S(1)}, bf16[32,4608]{1,0:T(8,128)(2,1)S(1)}, u32[]{:S(2)}, u32[]{:S(2)}) collective-permute-start(bf16[32,4608]{1,0:T(8,128)(2,1)S(1)} %get-tuple-element.104), channel_id=1, source_target_pairs={{0,8},{4,12},{8,0},{12,4},{16,24},{20,28},{24,16},{28,20},{1,9},{5... | collective-permute-start | bytes 884744 | tf_op jit(solution)/shard_map/ppermute | solution.py:297
  79.0 2.1 %collective-permute-start.33 = (bf16[32,512]{1,0:T(8,128)(2,1)S(1)}, bf16[32,512]{1,0:T(8,128)(2,1)S(1)}, u32[]{:S(2)}, u32[]{:S(2)}) collective-permute-start(bf16[32,512]{1,0:T(8,128)(2,1)S(1)} %get-tuple-element.106.refs_3_), channel_id=1, source_target_pairs={{0,24},{4,28},{8,16},{12,20},{16,8},{20,12},{24,0},{28,4},{1,25},{... | collective-permute-start | bytes 98312 | tf_op jit(solution)/shard_map/ppermute | solution.py:297
  81.2 5.4 %collective-permute-done.33.refs_4_ = bf16[32,512]{1,0:T(8,128)(2,1)S(1)} collective-permute-done((bf16[32,512]{1,0:T(8,128)(2,1)S(1)}, bf16[32,512]{1,0:T(8,128)(2,1)S(1)}, u32[]{:S(2)}, u32[]{:S(2)}) %collective-permute-start.33) | collective-permute-done | bytes 32800 | tf_op jit(solution)/shard_map/ppermute | solution.py:297
  87.1 1.1 %collective-permute-done.32.refs_2_ = bf16[32,4608]{1,0:T(8,128)(2,1)S(1)} collective-permute-done((bf16[32,4608]{1,0:T(8,128)(2,1)S(1)}, bf16[32,4608]{1,0:T(8,128)(2,1)S(1)}, u32[]{:S(2)}, u32[]{:S(2)}) %collective-permute-start.32) | collective-permute-done | bytes 294944 | tf_op jit(solution)/shard_map/ppermute | solution.py:297
  88.2 0.9 %finish.1 = (bf16[32,4096]{1,0:T(8,128)(2,1)}, f32[256,256]{1,0:T(8,128)}) custom-call(s32[1]{0:T(128)} %bitcast.row, bf16[32,4096]{1,0:T(8,128)(2,1)S(1)} %get-tuple-element.98.refs_0_, bf16[32,4608]{1,0:T(8,128)(2,1)S(1)} %collective-permute-done.31.refs_1_, bf16[32,4608]{1,0:T(8,128)(2,1)S(1)} %collective-permute-done.32.refs_2_, ...), custom_call_target="tpu_custom_call" | custom-call | flops 1 | bytes 1 | tf_op jit(solution)/shard_map/finish/pallas_call | solution.py:390
  (60 shorter events, 7.3 us)
Async XLA Ops:
  0.6 9.5 %collective-permute-start.1 = (bf16[32,4096]{1,0:T(8,128)(2,1)}, bf16[32,4096]{1,0:T(8,128)(2,1)S(1)}, u32[]{:S(2)}, u32[]{:S(2)}) collective-permute-start(bf16[32,4096]{1,0:T(8,128)(2,1)} %bitcast.7), channel_id=1, source_target_pairs={{0,8},{4,12},{8,0},{12,4},{16,24},{20,28},{24,16},{28,20},{1,9},{5... | collective-permute-start | bytes 786440 | tf_op jit(solution)/shard_map/ppermute | solution.py:297
  3.7 8.0 %collective-permute-start.3 = (bf16[32,4096]{1,0:T(8,128)(2,1)}, bf16[32,4096]{1,0:T(8,128)(2,1)S(1)}, u32[]{:S(2)}, u32[]{:S(2)}) collective-permute-start(bf16[32,4096]{1,0:T(8,128)(2,1)} %bitcast.8), channel_id=1, source_target_pairs={{0,16},{4,20},{8,24},{12,28},{16,0},{20,4},{24,8},{28,12},{1,17},{... | collective-permute-start | bytes 786440 | tf_op jit(solution)/shard_map/ppermute | solution.py:297
  5.2 9.4 %collective-permute-start = (bf16[32,4096]{1,0:T(8,128)(2,1)}, bf16[32,4096]{1,0:T(8,128)(2,1)S(1)}, u32[]{:S(2)}, u32[]{:S(2)}) collective-permute-start(bf16[32,4096]{1,0:T(8,128)(2,1)} %bitcast.9), channel_id=1, source_target_pairs={{0,4},{4,0},{8,12},{12,8},{16,20},{20,16},{24,28},{28,24},{1,5},{5... | collective-permute-start | bytes 786440 | tf_op jit(solution)/shard_map/ppermute | solution.py:297
  10.2 4.4 %collective-permute-start.2 = (bf16[32,4096]{1,0:T(8,128)(2,1)S(1)}, bf16[32,4096]{1,0:T(8,128)(2,1)S(1)}, u32[]{:S(2)}, u32[]{:S(2)}) collective-permute-start(bf16[32,4096]{1,0:T(8,128)(2,1)S(1)} %collective-permute-done.1.refs_2_), channel_id=1, source_target_pairs={{0,4},{4,0},{8,12},{12,8},{16,20},{20,16},{24,28},{28,24},{1,5},{5... | collective-permute-start | bytes 786440 | tf_op jit(solution)/shard_map/ppermute | solution.py:297
  11.6 2.9 %collective-permute-start.4 = (bf16[32,4096]{1,0:T(8,128)(2,1)S(1)}, bf16[32,4096]{1,0:T(8,128)(2,1)S(1)}, u32[]{:S(2)}, u32[]{:S(2)}) collective-permute-start(bf16[32,4096]{1,0:T(8,128)(2,1)S(1)} %collective-permute-done.3.refs_4_), channel_id=1, source_target_pairs={{0,4},{4,0},{8,12},{12,8},{16,20},{20,16},{24,28},{28,24},{1,5},{5... | collective-permute-start | bytes 786440 | tf_op jit(solution)/shard_map/ppermute | solution.py:297
  11.6 9.4 %collective-permute-start.7 = (bf16[16,4096]{1,0:T(8,128)(2,1)S(1)}, bf16[16,4096]{1,0:T(8,128)(2,1)S(1)}, u32[]{:S(2)}, u32[]{:S(2)}) collective-permute-start(bf16[16,4096]{1,0:T(8,128)(2,1)S(1)} %get-tuple-element.66), channel_id=1, source_target_pairs={{0,24},{4,28},{8,16},{12,20},{16,8},{20,12},{24,0},{28,4},{1,25},{... | collective-permute-start | bytes 393224 | tf_op jit(solution)/shard_map/ppermute | solution.py:297
  13.4 7.9 %collective-permute-start.6 = (bf16[16,4096]{1,0:T(8,128)(2,1)S(1)}, bf16[16,4096]{1,0:T(8,128)(2,1)S(1)}, u32[]{:S(2)}, u32[]{:S(2)}) collective-permute-start(bf16[16,4096]{1,0:T(8,128)(2,1)S(1)} %get-tuple-element.64), channel_id=1, source_target_pairs={{0,24},{4,28},{8,16},{12,20},{16,8},{20,12},{24,0},{28,4},{1,25},{... | collective-permute-start | bytes 393224 | tf_op jit(solution)/shard_map/ppermute | solution.py:297
  19.1 9.3 %collective-permute-start.5 = (bf16[320,512]{1,0:T(8,128)(2,1)S(1)}, bf16[320,512]{1,0:T(8,128)(2,1)S(1)}, u32[]{:S(2)}, u32[]{:S(2)}) collective-permute-start(bf16[320,512]{1,0:T(8,128)(2,1)S(1)} %get-tuple-element.63), channel_id=1, source_target_pairs={{0,1},{1,0},{2,3},{3,2},{4,5},{5,4},{6,7},{7,6},{8,9},{9,8},{10,11... | collective-permute-start | bytes 983048 | tf_op jit(solution)/shard_map/ppermute | solution.py:297
  21.1 1.3 %collective-permute-start.9 = (bf16[16,4096]{1,0:T(8,128)(2,1)S(1)}, bf16[16,4096]{1,0:T(8,128)(2,1)S(1)}, u32[]{:S(2)}, u32[]{:S(2)}) collective-permute-start(bf16[16,4096]{1,0:T(8,128)(2,1)S(1)} %collective-permute-done.7.refs_1_), channel_id=1, source_target_pairs={{0,4},{4,0},{8,12},{12,8},{16,20},{20,16},{24,28},{28,24},{1,5},{5... | collective-permute-start | bytes 393224 | tf_op jit(solution)/shard_map/ppermute | solution.py:297
  21.2 1.4 %collective-permute-start.8 = (bf16[16,4096]{1,0:T(8,128)(2,1)S(1)}, bf16[16,4096]{1,0:T(8,128)(2,1)S(1)}, u32[]{:S(2)}, u32[]{:S(2)}) collective-permute-start(bf16[16,4096]{1,0:T(8,128)(2,1)S(1)} %collective-permute-done.6.refs_0_), channel_id=1, source_target_pairs={{0,4},{4,0},{8,12},{12,8},{16,20},{20,16},{24,28},{28,24},{1,5},{5... | collective-permute-start | bytes 393224 | tf_op jit(solution)/shard_map/ppermute | solution.py:297
  26.5 10.4 %collective-permute-start.11 = (bf16[192,512]{1,0:T(8,128)(2,1)S(1)}, bf16[192,512]{1,0:T(8,128)(2,1)S(1)}, u32[]{:S(2)}, u32[]{:S(2)}) collective-permute-start(bf16[192,512]{1,0:T(8,128)(2,1)S(1)} %get-tuple-element.74), channel_id=1, source_target_pairs={{0,1},{1,0},{2,3},{3,2},{4,5},{5,4},{6,7},{7,6},{8,9},{9,8},{10,11... | collective-permute-start | bytes 589832 | tf_op jit(solution)/shard_map/ppermute | solution.py:297
  28.5 14.5 %collective-permute-start.10 = (bf16[160,512]{1,0:T(8,128)(2,1)S(1)}, bf16[160,512]{1,0:T(8,128)(2,1)S(1)}, u32[]{:S(2)}, u32[]{:S(2)}) collective-permute-start(bf16[160,512]{1,0:T(8,128)(2,1)S(1)} %pass_on.2), channel_id=1, source_target_pairs={{0,2},{1,3},{2,0},{3,1},{4,6},{5,7},{6,4},{7,5},{8,10},{9,11},{10,... | collective-permute-start | bytes 491528 | tf_op jit(solution)/shard_map/ppermute | solution.py:297
  36.9 6.1 %collective-permute-start.12 = (bf16[96,512]{1,0:T(8,128)(2,1)S(1)}, bf16[96,512]{1,0:T(8,128)(2,1)S(1)}, u32[]{:S(2)}, u32[]{:S(2)}) collective-permute-start(bf16[96,512]{1,0:T(8,128)(2,1)S(1)} %pass_on.3), channel_id=1, source_target_pairs={{0,2},{1,3},{2,0},{3,1},{4,6},{5,7},{6,4},{7,5},{8,10},{9,11},{10,... | collective-permute-start | bytes 294920 | tf_op jit(solution)/shard_map/ppermute | solution.py:297
  44.1 16.0 %collective-permute-start.13 = (bf16[256,512]{1,0:T(8,128)(2,1)S(1)}, bf16[256,512]{1,0:T(8,128)(2,1)S(1)}, u32[]{:S(2)}, u32[]{:S(2)}) collective-permute-start(bf16[256,512]{1,0:T(8,128)(2,1)S(1)} %get-tuple-element.78.refs_0_), channel_id=1, source_target_pairs={{0,1},{1,0},{2,3},{3,2},{4,5},{5,4},{6,7},{7,6},{8,9},{9,8},{10,11... | collective-permute-start | bytes 786440 | tf_op jit(solution)/shard_map/ppermute | solution.py:297
  44.1 8.9 %collective-permute-start.14 = (bf16[144,512]{1,0:T(8,128)(2,1)S(1)}, bf16[144,512]{1,0:T(8,128)(2,1)S(1)}, u32[]{:S(2)}, u32[]{:S(2)}) collective-permute-start(bf16[144,512]{1,0:T(8,128)(2,1)S(1)} %get-tuple-element.79), channel_id=1, source_target_pairs={{0,2},{1,3},{2,0},{3,1},{4,6},{5,7},{6,4},{7,5},{8,10},{9,11},{10,... | collective-permute-start | bytes 442376 | tf_op jit(solution)/shard_map/ppermute | solution.py:297
  47.2 1.4 %collective-permute-start.16 = (f32[2,32,256]{2,1,0:T(8,128)S(1)}, f32[2,32,256]{2,1,0:T(8,128)S(1)}, u32[]{:S(2)}, u32[]{:S(2)}) collective-permute-start(f32[2,32,256]{2,1,0:T(8,128)S(1)} %get-tuple-element.84), channel_id=1, source_target_pairs={{0,4},{4,0},{8,12},{12,8},{16,20},{20,16},{24,28},{28,24},{1,5},{5... | collective-permute-start | bytes 196616 | tf_op jit(solution)/shard_map/ppermute | solution.py:297
  48.6 4.4 %collective-permute-start.17 = (f32[2,32,256]{2,1,0:T(8,128)S(1)}, f32[2,32,256]{2,1,0:T(8,128)S(1)}, u32[]{:S(2)}, u32[]{:S(2)}) collective-permute-start(f32[2,32,256]{2,1,0:T(8,128)S(1)} %get-tuple-element.86), channel_id=1, source_target_pairs={{0,8},{4,12},{8,0},{12,4},{16,24},{20,28},{24,16},{28,20},{1,9},{5... | collective-permute-start | bytes 196616 | tf_op jit(solution)/shard_map/ppermute | solution.py:297
  50.4 9.7 %collective-permute-start.18 = (bf16[112,512]{1,0:T(8,128)(2,1)S(1)}, bf16[112,512]{1,0:T(8,128)(2,1)S(1)}, u32[]{:S(2)}, u32[]{:S(2)}) collective-permute-start(bf16[112,512]{1,0:T(8,128)(2,1)S(1)} %get-tuple-element.89), channel_id=1, source_target_pairs={{0,2},{1,3},{2,0},{3,1},{4,6},{5,7},{6,4},{7,5},{8,10},{9,11},{10,... | collective-permute-start | bytes 344072 | tf_op jit(solution)/shard_map/ppermute | solution.py:297
  53.1 8.4 %collective-permute-start.20 = (bf16[144,512]{1,0:T(8,128)(2,1)S(1)}, bf16[144,512]{1,0:T(8,128)(2,1)S(1)}, u32[]{:S(2)}, u32[]{:S(2)}) collective-permute-start(bf16[144,512]{1,0:T(8,128)(2,1)S(1)} %collective-permute-done.14.refs_2_), channel_id=1, source_target_pairs={{0,1},{1,0},{2,3},{3,2},{4,5},{5,4},{6,7},{7,6},{8,9},{9,8},{10,11... | collective-permute-start | bytes 442376 | tf_op jit(solution)/shard_map/ppermute | solution.py:297
  57.3 3.9 %collective-permute-start.19 = (f32[1,32,256]{2,1,0:T(8,128)S(1)}, f32[1,32,256]{2,1,0:T(8,128)S(1)}, u32[]{:S(2)}, u32[]{:S(2)}) collective-permute-start(f32[1,32,256]{2,1,0:T(8,128)S(1)} %get-tuple-element.87), channel_id=1, source_target_pairs={{0,16},{4,20},{8,24},{12,28},{16,0},{20,4},{24,8},{28,12},{1,17},{... | collective-permute-start | bytes 98312 | tf_op jit(solution)/shard_map/ppermute | solution.py:297
  61.3 5.2 %collective-permute-start.25 = (bf16[144,512]{1,0:T(8,128)(2,1)S(1)}, bf16[144,512]{1,0:T(8,128)(2,1)S(1)}, u32[]{:S(2)}, u32[]{:S(2)}) collective-permute-start(bf16[144,512]{1,0:T(8,128)(2,1)S(1)} %with_chunk.1.refs_0_), channel_id=1, source_target_pairs={{0,1},{1,0},{2,3},{3,2},{4,5},{5,4},{6,7},{7,6},{8,9},{9,8},{10,11... | collective-permute-start | bytes 442376 | tf_op jit(solution)/shard_map/ppermute | solution.py:297
  64.9 1.7 %collective-permute-start.21 = (bf16[16,4096]{1,0:T(8,128)(2,1)S(1)}, bf16[16,4096]{1,0:T(8,128)(2,1)S(1)}, u32[]{:S(2)}, u32[]{:S(2)}) collective-permute-start(bf16[16,4096]{1,0:T(8,128)(2,1)S(1)} %get-tuple-element.94), channel_id=1, source_target_pairs={{0,4},{4,0},{8,12},{12,8},{16,20},{20,16},{24,28},{28,24},{1,5},{5... | collective-permute-start | bytes 393224 | tf_op jit(solution)/shard_map/ppermute | solution.py:297
  64.9 1.6 %collective-permute-start.22 = (bf16[16,4096]{1,0:T(8,128)(2,1)S(1)}, bf16[16,4096]{1,0:T(8,128)(2,1)S(1)}, u32[]{:S(2)}, u32[]{:S(2)}) collective-permute-start(bf16[16,4096]{1,0:T(8,128)(2,1)S(1)} %get-tuple-element.95), channel_id=1, source_target_pairs={{0,4},{4,0},{8,12},{12,8},{16,20},{20,16},{24,28},{28,24},{1,5},{5... | collective-permute-start | bytes 393224 | tf_op jit(solution)/shard_map/ppermute | solution.py:297
  65.5 1.5 %collective-permute-start.24 = (bf16[16,4096]{1,0:T(8,128)(2,1)S(1)}, bf16[16,4096]{1,0:T(8,128)(2,1)S(1)}, u32[]{:S(2)}, u32[]{:S(2)}) collective-permute-start(bf16[16,4096]{1,0:T(8,128)(2,1)S(1)} %get-tuple-element.97), channel_id=1, source_target_pairs={{0,4},{4,0},{8,12},{12,8},{16,20},{20,16},{24,28},{28,24},{1,5},{5... | collective-permute-start | bytes 393224 | tf_op jit(solution)/shard_map/ppermute | solution.py:297
  66.5 5.2 %collective-permute-start.26 = (f32[32,256]{1,0:T(8,128)S(1)}, f32[32,256]{1,0:T(8,128)S(1)}, u32[]{:S(2)}, u32[]{:S(2)}) collective-permute-start(f32[32,256]{1,0:T(8,128)S(1)} %chunk_sum.2.refs_0_), channel_id=1, source_target_pairs={{0,2},{1,3},{2,0},{3,1},{4,6},{5,7},{6,4},{7,5},{8,10},{9,11},{10,... | collective-permute-start | bytes 98312 | tf_op jit(solution)/shard_map/ppermute | solution.py:297
  67.1 10.0 %collective-permute-start.28 = (bf16[32,4224]{1,0:T(8,128)(2,1)S(1)}, bf16[32,4224]{1,0:T(8,128)(2,1)S(1)}, u32[]{:S(2)}, u32[]{:S(2)}) collective-permute-start(bf16[32,4224]{1,0:T(8,128)(2,1)S(1)} %get-tuple-element.99), channel_id=1, source_target_pairs={{0,8},{4,20},{8,0},{12,28},{16,24},{20,4},{24,16},{28,12},{1,9},{5... | collective-permute-start | bytes 811016 | tf_op jit(solution)/shard_map/ppermute | solution.py:493
  75.1 2.0 %collective-permute-start.29 = (bf16[32,4096]{1,0:T(8,128)(2,1)S(1)}, bf16[32,4096]{1,0:T(8,128)(2,1)S(1)}, u32[]{:S(2)}, u32[]{:S(2)}) collective-permute-start(bf16[32,4096]{1,0:T(8,128)(2,1)S(1)} %get-tuple-element.102), channel_id=1, source_target_pairs={{0,4},{4,0},{8,12},{12,8},{16,20},{20,16},{24,28},{28,24},{1,5},{5... | collective-permute-start | bytes 786440 | tf_op jit(solution)/shard_map/ppermute | solution.py:297
  75.2 2.0 %collective-permute-start.30 = (bf16[32,4096]{1,0:T(8,128)(2,1)S(1)}, bf16[32,4096]{1,0:T(8,128)(2,1)S(1)}, u32[]{:S(2)}, u32[]{:S(2)}) collective-permute-start(bf16[32,4096]{1,0:T(8,128)(2,1)S(1)} %get-tuple-element.103), channel_id=1, source_target_pairs={{0,4},{4,0},{8,12},{12,8},{16,20},{20,16},{24,28},{28,24},{1,5},{5... | collective-permute-start | bytes 786440 | tf_op jit(solution)/shard_map/ppermute | solution.py:297
  75.7 1.4 %collective-permute-start.27 = (f32[32,256]{1,0:T(8,128)S(1)}, f32[32,256]{1,0:T(8,128)S(1)}, u32[]{:S(2)}, u32[]{:S(2)}) collective-permute-start(f32[32,256]{1,0:T(8,128)S(1)} %chunk_sum.3.chunk), channel_id=1, source_target_pairs={{0,4},{4,0},{8,12},{12,8},{16,20},{20,16},{24,28},{28,24},{1,5},{5... | collective-permute-start | bytes 98312 | tf_op jit(solution)/shard_map/ppermute | solution.py:297
  77.6 9.5 %collective-permute-start.31 = (bf16[32,4608]{1,0:T(8,128)(2,1)S(1)}, bf16[32,4608]{1,0:T(8,128)(2,1)S(1)}, u32[]{:S(2)}, u32[]{:S(2)}) collective-permute-start(bf16[32,4608]{1,0:T(8,128)(2,1)S(1)} %get-tuple-element.104), channel_id=1, source_target_pairs={{0,8},{4,12},{8,0},{12,4},{16,24},{20,28},{24,16},{28,20},{1,9},{5... | collective-permute-start | bytes 884744 | tf_op jit(solution)/shard_map/ppermute | solution.py:297
  78.7 9.5 %collective-permute-start.32 = (bf16[32,4608]{1,0:T(8,128)(2,1)S(1)}, bf16[32,4608]{1,0:T(8,128)(2,1)S(1)}, u32[]{:S(2)}, u32[]{:S(2)}) collective-permute-start(bf16[32,4608]{1,0:T(8,128)(2,1)S(1)} %get-tuple-element.105), channel_id=1, source_target_pairs={{0,16},{4,20},{8,24},{12,28},{16,0},{20,4},{24,8},{28,12},{1,17},{... | collective-permute-start | bytes 884744 | tf_op jit(solution)/shard_map/ppermute | solution.py:297
  79.0 7.6 %collective-permute-start.33 = (bf16[32,512]{1,0:T(8,128)(2,1)S(1)}, bf16[32,512]{1,0:T(8,128)(2,1)S(1)}, u32[]{:S(2)}, u32[]{:S(2)}) collective-permute-start(bf16[32,512]{1,0:T(8,128)(2,1)S(1)} %get-tuple-element.106.refs_3_), channel_id=1, source_target_pairs={{0,24},{4,28},{8,16},{12,20},{16,8},{20,12},{24,0},{28,4},{1,25},{... | collective-permute-start | bytes 98312 | tf_op jit(solution)/shard_map/ppermute | solution.py:297
  (5 other events, 64.4 us)

commit v8 on v3

--- a/solution.py
+++ b/solution.py
@@ -47,7 +47,7 @@
 
 
 def product_loop(count, source_ids, target_ids, adj, source, total, dims):
-    turn = turn_of(adj.shape[0])
+    turn = math.gcd(adj.shape[0], 24)
     spare = total.shape[0] - 1
     total[...] = jnp.zeros_like(total)
 

time: 88.8 us -> 86 us (0.968); the launches traced: 89.6 us -> 85.8 us
  starting transfers between devices: 40.7 us -> 35.2 us
  Pallas kernels: 12.3 us -> 14.6 us
    ppermute x33, starting transfers between devices: 39.8 us -> 33.2 us  [swap(): return lax.ppermute(value, axis, [(i, i ^ k) for i in range(size)])]
    pallas_call x2, Pallas kernels: 4.16 us -> 5.65 us  [forward(): pl.pallas_call(functools.partial(forward_kernel, len(parts), depths, layo...]
    ppermute x1, starting transfers between devices: 0.98 us -> 1.99 us  [shards_exchanged(): lax.ppermute(far_sum, 'row', [(i, i ^ (4 if i % 2 else 2)) for i in range...]
    ppermute x33, waiting for transfers between devices: 35.1 us -> 34.1 us  [swap(): return lax.ppermute(value, axis, [(i, i ^ k) for i in range(size)])]
  transfers between devices with their start and end apart: 34 -> 34, of which waited for: 20 -> 19; matrix products, arithmetic and copies ran while one was open for 0% -> 0% of each run, Pallas kernels for 11% -> 14%
where the time goes in v8:
time: 86 us; the launch traced here: 85.8 us
  starting transfers between devices  35.2 us (41%)
  waiting for transfers between devices  34.6 us (40%)
  Pallas kernels  14.6 us (17%)
  between operations  1.46 us (2%)
    ppermute x33, waiting for transfers between devices, swap(): return lax.ppermute(value, axis, [(i, i ^ k) for i in range(size)])  34.1 us
    ppermute x33, starting transfers between devices, swap(): return lax.ppermute(value, axis, [(i, i ^ k) for i in range(size)])  33.2 us
    pallas_call x2, Pallas kernels, forward(): pl.pallas_call(functools.partial(forward_kernel, len(parts), depths, layo...  5.65 us
    pallas_call x2, Pallas kernels, backward(): pl.pallas_call(functools.partial(backward_kernel, spots, depths), out_sha...  4.14 us
    ppermute x1, starting transfers between devices, shards_exchanged(): lax.ppermute(far_sum, 'row', [(i, i ^ (4 if i % 2 else 2)) for i in range...  1.99 us
    pallas_call x1, Pallas kernels, fetch(): pl.pallas_call(fetch_kernel, out_shape=outs + [jax.ShapeDtypeStruct(tile....  1.9 us
  transfers between devices with their start and end apart: 34, of which 19 were waited for; matrix products, arithmetic and copies ran while one was open for 0% of the time, Pallas kernels for 14%

profile of v8, /device:TPU:0, one launch (start us, length us, event | category | flops | bytes accessed | tf_op | source)
XLA Modules:
  0.0 85.8 jit_solution(11183837545097977670)
XLA Ops:
  0.6 3.0 %collective-permute-start.1 = (bf16[32,4096]{1,0:T(8,128)(2,1)}, bf16[32,4096]{1,0:T(8,128)(2,1)S(1)}, u32[]{:S(2)}, u32[]{:S(2)}) collective-permute-start(bf16[32,4096]{1,0:T(8,128)(2,1)} %bitcast.7), channel_id=1, source_target_pairs={{0,8},{4,12},{8,0},{12,4},{16,24},{20,28},{24,16},{28,20},{1,9},{5... | collective-permute-start | bytes 786440 | tf_op jit(solution)/shard_map/ppermute | solution.py:297
  3.7 1.5 %collective-permute-start.3 = (bf16[32,4096]{1,0:T(8,128)(2,1)}, bf16[32,4096]{1,0:T(8,128)(2,1)S(1)}, u32[]{:S(2)}, u32[]{:S(2)}) collective-permute-start(bf16[32,4096]{1,0:T(8,128)(2,1)} %bitcast.8), channel_id=1, source_target_pairs={{0,16},{4,20},{8,24},{12,28},{16,0},{20,4},{24,8},{28,12},{1,17},{... | collective-permute-start | bytes 786440 | tf_op jit(solution)/shard_map/ppermute | solution.py:297
  5.8 1.9 %fetch.1 = (s32[96]{0:T(128)S(1)}, s32[96]{0:T(128)S(1)}, bf16[16,4096]{1,0:T(8,128)(2,1)S(1)}, bf16[16,4096]{1,0:T(8,128)(2,1)S(1)}, bf16[96,128,128]{2,1,0:T(8,128)(2,1)S(1)}) custom-call(s32[1,1]{1,0:T(1,128)S(6)} %copy.10.count, s32[96]{0:T(128)} %bitcast.13, s32[96]{0:T(128)} %bitcast.14, bf16[32,4096]{1,0:T(8,128)(2,1)} %bitcast.10, ...), custom_call_target="tpu_custom_call" | custom-call | flops 1 | bytes 1 | tf_op jit(solution)/shard_map/fetch/pallas_call | solution.py:103
  7.7 2.4 %collective-permute-done.1.refs_2_ = bf16[32,4096]{1,0:T(8,128)(2,1)S(1)} collective-permute-done((bf16[32,4096]{1,0:T(8,128)(2,1)}, bf16[32,4096]{1,0:T(8,128)(2,1)S(1)}, u32[]{:S(2)}, u32[]{:S(2)}) %collective-permute-start.1) | collective-permute-done | bytes 262176 | tf_op jit(solution)/shard_map/ppermute | solution.py:297
  10.2 1.5 %collective-permute-done.3.refs_4_ = bf16[32,4096]{1,0:T(8,128)(2,1)S(1)} collective-permute-done((bf16[32,4096]{1,0:T(8,128)(2,1)}, bf16[32,4096]{1,0:T(8,128)(2,1)S(1)}, u32[]{:S(2)}, u32[]{:S(2)}) %collective-permute-start.3) | collective-permute-done | bytes 262176 | tf_op jit(solution)/shard_map/ppermute | solution.py:297
  11.6 1.7 %collective-permute-start.7 = (bf16[16,4096]{1,0:T(8,128)(2,1)S(1)}, bf16[16,4096]{1,0:T(8,128)(2,1)S(1)}, u32[]{:S(2)}, u32[]{:S(2)}) collective-permute-start(bf16[16,4096]{1,0:T(8,128)(2,1)S(1)} %get-tuple-element.67), channel_id=1, source_target_pairs={{0,24},{4,28},{8,16},{12,20},{16,8},{20,12},{24,0},{28,4},{1,25},{... | collective-permute-start | bytes 393224 | tf_op jit(solution)/shard_map/ppermute | solution.py:297
  13.4 1.2 %collective-permute-start.6 = (bf16[16,4096]{1,0:T(8,128)(2,1)S(1)}, bf16[16,4096]{1,0:T(8,128)(2,1)S(1)}, u32[]{:S(2)}, u32[]{:S(2)}) collective-permute-start(bf16[16,4096]{1,0:T(8,128)(2,1)S(1)} %get-tuple-element.65), channel_id=1, source_target_pairs={{0,24},{4,28},{8,16},{12,20},{16,8},{20,12},{24,0},{28,4},{1,25},{... | collective-permute-start | bytes 393224 | tf_op jit(solution)/shard_map/ppermute | solution.py:297
  14.6 3.0 %forward_products.2 = (bf16[160,512]{1,0:T(8,128)(2,1)S(1)}, bf16[160,512]{1,0:T(8,128)(2,1)S(1)}, bf16[320,512]{1,0:T(8,128)(2,1)S(1)}, bf16[32,512]{1,0:T(8,12...) custom-call(s32[1]{0:T(128)} %bitcast.1.place, s32[1,1]{1,0:T(1,128)S(6)} %copy.10.count, ...), custom_call_target="tpu_custom_call" | custom-call | flops 1 | bytes 1 | tf_op jit(solution)/shard_map/forward_products/pallas_call | solution.py:160
  17.6 1.6 %collective-permute-start.5 = (bf16[320,512]{1,0:T(8,128)(2,1)S(1)}, bf16[320,512]{1,0:T(8,128)(2,1)S(1)}, u32[]{:S(2)}, u32[]{:S(2)}) collective-permute-start(bf16[320,512]{1,0:T(8,128)(2,1)S(1)} %get-tuple-element.64), channel_id=1, source_target_pairs={{0,1},{1,0},{2,3},{3,2},{4,5},{5,4},{6,7},{7,6},{8,9},{9,8},{10,11... | collective-permute-start | bytes 983048 | tf_op jit(solution)/shard_map/ppermute | solution.py:297
  19.3 2.0 %collective-permute-done.6.refs_0_ = bf16[16,4096]{1,0:T(8,128)(2,1)S(1)} collective-permute-done((bf16[16,4096]{1,0:T(8,128)(2,1)S(1)}, bf16[16,4096]{1,0:T(8,128)(2,1)S(1)}, u32[]{:S(2)}, u32[]{:S(2)}) %collective-permute-start.6) | collective-permute-done | bytes 131104 | tf_op jit(solution)/shard_map/ppermute | solution.py:297
  21.3 1.3 %collective-permute-done.8.refs_2_ = bf16[16,4096]{1,0:T(8,128)(2,1)S(1)} collective-permute-done((bf16[16,4096]{1,0:T(8,128)(2,1)S(1)}, bf16[16,4096]{1,0:T(8,128)(2,1)S(1)}, u32[]{:S(2)}, u32[]{:S(2)}) %collective-permute-start.8) | collective-permute-done | bytes 131104 | tf_op jit(solution)/shard_map/ppermute | solution.py:297
  22.6 2.6 %forward_products.3 = (bf16[96,512]{1,0:T(8,128)(2,1)S(1)}, bf16[96,512]{1,0:T(8,128)(2,1)S(1)}, bf16[192,512]{1,0:T(8,128)(2,1)S(1)}) custom-call(s32[1]{0:T(128)} %bitcast.1.place, s32[1,1]{1,0:T(1,128)S(6)} %copy.10.count, s32[96]{0:T(128)S(1)} %get-tuple-element.58.rows, s32[96]{0:T(128)S(1)} %get-tuple-element.59.cols, ...), custom_call_target="tpu_custom_call" | custom-call | flops 1 | bytes 1 | tf_op jit(solution)/shard_map/forward_products/pallas_call | solution.py:160
  25.2 1.6 %collective-permute-start.11 = (bf16[192,512]{1,0:T(8,128)(2,1)S(1)}, bf16[192,512]{1,0:T(8,128)(2,1)S(1)}, u32[]{:S(2)}, u32[]{:S(2)}) collective-permute-start(bf16[192,512]{1,0:T(8,128)(2,1)S(1)} %get-tuple-element.75), channel_id=1, source_target_pairs={{0,1},{1,0},{2,3},{3,2},{4,5},{5,4},{6,7},{7,6},{8,9},{9,8},{10,11... | collective-permute-start | bytes 589832 | tf_op jit(solution)/shard_map/ppermute | solution.py:297
  26.9 2.7 %collective-permute-start.10 = (bf16[160,512]{1,0:T(8,128)(2,1)S(1)}, bf16[160,512]{1,0:T(8,128)(2,1)S(1)}, u32[]{:S(2)}, u32[]{:S(2)}) collective-permute-start(bf16[160,512]{1,0:T(8,128)(2,1)S(1)} %pass_on.2), channel_id=1, source_target_pairs={{0,2},{1,3},{2,0},{3,1},{4,6},{5,7},{6,4},{7,5},{8,10},{9,11},{10,... | collective-permute-start | bytes 491528 | tf_op jit(solution)/shard_map/ppermute | solution.py:297
  29.6 5.5 %collective-permute-done.11.refs_1_.refs_4_ = bf16[192,512]{1,0:T(8,128)(2,1)S(1)} collective-permute-done((bf16[192,512]{1,0:T(8,128)(2,1)S(1)}, bf16[192,512]{1,0:T(8,128)(2,1)S(1)}, u32[]{:S(2)}, u32[]{:S(2)}) %collective-permute-start.11) | collective-permute-done | bytes 196640 | tf_op jit(solution)/shard_map/ppermute | solution.py:297
  35.8 5.6 %collective-permute-done.12.refs_5_ = bf16[96,512]{1,0:T(8,128)(2,1)S(1)} collective-permute-done((bf16[96,512]{1,0:T(8,128)(2,1)S(1)}, bf16[96,512]{1,0:T(8,128)(2,1)S(1)}, u32[]{:S(2)}, u32[]{:S(2)}) %collective-permute-start.12) | collective-permute-done | bytes 98336 | tf_op jit(solution)/shard_map/ppermute | solution.py:297
  41.4 1.1 %layer.1 = (bf16[512,256]{1,0:T(8,128)(2,1)}, bf16[512,256]{1,0:T(8,128)(2,1)S(1)}, bf16[256,512]{1,0:T(8,128)(2,1)S(1)}, bf16[256,512]{1,0:T(8,128)(2,1)S(1)}, ...) custom-call(s32[1]{0:T(128)} %bitcast.row, bf16[256,256]{1,0:T(8,128)(2,1)S(1)} %copy-done.2, ...), custom_call_target="tpu_custom_call" | custom-call | flops 1 | bytes 1 | tf_op jit(solution)/shard_map/layer/pallas_call | solution.py:261
  43.4 2.6 %collective-permute-start.13 = (bf16[256,512]{1,0:T(8,128)(2,1)S(1)}, bf16[256,512]{1,0:T(8,128)(2,1)S(1)}, u32[]{:S(2)}, u32[]{:S(2)}) collective-permute-start(bf16[256,512]{1,0:T(8,128)(2,1)S(1)} %get-tuple-element.79.refs_0_), channel_id=1, source_target_pairs={{0,1},{1,0},{2,3},{3,2},{4,5},{5,4},{6,7},{7,6},{8,9},{9,8},{10,11... | collective-permute-start | bytes 786440 | tf_op jit(solution)/shard_map/ppermute | solution.py:297
  46.0 1.7 %collective-permute-start.17 = (f32[2,32,256]{2,1,0:T(8,128)S(1)}, f32[2,32,256]{2,1,0:T(8,128)S(1)}, u32[]{:S(2)}, u32[]{:S(2)}) collective-permute-start(f32[2,32,256]{2,1,0:T(8,128)S(1)} %get-tuple-element.87), channel_id=1, source_target_pairs={{0,8},{4,12},{8,0},{12,4},{16,24},{20,28},{24,16},{28,20},{1,9},{5... | collective-permute-start | bytes 196616 | tf_op jit(solution)/shard_map/ppermute | solution.py:297
  47.7 1.1 %collective-permute-start.18 = (bf16[112,512]{1,0:T(8,128)(2,1)S(1)}, bf16[112,512]{1,0:T(8,128)(2,1)S(1)}, u32[]{:S(2)}, u32[]{:S(2)}) collective-permute-start(bf16[112,512]{1,0:T(8,128)(2,1)S(1)} %get-tuple-element.90), channel_id=1, source_target_pairs={{0,2},{1,3},{2,0},{3,1},{4,6},{5,7},{6,4},{7,5},{8,10},{9,11},{10,... | collective-permute-start | bytes 344072 | tf_op jit(solution)/shard_map/ppermute | solution.py:297
  48.8 1.5 %collective-permute-done.17.refs_1_ = f32[2,32,256]{2,1,0:T(8,128)S(1)} collective-permute-done((f32[2,32,256]{2,1,0:T(8,128)S(1)}, f32[2,32,256]{2,1,0:T(8,128)S(1)}, u32[]{:S(2)}, u32[]{:S(2)}) %collective-permute-start.17) | collective-permute-done | bytes 65568 | tf_op jit(solution)/shard_map/ppermute | solution.py:297
  51.4 2.0 %collective-permute-start.19 = (f32[1,32,256]{2,1,0:T(8,128)S(1)}, f32[1,32,256]{2,1,0:T(8,128)S(1)}, u32[]{:S(2)}, u32[]{:S(2)}) collective-permute-start(f32[1,32,256]{2,1,0:T(8,128)S(1)} %get-tuple-element.88), channel_id=1, source_target_pairs={{0,16},{4,20},{8,24},{12,28},{16,0},{20,4},{24,8},{28,12},{1,17},{... | collective-permute-start | bytes 98312 | tf_op jit(solution)/shard_map/ppermute | solution.py:297
  53.4 1.7 %collective-permute-done.18.refs_0_.refs_4_ = bf16[112,512]{1,0:T(8,128)(2,1)S(1)} collective-permute-done((bf16[112,512]{1,0:T(8,128)(2,1)S(1)}, bf16[112,512]{1,0:T(8,128)(2,1)S(1)}, u32[]{:S(2)}, u32[]{:S(2)}) %collective-permute-start.18) | collective-permute-done | bytes 114720 | tf_op jit(solution)/shard_map/ppermute | solution.py:297
  55.3 3.2 %collective-permute-start.20 = (f32[32,256]{1,0:T(8,128)S(1)}, f32[32,256]{1,0:T(8,128)S(1)}, u32[]{:S(2)}, u32[]{:S(2)}) collective-permute-start(f32[32,256]{1,0:T(8,128)S(1)} %gradient_sum.5.refs_1_), channel_id=1, source_target_pairs={{0,2},{1,3},{2,0},{3,1},{4,6},{5,7},{6,4},{7,5},{8,10},{9,11},{10,... | collective-permute-start | bytes 98312 | tf_op jit(solution)/shard_map/ppermute | solution.py:297
  58.6 2.0 %collective-permute-done.20.refs_2_ = f32[32,256]{1,0:T(8,128)S(1)} collective-permute-done((f32[32,256]{1,0:T(8,128)S(1)}, f32[32,256]{1,0:T(8,128)S(1)}, u32[]{:S(2)}, u32[]{:S(2)}) %collective-permute-start.20) | collective-permute-done | bytes 32800 | tf_op jit(solution)/shard_map/ppermute | solution.py:297
  60.6 2.2 %collective-permute-start.26 = (bf16[144,512]{1,0:T(8,128)(2,1)S(1)}, bf16[144,512]{1,0:T(8,128)(2,1)S(1)}, u32[]{:S(2)}, u32[]{:S(2)}) collective-permute-start(bf16[144,512]{1,0:T(8,128)(2,1)S(1)} %with_chunk.1.refs_0_), channel_id=1, source_target_pairs={{0,1},{1,0},{2,3},{3,2},{4,5},{5,4},{6,7},{7,6},{8,9},{9,8},{10,11... | collective-permute-start | bytes 442376 | tf_op jit(solution)/shard_map/ppermute | solution.py:297
  62.9 2.1 %backward_products.2 = (bf16[64,4096]{1,0:T(8,128)(2,1)S(1)}, bf16[16,4096]{1,0:T(8,128)(2,1)S(1)}, bf16[16,4096]{1,0:T(8,128)(2,1)S(1)}, bf16[16,4096]{1,0:T(8,128)(2,1)S(1)}, bf16[16,4096]{1,0:T(8,128)(2,1)S(1)}) custom-call(s32[1]{0:T(128)} %bitcast.1.place, s32[1,1]{1,0:T(1,128)S(6)} %copy.10.count, s32[96]{0:T(128)S(1)} %get-tuple-element.58.rows, ...), custom_call_target="tpu_custom_call" | custom-call | flops 1 | bytes 1 | tf_op jit(solution)/shard_map/backward_products/pallas_call | solution.py:203
  67.2 2.0 %collective-permute-start.28 = (bf16[32,4224]{1,0:T(8,128)(2,1)S(1)}, bf16[32,4224]{1,0:T(8,128)(2,1)S(1)}, u32[]{:S(2)}, u32[]{:S(2)}) collective-permute-start(bf16[32,4224]{1,0:T(8,128)(2,1)S(1)} %get-tuple-element.100), channel_id=1, source_target_pairs={{0,8},{4,20},{8,0},{12,28},{16,24},{20,4},{24,16},{28,12},{1,9},{5... | collective-permute-start | bytes 811016 | tf_op jit(solution)/shard_map/ppermute | solution.py:496
  69.2 2.1 %backward_products.3 = (bf16[64,4096]{1,0:T(8,128)(2,1)S(1)}, bf16[32,4096]{1,0:T(8,128)(2,1)S(1)}, bf16[32,4096]{1,0:T(8,128)(2,1)S(1)}) custom-call(s32[1]{0:T(128)} %bitcast.1.place, s32[1,1]{1,0:T(1,128)S(6)} %copy.10.count, s32[96]{0:T(128)S(1)} %get-tuple-element.58.rows, s32[96]{0:T(128)S(1)} %get-tuple-element.59.cols, ...), custom_call_target="tpu_custom_call" | custom-call | flops 1 | bytes 1 | tf_op jit(solution)/shard_map/backward_products/pallas_call | solution.py:203
  71.9 1.4 %collective-permute-done.27.sibling = f32[32,256]{1,0:T(8,128)S(1)} collective-permute-done((f32[32,256]{1,0:T(8,128)S(1)}, f32[32,256]{1,0:T(8,128)S(1)}, u32[]{:S(2)}, u32[]{:S(2)}) %collective-permute-start.27) | collective-permute-done | bytes 32800 | tf_op jit(solution)/shard_map/ppermute | solution.py:297
  74.1 2.0 %collective-permute-start.31 = (bf16[32,4608]{1,0:T(8,128)(2,1)S(1)}, bf16[32,4608]{1,0:T(8,128)(2,1)S(1)}, u32[]{:S(2)}, u32[]{:S(2)}) collective-permute-start(bf16[32,4608]{1,0:T(8,128)(2,1)S(1)} %get-tuple-element.106), channel_id=1, source_target_pairs={{0,8},{4,12},{8,0},{12,4},{16,24},{20,28},{24,16},{28,20},{1,9},{5... | collective-permute-start | bytes 884744 | tf_op jit(solution)/shard_map/ppermute | solution.py:297
  77.7 7.0 %collective-permute-done.33.refs_4_ = bf16[32,512]{1,0:T(8,128)(2,1)S(1)} collective-permute-done((bf16[32,512]{1,0:T(8,128)(2,1)S(1)}, bf16[32,512]{1,0:T(8,128)(2,1)S(1)}, u32[]{:S(2)}, u32[]{:S(2)}) %collective-permute-start.33) | collective-permute-done | bytes 32800 | tf_op jit(solution)/shard_map/ppermute | solution.py:297
  (59 shorter events, 9.4 us)
Async XLA Ops:
  0.6 9.5 %collective-permute-start.1 = (bf16[32,4096]{1,0:T(8,128)(2,1)}, bf16[32,4096]{1,0:T(8,128)(2,1)S(1)}, u32[]{:S(2)}, u32[]{:S(2)}) collective-permute-start(bf16[32,4096]{1,0:T(8,128)(2,1)} %bitcast.7), channel_id=1, source_target_pairs={{0,8},{4,12},{8,0},{12,4},{16,24},{20,28},{24,16},{28,20},{1,9},{5... | collective-permute-start | bytes 786440 | tf_op jit(solution)/shard_map/ppermute | solution.py:297
  3.7 8.0 %collective-permute-start.3 = (bf16[32,4096]{1,0:T(8,128)(2,1)}, bf16[32,4096]{1,0:T(8,128)(2,1)S(1)}, u32[]{:S(2)}, u32[]{:S(2)}) collective-permute-start(bf16[32,4096]{1,0:T(8,128)(2,1)} %bitcast.8), channel_id=1, source_target_pairs={{0,16},{4,20},{8,24},{12,28},{16,0},{20,4},{24,8},{28,12},{1,17},{... | collective-permute-start | bytes 786440 | tf_op jit(solution)/shard_map/ppermute | solution.py:297
  5.2 9.4 %collective-permute-start = (bf16[32,4096]{1,0:T(8,128)(2,1)}, bf16[32,4096]{1,0:T(8,128)(2,1)S(1)}, u32[]{:S(2)}, u32[]{:S(2)}) collective-permute-start(bf16[32,4096]{1,0:T(8,128)(2,1)} %bitcast.9), channel_id=1, source_target_pairs={{0,4},{4,0},{8,12},{12,8},{16,20},{20,16},{24,28},{28,24},{1,5},{5... | collective-permute-start | bytes 786440 | tf_op jit(solution)/shard_map/ppermute | solution.py:297
  10.2 4.4 %collective-permute-start.2 = (bf16[32,4096]{1,0:T(8,128)(2,1)S(1)}, bf16[32,4096]{1,0:T(8,128)(2,1)S(1)}, u32[]{:S(2)}, u32[]{:S(2)}) collective-permute-start(bf16[32,4096]{1,0:T(8,128)(2,1)S(1)} %collective-permute-done.1.refs_2_), channel_id=1, source_target_pairs={{0,4},{4,0},{8,12},{12,8},{16,20},{20,16},{24,28},{28,24},{1,5},{5... | collective-permute-start | bytes 786440 | tf_op jit(solution)/shard_map/ppermute | solution.py:297
  11.6 2.9 %collective-permute-start.4 = (bf16[32,4096]{1,0:T(8,128)(2,1)S(1)}, bf16[32,4096]{1,0:T(8,128)(2,1)S(1)}, u32[]{:S(2)}, u32[]{:S(2)}) collective-permute-start(bf16[32,4096]{1,0:T(8,128)(2,1)S(1)} %collective-permute-done.3.refs_4_), channel_id=1, source_target_pairs={{0,4},{4,0},{8,12},{12,8},{16,20},{20,16},{24,28},{28,24},{1,5},{5... | collective-permute-start | bytes 786440 | tf_op jit(solution)/shard_map/ppermute | solution.py:297
  11.6 7.6 %collective-permute-start.7 = (bf16[16,4096]{1,0:T(8,128)(2,1)S(1)}, bf16[16,4096]{1,0:T(8,128)(2,1)S(1)}, u32[]{:S(2)}, u32[]{:S(2)}) collective-permute-start(bf16[16,4096]{1,0:T(8,128)(2,1)S(1)} %get-tuple-element.67), channel_id=1, source_target_pairs={{0,24},{4,28},{8,16},{12,20},{16,8},{20,12},{24,0},{28,4},{1,25},{... | collective-permute-start | bytes 393224 | tf_op jit(solution)/shard_map/ppermute | solution.py:297
  13.4 7.9 %collective-permute-start.6 = (bf16[16,4096]{1,0:T(8,128)(2,1)S(1)}, bf16[16,4096]{1,0:T(8,128)(2,1)S(1)}, u32[]{:S(2)}, u32[]{:S(2)}) collective-permute-start(bf16[16,4096]{1,0:T(8,128)(2,1)S(1)} %get-tuple-element.65), channel_id=1, source_target_pairs={{0,24},{4,28},{8,16},{12,20},{16,8},{20,12},{24,0},{28,4},{1,25},{... | collective-permute-start | bytes 393224 | tf_op jit(solution)/shard_map/ppermute | solution.py:297
  17.6 9.3 %collective-permute-start.5 = (bf16[320,512]{1,0:T(8,128)(2,1)S(1)}, bf16[320,512]{1,0:T(8,128)(2,1)S(1)}, u32[]{:S(2)}, u32[]{:S(2)}) collective-permute-start(bf16[320,512]{1,0:T(8,128)(2,1)S(1)} %get-tuple-element.64), channel_id=1, source_target_pairs={{0,1},{1,0},{2,3},{3,2},{4,5},{5,4},{6,7},{7,6},{8,9},{9,8},{10,11... | collective-permute-start | bytes 983048 | tf_op jit(solution)/shard_map/ppermute | solution.py:297
  19.3 2.0 %collective-permute-start.9 = (bf16[16,4096]{1,0:T(8,128)(2,1)S(1)}, bf16[16,4096]{1,0:T(8,128)(2,1)S(1)}, u32[]{:S(2)}, u32[]{:S(2)}) collective-permute-start(bf16[16,4096]{1,0:T(8,128)(2,1)S(1)} %collective-permute-done.7.refs_1_), channel_id=1, source_target_pairs={{0,4},{4,0},{8,12},{12,8},{16,20},{20,16},{24,28},{28,24},{1,5},{5... | collective-permute-start | bytes 393224 | tf_op jit(solution)/shard_map/ppermute | solution.py:297
  25.2 9.9 %collective-permute-start.11 = (bf16[192,512]{1,0:T(8,128)(2,1)S(1)}, bf16[192,512]{1,0:T(8,128)(2,1)S(1)}, u32[]{:S(2)}, u32[]{:S(2)}) collective-permute-start(bf16[192,512]{1,0:T(8,128)(2,1)S(1)} %get-tuple-element.75), channel_id=1, source_target_pairs={{0,1},{1,0},{2,3},{3,2},{4,5},{5,4},{6,7},{7,6},{8,9},{9,8},{10,11... | collective-permute-start | bytes 589832 | tf_op jit(solution)/shard_map/ppermute | solution.py:297
  26.9 14.4 %collective-permute-start.10 = (bf16[160,512]{1,0:T(8,128)(2,1)S(1)}, bf16[160,512]{1,0:T(8,128)(2,1)S(1)}, u32[]{:S(2)}, u32[]{:S(2)}) collective-permute-start(bf16[160,512]{1,0:T(8,128)(2,1)S(1)} %pass_on.2), channel_id=1, source_target_pairs={{0,2},{1,3},{2,0},{3,1},{4,6},{5,7},{6,4},{7,5},{8,10},{9,11},{10,... | collective-permute-start | bytes 491528 | tf_op jit(solution)/shard_map/ppermute | solution.py:297
  35.2 6.2 %collective-permute-start.12 = (bf16[96,512]{1,0:T(8,128)(2,1)S(1)}, bf16[96,512]{1,0:T(8,128)(2,1)S(1)}, u32[]{:S(2)}, u32[]{:S(2)}) collective-permute-start(bf16[96,512]{1,0:T(8,128)(2,1)S(1)} %pass_on.3), channel_id=1, source_target_pairs={{0,2},{1,3},{2,0},{3,1},{4,6},{5,7},{6,4},{7,5},{8,10},{9,11},{10,... | collective-permute-start | bytes 294920 | tf_op jit(solution)/shard_map/ppermute | solution.py:297
  42.5 8.5 %collective-permute-start.14 = (bf16[144,512]{1,0:T(8,128)(2,1)S(1)}, bf16[144,512]{1,0:T(8,128)(2,1)S(1)}, u32[]{:S(2)}, u32[]{:S(2)}) collective-permute-start(bf16[144,512]{1,0:T(8,128)(2,1)S(1)} %get-tuple-element.80), channel_id=1, source_target_pairs={{0,2},{1,3},{2,0},{3,1},{4,6},{5,7},{6,4},{7,5},{8,10},{9,11},{10,... | collective-permute-start | bytes 442376 | tf_op jit(solution)/shard_map/ppermute | solution.py:297
  42.8 3.2 %collective-permute-start.15 = (f32[2,32,256]{2,1,0:T(8,128)S(1)}, f32[2,32,256]{2,1,0:T(8,128)S(1)}, u32[]{:S(2)}, u32[]{:S(2)}) collective-permute-start(f32[2,32,256]{2,1,0:T(8,128)S(1)} %get-tuple-element.84), channel_id=1, source_target_pairs={{0,4},{4,0},{8,12},{12,8},{16,20},{20,16},{24,28},{28,24},{1,5},{5... | collective-permute-start | bytes 196616 | tf_op jit(solution)/shard_map/ppermute | solution.py:297
  42.9 3.1 %collective-permute-start.16 = (f32[2,32,256]{2,1,0:T(8,128)S(1)}, f32[2,32,256]{2,1,0:T(8,128)S(1)}, u32[]{:S(2)}, u32[]{:S(2)}) collective-permute-start(f32[2,32,256]{2,1,0:T(8,128)S(1)} %get-tuple-element.85), channel_id=1, source_target_pairs={{0,4},{4,0},{8,12},{12,8},{16,20},{20,16},{24,28},{28,24},{1,5},{5... | collective-permute-start | bytes 196616 | tf_op jit(solution)/shard_map/ppermute | solution.py:297
  43.4 19.5 %collective-permute-start.13 = (bf16[256,512]{1,0:T(8,128)(2,1)S(1)}, bf16[256,512]{1,0:T(8,128)(2,1)S(1)}, u32[]{:S(2)}, u32[]{:S(2)}) collective-permute-start(bf16[256,512]{1,0:T(8,128)(2,1)S(1)} %get-tuple-element.79.refs_0_), channel_id=1, source_target_pairs={{0,1},{1,0},{2,3},{3,2},{4,5},{5,4},{6,7},{7,6},{8,9},{9,8},{10,11... | collective-permute-start | bytes 786440 | tf_op jit(solution)/shard_map/ppermute | solution.py:297
  46.0 4.3 %collective-permute-start.17 = (f32[2,32,256]{2,1,0:T(8,128)S(1)}, f32[2,32,256]{2,1,0:T(8,128)S(1)}, u32[]{:S(2)}, u32[]{:S(2)}) collective-permute-start(f32[2,32,256]{2,1,0:T(8,128)S(1)} %get-tuple-element.87), channel_id=1, source_target_pairs={{0,8},{4,12},{8,0},{12,4},{16,24},{20,28},{24,16},{28,20},{1,9},{5... | collective-permute-start | bytes 196616 | tf_op jit(solution)/shard_map/ppermute | solution.py:297
  47.7 7.4 %collective-permute-start.18 = (bf16[112,512]{1,0:T(8,128)(2,1)S(1)}, bf16[112,512]{1,0:T(8,128)(2,1)S(1)}, u32[]{:S(2)}, u32[]{:S(2)}) collective-permute-start(bf16[112,512]{1,0:T(8,128)(2,1)S(1)} %get-tuple-element.90), channel_id=1, source_target_pairs={{0,2},{1,3},{2,0},{3,1},{4,6},{5,7},{6,4},{7,5},{8,10},{9,11},{10,... | collective-permute-start | bytes 344072 | tf_op jit(solution)/shard_map/ppermute | solution.py:297
  51.1 11.8 %collective-permute-start.21 = (bf16[144,512]{1,0:T(8,128)(2,1)S(1)}, bf16[144,512]{1,0:T(8,128)(2,1)S(1)}, u32[]{:S(2)}, u32[]{:S(2)}) collective-permute-start(bf16[144,512]{1,0:T(8,128)(2,1)S(1)} %collective-permute-done.14.refs_2_), channel_id=1, source_target_pairs={{0,1},{1,0},{2,3},{3,2},{4,5},{5,4},{6,7},{7,6},{8,9},{9,8},{10,11... | collective-permute-start | bytes 442376 | tf_op jit(solution)/shard_map/ppermute | solution.py:297
  51.4 3.9 %collective-permute-start.19 = (f32[1,32,256]{2,1,0:T(8,128)S(1)}, f32[1,32,256]{2,1,0:T(8,128)S(1)}, u32[]{:S(2)}, u32[]{:S(2)}) collective-permute-start(f32[1,32,256]{2,1,0:T(8,128)S(1)} %get-tuple-element.88), channel_id=1, source_target_pairs={{0,16},{4,20},{8,24},{12,28},{16,0},{20,4},{24,8},{28,12},{1,17},{... | collective-permute-start | bytes 98312 | tf_op jit(solution)/shard_map/ppermute | solution.py:297
  55.3 5.3 %collective-permute-start.20 = (f32[32,256]{1,0:T(8,128)S(1)}, f32[32,256]{1,0:T(8,128)S(1)}, u32[]{:S(2)}, u32[]{:S(2)}) collective-permute-start(f32[32,256]{1,0:T(8,128)S(1)} %gradient_sum.5.refs_1_), channel_id=1, source_target_pairs={{0,2},{1,3},{2,0},{3,1},{4,6},{5,7},{6,4},{7,5},{8,10},{9,11},{10,... | collective-permute-start | bytes 98312 | tf_op jit(solution)/shard_map/ppermute | solution.py:297
  60.6 8.6 %collective-permute-start.26 = (bf16[144,512]{1,0:T(8,128)(2,1)S(1)}, bf16[144,512]{1,0:T(8,128)(2,1)S(1)}, u32[]{:S(2)}, u32[]{:S(2)}) collective-permute-start(bf16[144,512]{1,0:T(8,128)(2,1)S(1)} %with_chunk.1.refs_0_), channel_id=1, source_target_pairs={{0,1},{1,0},{2,3},{3,2},{4,5},{5,4},{6,7},{7,6},{8,9},{9,8},{10,11... | collective-permute-start | bytes 442376 | tf_op jit(solution)/shard_map/ppermute | solution.py:297
  64.9 1.4 %collective-permute-start.22 = (bf16[16,4096]{1,0:T(8,128)(2,1)S(1)}, bf16[16,4096]{1,0:T(8,128)(2,1)S(1)}, u32[]{:S(2)}, u32[]{:S(2)}) collective-permute-start(bf16[16,4096]{1,0:T(8,128)(2,1)S(1)} %get-tuple-element.95), channel_id=1, source_target_pairs={{0,4},{4,0},{8,12},{12,8},{16,20},{20,16},{24,28},{28,24},{1,5},{5... | collective-permute-start | bytes 393224 | tf_op jit(solution)/shard_map/ppermute | solution.py:297
  65.0 1.5 %collective-permute-start.23 = (bf16[16,4096]{1,0:T(8,128)(2,1)S(1)}, bf16[16,4096]{1,0:T(8,128)(2,1)S(1)}, u32[]{:S(2)}, u32[]{:S(2)}) collective-permute-start(bf16[16,4096]{1,0:T(8,128)(2,1)S(1)} %get-tuple-element.96), channel_id=1, source_target_pairs={{0,4},{4,0},{8,12},{12,8},{16,20},{20,16},{24,28},{28,24},{1,5},{5... | collective-permute-start | bytes 393224 | tf_op jit(solution)/shard_map/ppermute | solution.py:297
  65.6 1.5 %collective-permute-start.25 = (bf16[16,4096]{1,0:T(8,128)(2,1)S(1)}, bf16[16,4096]{1,0:T(8,128)(2,1)S(1)}, u32[]{:S(2)}, u32[]{:S(2)}) collective-permute-start(bf16[16,4096]{1,0:T(8,128)(2,1)S(1)} %get-tuple-element.98), channel_id=1, source_target_pairs={{0,4},{4,0},{8,12},{12,8},{16,20},{20,16},{24,28},{28,24},{1,5},{5... | collective-permute-start | bytes 393224 | tf_op jit(solution)/shard_map/ppermute | solution.py:297
  67.2 6.5 %collective-permute-start.28 = (bf16[32,4224]{1,0:T(8,128)(2,1)S(1)}, bf16[32,4224]{1,0:T(8,128)(2,1)S(1)}, u32[]{:S(2)}, u32[]{:S(2)}) collective-permute-start(bf16[32,4224]{1,0:T(8,128)(2,1)S(1)} %get-tuple-element.100), channel_id=1, source_target_pairs={{0,8},{4,20},{8,0},{12,28},{16,24},{20,4},{24,16},{28,12},{1,9},{5... | collective-permute-start | bytes 811016 | tf_op jit(solution)/shard_map/ppermute | solution.py:496
  71.3 2.0 %collective-permute-start.29 = (bf16[32,4096]{1,0:T(8,128)(2,1)S(1)}, bf16[32,4096]{1,0:T(8,128)(2,1)S(1)}, u32[]{:S(2)}, u32[]{:S(2)}) collective-permute-start(bf16[32,4096]{1,0:T(8,128)(2,1)S(1)} %get-tuple-element.104), channel_id=1, source_target_pairs={{0,4},{4,0},{8,12},{12,8},{16,20},{20,16},{24,28},{28,24},{1,5},{5... | collective-permute-start | bytes 786440 | tf_op jit(solution)/shard_map/ppermute | solution.py:297
  71.4 1.9 %collective-permute-start.30 = (bf16[32,4096]{1,0:T(8,128)(2,1)S(1)}, bf16[32,4096]{1,0:T(8,128)(2,1)S(1)}, u32[]{:S(2)}, u32[]{:S(2)}) collective-permute-start(bf16[32,4096]{1,0:T(8,128)(2,1)S(1)} %get-tuple-element.105), channel_id=1, source_target_pairs={{0,4},{4,0},{8,12},{12,8},{16,20},{20,16},{24,28},{28,24},{1,5},{5... | collective-permute-start | bytes 786440 | tf_op jit(solution)/shard_map/ppermute | solution.py:297
  71.9 1.4 %collective-permute-start.27 = (f32[32,256]{1,0:T(8,128)S(1)}, f32[32,256]{1,0:T(8,128)S(1)}, u32[]{:S(2)}, u32[]{:S(2)}) collective-permute-start(f32[32,256]{1,0:T(8,128)S(1)} %chunk_sum.1.chunk), channel_id=1, source_target_pairs={{0,4},{4,0},{8,12},{12,8},{16,20},{20,16},{24,28},{28,24},{1,5},{5... | collective-permute-start | bytes 98312 | tf_op jit(solution)/shard_map/ppermute | solution.py:297
  74.1 10.5 %collective-permute-start.31 = (bf16[32,4608]{1,0:T(8,128)(2,1)S(1)}, bf16[32,4608]{1,0:T(8,128)(2,1)S(1)}, u32[]{:S(2)}, u32[]{:S(2)}) collective-permute-start(bf16[32,4608]{1,0:T(8,128)(2,1)S(1)} %get-tuple-element.106), channel_id=1, source_target_pairs={{0,8},{4,12},{8,0},{12,4},{16,24},{20,28},{24,16},{28,20},{1,9},{5... | collective-permute-start | bytes 884744 | tf_op jit(solution)/shard_map/ppermute | solution.py:297
  76.1 8.8 %collective-permute-start.32 = (bf16[32,4608]{1,0:T(8,128)(2,1)S(1)}, bf16[32,4608]{1,0:T(8,128)(2,1)S(1)}, u32[]{:S(2)}, u32[]{:S(2)}) collective-permute-start(bf16[32,4608]{1,0:T(8,128)(2,1)S(1)} %get-tuple-element.107), channel_id=1, source_target_pairs={{0,16},{4,20},{8,24},{12,28},{16,0},{20,4},{24,8},{28,12},{1,17},{... | collective-permute-start | bytes 884744 | tf_op jit(solution)/shard_map/ppermute | solution.py:297
  77.0 7.7 %collective-permute-start.33 = (bf16[32,512]{1,0:T(8,128)(2,1)S(1)}, bf16[32,512]{1,0:T(8,128)(2,1)S(1)}, u32[]{:S(2)}, u32[]{:S(2)}) collective-permute-start(bf16[32,512]{1,0:T(8,128)(2,1)S(1)} %get-tuple-element.108.refs_3_), channel_id=1, source_target_pairs={{0,24},{4,28},{8,16},{12,20},{16,8},{20,12},{24,0},{28,4},{1,25},{... | collective-permute-start | bytes 98312 | tf_op jit(solution)/shard_map/ppermute | solution.py:297
  (5 other events, 64.2 us)

commit v9 on v8

--- a/solution.py
+++ b/solution.py
@@ -47,7 +47,7 @@
 
 
 def product_loop(count, source_ids, target_ids, adj, source, total, dims):
-    turn = math.gcd(adj.shape[0], 24)
+    turn = math.gcd(adj.shape[0], 48)
     spare = total.shape[0] - 1
     total[...] = jnp.zeros_like(total)
 

time: 86 us -> 86.4 us (level)
  waiting for transfers between devices: 34.6 us -> 32 us
  Pallas kernels: 14.6 us -> 16.1 us
  starting transfers between devices: 35.2 us -> 36.4 us
    ppermute x33, waiting for transfers between devices: 34.1 us -> 31.8 us  [swap(): return lax.ppermute(value, axis, [(i, i ^ k) for i in range(size)])]
    ppermute x33, starting transfers between devices: 33.2 us -> 34.4 us  [swap(): return lax.ppermute(value, axis, [(i, i ^ k) for i in range(size)])]
  transfers between devices with their start and end apart: 34 -> 34, of which waited for: 19 -> 18; matrix products, arithmetic and copies ran while one was open for 0% -> 0% of each run, Pallas kernels for 14% -> 16%
where the time goes in v9:
time: 86.4 us; the launch traced here: 86 us
  starting transfers between devices  36.4 us (42%)
  waiting for transfers between devices  32 us (37%)
  Pallas kernels  16.1 us (19%)
  between operations  1.47 us (2%)
    ppermute x33, starting transfers between devices, swap(): return lax.ppermute(value, axis, [(i, i ^ k) for i in range(size)])  34.4 us
    ppermute x33, waiting for transfers between devices, swap(): return lax.ppermute(value, axis, [(i, i ^ k) for i in range(size)])  31.8 us
    pallas_call x2, Pallas kernels, forward(): pl.pallas_call(functools.partial(forward_kernel, len(parts), depths, layo...  6.44 us
    pallas_call x2, Pallas kernels, backward(): pl.pallas_call(functools.partial(backward_kernel, spots, depths), out_sha...  4.53 us
    pallas_call x1, Pallas kernels, fetch(): pl.pallas_call(fetch_kernel, out_shape=outs + [jax.ShapeDtypeStruct(tile....  2.14 us
    ppermute x1, starting transfers between devices, shards_exchanged(): lax.ppermute(far_sum, 'row', [(i, i ^ (4 if i % 2 else 2)) for i in range...  2.01 us
  transfers between devices with their start and end apart: 34, of which 18 were waited for; matrix products, arithmetic and copies ran while one was open for 0% of the time, Pallas kernels for 16%

profile of v9, /device:TPU:0, one launch (start us, length us, event | category | flops | bytes accessed | tf_op | source)
XLA Modules:
  0.0 86.0 jit_solution(10076805018786566367)
XLA Ops:
  0.6 3.0 %collective-permute-start.1 = (bf16[32,4096]{1,0:T(8,128)(2,1)}, bf16[32,4096]{1,0:T(8,128)(2,1)S(1)}, u32[]{:S(2)}, u32[]{:S(2)}) collective-permute-start(bf16[32,4096]{1,0:T(8,128)(2,1)} %bitcast.7), channel_id=1, source_target_pairs={{0,8},{4,12},{8,0},{12,4},{16,24},{20,28},{24,16},{28,20},{1,9},{5... | collective-permute-start | bytes 786440 | tf_op jit(solution)/shard_map/ppermute | solution.py:297
  3.7 1.5 %collective-permute-start.3 = (bf16[32,4096]{1,0:T(8,128)(2,1)}, bf16[32,4096]{1,0:T(8,128)(2,1)S(1)}, u32[]{:S(2)}, u32[]{:S(2)}) collective-permute-start(bf16[32,4096]{1,0:T(8,128)(2,1)} %bitcast.8), channel_id=1, source_target_pairs={{0,16},{4,20},{8,24},{12,28},{16,0},{20,4},{24,8},{28,12},{1,17},{... | collective-permute-start | bytes 786440 | tf_op jit(solution)/shard_map/ppermute | solution.py:297
  5.8 2.1 %fetch.1 = (s32[96]{0:T(128)S(1)}, s32[96]{0:T(128)S(1)}, bf16[16,4096]{1,0:T(8,128)(2,1)S(1)}, bf16[16,4096]{1,0:T(8,128)(2,1)S(1)}, bf16[96,128,128]{2,1,0:T(8,128)(2,1)S(1)}) custom-call(s32[1,1]{1,0:T(1,128)S(6)} %copy.10.count, s32[96]{0:T(128)} %bitcast.13, s32[96]{0:T(128)} %bitcast.14, bf16[32,4096]{1,0:T(8,128)(2,1)} %bitcast.10, ...), custom_call_target="tpu_custom_call" | custom-call | flops 1 | bytes 1 | tf_op jit(solution)/shard_map/fetch/pallas_call | solution.py:103
  8.0 2.2 %collective-permute-done.1.refs_2_ = bf16[32,4096]{1,0:T(8,128)(2,1)S(1)} collective-permute-done((bf16[32,4096]{1,0:T(8,128)(2,1)}, bf16[32,4096]{1,0:T(8,128)(2,1)S(1)}, u32[]{:S(2)}, u32[]{:S(2)}) %collective-permute-start.1) | collective-permute-done | bytes 262176 | tf_op jit(solution)/shard_map/ppermute | solution.py:297
  10.2 1.5 %collective-permute-done.3.refs_4_ = bf16[32,4096]{1,0:T(8,128)(2,1)S(1)} collective-permute-done((bf16[32,4096]{1,0:T(8,128)(2,1)}, bf16[32,4096]{1,0:T(8,128)(2,1)S(1)}, u32[]{:S(2)}, u32[]{:S(2)}) %collective-permute-start.3) | collective-permute-done | bytes 262176 | tf_op jit(solution)/shard_map/ppermute | solution.py:297
  11.6 1.7 %collective-permute-start.7 = (bf16[16,4096]{1,0:T(8,128)(2,1)S(1)}, bf16[16,4096]{1,0:T(8,128)(2,1)S(1)}, u32[]{:S(2)}, u32[]{:S(2)}) collective-permute-start(bf16[16,4096]{1,0:T(8,128)(2,1)S(1)} %get-tuple-element.67), channel_id=1, source_target_pairs={{0,24},{4,28},{8,16},{12,20},{16,8},{20,12},{24,0},{28,4},{1,25},{... | collective-permute-start | bytes 393224 | tf_op jit(solution)/shard_map/ppermute | solution.py:297
  14.6 3.4 %forward_products.2 = (bf16[160,512]{1,0:T(8,128)(2,1)S(1)}, bf16[160,512]{1,0:T(8,128)(2,1)S(1)}, bf16[320,512]{1,0:T(8,128)(2,1)S(1)}, bf16[32,512]{1,0:T(8,12...) custom-call(s32[1]{0:T(128)} %bitcast.1.place, s32[1,1]{1,0:T(1,128)S(6)} %copy.10.count, ...), custom_call_target="tpu_custom_call" | custom-call | flops 1 | bytes 1 | tf_op jit(solution)/shard_map/forward_products/pallas_call | solution.py:160
  18.0 1.6 %collective-permute-start.5 = (bf16[320,512]{1,0:T(8,128)(2,1)S(1)}, bf16[320,512]{1,0:T(8,128)(2,1)S(1)}, u32[]{:S(2)}, u32[]{:S(2)}) collective-permute-start(bf16[320,512]{1,0:T(8,128)(2,1)S(1)} %get-tuple-element.64), channel_id=1, source_target_pairs={{0,1},{1,0},{2,3},{3,2},{4,5},{5,4},{6,7},{7,6},{8,9},{9,8},{10,11... | collective-permute-start | bytes 983048 | tf_op jit(solution)/shard_map/ppermute | solution.py:297
  19.6 1.6 %collective-permute-done.6.refs_0_ = bf16[16,4096]{1,0:T(8,128)(2,1)S(1)} collective-permute-done((bf16[16,4096]{1,0:T(8,128)(2,1)S(1)}, bf16[16,4096]{1,0:T(8,128)(2,1)S(1)}, u32[]{:S(2)}, u32[]{:S(2)}) %collective-permute-start.6) | collective-permute-done | bytes 131104 | tf_op jit(solution)/shard_map/ppermute | solution.py:297
  21.3 1.3 %collective-permute-done.8.refs_2_ = bf16[16,4096]{1,0:T(8,128)(2,1)S(1)} collective-permute-done((bf16[16,4096]{1,0:T(8,128)(2,1)S(1)}, bf16[16,4096]{1,0:T(8,128)(2,1)S(1)}, u32[]{:S(2)}, u32[]{:S(2)}) %collective-permute-start.8) | collective-permute-done | bytes 131104 | tf_op jit(solution)/shard_map/ppermute | solution.py:297
  22.6 3.1 %forward_products.3 = (bf16[96,512]{1,0:T(8,128)(2,1)S(1)}, bf16[96,512]{1,0:T(8,128)(2,1)S(1)}, bf16[192,512]{1,0:T(8,128)(2,1)S(1)}) custom-call(s32[1]{0:T(128)} %bitcast.1.place, s32[1,1]{1,0:T(1,128)S(6)} %copy.10.count, s32[96]{0:T(128)S(1)} %get-tuple-element.58.rows, s32[96]{0:T(128)S(1)} %get-tuple-element.59.cols, ...), custom_call_target="tpu_custom_call" | custom-call | flops 1 | bytes 1 | tf_op jit(solution)/shard_map/forward_products/pallas_call | solution.py:160
  25.7 1.6 %collective-permute-start.11 = (bf16[192,512]{1,0:T(8,128)(2,1)S(1)}, bf16[192,512]{1,0:T(8,128)(2,1)S(1)}, u32[]{:S(2)}, u32[]{:S(2)}) collective-permute-start(bf16[192,512]{1,0:T(8,128)(2,1)S(1)} %get-tuple-element.75), channel_id=1, source_target_pairs={{0,1},{1,0},{2,3},{3,2},{4,5},{5,4},{6,7},{7,6},{8,9},{9,8},{10,11... | collective-permute-start | bytes 589832 | tf_op jit(solution)/shard_map/ppermute | solution.py:297
  27.4 2.7 %collective-permute-start.10 = (bf16[160,512]{1,0:T(8,128)(2,1)S(1)}, bf16[160,512]{1,0:T(8,128)(2,1)S(1)}, u32[]{:S(2)}, u32[]{:S(2)}) collective-permute-start(bf16[160,512]{1,0:T(8,128)(2,1)S(1)} %pass_on.2), channel_id=1, source_target_pairs={{0,2},{1,3},{2,0},{3,1},{4,6},{5,7},{6,4},{7,5},{8,10},{9,11},{10,... | collective-permute-start | bytes 491528 | tf_op jit(solution)/shard_map/ppermute | solution.py:297
  30.0 4.6 %collective-permute-done.11.refs_1_.refs_4_ = bf16[192,512]{1,0:T(8,128)(2,1)S(1)} collective-permute-done((bf16[192,512]{1,0:T(8,128)(2,1)S(1)}, bf16[192,512]{1,0:T(8,128)(2,1)S(1)}, u32[]{:S(2)}, u32[]{:S(2)}) %collective-permute-start.11) | collective-permute-done | bytes 196640 | tf_op jit(solution)/shard_map/ppermute | solution.py:297
  34.7 1.5 %collective-permute-start.12 = (bf16[96,512]{1,0:T(8,128)(2,1)S(1)}, bf16[96,512]{1,0:T(8,128)(2,1)S(1)}, u32[]{:S(2)}, u32[]{:S(2)}) collective-permute-start(bf16[96,512]{1,0:T(8,128)(2,1)S(1)} %pass_on.3), channel_id=1, source_target_pairs={{0,2},{1,3},{2,0},{3,1},{4,6},{5,7},{6,4},{7,5},{8,10},{9,11},{10,... | collective-permute-start | bytes 294920 | tf_op jit(solution)/shard_map/ppermute | solution.py:297
  36.2 5.2 %collective-permute-done.12.refs_5_ = bf16[96,512]{1,0:T(8,128)(2,1)S(1)} collective-permute-done((bf16[96,512]{1,0:T(8,128)(2,1)S(1)}, bf16[96,512]{1,0:T(8,128)(2,1)S(1)}, u32[]{:S(2)}, u32[]{:S(2)}) %collective-permute-start.12) | collective-permute-done | bytes 98336 | tf_op jit(solution)/shard_map/ppermute | solution.py:297
  43.6 2.5 %collective-permute-start.13 = (bf16[256,512]{1,0:T(8,128)(2,1)S(1)}, bf16[256,512]{1,0:T(8,128)(2,1)S(1)}, u32[]{:S(2)}, u32[]{:S(2)}) collective-permute-start(bf16[256,512]{1,0:T(8,128)(2,1)S(1)} %get-tuple-element.79.refs_0_), channel_id=1, source_target_pairs={{0,1},{1,0},{2,3},{3,2},{4,5},{5,4},{6,7},{7,6},{8,9},{9,8},{10,11... | collective-permute-start | bytes 786440 | tf_op jit(solution)/shard_map/ppermute | solution.py:297
  46.2 2.2 %collective-permute-start.17 = (f32[2,32,256]{2,1,0:T(8,128)S(1)}, f32[2,32,256]{2,1,0:T(8,128)S(1)}, u32[]{:S(2)}, u32[]{:S(2)}) collective-permute-start(f32[2,32,256]{2,1,0:T(8,128)S(1)} %get-tuple-element.87), channel_id=1, source_target_pairs={{0,8},{4,12},{8,0},{12,4},{16,24},{20,28},{24,16},{28,20},{1,9},{5... | collective-permute-start | bytes 196616 | tf_op jit(solution)/shard_map/ppermute | solution.py:297
  49.0 1.6 %collective-permute-done.17.refs_1_ = f32[2,32,256]{2,1,0:T(8,128)S(1)} collective-permute-done((f32[2,32,256]{2,1,0:T(8,128)S(1)}, f32[2,32,256]{2,1,0:T(8,128)S(1)}, u32[]{:S(2)}, u32[]{:S(2)}) %collective-permute-start.17) | collective-permute-done | bytes 65568 | tf_op jit(solution)/shard_map/ppermute | solution.py:297
  50.6 1.3 %collective-permute-start.21 = (bf16[144,512]{1,0:T(8,128)(2,1)S(1)}, bf16[144,512]{1,0:T(8,128)(2,1)S(1)}, u32[]{:S(2)}, u32[]{:S(2)}) collective-permute-start(bf16[144,512]{1,0:T(8,128)(2,1)S(1)} %collective-permute-done.14.refs_2_), channel_id=1, source_target_pairs={{0,1},{1,0},{2,3},{3,2},{4,5},{5,4},{6,7},{7,6},{8,9},{9,8},{10,11... | collective-permute-start | bytes 442376 | tf_op jit(solution)/shard_map/ppermute | solution.py:297
  51.9 1.7 %collective-permute-start.19 = (f32[1,32,256]{2,1,0:T(8,128)S(1)}, f32[1,32,256]{2,1,0:T(8,128)S(1)}, u32[]{:S(2)}, u32[]{:S(2)}) collective-permute-start(f32[1,32,256]{2,1,0:T(8,128)S(1)} %get-tuple-element.88), channel_id=1, source_target_pairs={{0,16},{4,20},{8,24},{12,28},{16,0},{20,4},{24,8},{28,12},{1,17},{... | collective-permute-start | bytes 98312 | tf_op jit(solution)/shard_map/ppermute | solution.py:297
  53.6 2.1 %collective-permute-done.18.refs_0_.refs_4_ = bf16[112,512]{1,0:T(8,128)(2,1)S(1)} collective-permute-done((bf16[112,512]{1,0:T(8,128)(2,1)S(1)}, bf16[112,512]{1,0:T(8,128)(2,1)S(1)}, u32[]{:S(2)}, u32[]{:S(2)}) %collective-permute-start.18) | collective-permute-done | bytes 114720 | tf_op jit(solution)/shard_map/ppermute | solution.py:297
  55.9 2.9 %collective-permute-start.20 = (f32[32,256]{1,0:T(8,128)S(1)}, f32[32,256]{1,0:T(8,128)S(1)}, u32[]{:S(2)}, u32[]{:S(2)}) collective-permute-start(f32[32,256]{1,0:T(8,128)S(1)} %gradient_sum.5.refs_1_), channel_id=1, source_target_pairs={{0,2},{1,3},{2,0},{3,1},{4,6},{5,7},{6,4},{7,5},{8,10},{9,11},{10,... | collective-permute-start | bytes 98312 | tf_op jit(solution)/shard_map/ppermute | solution.py:297
  58.7 1.9 %collective-permute-done.20.refs_2_ = f32[32,256]{1,0:T(8,128)S(1)} collective-permute-done((f32[32,256]{1,0:T(8,128)S(1)}, f32[32,256]{1,0:T(8,128)S(1)}, u32[]{:S(2)}, u32[]{:S(2)}) %collective-permute-start.20) | collective-permute-done | bytes 32800 | tf_op jit(solution)/shard_map/ppermute | solution.py:297
  60.7 2.1 %collective-permute-start.26 = (bf16[144,512]{1,0:T(8,128)(2,1)S(1)}, bf16[144,512]{1,0:T(8,128)(2,1)S(1)}, u32[]{:S(2)}, u32[]{:S(2)}) collective-permute-start(bf16[144,512]{1,0:T(8,128)(2,1)S(1)} %with_chunk.1.refs_0_), channel_id=1, source_target_pairs={{0,1},{1,0},{2,3},{3,2},{4,5},{5,4},{6,7},{7,6},{8,9},{9,8},{10,11... | collective-permute-start | bytes 442376 | tf_op jit(solution)/shard_map/ppermute | solution.py:297
  62.8 2.3 %backward_products.2 = (bf16[64,4096]{1,0:T(8,128)(2,1)S(1)}, bf16[16,4096]{1,0:T(8,128)(2,1)S(1)}, bf16[16,4096]{1,0:T(8,128)(2,1)S(1)}, bf16[16,4096]{1,0:T(8,128)(2,1)S(1)}, bf16[16,4096]{1,0:T(8,128)(2,1)S(1)}) custom-call(s32[1]{0:T(128)} %bitcast.1.place, s32[1,1]{1,0:T(1,128)S(6)} %copy.10.count, s32[96]{0:T(128)S(1)} %get-tuple-element.58.rows, ...), custom_call_target="tpu_custom_call" | custom-call | flops 1 | bytes 1 | tf_op jit(solution)/shard_map/backward_products/pallas_call | solution.py:203
  67.3 2.0 %collective-permute-start.28 = (bf16[32,4224]{1,0:T(8,128)(2,1)S(1)}, bf16[32,4224]{1,0:T(8,128)(2,1)S(1)}, u32[]{:S(2)}, u32[]{:S(2)}) collective-permute-start(bf16[32,4224]{1,0:T(8,128)(2,1)S(1)} %get-tuple-element.100), channel_id=1, source_target_pairs={{0,8},{4,20},{8,0},{12,28},{16,24},{20,4},{24,16},{28,12},{1,9},{5... | collective-permute-start | bytes 811016 | tf_op jit(solution)/shard_map/ppermute | solution.py:496
  69.3 2.3 %backward_products.3 = (bf16[64,4096]{1,0:T(8,128)(2,1)S(1)}, bf16[32,4096]{1,0:T(8,128)(2,1)S(1)}, bf16[32,4096]{1,0:T(8,128)(2,1)S(1)}) custom-call(s32[1]{0:T(128)} %bitcast.1.place, s32[1,1]{1,0:T(1,128)S(6)} %copy.10.count, s32[96]{0:T(128)S(1)} %get-tuple-element.58.rows, s32[96]{0:T(128)S(1)} %get-tuple-element.59.cols, ...), custom_call_target="tpu_custom_call" | custom-call | flops 1 | bytes 1 | tf_op jit(solution)/shard_map/backward_products/pallas_call | solution.py:203
  72.3 1.4 %collective-permute-done.27.sibling = f32[32,256]{1,0:T(8,128)S(1)} collective-permute-done((f32[32,256]{1,0:T(8,128)S(1)}, f32[32,256]{1,0:T(8,128)S(1)}, u32[]{:S(2)}, u32[]{:S(2)}) %collective-permute-start.27) | collective-permute-done | bytes 32800 | tf_op jit(solution)/shard_map/ppermute | solution.py:297
  74.3 2.0 %collective-permute-start.31 = (bf16[32,4608]{1,0:T(8,128)(2,1)S(1)}, bf16[32,4608]{1,0:T(8,128)(2,1)S(1)}, u32[]{:S(2)}, u32[]{:S(2)}) collective-permute-start(bf16[32,4608]{1,0:T(8,128)(2,1)S(1)} %get-tuple-element.106), channel_id=1, source_target_pairs={{0,8},{4,12},{8,0},{12,4},{16,24},{20,28},{24,16},{28,20},{1,9},{5... | collective-permute-start | bytes 884744 | tf_op jit(solution)/shard_map/ppermute | solution.py:297
  76.3 1.5 %collective-permute-start.33 = (bf16[32,512]{1,0:T(8,128)(2,1)S(1)}, bf16[32,512]{1,0:T(8,128)(2,1)S(1)}, u32[]{:S(2)}, u32[]{:S(2)}) collective-permute-start(bf16[32,512]{1,0:T(8,128)(2,1)S(1)} %get-tuple-element.108.refs_3_), channel_id=1, source_target_pairs={{0,24},{4,28},{8,16},{12,20},{16,8},{20,12},{24,0},{28,4},{1,25},{... | collective-permute-start | bytes 98312 | tf_op jit(solution)/shard_map/ppermute | solution.py:297
  77.8 6.5 %collective-permute-done.33.refs_4_ = bf16[32,512]{1,0:T(8,128)(2,1)S(1)} collective-permute-done((bf16[32,512]{1,0:T(8,128)(2,1)S(1)}, bf16[32,512]{1,0:T(8,128)(2,1)S(1)}, u32[]{:S(2)}, u32[]{:S(2)}) %collective-permute-start.33) | collective-permute-done | bytes 32800 | tf_op jit(solution)/shard_map/ppermute | solution.py:297
  (59 shorter events, 9.6 us)
Async XLA Ops:
  0.6 9.5 %collective-permute-start.1 = (bf16[32,4096]{1,0:T(8,128)(2,1)}, bf16[32,4096]{1,0:T(8,128)(2,1)S(1)}, u32[]{:S(2)}, u32[]{:S(2)}) collective-permute-start(bf16[32,4096]{1,0:T(8,128)(2,1)} %bitcast.7), channel_id=1, source_target_pairs={{0,8},{4,12},{8,0},{12,4},{16,24},{20,28},{24,16},{28,20},{1,9},{5... | collective-permute-start | bytes 786440 | tf_op jit(solution)/shard_map/ppermute | solution.py:297
  3.7 8.0 %collective-permute-start.3 = (bf16[32,4096]{1,0:T(8,128)(2,1)}, bf16[32,4096]{1,0:T(8,128)(2,1)S(1)}, u32[]{:S(2)}, u32[]{:S(2)}) collective-permute-start(bf16[32,4096]{1,0:T(8,128)(2,1)} %bitcast.8), channel_id=1, source_target_pairs={{0,16},{4,20},{8,24},{12,28},{16,0},{20,4},{24,8},{28,12},{1,17},{... | collective-permute-start | bytes 786440 | tf_op jit(solution)/shard_map/ppermute | solution.py:297
  5.2 9.4 %collective-permute-start = (bf16[32,4096]{1,0:T(8,128)(2,1)}, bf16[32,4096]{1,0:T(8,128)(2,1)S(1)}, u32[]{:S(2)}, u32[]{:S(2)}) collective-permute-start(bf16[32,4096]{1,0:T(8,128)(2,1)} %bitcast.9), channel_id=1, source_target_pairs={{0,4},{4,0},{8,12},{12,8},{16,20},{20,16},{24,28},{28,24},{1,5},{5... | collective-permute-start | bytes 786440 | tf_op jit(solution)/shard_map/ppermute | solution.py:297
  10.2 4.4 %collective-permute-start.2 = (bf16[32,4096]{1,0:T(8,128)(2,1)S(1)}, bf16[32,4096]{1,0:T(8,128)(2,1)S(1)}, u32[]{:S(2)}, u32[]{:S(2)}) collective-permute-start(bf16[32,4096]{1,0:T(8,128)(2,1)S(1)} %collective-permute-done.1.refs_2_), channel_id=1, source_target_pairs={{0,4},{4,0},{8,12},{12,8},{16,20},{20,16},{24,28},{28,24},{1,5},{5... | collective-permute-start | bytes 786440 | tf_op jit(solution)/shard_map/ppermute | solution.py:297
  11.6 2.9 %collective-permute-start.4 = (bf16[32,4096]{1,0:T(8,128)(2,1)S(1)}, bf16[32,4096]{1,0:T(8,128)(2,1)S(1)}, u32[]{:S(2)}, u32[]{:S(2)}) collective-permute-start(bf16[32,4096]{1,0:T(8,128)(2,1)S(1)} %collective-permute-done.3.refs_4_), channel_id=1, source_target_pairs={{0,4},{4,0},{8,12},{12,8},{16,20},{20,16},{24,28},{28,24},{1,5},{5... | collective-permute-start | bytes 786440 | tf_op jit(solution)/shard_map/ppermute | solution.py:297
  11.6 8.0 %collective-permute-start.7 = (bf16[16,4096]{1,0:T(8,128)(2,1)S(1)}, bf16[16,4096]{1,0:T(8,128)(2,1)S(1)}, u32[]{:S(2)}, u32[]{:S(2)}) collective-permute-start(bf16[16,4096]{1,0:T(8,128)(2,1)S(1)} %get-tuple-element.67), channel_id=1, source_target_pairs={{0,24},{4,28},{8,16},{12,20},{16,8},{20,12},{24,0},{28,4},{1,25},{... | collective-permute-start | bytes 393224 | tf_op jit(solution)/shard_map/ppermute | solution.py:297
  13.4 7.9 %collective-permute-start.6 = (bf16[16,4096]{1,0:T(8,128)(2,1)S(1)}, bf16[16,4096]{1,0:T(8,128)(2,1)S(1)}, u32[]{:S(2)}, u32[]{:S(2)}) collective-permute-start(bf16[16,4096]{1,0:T(8,128)(2,1)S(1)} %get-tuple-element.65), channel_id=1, source_target_pairs={{0,24},{4,28},{8,16},{12,20},{16,8},{20,12},{24,0},{28,4},{1,25},{... | collective-permute-start | bytes 393224 | tf_op jit(solution)/shard_map/ppermute | solution.py:297
  18.0 9.3 %collective-permute-start.5 = (bf16[320,512]{1,0:T(8,128)(2,1)S(1)}, bf16[320,512]{1,0:T(8,128)(2,1)S(1)}, u32[]{:S(2)}, u32[]{:S(2)}) collective-permute-start(bf16[320,512]{1,0:T(8,128)(2,1)S(1)} %get-tuple-element.64), channel_id=1, source_target_pairs={{0,1},{1,0},{2,3},{3,2},{4,5},{5,4},{6,7},{7,6},{8,9},{9,8},{10,11... | collective-permute-start | bytes 983048 | tf_op jit(solution)/shard_map/ppermute | solution.py:297
  19.6 1.6 %collective-permute-start.9 = (bf16[16,4096]{1,0:T(8,128)(2,1)S(1)}, bf16[16,4096]{1,0:T(8,128)(2,1)S(1)}, u32[]{:S(2)}, u32[]{:S(2)}) collective-permute-start(bf16[16,4096]{1,0:T(8,128)(2,1)S(1)} %collective-permute-done.7.refs_1_), channel_id=1, source_target_pairs={{0,4},{4,0},{8,12},{12,8},{16,20},{20,16},{24,28},{28,24},{1,5},{5... | collective-permute-start | bytes 393224 | tf_op jit(solution)/shard_map/ppermute | solution.py:297
  25.7 9.0 %collective-permute-start.11 = (bf16[192,512]{1,0:T(8,128)(2,1)S(1)}, bf16[192,512]{1,0:T(8,128)(2,1)S(1)}, u32[]{:S(2)}, u32[]{:S(2)}) collective-permute-start(bf16[192,512]{1,0:T(8,128)(2,1)S(1)} %get-tuple-element.75), channel_id=1, source_target_pairs={{0,1},{1,0},{2,3},{3,2},{4,5},{5,4},{6,7},{7,6},{8,9},{9,8},{10,11... | collective-permute-start | bytes 589832 | tf_op jit(solution)/shard_map/ppermute | solution.py:297
  27.4 14.0 %collective-permute-start.10 = (bf16[160,512]{1,0:T(8,128)(2,1)S(1)}, bf16[160,512]{1,0:T(8,128)(2,1)S(1)}, u32[]{:S(2)}, u32[]{:S(2)}) collective-permute-start(bf16[160,512]{1,0:T(8,128)(2,1)S(1)} %pass_on.2), channel_id=1, source_target_pairs={{0,2},{1,3},{2,0},{3,1},{4,6},{5,7},{6,4},{7,5},{8,10},{9,11},{10,... | collective-permute-start | bytes 491528 | tf_op jit(solution)/shard_map/ppermute | solution.py:297
  34.7 6.6 %collective-permute-start.12 = (bf16[96,512]{1,0:T(8,128)(2,1)S(1)}, bf16[96,512]{1,0:T(8,128)(2,1)S(1)}, u32[]{:S(2)}, u32[]{:S(2)}) collective-permute-start(bf16[96,512]{1,0:T(8,128)(2,1)S(1)} %pass_on.3), channel_id=1, source_target_pairs={{0,2},{1,3},{2,0},{3,1},{4,6},{5,7},{6,4},{7,5},{8,10},{9,11},{10,... | collective-permute-start | bytes 294920 | tf_op jit(solution)/shard_map/ppermute | solution.py:297
  42.5 8.2 %collective-permute-start.14 = (bf16[144,512]{1,0:T(8,128)(2,1)S(1)}, bf16[144,512]{1,0:T(8,128)(2,1)S(1)}, u32[]{:S(2)}, u32[]{:S(2)}) collective-permute-start(bf16[144,512]{1,0:T(8,128)(2,1)S(1)} %get-tuple-element.80), channel_id=1, source_target_pairs={{0,2},{1,3},{2,0},{3,1},{4,6},{5,7},{6,4},{7,5},{8,10},{9,11},{10,... | collective-permute-start | bytes 442376 | tf_op jit(solution)/shard_map/ppermute | solution.py:297
  43.0 3.1 %collective-permute-start.15 = (f32[2,32,256]{2,1,0:T(8,128)S(1)}, f32[2,32,256]{2,1,0:T(8,128)S(1)}, u32[]{:S(2)}, u32[]{:S(2)}) collective-permute-start(f32[2,32,256]{2,1,0:T(8,128)S(1)} %get-tuple-element.84), channel_id=1, source_target_pairs={{0,4},{4,0},{8,12},{12,8},{16,20},{20,16},{24,28},{28,24},{1,5},{5... | collective-permute-start | bytes 196616 | tf_op jit(solution)/shard_map/ppermute | solution.py:297
  43.1 3.0 %collective-permute-start.16 = (f32[2,32,256]{2,1,0:T(8,128)S(1)}, f32[2,32,256]{2,1,0:T(8,128)S(1)}, u32[]{:S(2)}, u32[]{:S(2)}) collective-permute-start(f32[2,32,256]{2,1,0:T(8,128)S(1)} %get-tuple-element.85), channel_id=1, source_target_pairs={{0,4},{4,0},{8,12},{12,8},{16,20},{20,16},{24,28},{28,24},{1,5},{5... | collective-permute-start | bytes 196616 | tf_op jit(solution)/shard_map/ppermute | solution.py:297
  43.6 19.2 %collective-permute-start.13 = (bf16[256,512]{1,0:T(8,128)(2,1)S(1)}, bf16[256,512]{1,0:T(8,128)(2,1)S(1)}, u32[]{:S(2)}, u32[]{:S(2)}) collective-permute-start(bf16[256,512]{1,0:T(8,128)(2,1)S(1)} %get-tuple-element.79.refs_0_), channel_id=1, source_target_pairs={{0,1},{1,0},{2,3},{3,2},{4,5},{5,4},{6,7},{7,6},{8,9},{9,8},{10,11... | collective-permute-start | bytes 786440 | tf_op jit(solution)/shard_map/ppermute | solution.py:297
  46.2 4.4 %collective-permute-start.17 = (f32[2,32,256]{2,1,0:T(8,128)S(1)}, f32[2,32,256]{2,1,0:T(8,128)S(1)}, u32[]{:S(2)}, u32[]{:S(2)}) collective-permute-start(f32[2,32,256]{2,1,0:T(8,128)S(1)} %get-tuple-element.87), channel_id=1, source_target_pairs={{0,8},{4,12},{8,0},{12,4},{16,24},{20,28},{24,16},{28,20},{1,9},{5... | collective-permute-start | bytes 196616 | tf_op jit(solution)/shard_map/ppermute | solution.py:297
  48.3 7.4 %collective-permute-start.18 = (bf16[112,512]{1,0:T(8,128)(2,1)S(1)}, bf16[112,512]{1,0:T(8,128)(2,1)S(1)}, u32[]{:S(2)}, u32[]{:S(2)}) collective-permute-start(bf16[112,512]{1,0:T(8,128)(2,1)S(1)} %get-tuple-element.90), channel_id=1, source_target_pairs={{0,2},{1,3},{2,0},{3,1},{4,6},{5,7},{6,4},{7,5},{8,10},{9,11},{10,... | collective-permute-start | bytes 344072 | tf_op jit(solution)/shard_map/ppermute | solution.py:297
  50.6 12.2 %collective-permute-start.21 = (bf16[144,512]{1,0:T(8,128)(2,1)S(1)}, bf16[144,512]{1,0:T(8,128)(2,1)S(1)}, u32[]{:S(2)}, u32[]{:S(2)}) collective-permute-start(bf16[144,512]{1,0:T(8,128)(2,1)S(1)} %collective-permute-done.14.refs_2_), channel_id=1, source_target_pairs={{0,1},{1,0},{2,3},{3,2},{4,5},{5,4},{6,7},{7,6},{8,9},{9,8},{10,11... | collective-permute-start | bytes 442376 | tf_op jit(solution)/shard_map/ppermute | solution.py:297
  51.9 3.9 %collective-permute-start.19 = (f32[1,32,256]{2,1,0:T(8,128)S(1)}, f32[1,32,256]{2,1,0:T(8,128)S(1)}, u32[]{:S(2)}, u32[]{:S(2)}) collective-permute-start(f32[1,32,256]{2,1,0:T(8,128)S(1)} %get-tuple-element.88), channel_id=1, source_target_pairs={{0,16},{4,20},{8,24},{12,28},{16,0},{20,4},{24,8},{28,12},{1,17},{... | collective-permute-start | bytes 98312 | tf_op jit(solution)/shard_map/ppermute | solution.py:297
  55.9 4.8 %collective-permute-start.20 = (f32[32,256]{1,0:T(8,128)S(1)}, f32[32,256]{1,0:T(8,128)S(1)}, u32[]{:S(2)}, u32[]{:S(2)}) collective-permute-start(f32[32,256]{1,0:T(8,128)S(1)} %gradient_sum.5.refs_1_), channel_id=1, source_target_pairs={{0,2},{1,3},{2,0},{3,1},{4,6},{5,7},{6,4},{7,5},{8,10},{9,11},{10,... | collective-permute-start | bytes 98312 | tf_op jit(solution)/shard_map/ppermute | solution.py:297
  60.7 8.6 %collective-permute-start.26 = (bf16[144,512]{1,0:T(8,128)(2,1)S(1)}, bf16[144,512]{1,0:T(8,128)(2,1)S(1)}, u32[]{:S(2)}, u32[]{:S(2)}) collective-permute-start(bf16[144,512]{1,0:T(8,128)(2,1)S(1)} %with_chunk.1.refs_0_), channel_id=1, source_target_pairs={{0,1},{1,0},{2,3},{3,2},{4,5},{5,4},{6,7},{7,6},{8,9},{9,8},{10,11... | collective-permute-start | bytes 442376 | tf_op jit(solution)/shard_map/ppermute | solution.py:297
  65.1 1.4 %collective-permute-start.22 = (bf16[16,4096]{1,0:T(8,128)(2,1)S(1)}, bf16[16,4096]{1,0:T(8,128)(2,1)S(1)}, u32[]{:S(2)}, u32[]{:S(2)}) collective-permute-start(bf16[16,4096]{1,0:T(8,128)(2,1)S(1)} %get-tuple-element.95), channel_id=1, source_target_pairs={{0,4},{4,0},{8,12},{12,8},{16,20},{20,16},{24,28},{28,24},{1,5},{5... | collective-permute-start | bytes 393224 | tf_op jit(solution)/shard_map/ppermute | solution.py:297
  65.1 1.5 %collective-permute-start.23 = (bf16[16,4096]{1,0:T(8,128)(2,1)S(1)}, bf16[16,4096]{1,0:T(8,128)(2,1)S(1)}, u32[]{:S(2)}, u32[]{:S(2)}) collective-permute-start(bf16[16,4096]{1,0:T(8,128)(2,1)S(1)} %get-tuple-element.96), channel_id=1, source_target_pairs={{0,4},{4,0},{8,12},{12,8},{16,20},{20,16},{24,28},{28,24},{1,5},{5... | collective-permute-start | bytes 393224 | tf_op jit(solution)/shard_map/ppermute | solution.py:297
  65.7 1.5 %collective-permute-start.25 = (bf16[16,4096]{1,0:T(8,128)(2,1)S(1)}, bf16[16,4096]{1,0:T(8,128)(2,1)S(1)}, u32[]{:S(2)}, u32[]{:S(2)}) collective-permute-start(bf16[16,4096]{1,0:T(8,128)(2,1)S(1)} %get-tuple-element.98), channel_id=1, source_target_pairs={{0,4},{4,0},{8,12},{12,8},{16,20},{20,16},{24,28},{28,24},{1,5},{5... | collective-permute-start | bytes 393224 | tf_op jit(solution)/shard_map/ppermute | solution.py:297
  67.3 6.5 %collective-permute-start.28 = (bf16[32,4224]{1,0:T(8,128)(2,1)S(1)}, bf16[32,4224]{1,0:T(8,128)(2,1)S(1)}, u32[]{:S(2)}, u32[]{:S(2)}) collective-permute-start(bf16[32,4224]{1,0:T(8,128)(2,1)S(1)} %get-tuple-element.100), channel_id=1, source_target_pairs={{0,8},{4,20},{8,0},{12,28},{16,24},{20,4},{24,16},{28,12},{1,9},{5... | collective-permute-start | bytes 811016 | tf_op jit(solution)/shard_map/ppermute | solution.py:496
  71.6 2.0 %collective-permute-start.29 = (bf16[32,4096]{1,0:T(8,128)(2,1)S(1)}, bf16[32,4096]{1,0:T(8,128)(2,1)S(1)}, u32[]{:S(2)}, u32[]{:S(2)}) collective-permute-start(bf16[32,4096]{1,0:T(8,128)(2,1)S(1)} %get-tuple-element.104), channel_id=1, source_target_pairs={{0,4},{4,0},{8,12},{12,8},{16,20},{20,16},{24,28},{28,24},{1,5},{5... | collective-permute-start | bytes 786440 | tf_op jit(solution)/shard_map/ppermute | solution.py:297
  71.7 1.9 %collective-permute-start.30 = (bf16[32,4096]{1,0:T(8,128)(2,1)S(1)}, bf16[32,4096]{1,0:T(8,128)(2,1)S(1)}, u32[]{:S(2)}, u32[]{:S(2)}) collective-permute-start(bf16[32,4096]{1,0:T(8,128)(2,1)S(1)} %get-tuple-element.105), channel_id=1, source_target_pairs={{0,4},{4,0},{8,12},{12,8},{16,20},{20,16},{24,28},{28,24},{1,5},{5... | collective-permute-start | bytes 786440 | tf_op jit(solution)/shard_map/ppermute | solution.py:297
  72.2 1.4 %collective-permute-start.27 = (f32[32,256]{1,0:T(8,128)S(1)}, f32[32,256]{1,0:T(8,128)S(1)}, u32[]{:S(2)}, u32[]{:S(2)}) collective-permute-start(f32[32,256]{1,0:T(8,128)S(1)} %chunk_sum.1.chunk), channel_id=1, source_target_pairs={{0,4},{4,0},{8,12},{12,8},{16,20},{20,16},{24,28},{28,24},{1,5},{5... | collective-permute-start | bytes 98312 | tf_op jit(solution)/shard_map/ppermute | solution.py:297
  74.3 10.1 %collective-permute-start.31 = (bf16[32,4608]{1,0:T(8,128)(2,1)S(1)}, bf16[32,4608]{1,0:T(8,128)(2,1)S(1)}, u32[]{:S(2)}, u32[]{:S(2)}) collective-permute-start(bf16[32,4608]{1,0:T(8,128)(2,1)S(1)} %get-tuple-element.106), channel_id=1, source_target_pairs={{0,8},{4,12},{8,0},{12,4},{16,24},{20,28},{24,16},{28,20},{1,9},{5... | collective-permute-start | bytes 884744 | tf_op jit(solution)/shard_map/ppermute | solution.py:297
  76.3 8.8 %collective-permute-start.32 = (bf16[32,4608]{1,0:T(8,128)(2,1)S(1)}, bf16[32,4608]{1,0:T(8,128)(2,1)S(1)}, u32[]{:S(2)}, u32[]{:S(2)}) collective-permute-start(bf16[32,4608]{1,0:T(8,128)(2,1)S(1)} %get-tuple-element.107), channel_id=1, source_target_pairs={{0,16},{4,20},{8,24},{12,28},{16,0},{20,4},{24,8},{28,12},{1,17},{... | collective-permute-start | bytes 884744 | tf_op jit(solution)/shard_map/ppermute | solution.py:297
  76.3 8.0 %collective-permute-start.33 = (bf16[32,512]{1,0:T(8,128)(2,1)S(1)}, bf16[32,512]{1,0:T(8,128)(2,1)S(1)}, u32[]{:S(2)}, u32[]{:S(2)}) collective-permute-start(bf16[32,512]{1,0:T(8,128)(2,1)S(1)} %get-tuple-element.108.refs_3_), channel_id=1, source_target_pairs={{0,24},{4,28},{8,16},{12,20},{16,8},{20,12},{24,0},{28,4},{1,25},{... | collective-permute-start | bytes 98312 | tf_op jit(solution)/shard_map/ppermute | solution.py:297
  (5 other events, 63.4 us)
